TPU v7x, 256 devices: a whole 4x4x8 slice. The times are simulated.
256 devices in a mesh: seq: 32 (over z, x), mp: 8 (over y, core), dp: 1.
Axes of the slice: x: 4, y: 4, z: 8, core: 2. Of those that a mesh axis runs over, the one named last changes fastest.
Arguments:
- tokens: bfloat16 [65536, 4096], P(('dp', 'seq'), 'mp'), may hold values from -6 to 6
- flags: int32 [65536], P(('dp', 'seq')), may hold values from 0 to 1, as said below
- norm_gain: float32 [4096], replicated, may hold values from 0.5 to 1.5
- w_query: bfloat16 [4096, 2048], P(None, 'mp'), may hold values from -0.09375 to 0.09375
- w_key: bfloat16 [4096, 2048], P(None, 'mp'), may hold values from -0.09375 to 0.09375
- w_value: bfloat16 [4096, 2048], P(None, 'mp'), may hold values from -0.09375 to 0.09375
- w_out: bfloat16 [2048, 4096], P('mp'), may hold values from -0.5 to 0.5
Outputs:
- upsampled: bfloat16 [65536, 4096], P(('dp', 'seq'), 'mp')
Inputs may be any that keep to these rules, and one draw needn't show every extreme that they name: flags of the first token is 1, and each aligned block of 2048 tokens holds exactly 256 flags equal to 1.
All inputs are finite; a program needn't handle non-finite values.
Results may differ from a plain program's by a relative error of at most 0.019.
Values may be sent and summed in bfloat16 or wider, within the bound.
No kernel may reach another device: no remote copies, remote signals or barrier semaphores. Data moves between devices by JAX's collectives and lax.ppermute only.
A program may use at most 128 MiB of HBM per device.

v0:
```python
import functools

import jax
import jax.numpy as jnp
import numpy as np
from jax import lax
from jax.experimental import pallas as pl
from jax.experimental.pallas import tpu as pltpu
from jax.sharding import PartitionSpec as P

HD = 128
NZ, NX, NY, NC = 8, 4, 4, 2
SEG = 256
ROWS = SEG + 16
TOK = 2048
FEAT = 512
COLS = 256
WIDTH = 4096
SCORE = 1.4426950408889634 * HD**-0.5
LOG2E = 1.4426950408889634
LOW = -1e30
VMEM_LIMIT = 20 * 1024 * 1024
F32, BF16 = jnp.float32, jnp.bfloat16


def number(z, x, y, c):
    return ((z % NZ) * NX + x % NX) * (NY * NC) + (y % NY) * NC + c % NC


def everywhere():
    return [(z, x, y, c) for z in range(NZ) for x in range(NX) for y in range(NY) for c in range(NC)]


def way(c):
    return 1 if c == 0 else -1


def move(value, target):
    pairs = [(number(*d), number(*target(*d))) for d in everywhere()]
    return lax.ppermute(value, ("seq", "mp"), pairs)


def swap(value):
    return move(value, lambda z, x, y, c: (z, x, y, 1 - c))


def y_one(value):
    return move(value, lambda z, x, y, c: (z, x, y + way(c), c))


def y_other(value):
    return move(value, lambda z, x, y, c: (z, x, y - way(c), c))


def z_one(value):
    return move(value, lambda z, x, y, c: (z + way(c), x, y, c))


def z_other(value):
    return move(value, lambda z, x, y, c: (z - way(c), x, y, c))


def x_by(value, by):
    return move(value, lambda z, x, y, c: (z, x + by, y, c))


def sources(y, c):
    own = [(y, c), (y - way(c), c), (y + way(c), c), (y + 2, c)]
    o = 1 - c
    other = [(y, o), (y - way(o), o), (y + way(o), o), (y + 2, o)]
    return [((b[0] % NY) * NC + b[1]) for b in own + other]


def mp_exchange(value):
    first = y_one(value)
    second = y_other(value)
    sibling = swap(value)
    far = y_one(first)
    return [value, first, second, far, sibling, swap(first), swap(second), swap(far)]


def device_table():
    rows = []
    for z, x, y, c in everywhere():
        row = [y * NC + c] + sources(y, c)
        row += [x] + [(x - k) % NX for k in (1, 2, 3)]
        for k in (1, 2, 3, 4):
            row += [int((z - way(c) * k) % NZ < z), int((z + way(c) * k) % NZ < z)]
        for o in (c, 1 - c):
            row += [(v % NY) * NC + o for v in (y, y + way(o), y - way(o), y + 2)]
        row += [0] * (32 - len(row))
        rows.append(row)
    return np.asarray(rows, np.int32)


I_MP, I_SRC, I_X, I_OK, I_CUT = 0, 1, 9, 13, 21
SMEM = pl.BlockSpec(memory_space=pltpu.SMEM)
WHOLE = pl.BlockSpec(memory_space=pltpu.VMEM)
FAR = pl.BlockSpec(memory_space=pl.ANY)
DISTANT = pl.BlockSpec(memory_space=pltpu.HBM)


def call(body, outs, ins, flops=0, moved=0, scratch=(), aliases=None, far_in=(), far_out=(), far=FAR):
    return pl.pallas_call(
        body,
        out_shape=outs,
        in_specs=[SMEM] + [far if i in far_in else WHOLE for i in range(1, len(ins))],
        out_specs=[far if i in far_out else WHOLE for i in range(len(outs))],
        scratch_shapes=list(scratch),
        input_output_aliases=aliases or {},
        compiler_params=pltpu.CompilerParams(vmem_limit_bytes=VMEM_LIMIT),
        cost_estimate=pl.CostEstimate(flops=flops, bytes_accessed=moved, transcendentals=0),
    )(*ins)


def gate_kernel(info, *refs):
    pass


def gate(info, values, token):
    ins = [info] + list(values) + [token]
    count = len(values)
    return call(
        gate_kernel,
        [shape(v.shape, v.dtype) for v in values],
        ins,
        aliases={i + 1: i for i in range(count)},
        far_in=range(1, count + 2),
        far_out=range(count),
    )


def shape(dims, dtype):
    return jax.ShapeDtypeStruct(dims, dtype)


def dot(a, b):
    return jnp.dot(a, b, preferred_element_type=F32)


def iota(dims, axis):
    return lax.broadcasted_iota(jnp.int32, dims, axis)


def ones_where(condition):
    return jnp.where(condition, 1.0, 0.0).astype(BF16)


def edge_kernel(info, flags, tokens, ids_out, head_out, tail_out, marks):
    f = flags[...].astype(F32).astype(BF16)
    upto = ones_where(iota((128, 128), 0) <= iota((128, 128), 1))
    inside = dot(f, upto)
    rows = dot(f, jnp.ones((128, 128), BF16)).astype(BF16)
    before = dot(ones_where(iota((16, 16), 1) < iota((16, 16), 0)), rows)
    ids_out[...] = (inside + before - 1.0).astype(jnp.int32)
    wanted = jnp.where(iota((16, 128), 0) < 8, -1, SEG - 1)
    for r in range(16):
        marks[:, r * 128 : (r + 1) * 128] = ones_where(ids_out[r : r + 1, :] == wanted)
    sums = dot(marks[...], tokens[...])
    counts = dot(marks[...], jnp.ones((TOK, 128), BF16))
    head_out[:, :FEAT] = sums[:8]
    head_out[:, FEAT:] = counts[:8]
    tail_out[:, :FEAT] = sums[8:]
    tail_out[:, FEAT:] = counts[8:]


def pool_kernel(info, ids, tokens, sums_out, counts_out, hot):
    segment = iota((SEG, 128), 0)
    for r in range(16):
        hot[:, r * 128 : (r + 1) * 128] = ones_where(ids[r : r + 1, :] == segment)
    sums_out[...] = dot(hot[...], tokens[...])
    counts_out[...] = dot(hot[...], jnp.ones((TOK, 128), BF16))


def wide(column, times):
    return jnp.concatenate([column] * times, axis=1)


def split(value, parts):
    out = []
    for _ in range(parts):
        high = value.astype(BF16).astype(F32)
        out.append(high)
        value = value - high
    return out


def norm_kernel(info, sums, counts, head, above, below, gain, means_out, u_out, bias_out):
    g = gain[pl.ds(info[I_MP], 1), :]
    last = iota((SEG, 128), 0) == SEG - 1
    size = counts[...] + jnp.where(last, above[0:1, FEAT:], 0.0)
    total = sums[...] + jnp.where(iota((SEG, FEAT), 0) == SEG - 1, above[0:1, :FEAT], 0.0)
    size = jnp.maximum(size, 1.0)
    means = total / wide(size, 4)
    means_out[:SEG, :] = means
    u_out[:SEG, :] = (means * g).astype(BF16)
    squares = jnp.sum(means * means, axis=1, keepdims=True)
    squares = jnp.transpose(jnp.broadcast_to(squares, (SEG, 128)))[:16]
    high, low = split(squares, 2)
    extra_size = jnp.maximum(head[0:1, FEAT:] + below[0:1, FEAT:], 1.0)
    extra = (head[0:1, :FEAT] + below[0:1, :FEAT]) / wide(extra_size, 4)
    extra_squares = jnp.broadcast_to(jnp.sum(extra * extra, axis=1, keepdims=True), (16, SEG))
    extra_high, extra_low = split(extra_squares, 2)
    row = iota((16, FEAT), 0)
    means_out[SEG:, :] = jnp.where(row == 0, extra, 0.0)
    tail = jnp.where(row == 0, extra * g, 0.0)
    tail = jnp.where(row == 1, jnp.concatenate([high, low], axis=1), tail)
    tail = jnp.where(row == 2, jnp.concatenate([extra_high, extra_low], axis=1), tail)
    u_out[SEG:, :] = tail.astype(BF16)
    bias = jnp.log(jnp.transpose(size)[:16])
    bias_out[...] = jnp.concatenate([bias, bias], axis=1).astype(BF16)


EARLY = (0, 1, 4, 5)
LATE = (2, 3, 6, 7)


def row_scale(tail):
    squares = tail[:, :SEG] + tail[:, SEG:]
    scale = lax.rsqrt(squares / WIDTH + 1e-05)
    column = jnp.transpose(jnp.broadcast_to(scale[1:2, :], (128, SEG)))
    return scale, wide(column, 2)


def product(acc, blocks, weight, rows):
    for i, u in enumerate(blocks):
        part = dot(u[:rows, :], weight[i])
        acc = part if acc is None else acc + part
    return acc


def early_kernel(info, *refs):
    blocks, weights = refs[:4], refs[4:7]
    sums, kept, early, sems = refs[8:11], refs[11:14], refs[14:17], refs[17]
    copies = {}
    for side, (which, target) in enumerate(((EARLY, early), (LATE, kept))):
        for i in range(4):
            start = pl.multiple_of(info[I_SRC + which[i]] * FEAT, FEAT)
            for n in range(3):
                copies[side, i, n] = pltpu.make_async_copy(
                    weights[n].at[pl.ds(start, FEAT), :], target[n].at[i], sems.at[side, i, n]
                )
                copies[side, i, n].start()
    for i, u in enumerate(blocks):
        for n, rows in enumerate((ROWS, SEG, SEG)):
            copies[0, i, n].wait()
            part = dot(u[:rows, :], early[n][i])
            sums[n][...] = part if i == 0 else sums[n][...] + part
    for i in range(4):
        for n in range(3):
            copies[1, i, n].wait()


def square_rows(blocks):
    tail = jnp.zeros((16, FEAT), F32)
    for u in blocks:
        tail = tail + u[SEG:, :].astype(F32)
    return tail


def key_value_kernel(info, *refs):
    blocks, late = refs[:8], [refs[i] for i in LATE]
    w_key, w_value, keys, values, bias, kv_out = refs[8:]
    _, column = row_scale(square_rows(blocks))
    kv_out[:SEG, :COLS] = (product(keys[...], late, w_key, SEG) * column).astype(BF16)
    kv_out[:SEG, COLS:] = (product(values[...], late, w_value, SEG) * column).astype(BF16)
    kv_out[SEG:, :] = bias[...]


def query_kernel(info, *refs):
    blocks, late = refs[:8], [refs[i] for i in LATE]
    w_query, partial, q_out = refs[8:]
    scale, column = row_scale(square_rows(blocks))
    query = product(partial[...], late, w_query, ROWS)
    q_out[:SEG, :] = (query[:SEG] * column * SCORE).astype(BF16)
    extra = query[SEG:] * scale[2:3, :] * SCORE
    q_out[SEG:, :] = jnp.where(iota((16, COLS), 0) == 0, extra, 0.0).astype(BF16)


def nt_dot(a, b):
    return lax.dot_general(a, b, (((1,), (1,)), ((), ())), preferred_element_type=F32)


def attend(q, k, v, bias, acc_ref, m_ref, j, h, mask=None):
    scores = nt_dot(q[:, h * HD : (h + 1) * HD], k) + bias
    if mask is not None:
        scores = jnp.where(mask, scores, LOW)
    old = m_ref[j, h]
    peak = jnp.maximum(old, jnp.max(scores, axis=1, keepdims=True))
    expo = jnp.exp2(scores - wide(peak, scores.shape[1] // 128))
    if mask is not None:
        expo = jnp.where(mask, expo, 0.0)
    m_ref[j, h] = peak
    acc_ref[j, h] = acc_ref[j, h] * wide(jnp.exp2(old - peak), 2) + dot(expo.astype(BF16), v)


def keys_of(blocks, h):
    return jnp.concatenate([kv[:SEG, h * HD : (h + 1) * HD] for kv in blocks], axis=0)


def values_of(blocks, h):
    lanes = slice(COLS + h * HD, COLS + (h + 1) * HD)
    values = jnp.concatenate([kv[:SEG, lanes] for kv in blocks], axis=0)
    return jnp.concatenate([values, jnp.ones(values.shape, BF16)], axis=1)


def attend_kernel(step, first, final, info, *refs):
    refs = list(refs)
    queries = [refs.pop(0) for _ in range(4)]
    own = refs.pop(0) if first else None
    others = [refs.pop(0) for _ in range(1 if final else 2)]
    if not first:
        state_in = [refs.pop(0) for _ in range(2)]
    if final:
        payloads = [refs.pop(0) for _ in range(4)]
        acc, m = state_in
    else:
        acc, m, done = refs[:3]
        done[...] = jnp.zeros_like(done)
    if first:
        acc[...] = jnp.zeros_like(acc)
        m[...] = jnp.full(m.shape, LOW, F32)
        bias = own[SEG : SEG + 1, :SEG].astype(F32) * LOG2E
        for j in range(4):

            def one(j=j):
                mask = None
                if j == 0:
                    r, k = iota((ROWS, SEG), 0), iota((ROWS, SEG), 1)
                    mask = (k <= r) & (r < SEG)
                for h in range(2):
                    attend(queries[j], keys_of([own], h), values_of([own], h), bias, acc, m, j, h, mask)

            if j == 0:
                one()
            else:
                pl.when(info[I_X] < info[I_X + j])(one)
    ok = [info[I_OK + 2 * (step - 1) + i] for i in range(len(others))]
    some = ok[0] if final else ok[0] + ok[1]

    @pl.when(some > 0)
    def _():
        biases = []
        for kv, good in zip(others, ok):
            row = kv[SEG : SEG + 1, :SEG].astype(F32) * LOG2E
            biases.append(jnp.where(good > 0, row, LOW))
        bias = jnp.concatenate(biases, axis=1)
        for h in range(2):
            k, v = keys_of(others, h), values_of(others, h)
            for j in range(4):
                attend(queries[j], k, v, bias, acc, m, j, h)

    if final:
        row = iota((16, COLS), 0)
        for j in range(4):
            tail = jnp.zeros((16, COLS), F32)
            ends = []
            for h in range(2):
                total = acc[j, h][:, HD:]
                some_keys = total > 0.0
                total = jnp.where(some_keys, total, 1.0)
                out = acc[j, h][:, :HD] / total
                logs = jnp.where(some_keys, m[j, h] + jnp.log2(total), LOW)
                payloads[j][:SEG, h * HD : (h + 1) * HD] = out[:SEG].astype(BF16)
                ends.append(out[SEG:])
                parts = split(jnp.transpose(logs[:SEG])[:16], 3)
                for i, part in enumerate(parts):
                    tail = jnp.where(row == 1 + 3 * h + i, part, tail)
                parts = split(wide(logs[SEG : SEG + 1], 2), 3)
                for i, part in enumerate(parts):
                    tail = jnp.where(row == 7 + 3 * h + i, part, tail)
            tail = jnp.where(row == 0, jnp.concatenate(ends, axis=1), tail)
            payloads[j][SEG:, :] = tail.astype(BF16)


STATE = [shape((4, 2, ROWS, 2 * HD), F32), shape((4, 2, ROWS, HD), F32), shape((8, 128), F32)]


def attend_step(step, info, queries, own, others, state):
    first, final = own is not None, len(others) == 1
    ins = [info] + queries + ([own] if first else []) + others + list(state or [])
    flops = 4 * 1088 * SEG * (len(others) + (1 if first else 0)) * COLS
    body = functools.partial(attend_kernel, step, first, final)
    if final:
        outs = [shape((ROWS, COLS), BF16)] * 4 + STATE[:2]
        aliases = {len(ins) - 2: 4, len(ins) - 1: 5}

        def body(*refs):
            refs = list(refs)
            payloads, state = refs[-6:-2], refs[-2:]
            attend_kernel(step, first, final, *refs[:-8], *state, *payloads)

        return call(body, outs, ins, flops=flops, moved=4 << 20, aliases=aliases)[:4]
    aliases = {} if first else {len(ins) - 2: 0, len(ins) - 1: 1}
    return call(body, STATE, ins, flops=flops, moved=4 << 20, aliases=aliases)


def merge_kernel(info, a, b, c, d, out):
    parts = (a, b, c, d)
    tails = [p[SEG:, :].astype(F32) for p in parts]
    weights, end_weights = [], []
    for h in range(2):
        for base, store in ((1 + 3 * h, weights), (7 + 3 * h, end_weights)):
            logs = [t[base : base + 1] + t[base + 1 : base + 2] + t[base + 2 : base + 3] for t in tails]
            peak = functools.reduce(jnp.maximum, logs)
            expo = [jnp.exp2(v - peak) for v in logs]
            whole = functools.reduce(jnp.add, expo)
            store.append([e / whole for e in expo])
    flat = weights[0] + weights[1]
    columns = jnp.transpose(jnp.concatenate(flat + [jnp.zeros((120, SEG), F32)], axis=0))
    ends = []
    for h in range(2):
        lanes = slice(h * HD, (h + 1) * HD)
        acc = jnp.zeros((SEG, HD), F32)
        end = jnp.zeros((16, HD), F32)
        for j, p in enumerate(parts):
            acc = acc + columns[:, 4 * h + j : 4 * h + j + 1] * p[:SEG, lanes].astype(F32)
            end = end + end_weights[h][j][:, :HD] * tails[j][:, lanes]
        out[:SEG, lanes] = acc.astype(BF16)
        ends.append(end)
    end = jnp.concatenate(ends, axis=1)
    out[SEG:, :] = jnp.where(iota((16, COLS), 0) == 0, end, 0.0).astype(BF16)


BLOCK = 512
TALL = 384
PAIR = (0, 1, 2, 3, 0, 2, 1, 3)


def output_kernel(*refs):
    attended, weights = refs[:8], refs[8:12]
    means, ids, tokens, out, coarse = refs[12:]

    @pl.when(pl.program_id(0) == 0)
    def _():
        acc = means[...]
        for i, a in enumerate(attended):
            acc = acc + dot(a[...], weights[PAIR[i]][i // 4])
        coarse[:ROWS, :] = acc.astype(BF16)
        coarse[ROWS:, :] = jnp.zeros((TALL - ROWS, FEAT), BF16)

    base = pl.multiple_of(pl.program_id(0) * (BLOCK // 128), BLOCK // 128)
    lane = iota((128, 128), 1)
    chunks = []
    for r in range(BLOCK // 128):
        row = ids[pl.ds(base + r, 1), :].astype(F32)
        column = jnp.transpose(jnp.broadcast_to(row, (128, 128))).astype(jnp.int32)
        chunks.append(
            jnp.concatenate(
                [
                    ones_where(column == lane),
                    ones_where(column == lane + 128),
                    ones_where((column == -1) & (lane == 0)),
                ],
                axis=1,
            )
        )
    hot = jnp.concatenate(chunks, axis=0)
    picked = dot(hot, coarse[...])
    out[...] = (tokens[...].astype(F32) + picked).astype(BF16)


def output(attended, weights, means, ids, tokens):
    whole = [WHOLE] * 14
    return pl.pallas_call(
        output_kernel,
        grid=(TOK // BLOCK,),
        out_shape=shape((TOK, FEAT), BF16),
        in_specs=whole + [pl.BlockSpec((BLOCK, FEAT), lambda i: (i, 0))],
        out_specs=pl.BlockSpec((BLOCK, FEAT), lambda i: (i, 0)),
        scratch_shapes=[pltpu.VMEM((TALL, FEAT), BF16)],
        compiler_params=pltpu.CompilerParams(vmem_limit_bytes=VMEM_LIMIT),
        cost_estimate=pl.CostEstimate(flops=2 << 30, bytes_accessed=6 << 20, transcendentals=0),
    )(*attended, *weights, means, ids, tokens)


def cut_kernel(info, w_out, mine, sibling, sems):
    copies = []
    for i in range(4):
        for side, out in enumerate((mine, sibling)):
            start = pl.multiple_of(info[I_CUT + 4 * side + i] * FEAT, FEAT)
            copies.append(pltpu.make_async_copy(w_out.at[:, pl.ds(start, FEAT)], out.at[i], sems.at[side, i]))
            copies[-1].start()
    for copy in copies:
        copy.wait()


def pair_kernel(info, *refs):
    sources, outs, sems = refs[:2], refs[2:6], refs[6]
    copies = []
    for i, out in enumerate(outs):
        for side, source in enumerate(sources):
            copies.append(pltpu.make_async_copy(source.at[i], out.at[side], sems.at[side, i]))
            copies[-1].start()
    for copy in copies:
        copy.wait()


def y_far(value):
    return move(value, lambda z, x, y, c: (z, x, y + 2, c))


def shards(tokens, flags, norm_gain, w_query, w_key, w_value, w_out):
    seq, mp = lax.axis_index("seq"), lax.axis_index("mp")
    info = jnp.asarray(device_table())[seq * (NY * NC) + mp]
    edge = shape((8, FEAT + 128), F32)
    ids, head, tail = call(
        edge_kernel,
        [shape((16, 128), jnp.int32), edge, edge],
        [info, flags.reshape(16, 128), tokens],
        flops=1 << 28,
        moved=2 << 20,
        scratch=[pltpu.VMEM((16, TOK), BF16)],
    )
    count = NZ * NX
    above = lax.ppermute(head, "seq", [(i, i - 1) for i in range(1, count)])
    below = lax.ppermute(tail, "seq", [(i, i + 1) for i in range(count - 1)])
    sums, sizes = call(
        pool_kernel,
        [shape((SEG, FEAT), F32), shape((SEG, 128), F32)],
        [info, ids, tokens],
        flops=1 << 30,
        moved=2 << 20,
        scratch=[pltpu.VMEM((SEG, TOK), BF16)],
    )
    means, u, bias = call(
        norm_kernel,
        [shape((ROWS, FEAT), F32), shape((ROWS, FEAT), BF16), shape((16, FEAT), BF16)],
        [info, sums, sizes, head, above, below, norm_gain.reshape(8, FEAT)],
        moved=2 << 20,
    )
    cut = shape((4, SEG, FEAT), BF16)
    sems = [pltpu.SemaphoreType.DMA((2, 4))]
    mine, theirs = call(
        cut_kernel, [cut, cut], [info, w_out], moved=4 << 20, scratch=sems, far_in=(1,), far_out=(0, 1), far=DISTANT
    )
    first, sibling, second = y_one(u), swap(u), y_other(u)
    part, part_query = shape((SEG, COLS), F32), shape((ROWS, COLS), F32)
    kept = shape((4, FEAT, COLS), BF16)
    across = swap(first)
    queried, keyed, valued, *late = call(
        early_kernel,
        [part_query, part, part] + [kept] * 3,
        [info, u, first, sibling, across, w_query, w_key, w_value, mine],
        flops=ROWS * WIDTH * 3 * COLS,
        moved=8 << 20,
        scratch=[pltpu.VMEM((4, FEAT, COLS), BF16)] * 3 + [pltpu.SemaphoreType.DMA((2, 4, 3))],
        far_in=(5, 6, 7, 8),
    )
    (far,) = gate(info, [y_one(first)], queried)
    theirs = swap(theirs)
    blocks = [u, first, second, far, sibling, across, swap(second), swap(far)]
    (kv,) = call(
        key_value_kernel,
        [shape((ROWS, 2 * COLS), BF16)],
        [info] + blocks + [late[1], late[2], keyed, valued, bias],
        flops=ROWS * WIDTH * 2 * COLS,
        moved=4 << 20,
    )
    (query,) = call(
        query_kernel,
        [shape((ROWS, COLS), BF16)],
        [info] + blocks + [late[0], queried],
        flops=ROWS * WIDTH * COLS,
        moved=2 << 20,
    )
    one, other = z_one(kv), z_other(kv)
    queries = [query] + [x_by(query, k) for k in (1, 2, 3)]
    pair = shape((2, SEG, FEAT), BF16)
    pairs = call(
        pair_kernel,
        [pair] * 4,
        [info, mine, theirs],
        moved=4 << 20,
        scratch=sems,
        far_in=(1, 2),
        far_out=range(4),
        far=DISTANT,
    )
    queries[0], *pairs = gate(info, [query, *pairs], info)
    weights = [pairs[0], y_one(pairs[1]), y_other(pairs[2]), y_far(pairs[3])]
    *state, done = attend_step(1, info, queries, kv, [one, other], None)
    one, other = gate(info, [z_one(one), z_other(other)], done)
    *state, done = attend_step(2, info, queries, None, [one, other], state)
    one, other, weights[1], weights[2] = gate(info, [z_one(one), z_other(other), weights[1], weights[2]], done)
    *state, done = attend_step(3, info, queries, None, [one, other], state)
    one, weights[3] = gate(info, [z_one(one), weights[3]], done)
    partial = attend_step(4, info, queries, None, [one], state)
    partial = [partial[0]] + [x_by(partial[k], -k) for k in (1, 2, 3)]
    (attended,) = call(merge_kernel, [shape((ROWS, COLS), BF16)], [info] + partial, moved=1 << 20)
    return output(mp_exchange(attended), weights, means, ids, tokens)


def solution(mesh):
    placed = (
        P(("dp", "seq"), "mp"),
        P(("dp", "seq")),
        P(),
        P(None, "mp"),
        P(None, "mp"),
        P(None, "mp"),
        P("mp", None),
    )
    return jax.shard_map(
        shards, mesh=mesh, in_specs=placed, out_specs=P(("dp", "seq"), "mp"), check_vma=False
    )
```

profile of v0, /device:TPU:65, one launch (start us, length us, event | category | flops | bytes accessed | tf_op | source)
XLA Modules:
  0.0 121.3 jit_solution(375356879718732403)
XLA Ops:
  0.7 1.6 %copy-done = bf16[2048,512]{1,0:T(8,128)(2,1)S(1)} copy-done((bf16[2048,512]{1,0:T(8,128)(2,1)S(1)}, bf16[2048,512]{1,0:T(8,128)(2,1)}, u32[]{:S(2)}) %copy-start) | copy-done | bytes 2097176
  4.2 3.3 %collective-permute-start.1 = (f32[8,640]{1,0:T(8,128)S(1)}, f32[8,640]{1,0:T(8,128)S(1)}, u32[]{:S(2)}, u32[]{:S(2)}) collective-permute-start(f32[8,640]{1,0:T(8,128)S(1)} %get-tuple-element.55), channel_id=1, source_target_pairs={{0,8},{8,16},{16,24},{24,32},{32,40},{40,48},{48,56},{56,64},{64,7... | collective-permute-start | bytes 61448 | tf_op jit(solution)/shard_map/ppermute | solution.py:517
  7.5 4.3 %collective-permute-start = (f32[8,640]{1,0:T(8,128)S(1)}, f32[8,640]{1,0:T(8,128)S(1)}, u32[]{:S(2)}, u32[]{:S(2)}) collective-permute-start(f32[8,640]{1,0:T(8,128)S(1)} %get-tuple-element.54.head), channel_id=1, source_target_pairs={{8,0},{16,8},{24,16},{32,24},{40,32},{48,40},{56,48},{64,56},{72,6... | collective-permute-start | bytes 61448 | tf_op jit(solution)/shard_map/ppermute | solution.py:516
  11.8 1.5 %shard_map.83 = (f32[256,512]{1,0:T(8,128)S(1)}, f32[256,128]{1,0:T(8,128)S(1)}) custom-call(s32[32]{0:T(128)S(1)} %dynamic-slice_bitcast_fusion.info.refs_5_.refs_0_, s32[16,128]{1,0:T(8,128)S(1)} %get-tuple-element.51.ids.refs_13_, bf16[2048,512]{1,0:T(8,128)(2,1)S(1)} %copy-done.1), custom_call_target="tpu_custom_call" | custom-call | flops 1073741824 | bytes 2097152 | tf_op jit(solution)/shard_map/pallas_call | solution.py:104
  14.2 2.8 %collective-permute-start.2 = (bf16[272,512]{1,0:T(8,128)(2,1)S(1)}, bf16[272,512]{1,0:T(8,128)(2,1)S(1)}, u32[]{:S(2)}, u32[]{:S(2)}) collective-permute-start(bf16[272,512]{1,0:T(8,128)(2,1)S(1)} %get-tuple-element.56.refs_0_), channel_id=1, source_target_pairs={{0,2},{1,7},{2,4},{3,1},{4,6},{5,3},{6,0},{7,5},{8,10},{9,15},{10,... | collective-permute-start | bytes 835592 | tf_op jit(solution)/shard_map/ppermute | solution.py:40
  17.0 1.6 %copy-done.2 = bf16[256,4096]{1,0:T(8,128)(2,1)S(1)} copy-done((bf16[256,4096]{1,0:T(8,128)(2,1)S(1)}, bf16[256,4096]{1,0:T(8,128)(2,1)}, u32[]{:S(2)}) %copy-start.2) | copy-done | bytes 2097176
  21.3 1.9 %collective-permute-start.6 = (bf16[272,512]{1,0:T(8,128)(2,1)S(1)}, bf16[272,512]{1,0:T(8,128)(2,1)S(1)}, u32[]{:S(2)}, u32[]{:S(2)}) collective-permute-start(bf16[272,512]{1,0:T(8,128)(2,1)S(1)} %collective-permute-done.2.refs_1_), channel_id=1, source_target_pairs={{0,1},{1,0},{2,3},{3,2},{4,5},{5,4},{6,7},{7,6},{8,9},{9,8},{10,11... | collective-permute-start | bytes 835592 | tf_op jit(solution)/shard_map/ppermute | solution.py:40
  23.2 2.1 %collective-permute-start.4 = (bf16[272,512]{1,0:T(8,128)(2,1)S(1)}, bf16[272,512]{1,0:T(8,128)(2,1)S(1)}, u32[]{:S(2)}, u32[]{:S(2)}) collective-permute-start(bf16[272,512]{1,0:T(8,128)(2,1)S(1)} %collective-permute-done.2.refs_1_), channel_id=1, source_target_pairs={{0,2},{1,7},{2,4},{3,1},{4,6},{5,3},{6,0},{7,5},{8,10},{9,15},{10,... | collective-permute-start | bytes 835592 | tf_op jit(solution)/shard_map/ppermute | solution.py:40
  26.7 1.6 %copy-done.4 = bf16[4096,256]{1,0:T(8,128)(2,1)S(1)} copy-done((bf16[4096,256]{1,0:T(8,128)(2,1)S(1)}, bf16[4096,256]{1,0:T(8,128)(2,1)}, u32[]{:S(2)}) %copy-start.4) | copy-done | bytes 2097176
  28.3 1.6 %copy-done.5 = bf16[4096,256]{1,0:T(8,128)(2,1)S(1)} copy-done((bf16[4096,256]{1,0:T(8,128)(2,1)S(1)}, bf16[4096,256]{1,0:T(8,128)(2,1)}, u32[]{:S(2)}) %copy-start.5) | copy-done | bytes 2097176
  29.8 3.8 %shard_map.86 = (f32[272,256]{1,0:T(8,128)S(1)}, f32[256,256]{1,0:T(8,128)S(1)}, f32[256,256]{1,0:T(8,128)S(1)}, bf16[4,512,256]{2,1,0:T(8,128)(2,1)S(1)}, bf16[...) custom-call(s32[32]{0:T(128)S(1)} %dynamic-slice_bitcast_fusion.info.refs_5_.refs_0_, ...), custom_call_target="tpu_custom_call" | custom-call | flops 855638016 | bytes 8388608 | tf_op jit(solution)/shard_map/pallas_call | solution.py:104
  34.3 1.5 %collective-permute-done.8.refs_7_ = bf16[272,512]{1,0:T(8,128)(2,1)S(1)} collective-permute-done((bf16[272,512]{1,0:T(8,128)(2,1)S(1)}, bf16[272,512]{1,0:T(8,128)(2,1)S(1)}, u32[]{:S(2)}, u32[]{:S(2)}) %collective-permute-start.8) | collective-permute-done | bytes 278560 | tf_op jit(solution)/shard_map/ppermute | solution.py:40
  37.1 1.7 %collective-permute-start.15 = (bf16[272,512]{1,0:T(8,128)(2,1)S(1)}, bf16[272,512]{1,0:T(8,128)(2,1)S(1)}, u32[]{:S(2)}, u32[]{:S(2)}) collective-permute-start(bf16[272,512]{1,0:T(8,128)(2,1)S(1)} %shard_map.91.refs_4_), channel_id=1, source_target_pairs={{0,224},{1,33},{2,226},{3,35},{4,228},{5,37},{6,230},{7,39},{8,232... | collective-permute-start | bytes 835592 | tf_op jit(solution)/shard_map/ppermute | solution.py:40
  39.8 6.6 %collective-permute-start.12 = (bf16[272,256]{1,0:T(8,128)(2,1)S(1)}, bf16[272,256]{1,0:T(8,128)(2,1)S(1)}, u32[]{:S(2)}, u32[]{:S(2)}) collective-permute-start(bf16[272,256]{1,0:T(8,128)(2,1)S(1)} %shard_map.88.refs_0_), channel_id=1, source_target_pairs={{0,24},{1,25},{2,26},{3,27},{4,28},{5,29},{6,30},{7,31},{8,0},{9,1... | collective-permute-start | bytes 417800 | tf_op jit(solution)/shard_map/ppermute | solution.py:40
  47.3 1.5 %collective-permute-start.16 = (bf16[272,512]{1,0:T(8,128)(2,1)S(1)}, bf16[272,512]{1,0:T(8,128)(2,1)S(1)}, u32[]{:S(2)}, u32[]{:S(2)}) collective-permute-start(bf16[272,512]{1,0:T(8,128)(2,1)S(1)} %collective-permute-done.15.refs_6_), channel_id=1, source_target_pairs={{0,224},{1,33},{2,226},{3,35},{4,228},{5,37},{6,230},{7,39},{8,232... | collective-permute-start | bytes 835592 | tf_op jit(solution)/shard_map/ppermute | solution.py:40
  49.5 2.7 %collective-permute-done.12.refs_3_.refs_4_ = bf16[272,256]{1,0:T(8,128)(2,1)S(1)} collective-permute-done((bf16[272,256]{1,0:T(8,128)(2,1)S(1)}, bf16[272,256]{1,0:T(8,128)(2,1)S(1)}, u32[]{:S(2)}, u32[]{:S(2)}) %collective-permute-start.12) | collective-permute-done | bytes 139296 | tf_op jit(solution)/shard_map/ppermute | solution.py:40
  52.2 3.7 %collective-permute-done.10.refs_1_.refs_2_ = bf16[272,256]{1,0:T(8,128)(2,1)S(1)} collective-permute-done((bf16[272,256]{1,0:T(8,128)(2,1)S(1)}, bf16[272,256]{1,0:T(8,128)(2,1)S(1)}, u32[]{:S(2)}, u32[]{:S(2)}) %collective-permute-start.10) | collective-permute-done | bytes 139296 | tf_op jit(solution)/shard_map/ppermute | solution.py:40
  56.4 2.6 %collective-permute-start.19 = (bf16[2,256,512]{2,1,0:T(8,128)(2,1)S(1)}, bf16[2,256,512]{2,1,0:T(8,128)(2,1)S(1)}, u32[]{:S(2)}, u32[]{:S(2)}) collective-permute-start(bf16[2,256,512]{2,1,0:T(8,128)(2,1)S(1)} %get-tuple-element.74), channel_id=1, source_target_pairs={{0,2},{1,7},{2,4},{3,1},{4,6},{5,3},{6,0},{7,5},{8,10},{9,15},{10,... | collective-permute-start | bytes 1572872 | tf_op jit(solution)/shard_map/ppermute | solution.py:40
  59.0 4.7 %shard_map.92 = (f32[4,2,272,256]{3,2,1,0:T(8,128)S(1)}, f32[4,2,272,128]{3,2,1,0:T(8,128)S(1)}, f32[8,128]{1,0:T(8,128)S(1)}) custom-call(s32[32]{0:T(128)S(1)} %dynamic-slice_bitcast_fusion.info.refs_5_.refs_0_, bf16[272,256]{1,0:T(8,128)(2,1)S(1)} %get-tuple-element.65.refs_0_.refs_1_, bf16[272,256]{1,0:T(8,128)(2,1)S(1)} %collective-permute-done.10.refs_1_.refs_2_, ...), custom_call_target="tpu_custom_call" | custom-call | flops 855638016 | bytes 4194304 | tf_op jit(solution)/shard_map/pallas_call | solution.py:104
  64.3 1.5 %collective-permute-start.18 = (bf16[272,512]{1,0:T(8,128)(2,1)S(1)}, bf16[272,512]{1,0:T(8,128)(2,1)S(1)}, u32[]{:S(2)}, u32[]{:S(2)}) collective-permute-start(bf16[272,512]{1,0:T(8,128)(2,1)S(1)} %get-tuple-element.73.refs_5_), channel_id=1, source_target_pairs={{0,224},{1,33},{2,226},{3,35},{4,228},{5,37},{6,230},{7,39},{8,232... | collective-permute-start | bytes 835592 | tf_op jit(solution)/shard_map/ppermute | solution.py:40
  65.8 2.1 %collective-permute-start.22 = (bf16[2,256,512]{2,1,0:T(8,128)(2,1)S(1)}, bf16[2,256,512]{2,1,0:T(8,128)(2,1)S(1)}, u32[]{:S(2)}, u32[]{:S(2)}) collective-permute-start(bf16[2,256,512]{2,1,0:T(8,128)(2,1)S(1)} %get-tuple-element.80), channel_id=1, source_target_pairs={{0,4},{1,5},{2,6},{3,7},{4,0},{5,1},{6,2},{7,3},{8,12},{9,13},{10,... | collective-permute-start | bytes 1572872 | tf_op jit(solution)/shard_map/ppermute | solution.py:40
  67.8 2.4 %shard_map.94 = (f32[4,2,272,256]{3,2,1,0:T(8,128)S(1)}, f32[4,2,272,128]{3,2,1,0:T(8,128)S(1)}, f32[8,128]{1,0:T(8,128)S(1)}) custom-call(s32[32]{0:T(128)S(1)} %dynamic-slice_bitcast_fusion.info.refs_5_.refs_0_, bf16[272,256]{1,0:T(8,128)(2,1)S(1)} %get-tuple-element.65.refs_0_.refs_1_, ...), custom_call_target="tpu_custom_call", output_to_operand_aliasing={{0}: (7, {}), {1}: (8, {})} | custom-call | flops 570425344 | bytes 4194304 | tf_op jit(solution)/shard_map/pallas_call | solution.py:104
  70.3 2.4 %collective-permute-done.20.refs_3_ = bf16[2,256,512]{2,1,0:T(8,128)(2,1)S(1)} collective-permute-done((bf16[2,256,512]{2,1,0:T(8,128)(2,1)S(1)}, bf16[2,256,512]{2,1,0:T(8,128)(2,1)S(1)}, u32[]{:S(2)}, u32[]{:S(2)}) %collective-permute-start.20) | collective-permute-done | bytes 524320 | tf_op jit(solution)/shard_map/ppermute | solution.py:40
  74.1 10.4 %collective-permute-done.22.refs_1_ = bf16[2,256,512]{2,1,0:T(8,128)(2,1)S(1)} collective-permute-done((bf16[2,256,512]{2,1,0:T(8,128)(2,1)S(1)}, bf16[2,256,512]{2,1,0:T(8,128)(2,1)S(1)}, u32[]{:S(2)}, u32[]{:S(2)}) %collective-permute-start.22) | collective-permute-done | bytes 524320 | tf_op jit(solution)/shard_map/ppermute | solution.py:40
  85.9 6.3 %collective-permute-start.23 = (bf16[272,256]{1,0:T(8,128)(2,1)S(1)}, bf16[272,256]{1,0:T(8,128)(2,1)S(1)}, u32[]{:S(2)}, u32[]{:S(2)}) collective-permute-start(bf16[272,256]{1,0:T(8,128)(2,1)S(1)} %get-tuple-element.89), channel_id=1, source_target_pairs={{0,24},{1,25},{2,26},{3,27},{4,28},{5,29},{6,30},{7,31},{8,0},{9,1... | collective-permute-start | bytes 417800 | tf_op jit(solution)/shard_map/ppermute | solution.py:40
  92.9 5.0 %collective-permute-done.23.b = bf16[272,256]{1,0:T(8,128)(2,1)S(1)} collective-permute-done((bf16[272,256]{1,0:T(8,128)(2,1)S(1)}, bf16[272,256]{1,0:T(8,128)(2,1)S(1)}, u32[]{:S(2)}, u32[]{:S(2)}) %collective-permute-start.23) | collective-permute-done | bytes 139296 | tf_op jit(solution)/shard_map/ppermute | solution.py:40
  97.9 3.7 %collective-permute-done.25.d = bf16[272,256]{1,0:T(8,128)(2,1)S(1)} collective-permute-done((bf16[272,256]{1,0:T(8,128)(2,1)S(1)}, bf16[272,256]{1,0:T(8,128)(2,1)S(1)}, u32[]{:S(2)}, u32[]{:S(2)}) %collective-permute-start.25) | collective-permute-done | bytes 139296 | tf_op jit(solution)/shard_map/ppermute | solution.py:40
  102.8 1.5 %collective-permute-start.27 = (bf16[272,256]{1,0:T(8,128)(2,1)S(1)}, bf16[272,256]{1,0:T(8,128)(2,1)S(1)}, u32[]{:S(2)}, u32[]{:S(2)}) collective-permute-start(bf16[272,256]{1,0:T(8,128)(2,1)S(1)} %shard_map.99.refs_0_), channel_id=1, source_target_pairs={{0,6},{1,3},{2,0},{3,5},{4,2},{5,7},{6,4},{7,1},{8,14},{9,11},{10,... | collective-permute-start | bytes 417800 | tf_op jit(solution)/shard_map/ppermute | solution.py:40
  104.3 2.8 %collective-permute-done.26.refs_1_ = bf16[272,256]{1,0:T(8,128)(2,1)S(1)} collective-permute-done((bf16[272,256]{1,0:T(8,128)(2,1)S(1)}, bf16[272,256]{1,0:T(8,128)(2,1)S(1)}, u32[]{:S(2)}, u32[]{:S(2)}) %collective-permute-start.26) | collective-permute-done | bytes 139296 | tf_op jit(solution)/shard_map/ppermute | solution.py:40
  107.9 2.3 %collective-permute-start.29 = (bf16[272,256]{1,0:T(8,128)(2,1)S(1)}, bf16[272,256]{1,0:T(8,128)(2,1)S(1)}, u32[]{:S(2)}, u32[]{:S(2)}) collective-permute-start(bf16[272,256]{1,0:T(8,128)(2,1)S(1)} %shard_map.99.refs_0_), channel_id=1, source_target_pairs={{0,1},{1,0},{2,3},{3,2},{4,5},{5,4},{6,7},{7,6},{8,9},{9,8},{10,11... | collective-permute-start | bytes 417800 | tf_op jit(solution)/shard_map/ppermute | solution.py:40
  110.9 5.5 %collective-permute-start.32 = (bf16[272,256]{1,0:T(8,128)(2,1)S(1)}, bf16[272,256]{1,0:T(8,128)(2,1)S(1)}, u32[]{:S(2)}, u32[]{:S(2)}) collective-permute-start(bf16[272,256]{1,0:T(8,128)(2,1)S(1)} %collective-permute-done.28.refs_3_), channel_id=1, source_target_pairs={{0,1},{1,0},{2,3},{3,2},{4,5},{5,4},{6,7},{7,6},{8,9},{9,8},{10,11... | collective-permute-start | bytes 417800 | tf_op jit(solution)/shard_map/ppermute | solution.py:40
  117.5 3.8 %shard_map.100 = bf16[2048,512]{1,0:T(8,128)(2,1)} custom-call(bf16[272,256]{1,0:T(8,128)(2,1)S(1)} %shard_map.99.refs_0_, bf16[272,256]{1,0:T(8,128)(2,1)S(1)} %collective-permute-done.26.refs_1_, bf16[272,256]{1,0:T(8,128)(2,1)S(1)} %collective-permute-done.27.refs_2_, bf16[272,256]{1,0:T(8,128)(2,1)S(1)} %collective-permute-done.28.refs_3_, ...), custom_call_target="tpu_custom_call" | custom-call | flops 2147483648 | bytes 6291456 | tf_op jit(solution)/shard_map/pallas_call | solution.py:465
  (71 shorter events, 20.5 us)
Async XLA Ops:
  4.2 9.1 %collective-permute-start.1 = (f32[8,640]{1,0:T(8,128)S(1)}, f32[8,640]{1,0:T(8,128)S(1)}, u32[]{:S(2)}, u32[]{:S(2)}) collective-permute-start(f32[8,640]{1,0:T(8,128)S(1)} %get-tuple-element.55), channel_id=1, source_target_pairs={{0,8},{8,16},{16,24},{24,32},{32,40},{40,48},{48,56},{56,64},{64,7... | collective-permute-start | bytes 61448 | tf_op jit(solution)/shard_map/ppermute | solution.py:517
  7.5 5.9 %collective-permute-start = (f32[8,640]{1,0:T(8,128)S(1)}, f32[8,640]{1,0:T(8,128)S(1)}, u32[]{:S(2)}, u32[]{:S(2)}) collective-permute-start(f32[8,640]{1,0:T(8,128)S(1)} %get-tuple-element.54.head), channel_id=1, source_target_pairs={{8,0},{16,8},{24,16},{32,24},{40,32},{48,40},{56,48},{64,56},{72,6... | collective-permute-start | bytes 61448 | tf_op jit(solution)/shard_map/ppermute | solution.py:516
  14.2 7.1 %collective-permute-start.2 = (bf16[272,512]{1,0:T(8,128)(2,1)S(1)}, bf16[272,512]{1,0:T(8,128)(2,1)S(1)}, u32[]{:S(2)}, u32[]{:S(2)}) collective-permute-start(bf16[272,512]{1,0:T(8,128)(2,1)S(1)} %get-tuple-element.56.refs_0_), channel_id=1, source_target_pairs={{0,2},{1,7},{2,4},{3,1},{4,6},{5,3},{6,0},{7,5},{8,10},{9,15},{10,... | collective-permute-start | bytes 835592 | tf_op jit(solution)/shard_map/ppermute | solution.py:40
  19.4 27.0 %collective-permute-start.9 = (bf16[4,256,512]{2,1,0:T(8,128)(2,1)S(1)}, bf16[4,256,512]{2,1,0:T(8,128)(2,1)S(1)}, u32[]{:S(2)}, u32[]{:S(2)}) collective-permute-start(bf16[4,256,512]{2,1,0:T(8,128)(2,1)S(1)} %get-tuple-element.60), channel_id=1, source_target_pairs={{0,1},{1,0},{2,3},{3,2},{4,5},{5,4},{6,7},{7,6},{8,9},{9,8},{10,11... | collective-permute-start | bytes 3145736 | tf_op jit(solution)/shard_map/ppermute | solution.py:40
  19.5 6.6 %collective-permute-start.3 = (bf16[272,512]{1,0:T(8,128)(2,1)S(1)}, bf16[272,512]{1,0:T(8,128)(2,1)S(1)}, u32[]{:S(2)}, u32[]{:S(2)}) collective-permute-start(bf16[272,512]{1,0:T(8,128)(2,1)S(1)} %get-tuple-element.56.refs_0_), channel_id=1, source_target_pairs={{0,6},{1,3},{2,0},{3,5},{4,2},{5,7},{6,4},{7,1},{8,14},{9,11},{10,... | collective-permute-start | bytes 835592 | tf_op jit(solution)/shard_map/ppermute | solution.py:40
  20.8 5.8 %collective-permute-start.5 = (bf16[272,512]{1,0:T(8,128)(2,1)S(1)}, bf16[272,512]{1,0:T(8,128)(2,1)S(1)}, u32[]{:S(2)}, u32[]{:S(2)}) collective-permute-start(bf16[272,512]{1,0:T(8,128)(2,1)S(1)} %get-tuple-element.56.refs_0_), channel_id=1, source_target_pairs={{0,1},{1,0},{2,3},{3,2},{4,5},{5,4},{6,7},{7,6},{8,9},{9,8},{10,11... | collective-permute-start | bytes 835592 | tf_op jit(solution)/shard_map/ppermute | solution.py:40
  21.3 5.4 %collective-permute-start.6 = (bf16[272,512]{1,0:T(8,128)(2,1)S(1)}, bf16[272,512]{1,0:T(8,128)(2,1)S(1)}, u32[]{:S(2)}, u32[]{:S(2)}) collective-permute-start(bf16[272,512]{1,0:T(8,128)(2,1)S(1)} %collective-permute-done.2.refs_1_), channel_id=1, source_target_pairs={{0,1},{1,0},{2,3},{3,2},{4,5},{5,4},{6,7},{7,6},{8,9},{9,8},{10,11... | collective-permute-start | bytes 835592 | tf_op jit(solution)/shard_map/ppermute | solution.py:40
  23.2 10.4 %collective-permute-start.4 = (bf16[272,512]{1,0:T(8,128)(2,1)S(1)}, bf16[272,512]{1,0:T(8,128)(2,1)S(1)}, u32[]{:S(2)}, u32[]{:S(2)}) collective-permute-start(bf16[272,512]{1,0:T(8,128)(2,1)S(1)} %collective-permute-done.2.refs_1_), channel_id=1, source_target_pairs={{0,2},{1,7},{2,4},{3,1},{4,6},{5,3},{6,0},{7,5},{8,10},{9,15},{10,... | collective-permute-start | bytes 835592 | tf_op jit(solution)/shard_map/ppermute | solution.py:40
  26.2 8.2 %collective-permute-start.7 = (bf16[272,512]{1,0:T(8,128)(2,1)S(1)}, bf16[272,512]{1,0:T(8,128)(2,1)S(1)}, u32[]{:S(2)}, u32[]{:S(2)}) collective-permute-start(bf16[272,512]{1,0:T(8,128)(2,1)S(1)} %collective-permute-done.3.refs_2_), channel_id=1, source_target_pairs={{0,1},{1,0},{2,3},{3,2},{4,5},{5,4},{6,7},{7,6},{8,9},{9,8},{10,11... | collective-permute-start | bytes 835592 | tf_op jit(solution)/shard_map/ppermute | solution.py:40
  37.1 10.2 %collective-permute-start.15 = (bf16[272,512]{1,0:T(8,128)(2,1)S(1)}, bf16[272,512]{1,0:T(8,128)(2,1)S(1)}, u32[]{:S(2)}, u32[]{:S(2)}) collective-permute-start(bf16[272,512]{1,0:T(8,128)(2,1)S(1)} %shard_map.91.refs_4_), channel_id=1, source_target_pairs={{0,224},{1,33},{2,226},{3,35},{4,228},{5,37},{6,230},{7,39},{8,232... | collective-permute-start | bytes 835592 | tf_op jit(solution)/shard_map/ppermute | solution.py:40
  38.8 9.9 %collective-permute-start.13 = (bf16[272,512]{1,0:T(8,128)(2,1)S(1)}, bf16[272,512]{1,0:T(8,128)(2,1)S(1)}, u32[]{:S(2)}, u32[]{:S(2)}) collective-permute-start(bf16[272,512]{1,0:T(8,128)(2,1)S(1)} %shard_map.91.refs_4_), channel_id=1, source_target_pairs={{0,32},{1,225},{2,34},{3,227},{4,36},{5,229},{6,38},{7,231},{8,40}... | collective-permute-start | bytes 835592 | tf_op jit(solution)/shard_map/ppermute | solution.py:40
  39.8 12.4 %collective-permute-start.12 = (bf16[272,256]{1,0:T(8,128)(2,1)S(1)}, bf16[272,256]{1,0:T(8,128)(2,1)S(1)}, u32[]{:S(2)}, u32[]{:S(2)}) collective-permute-start(bf16[272,256]{1,0:T(8,128)(2,1)S(1)} %shard_map.88.refs_0_), channel_id=1, source_target_pairs={{0,24},{1,25},{2,26},{3,27},{4,28},{5,29},{6,30},{7,31},{8,0},{9,1... | collective-permute-start | bytes 417800 | tf_op jit(solution)/shard_map/ppermute | solution.py:40
  46.4 5.8 %collective-permute-start.11 = (bf16[272,256]{1,0:T(8,128)(2,1)S(1)}, bf16[272,256]{1,0:T(8,128)(2,1)S(1)}, u32[]{:S(2)}, u32[]{:S(2)}) collective-permute-start(bf16[272,256]{1,0:T(8,128)(2,1)S(1)} %shard_map.88.refs_0_), channel_id=1, source_target_pairs={{0,16},{1,17},{2,18},{3,19},{4,20},{5,21},{6,22},{7,23},{8,24},{9,... | collective-permute-start | bytes 417800 | tf_op jit(solution)/shard_map/ppermute | solution.py:40
  46.4 9.4 %collective-permute-start.10 = (bf16[272,256]{1,0:T(8,128)(2,1)S(1)}, bf16[272,256]{1,0:T(8,128)(2,1)S(1)}, u32[]{:S(2)}, u32[]{:S(2)}) collective-permute-start(bf16[272,256]{1,0:T(8,128)(2,1)S(1)} %shard_map.88.refs_0_), channel_id=1, source_target_pairs={{0,8},{1,9},{2,10},{3,11},{4,12},{5,13},{6,14},{7,15},{8,16},{9,17... | collective-permute-start | bytes 417800 | tf_op jit(solution)/shard_map/ppermute | solution.py:40
  47.3 16.4 %collective-permute-start.16 = (bf16[272,512]{1,0:T(8,128)(2,1)S(1)}, bf16[272,512]{1,0:T(8,128)(2,1)S(1)}, u32[]{:S(2)}, u32[]{:S(2)}) collective-permute-start(bf16[272,512]{1,0:T(8,128)(2,1)S(1)} %collective-permute-done.15.refs_6_), channel_id=1, source_target_pairs={{0,224},{1,33},{2,226},{3,35},{4,228},{5,37},{6,230},{7,39},{8,232... | collective-permute-start | bytes 835592 | tf_op jit(solution)/shard_map/ppermute | solution.py:40
  48.8 14.9 %collective-permute-start.14 = (bf16[272,512]{1,0:T(8,128)(2,1)S(1)}, bf16[272,512]{1,0:T(8,128)(2,1)S(1)}, u32[]{:S(2)}, u32[]{:S(2)}) collective-permute-start(bf16[272,512]{1,0:T(8,128)(2,1)S(1)} %collective-permute-done.13.refs_5_), channel_id=1, source_target_pairs={{0,32},{1,225},{2,34},{3,227},{4,36},{5,229},{6,38},{7,231},{8,40}... | collective-permute-start | bytes 835592 | tf_op jit(solution)/shard_map/ppermute | solution.py:40
  56.4 13.9 %collective-permute-start.19 = (bf16[2,256,512]{2,1,0:T(8,128)(2,1)S(1)}, bf16[2,256,512]{2,1,0:T(8,128)(2,1)S(1)}, u32[]{:S(2)}, u32[]{:S(2)}) collective-permute-start(bf16[2,256,512]{2,1,0:T(8,128)(2,1)S(1)} %get-tuple-element.74), channel_id=1, source_target_pairs={{0,2},{1,7},{2,4},{3,1},{4,6},{5,3},{6,0},{7,5},{8,10},{9,15},{10,... | collective-permute-start | bytes 1572872 | tf_op jit(solution)/shard_map/ppermute | solution.py:40
  59.0 13.7 %collective-permute-start.20 = (bf16[2,256,512]{2,1,0:T(8,128)(2,1)S(1)}, bf16[2,256,512]{2,1,0:T(8,128)(2,1)S(1)}, u32[]{:S(2)}, u32[]{:S(2)}) collective-permute-start(bf16[2,256,512]{2,1,0:T(8,128)(2,1)S(1)} %get-tuple-element.75), channel_id=1, source_target_pairs={{0,6},{1,3},{2,0},{3,5},{4,2},{5,7},{6,4},{7,1},{8,14},{9,11},{10,... | collective-permute-start | bytes 1572872 | tf_op jit(solution)/shard_map/ppermute | solution.py:40
  64.2 8.4 %collective-permute-start.17 = (bf16[272,512]{1,0:T(8,128)(2,1)S(1)}, bf16[272,512]{1,0:T(8,128)(2,1)S(1)}, u32[]{:S(2)}, u32[]{:S(2)}) collective-permute-start(bf16[272,512]{1,0:T(8,128)(2,1)S(1)} %get-tuple-element.72.refs_4_), channel_id=1, source_target_pairs={{0,32},{1,225},{2,34},{3,227},{4,36},{5,229},{6,38},{7,231},{8,40}... | collective-permute-start | bytes 835592 | tf_op jit(solution)/shard_map/ppermute | solution.py:40
  64.3 8.3 %collective-permute-start.18 = (bf16[272,512]{1,0:T(8,128)(2,1)S(1)}, bf16[272,512]{1,0:T(8,128)(2,1)S(1)}, u32[]{:S(2)}, u32[]{:S(2)}) collective-permute-start(bf16[272,512]{1,0:T(8,128)(2,1)S(1)} %get-tuple-element.73.refs_5_), channel_id=1, source_target_pairs={{0,224},{1,33},{2,226},{3,35},{4,228},{5,37},{6,230},{7,39},{8,232... | collective-permute-start | bytes 835592 | tf_op jit(solution)/shard_map/ppermute | solution.py:40
  65.8 18.7 %collective-permute-start.22 = (bf16[2,256,512]{2,1,0:T(8,128)(2,1)S(1)}, bf16[2,256,512]{2,1,0:T(8,128)(2,1)S(1)}, u32[]{:S(2)}, u32[]{:S(2)}) collective-permute-start(bf16[2,256,512]{2,1,0:T(8,128)(2,1)S(1)} %get-tuple-element.80), channel_id=1, source_target_pairs={{0,4},{1,5},{2,6},{3,7},{4,0},{5,1},{6,2},{7,3},{8,12},{9,13},{10,... | collective-permute-start | bytes 1572872 | tf_op jit(solution)/shard_map/ppermute | solution.py:40
  73.2 11.2 %collective-permute-start.21 = (bf16[272,512]{1,0:T(8,128)(2,1)S(1)}, bf16[272,512]{1,0:T(8,128)(2,1)S(1)}, u32[]{:S(2)}, u32[]{:S(2)}) collective-permute-start(bf16[272,512]{1,0:T(8,128)(2,1)S(1)} %get-tuple-element.79.refs_4_), channel_id=1, source_target_pairs={{0,32},{1,225},{2,34},{3,227},{4,36},{5,229},{6,38},{7,231},{8,40}... | collective-permute-start | bytes 835592 | tf_op jit(solution)/shard_map/ppermute | solution.py:40
  85.9 12.0 %collective-permute-start.23 = (bf16[272,256]{1,0:T(8,128)(2,1)S(1)}, bf16[272,256]{1,0:T(8,128)(2,1)S(1)}, u32[]{:S(2)}, u32[]{:S(2)}) collective-permute-start(bf16[272,256]{1,0:T(8,128)(2,1)S(1)} %get-tuple-element.89), channel_id=1, source_target_pairs={{0,24},{1,25},{2,26},{3,27},{4,28},{5,29},{6,30},{7,31},{8,0},{9,1... | collective-permute-start | bytes 417800 | tf_op jit(solution)/shard_map/ppermute | solution.py:40
  92.2 5.7 %collective-permute-start.24 = (bf16[272,256]{1,0:T(8,128)(2,1)S(1)}, bf16[272,256]{1,0:T(8,128)(2,1)S(1)}, u32[]{:S(2)}, u32[]{:S(2)}) collective-permute-start(bf16[272,256]{1,0:T(8,128)(2,1)S(1)} %get-tuple-element.90), channel_id=1, source_target_pairs={{0,16},{1,17},{2,18},{3,19},{4,20},{5,21},{6,22},{7,23},{8,24},{9,... | collective-permute-start | bytes 417800 | tf_op jit(solution)/shard_map/ppermute | solution.py:40
  92.2 9.4 %collective-permute-start.25 = (bf16[272,256]{1,0:T(8,128)(2,1)S(1)}, bf16[272,256]{1,0:T(8,128)(2,1)S(1)}, u32[]{:S(2)}, u32[]{:S(2)}) collective-permute-start(bf16[272,256]{1,0:T(8,128)(2,1)S(1)} %get-tuple-element.91), channel_id=1, source_target_pairs={{0,8},{1,9},{2,10},{3,11},{4,12},{5,13},{6,14},{7,15},{8,16},{9,17... | collective-permute-start | bytes 417800 | tf_op jit(solution)/shard_map/ppermute | solution.py:40
  102.7 4.3 %collective-permute-start.26 = (bf16[272,256]{1,0:T(8,128)(2,1)S(1)}, bf16[272,256]{1,0:T(8,128)(2,1)S(1)}, u32[]{:S(2)}, u32[]{:S(2)}) collective-permute-start(bf16[272,256]{1,0:T(8,128)(2,1)S(1)} %shard_map.99.refs_0_), channel_id=1, source_target_pairs={{0,2},{1,7},{2,4},{3,1},{4,6},{5,3},{6,0},{7,5},{8,10},{9,15},{10,... | collective-permute-start | bytes 417800 | tf_op jit(solution)/shard_map/ppermute | solution.py:40
  102.8 7.4 %collective-permute-start.27 = (bf16[272,256]{1,0:T(8,128)(2,1)S(1)}, bf16[272,256]{1,0:T(8,128)(2,1)S(1)}, u32[]{:S(2)}, u32[]{:S(2)}) collective-permute-start(bf16[272,256]{1,0:T(8,128)(2,1)S(1)} %shard_map.99.refs_0_), channel_id=1, source_target_pairs={{0,6},{1,3},{2,0},{3,5},{4,2},{5,7},{6,4},{7,1},{8,14},{9,11},{10,... | collective-permute-start | bytes 417800 | tf_op jit(solution)/shard_map/ppermute | solution.py:40
  107.0 3.9 %collective-permute-start.28 = (bf16[272,256]{1,0:T(8,128)(2,1)S(1)}, bf16[272,256]{1,0:T(8,128)(2,1)S(1)}, u32[]{:S(2)}, u32[]{:S(2)}) collective-permute-start(bf16[272,256]{1,0:T(8,128)(2,1)S(1)} %collective-permute-done.26.refs_1_), channel_id=1, source_target_pairs={{0,2},{1,7},{2,4},{3,1},{4,6},{5,3},{6,0},{7,5},{8,10},{9,15},{10,... | collective-permute-start | bytes 417800 | tf_op jit(solution)/shard_map/ppermute | solution.py:40
  107.9 8.5 %collective-permute-start.29 = (bf16[272,256]{1,0:T(8,128)(2,1)S(1)}, bf16[272,256]{1,0:T(8,128)(2,1)S(1)}, u32[]{:S(2)}, u32[]{:S(2)}) collective-permute-start(bf16[272,256]{1,0:T(8,128)(2,1)S(1)} %shard_map.99.refs_0_), channel_id=1, source_target_pairs={{0,1},{1,0},{2,3},{3,2},{4,5},{5,4},{6,7},{7,6},{8,9},{9,8},{10,11... | collective-permute-start | bytes 417800 | tf_op jit(solution)/shard_map/ppermute | solution.py:40
  110.2 6.3 %collective-permute-start.30 = (bf16[272,256]{1,0:T(8,128)(2,1)S(1)}, bf16[272,256]{1,0:T(8,128)(2,1)S(1)}, u32[]{:S(2)}, u32[]{:S(2)}) collective-permute-start(bf16[272,256]{1,0:T(8,128)(2,1)S(1)} %collective-permute-done.26.refs_1_), channel_id=1, source_target_pairs={{0,1},{1,0},{2,3},{3,2},{4,5},{5,4},{6,7},{7,6},{8,9},{9,8},{10,11... | collective-permute-start | bytes 417800 | tf_op jit(solution)/shard_map/ppermute | solution.py:40
  110.2 6.3 %collective-permute-start.31 = (bf16[272,256]{1,0:T(8,128)(2,1)S(1)}, bf16[272,256]{1,0:T(8,128)(2,1)S(1)}, u32[]{:S(2)}, u32[]{:S(2)}) collective-permute-start(bf16[272,256]{1,0:T(8,128)(2,1)S(1)} %collective-permute-done.27.refs_2_), channel_id=1, source_target_pairs={{0,1},{1,0},{2,3},{3,2},{4,5},{5,4},{6,7},{7,6},{8,9},{9,8},{10,11... | collective-permute-start | bytes 417800 | tf_op jit(solution)/shard_map/ppermute | solution.py:40
  110.9 6.5 %collective-permute-start.32 = (bf16[272,256]{1,0:T(8,128)(2,1)S(1)}, bf16[272,256]{1,0:T(8,128)(2,1)S(1)}, u32[]{:S(2)}, u32[]{:S(2)}) collective-permute-start(bf16[272,256]{1,0:T(8,128)(2,1)S(1)} %collective-permute-done.28.refs_3_), channel_id=1, source_target_pairs={{0,1},{1,0},{2,3},{3,2},{4,5},{5,4},{6,7},{7,6},{8,9},{9,8},{10,11... | collective-permute-start | bytes 417800 | tf_op jit(solution)/shard_map/ppermute | solution.py:40
  (9 other events, 34.7 us)
where the time goes:
time: 122 us; the launch traced here: 121 us
  starting transfers between devices  51.5 us (42%)
  waiting for transfers between devices  34.2 us (28%)
  Pallas kernels  27.5 us (23%)
  local copies, waits for them, and re-layouts  7.76 us (6%)
    ppermute x31, starting transfers between devices, move(): return lax.ppermute(value, ('seq', 'mp'), pairs)  43.9 us
    ppermute x31, waiting for transfers between devices, move(): return lax.ppermute(value, ('seq', 'mp'), pairs)  34.2 us
    pallas_call x18, Pallas kernels, call(): pl.pallas_call(body, out_shape=outs, in_specs=[SMEM] + [far if i in far_i...  23.7 us
    unnamed x16, local copies, waits for them, and re-layouts  7.07 us
    ppermute x1, starting transfers between devices, shards(): above = lax.ppermute(head, 'seq', [(i, i - 1) for i in range(1, count)])  4.27 us
    pallas_call x1, Pallas kernels, output(): pl.pallas_call(output_kernel, grid=(TOK // BLOCK,), out_shape=shape((TOK,...  3.82 us
    ppermute x1, starting transfers between devices, shards(): below = lax.ppermute(tail, 'seq', [(i, i + 1) for i in range(count - 1)])  3.25 us
  transfers between devices with their start and end apart: 33, of which 11 were waited for; matrix products, arithmetic and copies ran while one was open for 0% of the time, Pallas kernels for 16%

commit v1 on v0

--- a/solution.py
+++ b/solution.py
@@ -20,6 +20,7 @@
 LOG2E = 1.4426950408889634
 LOW = -1e30
 VMEM_LIMIT = 20 * 1024 * 1024
+ROOM = 48 * 1024 * 1024
 F32, BF16 = jnp.float32, jnp.bfloat16
 
 
@@ -100,15 +101,15 @@
 DISTANT = pl.BlockSpec(memory_space=pltpu.HBM)
 
 
-def call(body, outs, ins, flops=0, moved=0, scratch=(), aliases=None, far_in=(), far_out=(), far=FAR):
+def call(body, outs, ins, flops=0, moved=0, scratch=(), aliases=None, far_in=(), far_out=(), far=FAR, scalars=0, room=VMEM_LIMIT):
     return pl.pallas_call(
         body,
         out_shape=outs,
-        in_specs=[SMEM] + [far if i in far_in else WHOLE for i in range(1, len(ins))],
+        in_specs=[SMEM if i == scalars else far if i in far_in else WHOLE for i in range(len(ins))],
         out_specs=[far if i in far_out else WHOLE for i in range(len(outs))],
         scratch_shapes=list(scratch),
         input_output_aliases=aliases or {},
-        compiler_params=pltpu.CompilerParams(vmem_limit_bytes=VMEM_LIMIT),
+        compiler_params=pltpu.CompilerParams(vmem_limit_bytes=room),
         cost_estimate=pl.CostEstimate(flops=flops, bytes_accessed=moved, transcendentals=0),
     )(*ins)
 
@@ -146,7 +147,7 @@
     return jnp.where(condition, 1.0, 0.0).astype(BF16)
 
 
-def edge_kernel(info, flags, tokens, ids_out, head_out, tail_out, marks):
+def edge_kernel(flags, tokens, ids_out, head_out, tail_out, marks):
     f = flags[...].astype(F32).astype(BF16)
     upto = ones_where(iota((128, 128), 0) <= iota((128, 128), 1))
     inside = dot(f, upto)
@@ -164,7 +165,7 @@
     tail_out[:, FEAT:] = counts[8:]
 
 
-def pool_kernel(info, ids, tokens, sums_out, counts_out, hot):
+def pool_kernel(ids, tokens, sums_out, counts_out, hot):
     segment = iota((SEG, 128), 0)
     for r in range(16):
         hot[:, r * 128 : (r + 1) * 128] = ones_where(ids[r : r + 1, :] == segment)
@@ -224,14 +225,13 @@
 
 def product(acc, blocks, weight, rows):
     for i, u in enumerate(blocks):
-        part = dot(u[:rows, :], weight[i])
-        acc = part if acc is None else acc + part
+        acc = acc + dot(u[:rows, :], weight[i])
     return acc
 
 
 def early_kernel(info, *refs):
     blocks, weights = refs[:4], refs[4:7]
-    sums, kept, early, sems = refs[8:11], refs[11:14], refs[14:17], refs[17]
+    sums, kept, early, sems = refs[7:10], refs[10:13], refs[13:16], refs[16]
     copies = {}
     for side, (which, target) in enumerate(((EARLY, early), (LATE, kept))):
         for i in range(4):
@@ -309,6 +309,8 @@
     queries = [refs.pop(0) for _ in range(4)]
     own = refs.pop(0) if first else None
     others = [refs.pop(0) for _ in range(1 if final else 2)]
+    if not final:
+        refs = refs[1:]
     if not first:
         state_in = [refs.pop(0) for _ in range(2)]
     if final:
@@ -376,9 +378,9 @@
 STATE = [shape((4, 2, ROWS, 2 * HD), F32), shape((4, 2, ROWS, HD), F32), shape((8, 128), F32)]
 
 
-def attend_step(step, info, queries, own, others, state):
+def attend_step(step, info, queries, own, others, state, ahead=None):
     first, final = own is not None, len(others) == 1
-    ins = [info] + queries + ([own] if first else []) + others + list(state or [])
+    ins = [info] + queries + ([own] if first else []) + others + ([] if final else [ahead]) + list(state or [])
     flops = 4 * 1088 * SEG * (len(others) + (1 if first else 0)) * COLS
     body = functools.partial(attend_kernel, step, first, final)
     if final:
@@ -392,7 +394,8 @@
 
         return call(body, outs, ins, flops=flops, moved=4 << 20, aliases=aliases)[:4]
     aliases = {} if first else {len(ins) - 2: 0, len(ins) - 1: 1}
-    return call(body, STATE, ins, flops=flops, moved=4 << 20, aliases=aliases)
+    ignored = 5 + len(others) + (1 if first else 0)
+    return call(body, STATE, ins, flops=flops, moved=4 << 20, aliases=aliases, far_in=(ignored,))
 
 
 def merge_kernel(info, a, b, c, d, out):
@@ -474,7 +477,7 @@
     )(*attended, *weights, means, ids, tokens)
 
 
-def cut_kernel(info, w_out, mine, sibling, sems):
+def cut_kernel(info, w_out, _, mine, sibling, sems):
     copies = []
     for i in range(4):
         for side, out in enumerate((mine, sibling)):
@@ -486,7 +489,7 @@
 
 
 def pair_kernel(info, *refs):
-    sources, outs, sems = refs[:2], refs[2:6], refs[6]
+    sources, outs, sems = refs[:2], refs[3:7], refs[7]
     copies = []
     for i, out in enumerate(outs):
         for side, source in enumerate(sources):
@@ -507,7 +510,8 @@
     ids, head, tail = call(
         edge_kernel,
         [shape((16, 128), jnp.int32), edge, edge],
-        [info, flags.reshape(16, 128), tokens],
+        [flags.reshape(16, 128), tokens],
+        scalars=None,
         flops=1 << 28,
         moved=2 << 20,
         scratch=[pltpu.VMEM((16, TOK), BF16)],
@@ -518,7 +522,8 @@
     sums, sizes = call(
         pool_kernel,
         [shape((SEG, FEAT), F32), shape((SEG, 128), F32)],
-        [info, ids, tokens],
+        [ids, tokens],
+        scalars=None,
         flops=1 << 30,
         moved=2 << 20,
         scratch=[pltpu.VMEM((SEG, TOK), BF16)],
@@ -527,65 +532,57 @@
         norm_kernel,
         [shape((ROWS, FEAT), F32), shape((ROWS, FEAT), BF16), shape((16, FEAT), BF16)],
         [info, sums, sizes, head, above, below, norm_gain.reshape(8, FEAT)],
-        moved=2 << 20,
+    )
+    first, sibling, second = y_one(u), swap(u), y_other(u)
+    across, far = swap(first), y_one(first)
+    part, part_query = shape((SEG, COLS), F32), shape((ROWS, COLS), F32)
+    kept = shape((4, FEAT, COLS), BF16)
+    queried, keyed, valued, *late = call(
+        early_kernel,
+        [part_query, part, part] + [kept] * 3,
+        [info, u, first, sibling, across, w_query, w_key, w_value],
+        scratch=[pltpu.VMEM((4, FEAT, COLS), BF16)] * 3 + [pltpu.SemaphoreType.DMA((2, 4, 3))],
+        far_in=(5, 6, 7),
+        room=ROOM,
     )
     cut = shape((4, SEG, FEAT), BF16)
     sems = [pltpu.SemaphoreType.DMA((2, 4))]
     mine, theirs = call(
-        cut_kernel, [cut, cut], [info, w_out], moved=4 << 20, scratch=sems, far_in=(1,), far_out=(0, 1), far=DISTANT
-    )
-    first, sibling, second = y_one(u), swap(u), y_other(u)
-    part, part_query = shape((SEG, COLS), F32), shape((ROWS, COLS), F32)
-    kept = shape((4, FEAT, COLS), BF16)
-    across = swap(first)
-    queried, keyed, valued, *late = call(
-        early_kernel,
-        [part_query, part, part] + [kept] * 3,
-        [info, u, first, sibling, across, w_query, w_key, w_value, mine],
-        flops=ROWS * WIDTH * 3 * COLS,
-        moved=8 << 20,
-        scratch=[pltpu.VMEM((4, FEAT, COLS), BF16)] * 3 + [pltpu.SemaphoreType.DMA((2, 4, 3))],
-        far_in=(5, 6, 7, 8),
-    )
-    (far,) = gate(info, [y_one(first)], queried)
+        cut_kernel, [cut, cut], [info, w_out, second], scratch=sems, far_in=(1, 2), far_out=(0, 1), room=ROOM
+    )
     theirs = swap(theirs)
     blocks = [u, first, second, far, sibling, across, swap(second), swap(far)]
     (kv,) = call(
         key_value_kernel,
         [shape((ROWS, 2 * COLS), BF16)],
         [info] + blocks + [late[1], late[2], keyed, valued, bias],
-        flops=ROWS * WIDTH * 2 * COLS,
-        moved=4 << 20,
     )
     (query,) = call(
         query_kernel,
         [shape((ROWS, COLS), BF16)],
         [info] + blocks + [late[0], queried],
-        flops=ROWS * WIDTH * COLS,
-        moved=2 << 20,
-    )
+    )
+    queries = [query] + [x_by(query, k) for k in (1, 2, 3)]
     one, other = z_one(kv), z_other(kv)
-    queries = [query] + [x_by(query, k) for k in (1, 2, 3)]
     pair = shape((2, SEG, FEAT), BF16)
     pairs = call(
         pair_kernel,
         [pair] * 4,
-        [info, mine, theirs],
-        moved=4 << 20,
+        [info, mine, theirs, one],
         scratch=sems,
-        far_in=(1, 2),
+        far_in=(1, 2, 3),
         far_out=range(4),
-        far=DISTANT,
-    )
-    queries[0], *pairs = gate(info, [query, *pairs], info)
+    )
     weights = [pairs[0], y_one(pairs[1]), y_other(pairs[2]), y_far(pairs[3])]
-    *state, done = attend_step(1, info, queries, kv, [one, other], None)
-    one, other = gate(info, [z_one(one), z_other(other)], done)
-    *state, done = attend_step(2, info, queries, None, [one, other], state)
-    one, other, weights[1], weights[2] = gate(info, [z_one(one), z_other(other), weights[1], weights[2]], done)
-    *state, done = attend_step(3, info, queries, None, [one, other], state)
-    one, weights[3] = gate(info, [z_one(one), weights[3]], done)
-    partial = attend_step(4, info, queries, None, [one], state)
+    one2, other2 = z_one(one), z_other(other)
+    one3, other3 = z_one(one2), z_other(other2)
+    *state, done = attend_step(1, info, queries, kv, [one, other], None, pairs[0])
+    *state, done = attend_step(2, info, queries, None, [one2, other2], state, weights[1])
+    one3, other3 = gate(info, [one3, other3], done)
+    one4 = z_one(one3)
+    *state, done = attend_step(3, info, queries, None, [one3, other3], state, weights[2])
+    one4, weights[3] = gate(info, [one4, weights[3]], done)
+    partial = attend_step(4, info, queries, None, [one4], state)
     partial = [partial[0]] + [x_by(partial[k], -k) for k in (1, 2, 3)]
     (attended,) = call(merge_kernel, [shape((ROWS, COLS), BF16)], [info] + partial, moved=1 << 20)
     return output(mp_exchange(attended), weights, means, ids, tokens)

time: 122 us -> 123 us (level)
  the two profiles are of different devices: /device:TPU:65 before, /device:TPU:1 now
where the time goes in v1:
time: 123 us
  starting transfers between devices  55.2 us (45%)
  waiting for transfers between devices  40.5 us (33%)
  Pallas kernels  22 us (18%)
  local copies, waits for them, and re-layouts  4.59 us (4%)
    ppermute x31, starting transfers between devices, move(): return lax.ppermute(value, ('seq', 'mp'), pairs)  49.2 us
    ppermute x31, waiting for transfers between devices, move(): return lax.ppermute(value, ('seq', 'mp'), pairs)  40.5 us
    pallas_call x15, Pallas kernels, call(): pl.pallas_call(body, out_shape=outs, in_specs=[SMEM if i == scalars else...  18.2 us
    ppermute x1, starting transfers between devices, shards(): below = lax.ppermute(tail, 'seq', [(i, i + 1) for i in range(count - 1)])  4.57 us
    unnamed x10, local copies, waits for them, and re-layouts  3.89 us
    pallas_call x1, Pallas kernels, output(): pl.pallas_call(output_kernel, grid=(TOK // BLOCK,), out_shape=shape((TOK,...  3.82 us
  transfers between devices with their start and end apart: 33, of which 14 were waited for; matrix products, arithmetic and copies ran while one was open for 1% of the time, Pallas kernels for 12%

profile of v1, /device:TPU:1, one launch (start us, length us, event | category | flops | bytes accessed | tf_op | source)
XLA Modules:
  0.0 122.6 jit_solution(13091816017459423833)
XLA Ops:
  0.0 1.6 %copy-done = bf16[2048,512]{1,0:T(8,128)(2,1)S(1)} copy-done((bf16[2048,512]{1,0:T(8,128)(2,1)S(1)}, bf16[2048,512]{1,0:T(8,128)(2,1)}, u32[]{:S(2)}) %copy-start) | copy-done | bytes 2097176
  3.0 1.4 %collective-permute-start = (f32[8,640]{1,0:T(8,128)S(1)}, f32[8,640]{1,0:T(8,128)S(1)}, u32[]{:S(2)}, u32[]{:S(2)}) collective-permute-start(f32[8,640]{1,0:T(8,128)S(1)} %get-tuple-element.44.head), channel_id=1, source_target_pairs={{8,0},{16,8},{24,16},{32,24},{40,32},{48,40},{56,48},{64,56},{72,6... | collective-permute-start | bytes 61448 | tf_op jit(solution)/shard_map/ppermute | solution.py:520
  4.4 4.6 %collective-permute-start.1 = (f32[8,640]{1,0:T(8,128)S(1)}, f32[8,640]{1,0:T(8,128)S(1)}, u32[]{:S(2)}, u32[]{:S(2)}) collective-permute-start(f32[8,640]{1,0:T(8,128)S(1)} %get-tuple-element.45), channel_id=1, source_target_pairs={{0,8},{8,16},{16,24},{24,32},{32,40},{40,48},{48,56},{56,64},{64,7... | collective-permute-start | bytes 61448 | tf_op jit(solution)/shard_map/ppermute | solution.py:521
  11.6 1.6 %collective-permute-start.3 = (bf16[272,512]{1,0:T(8,128)(2,1)S(1)}, bf16[272,512]{1,0:T(8,128)(2,1)S(1)}, u32[]{:S(2)}, u32[]{:S(2)}) collective-permute-start(bf16[272,512]{1,0:T(8,128)(2,1)S(1)} %get-tuple-element.46.refs_0_), channel_id=1, source_target_pairs={{0,6},{1,3},{2,0},{3,5},{4,2},{5,7},{6,4},{7,1},{8,14},{9,11},{10,... | collective-permute-start | bytes 835592 | tf_op jit(solution)/shard_map/ppermute | solution.py:41
  13.2 1.5 %collective-permute-start.2 = (bf16[272,512]{1,0:T(8,128)(2,1)S(1)}, bf16[272,512]{1,0:T(8,128)(2,1)S(1)}, u32[]{:S(2)}, u32[]{:S(2)}) collective-permute-start(bf16[272,512]{1,0:T(8,128)(2,1)S(1)} %get-tuple-element.46.refs_0_), channel_id=1, source_target_pairs={{0,2},{1,7},{2,4},{3,1},{4,6},{5,3},{6,0},{7,5},{8,10},{9,15},{10,... | collective-permute-start | bytes 835592 | tf_op jit(solution)/shard_map/ppermute | solution.py:41
  14.7 3.8 %collective-permute-done.3.refs_2_._ = bf16[272,512]{1,0:T(8,128)(2,1)S(1)} collective-permute-done((bf16[272,512]{1,0:T(8,128)(2,1)S(1)}, bf16[272,512]{1,0:T(8,128)(2,1)S(1)}, u32[]{:S(2)}, u32[]{:S(2)}) %collective-permute-start.3) | collective-permute-done | bytes 278560 | tf_op jit(solution)/shard_map/ppermute | solution.py:41
  18.5 1.6 %copy-done.2 = bf16[256,4096]{1,0:T(8,128)(2,1)S(1)} copy-done((bf16[256,4096]{1,0:T(8,128)(2,1)S(1)}, bf16[256,4096]{1,0:T(8,128)(2,1)}, u32[]{:S(2)}) %copy-start.2) | copy-done | bytes 2097176
  21.0 3.8 %collective-permute-start.18 = (bf16[4,256,512]{2,1,0:T(8,128)(2,1)S(1)}, bf16[4,256,512]{2,1,0:T(8,128)(2,1)S(1)}, u32[]{:S(2)}, u32[]{:S(2)}) collective-permute-start(bf16[4,256,512]{2,1,0:T(8,128)(2,1)S(1)} %get-tuple-element.55), channel_id=1, source_target_pairs={{0,1},{1,0},{2,3},{3,2},{4,5},{5,4},{6,7},{7,6},{8,9},{9,8},{10,11... | collective-permute-start | bytes 3145736 | tf_op jit(solution)/shard_map/ppermute | solution.py:41
  24.7 2.7 %collective-permute-start.4 = (bf16[272,512]{1,0:T(8,128)(2,1)S(1)}, bf16[272,512]{1,0:T(8,128)(2,1)S(1)}, u32[]{:S(2)}, u32[]{:S(2)}) collective-permute-start(bf16[272,512]{1,0:T(8,128)(2,1)S(1)} %collective-permute-done.2.refs_1_), channel_id=1, source_target_pairs={{0,2},{1,7},{2,4},{3,1},{4,6},{5,3},{6,0},{7,5},{8,10},{9,15},{10,... | collective-permute-start | bytes 835592 | tf_op jit(solution)/shard_map/ppermute | solution.py:41
  28.0 3.0 %collective-permute-done.4.refs_3_ = bf16[272,512]{1,0:T(8,128)(2,1)S(1)} collective-permute-done((bf16[272,512]{1,0:T(8,128)(2,1)S(1)}, bf16[272,512]{1,0:T(8,128)(2,1)S(1)}, u32[]{:S(2)}, u32[]{:S(2)}) %collective-permute-start.4) | collective-permute-done | bytes 278560 | tf_op jit(solution)/shard_map/ppermute | solution.py:41
  31.0 1.6 %collective-permute-start.8 = (bf16[272,512]{1,0:T(8,128)(2,1)S(1)}, bf16[272,512]{1,0:T(8,128)(2,1)S(1)}, u32[]{:S(2)}, u32[]{:S(2)}) collective-permute-start(bf16[272,512]{1,0:T(8,128)(2,1)S(1)} %collective-permute-done.4.refs_3_), channel_id=1, source_target_pairs={{0,1},{1,0},{2,3},{3,2},{4,5},{5,4},{6,7},{7,6},{8,9},{9,8},{10,11... | collective-permute-start | bytes 835592 | tf_op jit(solution)/shard_map/ppermute | solution.py:41
  32.6 4.3 %shard_map.85 = (f32[272,256]{1,0:T(8,128)S(1)}, f32[256,256]{1,0:T(8,128)S(1)}, f32[256,256]{1,0:T(8,128)S(1)}, bf16[4,512,256]{2,1,0:T(8,128)(2,1)S(1)}, bf16[...) custom-call(s32[32]{0:T(128)S(1)} %dynamic-slice_bitcast_fusion.info.refs_0_, ...), custom_call_target="tpu_custom_call" | custom-call | tf_op jit(solution)/shard_map/pallas_call | solution.py:105
  36.9 1.3 %shard_map.87.refs_4_ = bf16[272,512]{1,0:T(8,128)(2,1)S(1)} custom-call(s32[32]{0:T(128)S(1)} %dynamic-slice_bitcast_fusion.info.refs_0_, bf16[272,512]{1,0:T(8,128)(2,1)S(1)} %get-tuple-element.46.refs_0_, bf16[272,512]{1,0:T(8,128)(2,1)S(1)} %collective-permute-done.2.refs_1_, bf16[272,512]{1,0:T(8,128)(2,1)S(1)} %collective-permute-done.3.refs_2_._, ...), custom_call_target="tpu_custom_call" | custom-call | tf_op jit(solution)/shard_map/pallas_call | solution.py:105
  38.2 10.1 %collective-permute-start.12 = (bf16[272,512]{1,0:T(8,128)(2,1)S(1)}, bf16[272,512]{1,0:T(8,128)(2,1)S(1)}, u32[]{:S(2)}, u32[]{:S(2)}) collective-permute-start(bf16[272,512]{1,0:T(8,128)(2,1)S(1)} %shard_map.87.refs_4_), channel_id=1, source_target_pairs={{0,32},{1,225},{2,34},{3,227},{4,36},{5,229},{6,38},{7,231},{8,40}... | collective-permute-start | bytes 835592 | tf_op jit(solution)/shard_map/ppermute | solution.py:41
  48.3 6.0 %collective-permute-done.12.refs_2_.refs_5_ = bf16[272,512]{1,0:T(8,128)(2,1)S(1)} collective-permute-done((bf16[272,512]{1,0:T(8,128)(2,1)S(1)}, bf16[272,512]{1,0:T(8,128)(2,1)S(1)}, u32[]{:S(2)}, u32[]{:S(2)}) %collective-permute-start.12) | collective-permute-done | bytes 278560 | tf_op jit(solution)/shard_map/ppermute | solution.py:41
  56.1 3.4 %collective-permute-start.13 = (bf16[272,512]{1,0:T(8,128)(2,1)S(1)}, bf16[272,512]{1,0:T(8,128)(2,1)S(1)}, u32[]{:S(2)}, u32[]{:S(2)}) collective-permute-start(bf16[272,512]{1,0:T(8,128)(2,1)S(1)} %collective-permute-done.12.refs_2_.refs_5_), channel_id=1, source_target_pairs={{0,32},{1,225},{2,34},{3,227},{4,36},{5,229},{6,38},{7,231},{8,40}... | collective-permute-start | bytes 835592 | tf_op jit(solution)/shard_map/ppermute | solution.py:41
  60.9 6.8 %collective-permute-done.10.refs_2_.refs_3_ = bf16[272,256]{1,0:T(8,128)(2,1)S(1)} collective-permute-done((bf16[272,256]{1,0:T(8,128)(2,1)S(1)}, bf16[272,256]{1,0:T(8,128)(2,1)S(1)}, u32[]{:S(2)}, u32[]{:S(2)}) %collective-permute-start.10) | collective-permute-done | bytes 139296 | tf_op jit(solution)/shard_map/ppermute | solution.py:41
  67.9 2.4 %collective-permute-start.14 = (bf16[272,512]{1,0:T(8,128)(2,1)S(1)}, bf16[272,512]{1,0:T(8,128)(2,1)S(1)}, u32[]{:S(2)}, u32[]{:S(2)}) collective-permute-start(bf16[272,512]{1,0:T(8,128)(2,1)S(1)} %collective-permute-done.13.refs_4_), channel_id=1, source_target_pairs={{0,32},{1,225},{2,34},{3,227},{4,36},{5,229},{6,38},{7,231},{8,40}... | collective-permute-start | bytes 835592 | tf_op jit(solution)/shard_map/ppermute | solution.py:41
  70.3 3.5 %collective-permute-done.9.refs_1_.refs_2_ = bf16[272,256]{1,0:T(8,128)(2,1)S(1)} collective-permute-done((bf16[272,256]{1,0:T(8,128)(2,1)S(1)}, bf16[272,256]{1,0:T(8,128)(2,1)S(1)}, u32[]{:S(2)}, u32[]{:S(2)}) %collective-permute-start.9) | collective-permute-done | bytes 139296 | tf_op jit(solution)/shard_map/ppermute | solution.py:41
  73.7 3.2 %shard_map.90 = (f32[4,2,272,256]{3,2,1,0:T(8,128)S(1)}, f32[4,2,272,128]{3,2,1,0:T(8,128)S(1)}, f32[8,128]{1,0:T(8,128)}) custom-call(s32[32]{0:T(128)S(1)} %dynamic-slice_bitcast_fusion.info.refs_0_, bf16[272,256]{1,0:T(8,128)(2,1)S(1)} %shard_map.86.refs_0_.refs_1_, bf16[272,256]{1,0:T(8,128)(2,1)S(1)} %collective-permute-done.9.refs_1_.refs_2_, ...), custom_call_target="tpu_custom_call" | custom-call | flops 855638016 | bytes 4194304 | tf_op jit(solution)/shard_map/pallas_call | solution.py:105
  77.5 1.9 %collective-permute-done.17.refs_1_ = bf16[272,512]{1,0:T(8,128)(2,1)S(1)} collective-permute-done((bf16[272,512]{1,0:T(8,128)(2,1)S(1)}, bf16[272,512]{1,0:T(8,128)(2,1)S(1)}, u32[]{:S(2)}, u32[]{:S(2)}) %collective-permute-start.17) | collective-permute-done | bytes 278560 | tf_op jit(solution)/shard_map/ppermute | solution.py:41
  80.0 4.3 %collective-permute-start.20 = (bf16[272,512]{1,0:T(8,128)(2,1)S(1)}, bf16[272,512]{1,0:T(8,128)(2,1)S(1)}, u32[]{:S(2)}, u32[]{:S(2)}) collective-permute-start(bf16[272,512]{1,0:T(8,128)(2,1)S(1)} %get-tuple-element.61.refs_4_), channel_id=1, source_target_pairs={{0,32},{1,225},{2,34},{3,227},{4,36},{5,229},{6,38},{7,231},{8,40}... | collective-permute-start | bytes 835592 | tf_op jit(solution)/shard_map/ppermute | solution.py:41
  85.0 2.3 %collective-permute-done.21.refs_1_ = bf16[2,256,512]{2,1,0:T(8,128)(2,1)S(1)} collective-permute-done((bf16[2,256,512]{2,1,0:T(8,128)(2,1)S(1)}, bf16[2,256,512]{2,1,0:T(8,128)(2,1)S(1)}, u32[]{:S(2)}, u32[]{:S(2)}) %collective-permute-start.21) | collective-permute-done | bytes 524320 | tf_op jit(solution)/shard_map/ppermute | solution.py:41
  89.2 4.3 %collective-permute-start.23 = (bf16[272,256]{1,0:T(8,128)(2,1)S(1)}, bf16[272,256]{1,0:T(8,128)(2,1)S(1)}, u32[]{:S(2)}, u32[]{:S(2)}) collective-permute-start(bf16[272,256]{1,0:T(8,128)(2,1)S(1)} %get-tuple-element.72), channel_id=1, source_target_pairs={{0,24},{1,25},{2,26},{3,27},{4,28},{5,29},{6,30},{7,31},{8,0},{9,1... | collective-permute-start | bytes 417800 | tf_op jit(solution)/shard_map/ppermute | solution.py:41
  94.2 5.2 %collective-permute-done.23.b = bf16[272,256]{1,0:T(8,128)(2,1)S(1)} collective-permute-done((bf16[272,256]{1,0:T(8,128)(2,1)S(1)}, bf16[272,256]{1,0:T(8,128)(2,1)S(1)}, u32[]{:S(2)}, u32[]{:S(2)}) %collective-permute-start.23) | collective-permute-done | bytes 139296 | tf_op jit(solution)/shard_map/ppermute | solution.py:41
  99.8 3.2 %collective-permute-done.25.d = bf16[272,256]{1,0:T(8,128)(2,1)S(1)} collective-permute-done((bf16[272,256]{1,0:T(8,128)(2,1)S(1)}, bf16[272,256]{1,0:T(8,128)(2,1)S(1)}, u32[]{:S(2)}, u32[]{:S(2)}) %collective-permute-start.25) | collective-permute-done | bytes 139296 | tf_op jit(solution)/shard_map/ppermute | solution.py:41
  102.9 1.1 shard_map.96.refs_0_
  104.1 1.5 %collective-permute-start.27 = (bf16[272,256]{1,0:T(8,128)(2,1)S(1)}, bf16[272,256]{1,0:T(8,128)(2,1)S(1)}, u32[]{:S(2)}, u32[]{:S(2)}) collective-permute-start(bf16[272,256]{1,0:T(8,128)(2,1)S(1)} %shard_map.96.refs_0_), channel_id=1, source_target_pairs={{0,6},{1,3},{2,0},{3,5},{4,2},{5,7},{6,4},{7,1},{8,14},{9,11},{10,... | collective-permute-start | bytes 417800 | tf_op jit(solution)/shard_map/ppermute | solution.py:41
  105.6 2.8 %collective-permute-done.26.refs_1_ = bf16[272,256]{1,0:T(8,128)(2,1)S(1)} collective-permute-done((bf16[272,256]{1,0:T(8,128)(2,1)S(1)}, bf16[272,256]{1,0:T(8,128)(2,1)S(1)}, u32[]{:S(2)}, u32[]{:S(2)}) %collective-permute-start.26) | collective-permute-done | bytes 139296 | tf_op jit(solution)/shard_map/ppermute | solution.py:41
  109.2 2.3 %collective-permute-start.29 = (bf16[272,256]{1,0:T(8,128)(2,1)S(1)}, bf16[272,256]{1,0:T(8,128)(2,1)S(1)}, u32[]{:S(2)}, u32[]{:S(2)}) collective-permute-start(bf16[272,256]{1,0:T(8,128)(2,1)S(1)} %shard_map.96.refs_0_), channel_id=1, source_target_pairs={{0,1},{1,0},{2,3},{3,2},{4,5},{5,4},{6,7},{7,6},{8,9},{9,8},{10,11... | collective-permute-start | bytes 417800 | tf_op jit(solution)/shard_map/ppermute | solution.py:41
  112.3 5.5 %collective-permute-start.32 = (bf16[272,256]{1,0:T(8,128)(2,1)S(1)}, bf16[272,256]{1,0:T(8,128)(2,1)S(1)}, u32[]{:S(2)}, u32[]{:S(2)}) collective-permute-start(bf16[272,256]{1,0:T(8,128)(2,1)S(1)} %collective-permute-done.28.refs_3_), channel_id=1, source_target_pairs={{0,1},{1,0},{2,3},{3,2},{4,5},{5,4},{6,7},{7,6},{8,9},{9,8},{10,11... | collective-permute-start | bytes 417800 | tf_op jit(solution)/shard_map/ppermute | solution.py:41
  118.8 3.8 %shard_map.97 = bf16[2048,512]{1,0:T(8,128)(2,1)} custom-call(bf16[272,256]{1,0:T(8,128)(2,1)S(1)} %shard_map.96.refs_0_, bf16[272,256]{1,0:T(8,128)(2,1)S(1)} %collective-permute-done.26.refs_1_, bf16[272,256]{1,0:T(8,128)(2,1)S(1)} %collective-permute-done.27.refs_2_, bf16[272,256]{1,0:T(8,128)(2,1)S(1)} %collective-permute-done.28.refs_3_, ...), custom_call_target="tpu_custom_call" | custom-call | flops 2147483648 | bytes 6291456 | tf_op jit(solution)/shard_map/pallas_call | solution.py:468
  (62 shorter events, 16.0 us)
Async XLA Ops:
  3.0 7.8 %collective-permute-start = (f32[8,640]{1,0:T(8,128)S(1)}, f32[8,640]{1,0:T(8,128)S(1)}, u32[]{:S(2)}, u32[]{:S(2)}) collective-permute-start(f32[8,640]{1,0:T(8,128)S(1)} %get-tuple-element.44.head), channel_id=1, source_target_pairs={{8,0},{16,8},{24,16},{32,24},{40,32},{48,40},{56,48},{64,56},{72,6... | collective-permute-start | bytes 61448 | tf_op jit(solution)/shard_map/ppermute | solution.py:520
  4.4 6.3 %collective-permute-start.1 = (f32[8,640]{1,0:T(8,128)S(1)}, f32[8,640]{1,0:T(8,128)S(1)}, u32[]{:S(2)}, u32[]{:S(2)}) collective-permute-start(f32[8,640]{1,0:T(8,128)S(1)} %get-tuple-element.45), channel_id=1, source_target_pairs={{0,8},{8,16},{16,24},{24,32},{32,40},{40,48},{48,56},{56,64},{64,7... | collective-permute-start | bytes 61448 | tf_op jit(solution)/shard_map/ppermute | solution.py:521
  11.6 7.0 %collective-permute-start.3 = (bf16[272,512]{1,0:T(8,128)(2,1)S(1)}, bf16[272,512]{1,0:T(8,128)(2,1)S(1)}, u32[]{:S(2)}, u32[]{:S(2)}) collective-permute-start(bf16[272,512]{1,0:T(8,128)(2,1)S(1)} %get-tuple-element.46.refs_0_), channel_id=1, source_target_pairs={{0,6},{1,3},{2,0},{3,5},{4,2},{5,7},{6,4},{7,1},{8,14},{9,11},{10,... | collective-permute-start | bytes 835592 | tf_op jit(solution)/shard_map/ppermute | solution.py:41
  13.2 11.6 %collective-permute-start.2 = (bf16[272,512]{1,0:T(8,128)(2,1)S(1)}, bf16[272,512]{1,0:T(8,128)(2,1)S(1)}, u32[]{:S(2)}, u32[]{:S(2)}) collective-permute-start(bf16[272,512]{1,0:T(8,128)(2,1)S(1)} %get-tuple-element.46.refs_0_), channel_id=1, source_target_pairs={{0,2},{1,7},{2,4},{3,1},{4,6},{5,3},{6,0},{7,5},{8,10},{9,15},{10,... | collective-permute-start | bytes 835592 | tf_op jit(solution)/shard_map/ppermute | solution.py:41
  21.0 33.3 %collective-permute-start.18 = (bf16[4,256,512]{2,1,0:T(8,128)(2,1)S(1)}, bf16[4,256,512]{2,1,0:T(8,128)(2,1)S(1)}, u32[]{:S(2)}, u32[]{:S(2)}) collective-permute-start(bf16[4,256,512]{2,1,0:T(8,128)(2,1)S(1)} %get-tuple-element.55), channel_id=1, source_target_pairs={{0,1},{1,0},{2,3},{3,2},{4,5},{5,4},{6,7},{7,6},{8,9},{9,8},{10,11... | collective-permute-start | bytes 3145736 | tf_op jit(solution)/shard_map/ppermute | solution.py:41
  24.7 6.2 %collective-permute-start.4 = (bf16[272,512]{1,0:T(8,128)(2,1)S(1)}, bf16[272,512]{1,0:T(8,128)(2,1)S(1)}, u32[]{:S(2)}, u32[]{:S(2)}) collective-permute-start(bf16[272,512]{1,0:T(8,128)(2,1)S(1)} %collective-permute-done.2.refs_1_), channel_id=1, source_target_pairs={{0,2},{1,7},{2,4},{3,1},{4,6},{5,3},{6,0},{7,5},{8,10},{9,15},{10,... | collective-permute-start | bytes 835592 | tf_op jit(solution)/shard_map/ppermute | solution.py:41
  27.5 5.1 %collective-permute-start.5 = (bf16[272,512]{1,0:T(8,128)(2,1)S(1)}, bf16[272,512]{1,0:T(8,128)(2,1)S(1)}, u32[]{:S(2)}, u32[]{:S(2)}) collective-permute-start(bf16[272,512]{1,0:T(8,128)(2,1)S(1)} %get-tuple-element.46.refs_0_), channel_id=1, source_target_pairs={{0,1},{1,0},{2,3},{3,2},{4,5},{5,4},{6,7},{7,6},{8,9},{9,8},{10,11... | collective-permute-start | bytes 835592 | tf_op jit(solution)/shard_map/ppermute | solution.py:41
  27.5 5.1 %collective-permute-start.6 = (bf16[272,512]{1,0:T(8,128)(2,1)S(1)}, bf16[272,512]{1,0:T(8,128)(2,1)S(1)}, u32[]{:S(2)}, u32[]{:S(2)}) collective-permute-start(bf16[272,512]{1,0:T(8,128)(2,1)S(1)} %collective-permute-done.2.refs_1_), channel_id=1, source_target_pairs={{0,1},{1,0},{2,3},{3,2},{4,5},{5,4},{6,7},{7,6},{8,9},{9,8},{10,11... | collective-permute-start | bytes 835592 | tf_op jit(solution)/shard_map/ppermute | solution.py:41
  28.0 8.9 %collective-permute-start.7 = (bf16[272,512]{1,0:T(8,128)(2,1)S(1)}, bf16[272,512]{1,0:T(8,128)(2,1)S(1)}, u32[]{:S(2)}, u32[]{:S(2)}) collective-permute-start(bf16[272,512]{1,0:T(8,128)(2,1)S(1)} %collective-permute-done.3.refs_2_._), channel_id=1, source_target_pairs={{0,1},{1,0},{2,3},{3,2},{4,5},{5,4},{6,7},{7,6},{8,9},{9,8},{10,11... | collective-permute-start | bytes 835592 | tf_op jit(solution)/shard_map/ppermute | solution.py:41
  31.0 5.9 %collective-permute-start.8 = (bf16[272,512]{1,0:T(8,128)(2,1)S(1)}, bf16[272,512]{1,0:T(8,128)(2,1)S(1)}, u32[]{:S(2)}, u32[]{:S(2)}) collective-permute-start(bf16[272,512]{1,0:T(8,128)(2,1)S(1)} %collective-permute-done.4.refs_3_), channel_id=1, source_target_pairs={{0,1},{1,0},{2,3},{3,2},{4,5},{5,4},{6,7},{7,6},{8,9},{9,8},{10,11... | collective-permute-start | bytes 835592 | tf_op jit(solution)/shard_map/ppermute | solution.py:41
  38.2 16.1 %collective-permute-start.12 = (bf16[272,512]{1,0:T(8,128)(2,1)S(1)}, bf16[272,512]{1,0:T(8,128)(2,1)S(1)}, u32[]{:S(2)}, u32[]{:S(2)}) collective-permute-start(bf16[272,512]{1,0:T(8,128)(2,1)S(1)} %shard_map.87.refs_4_), channel_id=1, source_target_pairs={{0,32},{1,225},{2,34},{3,227},{4,36},{5,229},{6,38},{7,231},{8,40}... | collective-permute-start | bytes 835592 | tf_op jit(solution)/shard_map/ppermute | solution.py:41
  48.3 11.2 %collective-permute-start.15 = (bf16[272,512]{1,0:T(8,128)(2,1)S(1)}, bf16[272,512]{1,0:T(8,128)(2,1)S(1)}, u32[]{:S(2)}, u32[]{:S(2)}) collective-permute-start(bf16[272,512]{1,0:T(8,128)(2,1)S(1)} %shard_map.87.refs_4_), channel_id=1, source_target_pairs={{0,224},{1,33},{2,226},{3,35},{4,228},{5,37},{6,230},{7,39},{8,232... | collective-permute-start | bytes 835592 | tf_op jit(solution)/shard_map/ppermute | solution.py:41
  55.0 21.9 %collective-permute-start.19 = (bf16[2,256,512]{2,1,0:T(8,128)(2,1)S(1)}, bf16[2,256,512]{2,1,0:T(8,128)(2,1)S(1)}, u32[]{:S(2)}, u32[]{:S(2)}) collective-permute-start(bf16[2,256,512]{2,1,0:T(8,128)(2,1)S(1)} %get-tuple-element.56), channel_id=1, source_target_pairs={{0,2},{1,7},{2,4},{3,1},{4,6},{5,3},{6,0},{7,5},{8,10},{9,15},{10,... | collective-permute-start | bytes 1572872 | tf_op jit(solution)/shard_map/ppermute | solution.py:41
  56.1 11.8 %collective-permute-start.13 = (bf16[272,512]{1,0:T(8,128)(2,1)S(1)}, bf16[272,512]{1,0:T(8,128)(2,1)S(1)}, u32[]{:S(2)}, u32[]{:S(2)}) collective-permute-start(bf16[272,512]{1,0:T(8,128)(2,1)S(1)} %collective-permute-done.12.refs_2_.refs_5_), channel_id=1, source_target_pairs={{0,32},{1,225},{2,34},{3,227},{4,36},{5,229},{6,38},{7,231},{8,40}... | collective-permute-start | bytes 835592 | tf_op jit(solution)/shard_map/ppermute | solution.py:41
  59.5 10.8 %collective-permute-start.16 = (bf16[272,512]{1,0:T(8,128)(2,1)S(1)}, bf16[272,512]{1,0:T(8,128)(2,1)S(1)}, u32[]{:S(2)}, u32[]{:S(2)}) collective-permute-start(bf16[272,512]{1,0:T(8,128)(2,1)S(1)} %collective-permute-done.15.refs_6_), channel_id=1, source_target_pairs={{0,224},{1,33},{2,226},{3,35},{4,228},{5,37},{6,230},{7,39},{8,232... | collective-permute-start | bytes 835592 | tf_op jit(solution)/shard_map/ppermute | solution.py:41
  60.5 7.2 %collective-permute-start.10 = (bf16[272,256]{1,0:T(8,128)(2,1)S(1)}, bf16[272,256]{1,0:T(8,128)(2,1)S(1)}, u32[]{:S(2)}, u32[]{:S(2)}) collective-permute-start(bf16[272,256]{1,0:T(8,128)(2,1)S(1)} %shard_map.86.refs_0_.refs_1_), channel_id=1, source_target_pairs={{0,16},{1,17},{2,18},{3,19},{4,20},{5,21},{6,22},{7,23},{8,24},{9,... | collective-permute-start | bytes 417800 | tf_op jit(solution)/shard_map/ppermute | solution.py:41
  60.6 7.1 %collective-permute-start.11 = (bf16[272,256]{1,0:T(8,128)(2,1)S(1)}, bf16[272,256]{1,0:T(8,128)(2,1)S(1)}, u32[]{:S(2)}, u32[]{:S(2)}) collective-permute-start(bf16[272,256]{1,0:T(8,128)(2,1)S(1)} %shard_map.86.refs_0_.refs_1_), channel_id=1, source_target_pairs={{0,24},{1,25},{2,26},{3,27},{4,28},{5,29},{6,30},{7,31},{8,0},{9,1... | collective-permute-start | bytes 417800 | tf_op jit(solution)/shard_map/ppermute | solution.py:41
  67.7 6.0 %collective-permute-start.9 = (bf16[272,256]{1,0:T(8,128)(2,1)S(1)}, bf16[272,256]{1,0:T(8,128)(2,1)S(1)}, u32[]{:S(2)}, u32[]{:S(2)}) collective-permute-start(bf16[272,256]{1,0:T(8,128)(2,1)S(1)} %shard_map.86.refs_0_.refs_1_), channel_id=1, source_target_pairs={{0,8},{1,9},{2,10},{3,11},{4,12},{5,13},{6,14},{7,15},{8,16},{9,17... | collective-permute-start | bytes 417800 | tf_op jit(solution)/shard_map/ppermute | solution.py:41
  67.7 16.5 %collective-permute-start.22 = (bf16[2,256,512]{2,1,0:T(8,128)(2,1)S(1)}, bf16[2,256,512]{2,1,0:T(8,128)(2,1)S(1)}, u32[]{:S(2)}, u32[]{:S(2)}) collective-permute-start(bf16[2,256,512]{2,1,0:T(8,128)(2,1)S(1)} %get-tuple-element.64), channel_id=1, source_target_pairs={{0,6},{1,3},{2,0},{3,5},{4,2},{5,7},{6,4},{7,1},{8,14},{9,11},{10,... | collective-permute-start | bytes 1572872 | tf_op jit(solution)/shard_map/ppermute | solution.py:41
  67.9 9.7 %collective-permute-start.14 = (bf16[272,512]{1,0:T(8,128)(2,1)S(1)}, bf16[272,512]{1,0:T(8,128)(2,1)S(1)}, u32[]{:S(2)}, u32[]{:S(2)}) collective-permute-start(bf16[272,512]{1,0:T(8,128)(2,1)S(1)} %collective-permute-done.13.refs_4_), channel_id=1, source_target_pairs={{0,32},{1,225},{2,34},{3,227},{4,36},{5,229},{6,38},{7,231},{8,40}... | collective-permute-start | bytes 835592 | tf_op jit(solution)/shard_map/ppermute | solution.py:41
  70.3 9.2 %collective-permute-start.17 = (bf16[272,512]{1,0:T(8,128)(2,1)S(1)}, bf16[272,512]{1,0:T(8,128)(2,1)S(1)}, u32[]{:S(2)}, u32[]{:S(2)}) collective-permute-start(bf16[272,512]{1,0:T(8,128)(2,1)S(1)} %collective-permute-done.16.refs_5_), channel_id=1, source_target_pairs={{0,224},{1,33},{2,226},{3,35},{4,228},{5,37},{6,230},{7,39},{8,232... | collective-permute-start | bytes 835592 | tf_op jit(solution)/shard_map/ppermute | solution.py:41
  73.7 13.6 %collective-permute-start.21 = (bf16[2,256,512]{2,1,0:T(8,128)(2,1)S(1)}, bf16[2,256,512]{2,1,0:T(8,128)(2,1)S(1)}, u32[]{:S(2)}, u32[]{:S(2)}) collective-permute-start(bf16[2,256,512]{2,1,0:T(8,128)(2,1)S(1)} %get-tuple-element.62), channel_id=1, source_target_pairs={{0,4},{1,5},{2,6},{3,7},{4,0},{5,1},{6,2},{7,3},{8,12},{9,13},{10,... | collective-permute-start | bytes 1572872 | tf_op jit(solution)/shard_map/ppermute | solution.py:41
  80.0 7.8 %collective-permute-start.20 = (bf16[272,512]{1,0:T(8,128)(2,1)S(1)}, bf16[272,512]{1,0:T(8,128)(2,1)S(1)}, u32[]{:S(2)}, u32[]{:S(2)}) collective-permute-start(bf16[272,512]{1,0:T(8,128)(2,1)S(1)} %get-tuple-element.61.refs_4_), channel_id=1, source_target_pairs={{0,32},{1,225},{2,34},{3,227},{4,36},{5,229},{6,38},{7,231},{8,40}... | collective-permute-start | bytes 835592 | tf_op jit(solution)/shard_map/ppermute | solution.py:41
  89.2 10.2 %collective-permute-start.23 = (bf16[272,256]{1,0:T(8,128)(2,1)S(1)}, bf16[272,256]{1,0:T(8,128)(2,1)S(1)}, u32[]{:S(2)}, u32[]{:S(2)}) collective-permute-start(bf16[272,256]{1,0:T(8,128)(2,1)S(1)} %get-tuple-element.72), channel_id=1, source_target_pairs={{0,24},{1,25},{2,26},{3,27},{4,28},{5,29},{6,30},{7,31},{8,0},{9,1... | collective-permute-start | bytes 417800 | tf_op jit(solution)/shard_map/ppermute | solution.py:41
  93.5 6.3 %collective-permute-start.24 = (bf16[272,256]{1,0:T(8,128)(2,1)S(1)}, bf16[272,256]{1,0:T(8,128)(2,1)S(1)}, u32[]{:S(2)}, u32[]{:S(2)}) collective-permute-start(bf16[272,256]{1,0:T(8,128)(2,1)S(1)} %get-tuple-element.73), channel_id=1, source_target_pairs={{0,16},{1,17},{2,18},{3,19},{4,20},{5,21},{6,22},{7,23},{8,24},{9,... | collective-permute-start | bytes 417800 | tf_op jit(solution)/shard_map/ppermute | solution.py:41
  93.5 9.4 %collective-permute-start.25 = (bf16[272,256]{1,0:T(8,128)(2,1)S(1)}, bf16[272,256]{1,0:T(8,128)(2,1)S(1)}, u32[]{:S(2)}, u32[]{:S(2)}) collective-permute-start(bf16[272,256]{1,0:T(8,128)(2,1)S(1)} %get-tuple-element.74), channel_id=1, source_target_pairs={{0,8},{1,9},{2,10},{3,11},{4,12},{5,13},{6,14},{7,15},{8,16},{9,17... | collective-permute-start | bytes 417800 | tf_op jit(solution)/shard_map/ppermute | solution.py:41
  104.0 4.3 %collective-permute-start.26 = (bf16[272,256]{1,0:T(8,128)(2,1)S(1)}, bf16[272,256]{1,0:T(8,128)(2,1)S(1)}, u32[]{:S(2)}, u32[]{:S(2)}) collective-permute-start(bf16[272,256]{1,0:T(8,128)(2,1)S(1)} %shard_map.96.refs_0_), channel_id=1, source_target_pairs={{0,2},{1,7},{2,4},{3,1},{4,6},{5,3},{6,0},{7,5},{8,10},{9,15},{10,... | collective-permute-start | bytes 417800 | tf_op jit(solution)/shard_map/ppermute | solution.py:41
  104.1 7.4 %collective-permute-start.27 = (bf16[272,256]{1,0:T(8,128)(2,1)S(1)}, bf16[272,256]{1,0:T(8,128)(2,1)S(1)}, u32[]{:S(2)}, u32[]{:S(2)}) collective-permute-start(bf16[272,256]{1,0:T(8,128)(2,1)S(1)} %shard_map.96.refs_0_), channel_id=1, source_target_pairs={{0,6},{1,3},{2,0},{3,5},{4,2},{5,7},{6,4},{7,1},{8,14},{9,11},{10,... | collective-permute-start | bytes 417800 | tf_op jit(solution)/shard_map/ppermute | solution.py:41
  109.2 8.5 %collective-permute-start.29 = (bf16[272,256]{1,0:T(8,128)(2,1)S(1)}, bf16[272,256]{1,0:T(8,128)(2,1)S(1)}, u32[]{:S(2)}, u32[]{:S(2)}) collective-permute-start(bf16[272,256]{1,0:T(8,128)(2,1)S(1)} %shard_map.96.refs_0_), channel_id=1, source_target_pairs={{0,1},{1,0},{2,3},{3,2},{4,5},{5,4},{6,7},{7,6},{8,9},{9,8},{10,11... | collective-permute-start | bytes 417800 | tf_op jit(solution)/shard_map/ppermute | solution.py:41
  111.5 6.3 %collective-permute-start.30 = (bf16[272,256]{1,0:T(8,128)(2,1)S(1)}, bf16[272,256]{1,0:T(8,128)(2,1)S(1)}, u32[]{:S(2)}, u32[]{:S(2)}) collective-permute-start(bf16[272,256]{1,0:T(8,128)(2,1)S(1)} %collective-permute-done.26.refs_1_), channel_id=1, source_target_pairs={{0,1},{1,0},{2,3},{3,2},{4,5},{5,4},{6,7},{7,6},{8,9},{9,8},{10,11... | collective-permute-start | bytes 417800 | tf_op jit(solution)/shard_map/ppermute | solution.py:41
  111.5 6.3 %collective-permute-start.31 = (bf16[272,256]{1,0:T(8,128)(2,1)S(1)}, bf16[272,256]{1,0:T(8,128)(2,1)S(1)}, u32[]{:S(2)}, u32[]{:S(2)}) collective-permute-start(bf16[272,256]{1,0:T(8,128)(2,1)S(1)} %collective-permute-done.27.refs_2_), channel_id=1, source_target_pairs={{0,1},{1,0},{2,3},{3,2},{4,5},{5,4},{6,7},{7,6},{8,9},{9,8},{10,11... | collective-permute-start | bytes 417800 | tf_op jit(solution)/shard_map/ppermute | solution.py:41
  112.3 6.5 %collective-permute-start.32 = (bf16[272,256]{1,0:T(8,128)(2,1)S(1)}, bf16[272,256]{1,0:T(8,128)(2,1)S(1)}, u32[]{:S(2)}, u32[]{:S(2)}) collective-permute-start(bf16[272,256]{1,0:T(8,128)(2,1)S(1)} %collective-permute-done.28.refs_3_), channel_id=1, source_target_pairs={{0,1},{1,0},{2,3},{3,2},{4,5},{5,4},{6,7},{7,6},{8,9},{9,8},{10,11... | collective-permute-start | bytes 417800 | tf_op jit(solution)/shard_map/ppermute | solution.py:41
  (6 other events, 22.9 us)

commit v2 on v1

--- a/solution.py
+++ b/solution.py
@@ -21,6 +21,7 @@
 LOW = -1e30
 VMEM_LIMIT = 20 * 1024 * 1024
 ROOM = 48 * 1024 * 1024
+CUT_ROOM = 52 * 1024 * 1024
 F32, BF16 = jnp.float32, jnp.bfloat16
 
 
@@ -165,7 +166,7 @@
     tail_out[:, FEAT:] = counts[8:]
 
 
-def pool_kernel(ids, tokens, sums_out, counts_out, hot):
+def pool_kernel(ids, tokens, _, sums_out, counts_out, hot):
     segment = iota((SEG, 128), 0)
     for r in range(16):
         hot[:, r * 128 : (r + 1) * 128] = ones_where(ids[r : r + 1, :] == segment)
@@ -212,8 +213,8 @@
     bias_out[...] = jnp.concatenate([bias, bias], axis=1).astype(BF16)
 
 
-EARLY = (0, 1, 4, 5)
-LATE = (2, 3, 6, 7)
+EARLY = (0, 1, 2, 4)
+LATE = (3, 5, 6, 7)
 
 
 def row_scale(tail):
@@ -269,7 +270,7 @@
 
 def query_kernel(info, *refs):
     blocks, late = refs[:8], [refs[i] for i in LATE]
-    w_query, partial, q_out = refs[8:]
+    w_query, partial, _, q_out = refs[8:]
     scale, column = row_scale(square_rows(blocks))
     query = product(partial[...], late, w_query, ROWS)
     q_out[:SEG, :] = (query[:SEG] * column * SCORE).astype(BF16)
@@ -477,19 +478,20 @@
     )(*attended, *weights, means, ids, tokens)
 
 
-def cut_kernel(info, w_out, _, mine, sibling, sems):
+def cut_kernel(info, w_out, _, mine, sibling, done, sems):
     copies = []
     for i in range(4):
         for side, out in enumerate((mine, sibling)):
             start = pl.multiple_of(info[I_CUT + 4 * side + i] * FEAT, FEAT)
             copies.append(pltpu.make_async_copy(w_out.at[:, pl.ds(start, FEAT)], out.at[i], sems.at[side, i]))
             copies[-1].start()
+    done[...] = jnp.zeros_like(done)
     for copy in copies:
         copy.wait()
 
 
 def pair_kernel(info, *refs):
-    sources, outs, sems = refs[:2], refs[3:7], refs[7]
+    sources, outs, sems = refs[:2], refs[7:11], refs[-1]
     copies = []
     for i, out in enumerate(outs):
         for side, source in enumerate(sources):
@@ -519,11 +521,18 @@
     count = NZ * NX
     above = lax.ppermute(head, "seq", [(i, i - 1) for i in range(1, count)])
     below = lax.ppermute(tail, "seq", [(i, i + 1) for i in range(count - 1)])
+    cut = shape((4, SEG, FEAT), BF16)
+    sems = [pltpu.SemaphoreType.DMA((2, 4))]
+    mine, theirs, cut_done = call(
+        cut_kernel, [cut, cut, shape((8, 128), F32)], [info, w_out, ids], scratch=sems, far_in=(1, 2), far_out=(0, 1), room=CUT_ROOM
+    )
+    theirs = swap(theirs)
     sums, sizes = call(
         pool_kernel,
         [shape((SEG, FEAT), F32), shape((SEG, 128), F32)],
-        [ids, tokens],
+        [ids, tokens, cut_done],
         scalars=None,
+        far_in=(2,),
         flops=1 << 30,
         moved=2 << 20,
         scratch=[pltpu.VMEM((SEG, TOK), BF16)],
@@ -540,17 +549,13 @@
     queried, keyed, valued, *late = call(
         early_kernel,
         [part_query, part, part] + [kept] * 3,
-        [info, u, first, sibling, across, w_query, w_key, w_value],
+        [info, u, first, second, sibling, w_query, w_key, w_value],
         scratch=[pltpu.VMEM((4, FEAT, COLS), BF16)] * 3 + [pltpu.SemaphoreType.DMA((2, 4, 3))],
+        flops=ROWS * WIDTH * 3 * COLS,
+        moved=6 << 20,
         far_in=(5, 6, 7),
         room=ROOM,
     )
-    cut = shape((4, SEG, FEAT), BF16)
-    sems = [pltpu.SemaphoreType.DMA((2, 4))]
-    mine, theirs = call(
-        cut_kernel, [cut, cut], [info, w_out, second], scratch=sems, far_in=(1, 2), far_out=(0, 1), room=ROOM
-    )
-    theirs = swap(theirs)
     blocks = [u, first, second, far, sibling, across, swap(second), swap(far)]
     (kv,) = call(
         key_value_kernel,
@@ -560,29 +565,36 @@
     (query,) = call(
         query_kernel,
         [shape((ROWS, COLS), BF16)],
-        [info] + blocks + [late[0], queried],
+        [info] + blocks + [late[0], queried, kv],
+        far_in=(11,),
     )
     queries = [query] + [x_by(query, k) for k in (1, 2, 3)]
     one, other = z_one(kv), z_other(kv)
     pair = shape((2, SEG, FEAT), BF16)
-    pairs = call(
+    block = shape(kv.shape, BF16)
+    *pairs, one, other = call(
         pair_kernel,
-        [pair] * 4,
-        [info, mine, theirs, one],
+        [pair] * 4 + [block] * 2,
+        [info, mine, theirs, one, other] + queries[1:],
         scratch=sems,
-        far_in=(1, 2, 3),
-        far_out=range(4),
-    )
-    weights = [pairs[0], y_one(pairs[1]), y_other(pairs[2]), y_far(pairs[3])]
+        aliases={3: 4, 4: 5},
+        far_in=range(1, 8),
+        far_out=range(6),
+    )
+    far_weights = y_far(pairs[3])
     one2, other2 = z_one(one), z_other(other)
+    *state, done = attend_step(1, info, queries, kv, [one, other], None, pairs[0])
+    one2, other2 = gate(info, [one2, other2], done)
     one3, other3 = z_one(one2), z_other(other2)
-    *state, done = attend_step(1, info, queries, kv, [one, other], None, pairs[0])
-    *state, done = attend_step(2, info, queries, None, [one2, other2], state, weights[1])
+    one_weights = y_one(pairs[1])
+    *state, done = attend_step(2, info, queries, None, [one2, other2], state, far_weights)
     one3, other3 = gate(info, [one3, other3], done)
     one4 = z_one(one3)
-    *state, done = attend_step(3, info, queries, None, [one3, other3], state, weights[2])
-    one4, weights[3] = gate(info, [one4, weights[3]], done)
+    other_weights = y_other(pairs[2])
+    *state, done = attend_step(3, info, queries, None, [one3, other3], state, one_weights)
+    one4, other_weights = gate(info, [one4, other_weights], done)
     partial = attend_step(4, info, queries, None, [one4], state)
+    weights = [pairs[0], one_weights, other_weights, far_weights]
     partial = [partial[0]] + [x_by(partial[k], -k) for k in (1, 2, 3)]
     (attended,) = call(merge_kernel, [shape((ROWS, COLS), BF16)], [info] + partial, moved=1 << 20)
     return output(mp_exchange(attended), weights, means, ids, tokens)

time: 123 us -> 152 us (1.24)
  the two profiles are of different devices: /device:TPU:1 before, /device:TPU:2 now
where the time goes in v2:
time: 152 us; the launch traced here: 149 us
  Pallas kernels  54.2 us (36%)
  waiting for transfers between devices  50.3 us (33%)
  starting transfers between devices  39.2 us (26%)
  local copies, waits for them, and re-layouts  4.82 us (3%)
    pallas_call x16, Pallas kernels, call(): pl.pallas_call(body, out_shape=outs, in_specs=[SMEM if i == scalars else...  50.3 us
    ppermute x31, waiting for transfers between devices, move(): return lax.ppermute(value, ('seq', 'mp'), pairs)  50.3 us
    ppermute x31, starting transfers between devices, move(): return lax.ppermute(value, ('seq', 'mp'), pairs)  33.4 us
    unnamed x12, local copies, waits for them, and re-layouts  4.12 us
    pallas_call x1, Pallas kernels, output(): pl.pallas_call(output_kernel, grid=(TOK // BLOCK,), out_shape=shape((TOK,...  3.82 us
    ppermute x1, starting transfers between devices, shards(): below = lax.ppermute(tail, 'seq', [(i, i + 1) for i in range(count - 1)])  3.4 us
  transfers between devices with their start and end apart: 33, of which 14 were waited for; matrix products, arithmetic and copies ran while one was open for 0% of the time, Pallas kernels for 31%

profile of v2, /device:TPU:2, one launch (start us, length us, event | category | flops | bytes accessed | tf_op | source)
XLA Modules:
  0.0 148.7 jit_solution(17842981786521711627)
XLA Ops:
  0.0 1.6 %copy-done = bf16[2048,512]{1,0:T(8,128)(2,1)S(1)} copy-done((bf16[2048,512]{1,0:T(8,128)(2,1)S(1)}, bf16[2048,512]{1,0:T(8,128)(2,1)}, u32[]{:S(2)}) %copy-start) | copy-done | bytes 2097176
  3.0 3.4 %collective-permute-start.1 = (f32[8,640]{1,0:T(8,128)S(1)}, f32[8,640]{1,0:T(8,128)S(1)}, u32[]{:S(2)}, u32[]{:S(2)}) collective-permute-start(f32[8,640]{1,0:T(8,128)S(1)} %get-tuple-element.52), channel_id=1, source_target_pairs={{0,8},{8,16},{16,24},{24,32},{32,40},{40,48},{48,56},{56,64},{64,7... | collective-permute-start | bytes 61448 | tf_op jit(solution)/shard_map/ppermute | solution.py:523
  6.4 2.4 %collective-permute-start = (f32[8,640]{1,0:T(8,128)S(1)}, f32[8,640]{1,0:T(8,128)S(1)}, u32[]{:S(2)}, u32[]{:S(2)}) collective-permute-start(f32[8,640]{1,0:T(8,128)S(1)} %get-tuple-element.51.head), channel_id=1, source_target_pairs={{8,0},{16,8},{24,16},{32,24},{40,32},{48,40},{56,48},{64,56},{72,6... | collective-permute-start | bytes 61448 | tf_op jit(solution)/shard_map/ppermute | solution.py:522
  9.5 33.5 %shard_map.83 = (bf16[4,256,512]{2,1,0:T(8,128)(2,1)S(1)}, bf16[4,256,512]{2,1,0:T(8,128)(2,1)}, f32[8,128]{1,0:T(8,128)S(1)}) custom-call(s32[32]{0:T(128)S(1)} %dynamic-slice_bitcast_fusion.info.refs_0_, bf16[256,4096]{1,0:T(8,128)(2,1)} %w_out.1, s32[16,128]{1,0:T(8,128)S(1)} %get-tuple-element.47._.ids.refs_13_), custom_call_target="tpu_custom_call" | custom-call | tf_op jit(solution)/shard_map/pallas_call | solution.py:106
  46.7 1.7 %collective-permute-start.2 = (bf16[272,512]{1,0:T(8,128)(2,1)S(1)}, bf16[272,512]{1,0:T(8,128)(2,1)S(1)}, u32[]{:S(2)}, u32[]{:S(2)}) collective-permute-start(bf16[272,512]{1,0:T(8,128)(2,1)S(1)} %get-tuple-element.53.refs_0_), channel_id=1, source_target_pairs={{0,2},{1,7},{2,4},{3,1},{4,6},{5,3},{6,0},{7,5},{8,10},{9,15},{10,... | collective-permute-start | bytes 835592 | tf_op jit(solution)/shard_map/ppermute | solution.py:42
  48.8 1.2 collective-permute-start.3
  50.0 6.4 %collective-permute-done.2.refs_1_ = bf16[272,512]{1,0:T(8,128)(2,1)S(1)} collective-permute-done((bf16[272,512]{1,0:T(8,128)(2,1)S(1)}, bf16[272,512]{1,0:T(8,128)(2,1)S(1)}, u32[]{:S(2)}, u32[]{:S(2)}) %collective-permute-start.2) | collective-permute-done | bytes 278560 | tf_op jit(solution)/shard_map/ppermute | solution.py:42
  57.4 6.8 %collective-permute-done.4.refs_3_ = bf16[272,512]{1,0:T(8,128)(2,1)S(1)} collective-permute-done((bf16[272,512]{1,0:T(8,128)(2,1)S(1)}, bf16[272,512]{1,0:T(8,128)(2,1)S(1)}, u32[]{:S(2)}, u32[]{:S(2)}) %collective-permute-start.4) | collective-permute-done | bytes 278560 | tf_op jit(solution)/shard_map/ppermute | solution.py:42
  64.2 4.3 %shard_map.86 = (f32[272,256]{1,0:T(8,128)S(1)}, f32[256,256]{1,0:T(8,128)S(1)}, f32[256,256]{1,0:T(8,128)S(1)}, bf16[4,512,256]{2,1,0:T(8,128)(2,1)S(1)}, bf16[...) custom-call(s32[32]{0:T(128)S(1)} %dynamic-slice_bitcast_fusion.info.refs_0_, ...), custom_call_target="tpu_custom_call" | custom-call | flops 855638016 | bytes 6291456 | tf_op jit(solution)/shard_map/pallas_call | solution.py:106
  68.5 1.3 shard_map.87.refs_10_.refs_4_
  70.8 8.5 %collective-permute-start.14 = (bf16[272,512]{1,0:T(8,128)(2,1)S(1)}, bf16[272,512]{1,0:T(8,128)(2,1)S(1)}, u32[]{:S(2)}, u32[]{:S(2)}) collective-permute-start(bf16[272,512]{1,0:T(8,128)(2,1)S(1)} %shard_map.87.refs_10_.refs_4_), channel_id=1, source_target_pairs={{0,224},{1,33},{2,226},{3,35},{4,228},{5,37},{6,230},{7,39},{8,232... | collective-permute-start | bytes 835592 | tf_op jit(solution)/shard_map/ppermute | solution.py:42
  79.6 1.8 %collective-permute-start.9 = (bf16[272,256]{1,0:T(8,128)(2,1)S(1)}, bf16[272,256]{1,0:T(8,128)(2,1)S(1)}, u32[]{:S(2)}, u32[]{:S(2)}) collective-permute-start(bf16[272,256]{1,0:T(8,128)(2,1)S(1)} %shard_map.88.refs_0_.refs_1_), channel_id=1, source_target_pairs={{0,8},{1,9},{2,10},{3,11},{4,12},{5,13},{6,14},{7,15},{8,16},{9,17... | collective-permute-start | bytes 417800 | tf_op jit(solution)/shard_map/ppermute | solution.py:42
  81.5 4.9 %collective-permute-done.10.refs_5_.refs_2_.refs_3_ = bf16[272,256]{1,0:T(8,128)(2,1)S(1)} collective-permute-done((bf16[272,256]{1,0:T(8,128)(2,1)S(1)}, bf16[272,256]{1,0:T(8,128)(2,1)S(1)}, u32[]{:S(2)}, u32[]{:S(2)}) %collective-permute-start.10) | collective-permute-done | bytes 139296 | tf_op jit(solution)/shard_map/ppermute | solution.py:42
  88.1 1.2 collective-permute-start.19
  89.3 3.2 %collective-permute-start.16 = (bf16[272,512]{1,0:T(8,128)(2,1)S(1)}, bf16[272,512]{1,0:T(8,128)(2,1)S(1)}, u32[]{:S(2)}, u32[]{:S(2)}) collective-permute-start(bf16[272,512]{1,0:T(8,128)(2,1)S(1)} %get-tuple-element.64.refs_6_), channel_id=1, source_target_pairs={{0,224},{1,33},{2,226},{3,35},{4,228},{5,37},{6,230},{7,39},{8,232... | collective-permute-start | bytes 835592 | tf_op jit(solution)/shard_map/ppermute | solution.py:42
  92.5 1.3 collective-permute-start.22
  93.8 2.1 %shard_map.90 = (f32[4,2,272,256]{3,2,1,0:T(8,128)S(1)}, f32[4,2,272,128]{3,2,1,0:T(8,128)S(1)}, f32[8,128]{1,0:T(8,128)S(1)}) custom-call(s32[32]{0:T(128)S(1)} %dynamic-slice_bitcast_fusion.info.refs_0_, bf16[272,256]{1,0:T(8,128)(2,1)S(1)} %shard_map.88.refs_0_.refs_1_, bf16[272,256]{1,0:T(8,128)(2,1)S(1)} %collective-permute-done.9.refs_4_.refs_1_.refs_2_, ...), custom_call_target="tpu_custom_call" | custom-call | flops 855638016 | bytes 4194304 | tf_op jit(solution)/shard_map/pallas_call | solution.py:106
  95.9 3.8 %collective-permute-done.15.refs_0_ = bf16[272,512]{1,0:T(8,128)(2,1)S(1)} collective-permute-done((bf16[272,512]{1,0:T(8,128)(2,1)S(1)}, bf16[272,512]{1,0:T(8,128)(2,1)S(1)}, u32[]{:S(2)}, u32[]{:S(2)}) %collective-permute-start.15) | collective-permute-done | bytes 278560 | tf_op jit(solution)/shard_map/ppermute | solution.py:42
  100.4 3.2 %collective-permute-start.18 = (bf16[272,512]{1,0:T(8,128)(2,1)S(1)}, bf16[272,512]{1,0:T(8,128)(2,1)S(1)}, u32[]{:S(2)}, u32[]{:S(2)}) collective-permute-start(bf16[272,512]{1,0:T(8,128)(2,1)S(1)} %get-tuple-element.68.refs_5_), channel_id=1, source_target_pairs={{0,224},{1,33},{2,226},{3,35},{4,228},{5,37},{6,230},{7,39},{8,232... | collective-permute-start | bytes 835592 | tf_op jit(solution)/shard_map/ppermute | solution.py:42
  104.9 5.8 %collective-permute-done.17.refs_0_ = bf16[272,512]{1,0:T(8,128)(2,1)S(1)} collective-permute-done((bf16[272,512]{1,0:T(8,128)(2,1)S(1)}, bf16[272,512]{1,0:T(8,128)(2,1)S(1)}, u32[]{:S(2)}, u32[]{:S(2)}) %collective-permute-start.17) | collective-permute-done | bytes 278560 | tf_op jit(solution)/shard_map/ppermute | solution.py:42
  112.8 6.2 %collective-permute-done.20.refs_0_ = bf16[272,512]{1,0:T(8,128)(2,1)S(1)} collective-permute-done((bf16[272,512]{1,0:T(8,128)(2,1)S(1)}, bf16[272,512]{1,0:T(8,128)(2,1)S(1)}, u32[]{:S(2)}, u32[]{:S(2)}) %collective-permute-start.20) | collective-permute-done | bytes 278560 | tf_op jit(solution)/shard_map/ppermute | solution.py:42
  120.5 2.8 %collective-permute-start.23 = (bf16[272,256]{1,0:T(8,128)(2,1)S(1)}, bf16[272,256]{1,0:T(8,128)(2,1)S(1)}, u32[]{:S(2)}, u32[]{:S(2)}) collective-permute-start(bf16[272,256]{1,0:T(8,128)(2,1)S(1)} %get-tuple-element.84), channel_id=1, source_target_pairs={{0,24},{1,25},{2,26},{3,27},{4,28},{5,29},{6,30},{7,31},{8,0},{9,1... | collective-permute-start | bytes 417800 | tf_op jit(solution)/shard_map/ppermute | solution.py:42
  123.4 1.9 %collective-permute-start.25 = (bf16[272,256]{1,0:T(8,128)(2,1)S(1)}, bf16[272,256]{1,0:T(8,128)(2,1)S(1)}, u32[]{:S(2)}, u32[]{:S(2)}) collective-permute-start(bf16[272,256]{1,0:T(8,128)(2,1)S(1)} %get-tuple-element.86), channel_id=1, source_target_pairs={{0,8},{1,9},{2,10},{3,11},{4,12},{5,13},{6,14},{7,15},{8,16},{9,17... | collective-permute-start | bytes 417800 | tf_op jit(solution)/shard_map/ppermute | solution.py:42
  125.3 1.2 collective-permute-done.23.b
  126.4 3.4 %collective-permute-done.24.c = bf16[272,256]{1,0:T(8,128)(2,1)S(1)} collective-permute-done((bf16[272,256]{1,0:T(8,128)(2,1)S(1)}, bf16[272,256]{1,0:T(8,128)(2,1)S(1)}, u32[]{:S(2)}, u32[]{:S(2)}) %collective-permute-start.24) | collective-permute-done | bytes 139296 | tf_op jit(solution)/shard_map/ppermute | solution.py:42
  129.8 1.1 shard_map.97.refs_0_
  130.9 1.2 collective-permute-start.26
  132.1 2.1 %collective-permute-start.27 = (bf16[272,256]{1,0:T(8,128)(2,1)S(1)}, bf16[272,256]{1,0:T(8,128)(2,1)S(1)}, u32[]{:S(2)}, u32[]{:S(2)}) collective-permute-start(bf16[272,256]{1,0:T(8,128)(2,1)S(1)} %shard_map.97.refs_0_), channel_id=1, source_target_pairs={{0,6},{1,3},{2,0},{3,5},{4,2},{5,7},{6,4},{7,1},{8,14},{9,11},{10,... | collective-permute-start | bytes 417800 | tf_op jit(solution)/shard_map/ppermute | solution.py:42
  134.2 3.0 %collective-permute-done.26.refs_1_ = bf16[272,256]{1,0:T(8,128)(2,1)S(1)} collective-permute-done((bf16[272,256]{1,0:T(8,128)(2,1)S(1)}, bf16[272,256]{1,0:T(8,128)(2,1)S(1)}, u32[]{:S(2)}, u32[]{:S(2)}) %collective-permute-start.26) | collective-permute-done | bytes 139296 | tf_op jit(solution)/shard_map/ppermute | solution.py:42
  138.2 5.3 %collective-permute-done.28.refs_3_ = bf16[272,256]{1,0:T(8,128)(2,1)S(1)} collective-permute-done((bf16[272,256]{1,0:T(8,128)(2,1)S(1)}, bf16[272,256]{1,0:T(8,128)(2,1)S(1)}, u32[]{:S(2)}, u32[]{:S(2)}) %collective-permute-start.28) | collective-permute-done | bytes 139296 | tf_op jit(solution)/shard_map/ppermute | solution.py:42
  143.6 1.3 collective-permute-done.32.refs_7_
  144.9 3.8 %shard_map.98 = bf16[2048,512]{1,0:T(8,128)(2,1)} custom-call(bf16[272,256]{1,0:T(8,128)(2,1)S(1)} %shard_map.97.refs_0_, bf16[272,256]{1,0:T(8,128)(2,1)S(1)} %collective-permute-done.26.refs_1_, bf16[272,256]{1,0:T(8,128)(2,1)S(1)} %collective-permute-done.27.refs_2_, bf16[272,256]{1,0:T(8,128)(2,1)S(1)} %collective-permute-done.28.refs_3_, ...), custom_call_target="tpu_custom_call" | custom-call | flops 2147483648 | bytes 6291456 | tf_op jit(solution)/shard_map/pallas_call | solution.py:469
  (65 shorter events, 16.8 us)
Async XLA Ops:
  3.0 41.9 %collective-permute-start.1 = (f32[8,640]{1,0:T(8,128)S(1)}, f32[8,640]{1,0:T(8,128)S(1)}, u32[]{:S(2)}, u32[]{:S(2)}) collective-permute-start(f32[8,640]{1,0:T(8,128)S(1)} %get-tuple-element.52), channel_id=1, source_target_pairs={{0,8},{8,16},{16,24},{24,32},{32,40},{40,48},{48,56},{56,64},{64,7... | collective-permute-start | bytes 61448 | tf_op jit(solution)/shard_map/ppermute | solution.py:523
  6.4 38.5 %collective-permute-start = (f32[8,640]{1,0:T(8,128)S(1)}, f32[8,640]{1,0:T(8,128)S(1)}, u32[]{:S(2)}, u32[]{:S(2)}) collective-permute-start(f32[8,640]{1,0:T(8,128)S(1)} %get-tuple-element.51.head), channel_id=1, source_target_pairs={{8,0},{16,8},{24,16},{32,24},{40,32},{48,40},{56,48},{64,56},{72,6... | collective-permute-start | bytes 61448 | tf_op jit(solution)/shard_map/ppermute | solution.py:522
  46.7 9.7 %collective-permute-start.2 = (bf16[272,512]{1,0:T(8,128)(2,1)S(1)}, bf16[272,512]{1,0:T(8,128)(2,1)S(1)}, u32[]{:S(2)}, u32[]{:S(2)}) collective-permute-start(bf16[272,512]{1,0:T(8,128)(2,1)S(1)} %get-tuple-element.53.refs_0_), channel_id=1, source_target_pairs={{0,2},{1,7},{2,4},{3,1},{4,6},{5,3},{6,0},{7,5},{8,10},{9,15},{10,... | collective-permute-start | bytes 835592 | tf_op jit(solution)/shard_map/ppermute | solution.py:42
  48.4 38.9 %collective-permute-start.12 = (bf16[4,256,512]{2,1,0:T(8,128)(2,1)}, bf16[4,256,512]{2,1,0:T(8,128)(2,1)S(1)}, u32[]{:S(2)}, u32[]{:S(2)}) collective-permute-start(bf16[4,256,512]{2,1,0:T(8,128)(2,1)} %get-tuple-element.62), channel_id=1, source_target_pairs={{0,1},{1,0},{2,3},{3,2},{4,5},{5,4},{6,7},{7,6},{8,9},{9,8},{10,11... | collective-permute-start | bytes 3145736 | tf_op jit(solution)/shard_map/ppermute | solution.py:42
  48.8 8.5 %collective-permute-start.3 = (bf16[272,512]{1,0:T(8,128)(2,1)S(1)}, bf16[272,512]{1,0:T(8,128)(2,1)S(1)}, u32[]{:S(2)}, u32[]{:S(2)}) collective-permute-start(bf16[272,512]{1,0:T(8,128)(2,1)S(1)} %get-tuple-element.53.refs_0_), channel_id=1, source_target_pairs={{0,6},{1,3},{2,0},{3,5},{4,2},{5,7},{6,4},{7,1},{8,14},{9,11},{10,... | collective-permute-start | bytes 835592 | tf_op jit(solution)/shard_map/ppermute | solution.py:42
  56.4 7.8 %collective-permute-start.4 = (bf16[272,512]{1,0:T(8,128)(2,1)S(1)}, bf16[272,512]{1,0:T(8,128)(2,1)S(1)}, u32[]{:S(2)}, u32[]{:S(2)}) collective-permute-start(bf16[272,512]{1,0:T(8,128)(2,1)S(1)} %collective-permute-done.2.refs_1_), channel_id=1, source_target_pairs={{0,2},{1,7},{2,4},{3,1},{4,6},{5,3},{6,0},{7,5},{8,10},{9,15},{10,... | collective-permute-start | bytes 835592 | tf_op jit(solution)/shard_map/ppermute | solution.py:42
  56.8 7.4 %collective-permute-start.5 = (bf16[272,512]{1,0:T(8,128)(2,1)S(1)}, bf16[272,512]{1,0:T(8,128)(2,1)S(1)}, u32[]{:S(2)}, u32[]{:S(2)}) collective-permute-start(bf16[272,512]{1,0:T(8,128)(2,1)S(1)} %get-tuple-element.53.refs_0_), channel_id=1, source_target_pairs={{0,1},{1,0},{2,3},{3,2},{4,5},{5,4},{6,7},{7,6},{8,9},{9,8},{10,11... | collective-permute-start | bytes 835592 | tf_op jit(solution)/shard_map/ppermute | solution.py:42
  56.8 11.7 %collective-permute-start.6 = (bf16[272,512]{1,0:T(8,128)(2,1)S(1)}, bf16[272,512]{1,0:T(8,128)(2,1)S(1)}, u32[]{:S(2)}, u32[]{:S(2)}) collective-permute-start(bf16[272,512]{1,0:T(8,128)(2,1)S(1)} %collective-permute-done.2.refs_1_), channel_id=1, source_target_pairs={{0,1},{1,0},{2,3},{3,2},{4,5},{5,4},{6,7},{7,6},{8,9},{9,8},{10,11... | collective-permute-start | bytes 835592 | tf_op jit(solution)/shard_map/ppermute | solution.py:42
  57.3 11.2 %collective-permute-start.7 = (bf16[272,512]{1,0:T(8,128)(2,1)S(1)}, bf16[272,512]{1,0:T(8,128)(2,1)S(1)}, u32[]{:S(2)}, u32[]{:S(2)}) collective-permute-start(bf16[272,512]{1,0:T(8,128)(2,1)S(1)} %collective-permute-done.3.refs_2_), channel_id=1, source_target_pairs={{0,1},{1,0},{2,3},{3,2},{4,5},{5,4},{6,7},{7,6},{8,9},{9,8},{10,11... | collective-permute-start | bytes 835592 | tf_op jit(solution)/shard_map/ppermute | solution.py:42
  64.2 4.3 %collective-permute-start.8 = (bf16[272,512]{1,0:T(8,128)(2,1)S(1)}, bf16[272,512]{1,0:T(8,128)(2,1)S(1)}, u32[]{:S(2)}, u32[]{:S(2)}) collective-permute-start(bf16[272,512]{1,0:T(8,128)(2,1)S(1)} %collective-permute-done.4.refs_3_), channel_id=1, source_target_pairs={{0,1},{1,0},{2,3},{3,2},{4,5},{5,4},{6,7},{7,6},{8,9},{9,8},{10,11... | collective-permute-start | bytes 835592 | tf_op jit(solution)/shard_map/ppermute | solution.py:42
  70.8 8.9 %collective-permute-start.11 = (bf16[272,256]{1,0:T(8,128)(2,1)S(1)}, bf16[272,256]{1,0:T(8,128)(2,1)S(1)}, u32[]{:S(2)}, u32[]{:S(2)}) collective-permute-start(bf16[272,256]{1,0:T(8,128)(2,1)S(1)} %shard_map.88.refs_0_.refs_1_), channel_id=1, source_target_pairs={{0,24},{1,25},{2,26},{3,27},{4,28},{5,29},{6,30},{7,31},{8,0},{9,1... | collective-permute-start | bytes 417800 | tf_op jit(solution)/shard_map/ppermute | solution.py:42
  70.8 16.4 %collective-permute-start.14 = (bf16[272,512]{1,0:T(8,128)(2,1)S(1)}, bf16[272,512]{1,0:T(8,128)(2,1)S(1)}, u32[]{:S(2)}, u32[]{:S(2)}) collective-permute-start(bf16[272,512]{1,0:T(8,128)(2,1)S(1)} %shard_map.87.refs_10_.refs_4_), channel_id=1, source_target_pairs={{0,224},{1,33},{2,226},{3,35},{4,228},{5,37},{6,230},{7,39},{8,232... | collective-permute-start | bytes 835592 | tf_op jit(solution)/shard_map/ppermute | solution.py:42
  79.3 8.0 %collective-permute-start.13 = (bf16[272,512]{1,0:T(8,128)(2,1)S(1)}, bf16[272,512]{1,0:T(8,128)(2,1)S(1)}, u32[]{:S(2)}, u32[]{:S(2)}) collective-permute-start(bf16[272,512]{1,0:T(8,128)(2,1)S(1)} %shard_map.87.refs_10_.refs_4_), channel_id=1, source_target_pairs={{0,32},{1,225},{2,34},{3,227},{4,36},{5,229},{6,38},{7,231},{8,40}... | collective-permute-start | bytes 835592 | tf_op jit(solution)/shard_map/ppermute | solution.py:42
  79.3 7.0 %collective-permute-start.10 = (bf16[272,256]{1,0:T(8,128)(2,1)S(1)}, bf16[272,256]{1,0:T(8,128)(2,1)S(1)}, u32[]{:S(2)}, u32[]{:S(2)}) collective-permute-start(bf16[272,256]{1,0:T(8,128)(2,1)S(1)} %shard_map.88.refs_0_.refs_1_), channel_id=1, source_target_pairs={{0,16},{1,17},{2,18},{3,19},{4,20},{5,21},{6,22},{7,23},{8,24},{9,... | collective-permute-start | bytes 417800 | tf_op jit(solution)/shard_map/ppermute | solution.py:42
  79.6 7.6 %collective-permute-start.9 = (bf16[272,256]{1,0:T(8,128)(2,1)S(1)}, bf16[272,256]{1,0:T(8,128)(2,1)S(1)}, u32[]{:S(2)}, u32[]{:S(2)}) collective-permute-start(bf16[272,256]{1,0:T(8,128)(2,1)S(1)} %shard_map.88.refs_0_.refs_1_), channel_id=1, source_target_pairs={{0,8},{1,9},{2,10},{3,11},{4,12},{5,13},{6,14},{7,15},{8,16},{9,17... | collective-permute-start | bytes 417800 | tf_op jit(solution)/shard_map/ppermute | solution.py:42
  88.1 16.2 %collective-permute-start.19 = (bf16[2,256,512]{2,1,0:T(8,128)(2,1)S(1)}, bf16[2,256,512]{2,1,0:T(8,128)(2,1)S(1)}, u32[]{:S(2)}, u32[]{:S(2)}) collective-permute-start(bf16[2,256,512]{2,1,0:T(8,128)(2,1)S(1)} %get-tuple-element.69), channel_id=1, source_target_pairs={{0,4},{1,5},{2,6},{3,7},{4,0},{5,1},{6,2},{7,3},{8,12},{9,13},{10,... | collective-permute-start | bytes 1572872 | tf_op jit(solution)/shard_map/ppermute | solution.py:42
  89.3 10.5 %collective-permute-start.15 = (bf16[272,512]{1,0:T(8,128)(2,1)S(1)}, bf16[272,512]{1,0:T(8,128)(2,1)S(1)}, u32[]{:S(2)}, u32[]{:S(2)}) collective-permute-start(bf16[272,512]{1,0:T(8,128)(2,1)S(1)} %get-tuple-element.63.refs_5_), channel_id=1, source_target_pairs={{0,32},{1,225},{2,34},{3,227},{4,36},{5,229},{6,38},{7,231},{8,40}... | collective-permute-start | bytes 835592 | tf_op jit(solution)/shard_map/ppermute | solution.py:42
  89.3 10.5 %collective-permute-start.16 = (bf16[272,512]{1,0:T(8,128)(2,1)S(1)}, bf16[272,512]{1,0:T(8,128)(2,1)S(1)}, u32[]{:S(2)}, u32[]{:S(2)}) collective-permute-start(bf16[272,512]{1,0:T(8,128)(2,1)S(1)} %get-tuple-element.64.refs_6_), channel_id=1, source_target_pairs={{0,224},{1,33},{2,226},{3,35},{4,228},{5,37},{6,230},{7,39},{8,232... | collective-permute-start | bytes 835592 | tf_op jit(solution)/shard_map/ppermute | solution.py:42
  92.5 18.8 %collective-permute-start.22 = (bf16[2,256,512]{2,1,0:T(8,128)(2,1)S(1)}, bf16[2,256,512]{2,1,0:T(8,128)(2,1)S(1)}, u32[]{:S(2)}, u32[]{:S(2)}) collective-permute-start(bf16[2,256,512]{2,1,0:T(8,128)(2,1)S(1)} %get-tuple-element.76), channel_id=1, source_target_pairs={{0,2},{1,7},{2,4},{3,1},{4,6},{5,3},{6,0},{7,5},{8,10},{9,15},{10,... | collective-permute-start | bytes 1572872 | tf_op jit(solution)/shard_map/ppermute | solution.py:42
  100.3 10.3 %collective-permute-start.17 = (bf16[272,512]{1,0:T(8,128)(2,1)S(1)}, bf16[272,512]{1,0:T(8,128)(2,1)S(1)}, u32[]{:S(2)}, u32[]{:S(2)}) collective-permute-start(bf16[272,512]{1,0:T(8,128)(2,1)S(1)} %get-tuple-element.67.refs_4_), channel_id=1, source_target_pairs={{0,32},{1,225},{2,34},{3,227},{4,36},{5,229},{6,38},{7,231},{8,40}... | collective-permute-start | bytes 835592 | tf_op jit(solution)/shard_map/ppermute | solution.py:42
  100.4 10.2 %collective-permute-start.18 = (bf16[272,512]{1,0:T(8,128)(2,1)S(1)}, bf16[272,512]{1,0:T(8,128)(2,1)S(1)}, u32[]{:S(2)}, u32[]{:S(2)}) collective-permute-start(bf16[272,512]{1,0:T(8,128)(2,1)S(1)} %get-tuple-element.68.refs_5_), channel_id=1, source_target_pairs={{0,224},{1,33},{2,226},{3,35},{4,228},{5,37},{6,230},{7,39},{8,232... | collective-permute-start | bytes 835592 | tf_op jit(solution)/shard_map/ppermute | solution.py:42
  103.7 9.2 %collective-permute-start.21 = (bf16[2,256,512]{2,1,0:T(8,128)(2,1)S(1)}, bf16[2,256,512]{2,1,0:T(8,128)(2,1)S(1)}, u32[]{:S(2)}, u32[]{:S(2)}) collective-permute-start(bf16[2,256,512]{2,1,0:T(8,128)(2,1)S(1)} %get-tuple-element.74), channel_id=1, source_target_pairs={{0,6},{1,3},{2,0},{3,5},{4,2},{5,7},{6,4},{7,1},{8,14},{9,11},{10,... | collective-permute-start | bytes 1572872 | tf_op jit(solution)/shard_map/ppermute | solution.py:42
  111.2 7.8 %collective-permute-start.20 = (bf16[272,512]{1,0:T(8,128)(2,1)S(1)}, bf16[272,512]{1,0:T(8,128)(2,1)S(1)}, u32[]{:S(2)}, u32[]{:S(2)}) collective-permute-start(bf16[272,512]{1,0:T(8,128)(2,1)S(1)} %get-tuple-element.73.refs_4_), channel_id=1, source_target_pairs={{0,32},{1,225},{2,34},{3,227},{4,36},{5,229},{6,38},{7,231},{8,40}... | collective-permute-start | bytes 835592 | tf_op jit(solution)/shard_map/ppermute | solution.py:42
  120.5 6.0 %collective-permute-start.23 = (bf16[272,256]{1,0:T(8,128)(2,1)S(1)}, bf16[272,256]{1,0:T(8,128)(2,1)S(1)}, u32[]{:S(2)}, u32[]{:S(2)}) collective-permute-start(bf16[272,256]{1,0:T(8,128)(2,1)S(1)} %get-tuple-element.84), channel_id=1, source_target_pairs={{0,24},{1,25},{2,26},{3,27},{4,28},{5,29},{6,30},{7,31},{8,0},{9,1... | collective-permute-start | bytes 417800 | tf_op jit(solution)/shard_map/ppermute | solution.py:42
  123.2 6.6 %collective-permute-start.24 = (bf16[272,256]{1,0:T(8,128)(2,1)S(1)}, bf16[272,256]{1,0:T(8,128)(2,1)S(1)}, u32[]{:S(2)}, u32[]{:S(2)}) collective-permute-start(bf16[272,256]{1,0:T(8,128)(2,1)S(1)} %get-tuple-element.85), channel_id=1, source_target_pairs={{0,16},{1,17},{2,18},{3,19},{4,20},{5,21},{6,22},{7,23},{8,24},{9,... | collective-permute-start | bytes 417800 | tf_op jit(solution)/shard_map/ppermute | solution.py:42
  123.4 6.4 %collective-permute-start.25 = (bf16[272,256]{1,0:T(8,128)(2,1)S(1)}, bf16[272,256]{1,0:T(8,128)(2,1)S(1)}, u32[]{:S(2)}, u32[]{:S(2)}) collective-permute-start(bf16[272,256]{1,0:T(8,128)(2,1)S(1)} %get-tuple-element.86), channel_id=1, source_target_pairs={{0,8},{1,9},{2,10},{3,11},{4,12},{5,13},{6,14},{7,15},{8,16},{9,17... | collective-permute-start | bytes 417800 | tf_op jit(solution)/shard_map/ppermute | solution.py:42
  130.9 6.3 %collective-permute-start.26 = (bf16[272,256]{1,0:T(8,128)(2,1)S(1)}, bf16[272,256]{1,0:T(8,128)(2,1)S(1)}, u32[]{:S(2)}, u32[]{:S(2)}) collective-permute-start(bf16[272,256]{1,0:T(8,128)(2,1)S(1)} %shard_map.97.refs_0_), channel_id=1, source_target_pairs={{0,2},{1,7},{2,4},{3,1},{4,6},{5,3},{6,0},{7,5},{8,10},{9,15},{10,... | collective-permute-start | bytes 417800 | tf_op jit(solution)/shard_map/ppermute | solution.py:42
  132.1 6.1 %collective-permute-start.27 = (bf16[272,256]{1,0:T(8,128)(2,1)S(1)}, bf16[272,256]{1,0:T(8,128)(2,1)S(1)}, u32[]{:S(2)}, u32[]{:S(2)}) collective-permute-start(bf16[272,256]{1,0:T(8,128)(2,1)S(1)} %shard_map.97.refs_0_), channel_id=1, source_target_pairs={{0,6},{1,3},{2,0},{3,5},{4,2},{5,7},{6,4},{7,1},{8,14},{9,11},{10,... | collective-permute-start | bytes 417800 | tf_op jit(solution)/shard_map/ppermute | solution.py:42
  137.3 6.3 %collective-permute-start.28 = (bf16[272,256]{1,0:T(8,128)(2,1)S(1)}, bf16[272,256]{1,0:T(8,128)(2,1)S(1)}, u32[]{:S(2)}, u32[]{:S(2)}) collective-permute-start(bf16[272,256]{1,0:T(8,128)(2,1)S(1)} %collective-permute-done.26.refs_1_), channel_id=1, source_target_pairs={{0,2},{1,7},{2,4},{3,1},{4,6},{5,3},{6,0},{7,5},{8,10},{9,15},{10,... | collective-permute-start | bytes 417800 | tf_op jit(solution)/shard_map/ppermute | solution.py:42
  137.3 6.3 %collective-permute-start.29 = (bf16[272,256]{1,0:T(8,128)(2,1)S(1)}, bf16[272,256]{1,0:T(8,128)(2,1)S(1)}, u32[]{:S(2)}, u32[]{:S(2)}) collective-permute-start(bf16[272,256]{1,0:T(8,128)(2,1)S(1)} %shard_map.97.refs_0_), channel_id=1, source_target_pairs={{0,1},{1,0},{2,3},{3,2},{4,5},{5,4},{6,7},{7,6},{8,9},{9,8},{10,11... | collective-permute-start | bytes 417800 | tf_op jit(solution)/shard_map/ppermute | solution.py:42
  137.3 6.3 %collective-permute-start.30 = (bf16[272,256]{1,0:T(8,128)(2,1)S(1)}, bf16[272,256]{1,0:T(8,128)(2,1)S(1)}, u32[]{:S(2)}, u32[]{:S(2)}) collective-permute-start(bf16[272,256]{1,0:T(8,128)(2,1)S(1)} %collective-permute-done.26.refs_1_), channel_id=1, source_target_pairs={{0,1},{1,0},{2,3},{3,2},{4,5},{5,4},{6,7},{7,6},{8,9},{9,8},{10,11... | collective-permute-start | bytes 417800 | tf_op jit(solution)/shard_map/ppermute | solution.py:42
  138.2 5.3 %collective-permute-start.31 = (bf16[272,256]{1,0:T(8,128)(2,1)S(1)}, bf16[272,256]{1,0:T(8,128)(2,1)S(1)}, u32[]{:S(2)}, u32[]{:S(2)}) collective-permute-start(bf16[272,256]{1,0:T(8,128)(2,1)S(1)} %collective-permute-done.27.refs_2_), channel_id=1, source_target_pairs={{0,1},{1,0},{2,3},{3,2},{4,5},{5,4},{6,7},{7,6},{8,9},{9,8},{10,11... | collective-permute-start | bytes 417800 | tf_op jit(solution)/shard_map/ppermute | solution.py:42
  (7 other events, 48.1 us)

commit v3 on v2

--- a/solution.py
+++ b/solution.py
@@ -21,7 +21,6 @@
 LOW = -1e30
 VMEM_LIMIT = 20 * 1024 * 1024
 ROOM = 48 * 1024 * 1024
-CUT_ROOM = 52 * 1024 * 1024
 F32, BF16 = jnp.float32, jnp.bfloat16
 
 
@@ -166,7 +165,7 @@
     tail_out[:, FEAT:] = counts[8:]
 
 
-def pool_kernel(ids, tokens, _, sums_out, counts_out, hot):
+def pool_kernel(ids, tokens, sums_out, counts_out, hot):
     segment = iota((SEG, 128), 0)
     for r in range(16):
         hot[:, r * 128 : (r + 1) * 128] = ones_where(ids[r : r + 1, :] == segment)
@@ -399,7 +398,7 @@
     return call(body, STATE, ins, flops=flops, moved=4 << 20, aliases=aliases, far_in=(ignored,))
 
 
-def merge_kernel(info, a, b, c, d, out):
+def merge_kernel(info, a, b, c, d, _, out):
     parts = (a, b, c, d)
     tails = [p[SEG:, :].astype(F32) for p in parts]
     weights, end_weights = [], []
@@ -478,20 +477,19 @@
     )(*attended, *weights, means, ids, tokens)
 
 
-def cut_kernel(info, w_out, _, mine, sibling, done, sems):
+def cut_kernel(info, w_out, _, mine, sibling, sems):
     copies = []
     for i in range(4):
         for side, out in enumerate((mine, sibling)):
             start = pl.multiple_of(info[I_CUT + 4 * side + i] * FEAT, FEAT)
             copies.append(pltpu.make_async_copy(w_out.at[:, pl.ds(start, FEAT)], out.at[i], sems.at[side, i]))
             copies[-1].start()
-    done[...] = jnp.zeros_like(done)
     for copy in copies:
         copy.wait()
 
 
 def pair_kernel(info, *refs):
-    sources, outs, sems = refs[:2], refs[7:11], refs[-1]
+    sources, outs, sems = refs[:2], refs[3:7], refs[7]
     copies = []
     for i, out in enumerate(outs):
         for side, source in enumerate(sources):
@@ -521,18 +519,11 @@
     count = NZ * NX
     above = lax.ppermute(head, "seq", [(i, i - 1) for i in range(1, count)])
     below = lax.ppermute(tail, "seq", [(i, i + 1) for i in range(count - 1)])
-    cut = shape((4, SEG, FEAT), BF16)
-    sems = [pltpu.SemaphoreType.DMA((2, 4))]
-    mine, theirs, cut_done = call(
-        cut_kernel, [cut, cut, shape((8, 128), F32)], [info, w_out, ids], scratch=sems, far_in=(1, 2), far_out=(0, 1), room=CUT_ROOM
-    )
-    theirs = swap(theirs)
     sums, sizes = call(
         pool_kernel,
         [shape((SEG, FEAT), F32), shape((SEG, 128), F32)],
-        [ids, tokens, cut_done],
+        [ids, tokens],
         scalars=None,
-        far_in=(2,),
         flops=1 << 30,
         moved=2 << 20,
         scratch=[pltpu.VMEM((SEG, TOK), BF16)],
@@ -543,7 +534,7 @@
         [info, sums, sizes, head, above, below, norm_gain.reshape(8, FEAT)],
     )
     first, sibling, second = y_one(u), swap(u), y_other(u)
-    across, far = swap(first), y_one(first)
+    across = swap(first)
     part, part_query = shape((SEG, COLS), F32), shape((ROWS, COLS), F32)
     kept = shape((4, FEAT, COLS), BF16)
     queried, keyed, valued, *late = call(
@@ -556,6 +547,7 @@
         far_in=(5, 6, 7),
         room=ROOM,
     )
+    (far,) = gate(info, [y_one(first)], queried)
     blocks = [u, first, second, far, sibling, across, swap(second), swap(far)]
     (kv,) = call(
         key_value_kernel,
@@ -570,33 +562,39 @@
     )
     queries = [query] + [x_by(query, k) for k in (1, 2, 3)]
     one, other = z_one(kv), z_other(kv)
+    cut = shape((4, SEG, FEAT), BF16)
+    sems = [pltpu.SemaphoreType.DMA((2, 4))]
+    mine, theirs = call(
+        cut_kernel, [cut, cut], [info, w_out, kv], scratch=sems, far_in=(1, 2), far_out=(0, 1)
+    )
+    theirs = swap(theirs)
+    one2, other2 = z_one(one), z_other(other)
+    *state, done = attend_step(1, info, queries, kv, [one, other], None, kv)
     pair = shape((2, SEG, FEAT), BF16)
-    block = shape(kv.shape, BF16)
-    *pairs, one, other = call(
+    pairs = call(
         pair_kernel,
-        [pair] * 4 + [block] * 2,
-        [info, mine, theirs, one, other] + queries[1:],
+        [pair] * 4,
+        [info, mine, theirs, done],
         scratch=sems,
-        aliases={3: 4, 4: 5},
-        far_in=range(1, 8),
-        far_out=range(6),
+        far_in=range(1, 4),
+        far_out=range(4),
     )
     far_weights = y_far(pairs[3])
-    one2, other2 = z_one(one), z_other(other)
-    *state, done = attend_step(1, info, queries, kv, [one, other], None, pairs[0])
     one2, other2 = gate(info, [one2, other2], done)
     one3, other3 = z_one(one2), z_other(other2)
     one_weights = y_one(pairs[1])
-    *state, done = attend_step(2, info, queries, None, [one2, other2], state, far_weights)
+    *state, done = attend_step(2, info, queries, None, [one2, other2], state, pairs[0])
     one3, other3 = gate(info, [one3, other3], done)
     one4 = z_one(one3)
     other_weights = y_other(pairs[2])
-    *state, done = attend_step(3, info, queries, None, [one3, other3], state, one_weights)
-    one4, other_weights = gate(info, [one4, other_weights], done)
+    *state, done = attend_step(3, info, queries, None, [one3, other3], state, far_weights)
+    one4, one_weights = gate(info, [one4, one_weights], done)
     partial = attend_step(4, info, queries, None, [one4], state)
     weights = [pairs[0], one_weights, other_weights, far_weights]
     partial = [partial[0]] + [x_by(partial[k], -k) for k in (1, 2, 3)]
-    (attended,) = call(merge_kernel, [shape((ROWS, COLS), BF16)], [info] + partial, moved=1 << 20)
+    (attended,) = call(
+        merge_kernel, [shape((ROWS, COLS), BF16)], [info] + partial + [other_weights], moved=1 << 20, far_in=(5,)
+    )
     return output(mp_exchange(attended), weights, means, ids, tokens)
 
 

time: 152 us -> 122 us (0.80)
  the two profiles are of different devices: /device:TPU:2 before, /device:TPU:225 now
where the time goes in v3:
time: 122 us
  starting transfers between devices  51 us (42%)
  waiting for transfers between devices  38 us (31%)
  Pallas kernels  29.4 us (24%)
  local copies, waits for them, and re-layouts  3.33 us (3%)
    ppermute x31, starting transfers between devices, move(): return lax.ppermute(value, ('seq', 'mp'), pairs)  44.1 us
    ppermute x31, waiting for transfers between devices, move(): return lax.ppermute(value, ('seq', 'mp'), pairs)  35 us
    pallas_call x17, Pallas kernels, call(): pl.pallas_call(body, out_shape=outs, in_specs=[SMEM if i == scalars else...  25.6 us
    ppermute x1, starting transfers between devices, shards(): above = lax.ppermute(head, 'seq', [(i, i - 1) for i in range(1, count)])  4.96 us
    pallas_call x1, Pallas kernels, output(): pl.pallas_call(output_kernel, grid=(TOK // BLOCK,), out_shape=shape((TOK,...  3.83 us
    ppermute x1, waiting for transfers between devices, shards(): below = lax.ppermute(tail, 'seq', [(i, i + 1) for i in range(count - 1)])  2.96 us
    unnamed x10, local copies, waits for them, and re-layouts  2.63 us
  transfers between devices with their start and end apart: 33, of which 15 were waited for; matrix products, arithmetic and copies ran while one was open for 1% of the time, Pallas kernels for 17%

profile of v3, /device:TPU:225, one launch (start us, length us, event | category | flops | bytes accessed | tf_op | source)
XLA Modules:
  0.0 121.9 jit_solution(1190768583018140104)
XLA Ops:
  0.0 1.6 %copy-done = bf16[2048,512]{1,0:T(8,128)(2,1)S(1)} copy-done((bf16[2048,512]{1,0:T(8,128)(2,1)S(1)}, bf16[2048,512]{1,0:T(8,128)(2,1)}, u32[]{:S(2)}) %copy-start) | copy-done | bytes 2097176
  3.0 5.0 %collective-permute-start = (f32[8,640]{1,0:T(8,128)S(1)}, f32[8,640]{1,0:T(8,128)S(1)}, u32[]{:S(2)}, u32[]{:S(2)}) collective-permute-start(f32[8,640]{1,0:T(8,128)S(1)} %get-tuple-element.47.head), channel_id=1, source_target_pairs={{8,0},{16,8},{24,16},{32,24},{40,32},{48,40},{56,48},{64,56},{72,6... | collective-permute-start | bytes 61448 | tf_op jit(solution)/shard_map/ppermute | solution.py:520
  8.0 1.9 %collective-permute-start.1 = (f32[8,640]{1,0:T(8,128)S(1)}, f32[8,640]{1,0:T(8,128)S(1)}, u32[]{:S(2)}, u32[]{:S(2)}) collective-permute-start(f32[8,640]{1,0:T(8,128)S(1)} %get-tuple-element.48), channel_id=1, source_target_pairs={{0,8},{8,16},{16,24},{24,32},{32,40},{40,48},{48,56},{56,64},{64,7... | collective-permute-start | bytes 61448 | tf_op jit(solution)/shard_map/ppermute | solution.py:521
  11.6 3.0 %collective-permute-done.1.below = f32[8,640]{1,0:T(8,128)S(1)} collective-permute-done((f32[8,640]{1,0:T(8,128)S(1)}, f32[8,640]{1,0:T(8,128)S(1)}, u32[]{:S(2)}, u32[]{:S(2)}) %collective-permute-start.1) | collective-permute-done | bytes 20512 | tf_op jit(solution)/shard_map/ppermute | solution.py:521
  15.4 2.8 %collective-permute-start.2 = (bf16[272,512]{1,0:T(8,128)(2,1)S(1)}, bf16[272,512]{1,0:T(8,128)(2,1)S(1)}, u32[]{:S(2)}, u32[]{:S(2)}) collective-permute-start(bf16[272,512]{1,0:T(8,128)(2,1)S(1)} %get-tuple-element.49.refs_0_), channel_id=1, source_target_pairs={{0,2},{1,7},{2,4},{3,1},{4,6},{5,3},{6,0},{7,5},{8,10},{9,15},{10,... | collective-permute-start | bytes 835592 | tf_op jit(solution)/shard_map/ppermute | solution.py:41
  18.2 2.6 %collective-permute-start.5 = (bf16[272,512]{1,0:T(8,128)(2,1)S(1)}, bf16[272,512]{1,0:T(8,128)(2,1)S(1)}, u32[]{:S(2)}, u32[]{:S(2)}) collective-permute-start(bf16[272,512]{1,0:T(8,128)(2,1)S(1)} %get-tuple-element.49.refs_0_), channel_id=1, source_target_pairs={{0,1},{1,0},{2,3},{3,2},{4,5},{5,4},{6,7},{7,6},{8,9},{9,8},{10,11... | collective-permute-start | bytes 835592 | tf_op jit(solution)/shard_map/ppermute | solution.py:41
  21.7 3.5 %collective-permute-start.4 = (bf16[272,512]{1,0:T(8,128)(2,1)S(1)}, bf16[272,512]{1,0:T(8,128)(2,1)S(1)}, u32[]{:S(2)}, u32[]{:S(2)}) collective-permute-start(bf16[272,512]{1,0:T(8,128)(2,1)S(1)} %collective-permute-done.2.refs_1_), channel_id=1, source_target_pairs={{0,2},{1,7},{2,4},{3,1},{4,6},{5,3},{6,0},{7,5},{8,10},{9,15},{10,... | collective-permute-start | bytes 835592 | tf_op jit(solution)/shard_map/ppermute | solution.py:41
  25.2 2.9 %collective-permute-start.6 = (bf16[272,512]{1,0:T(8,128)(2,1)S(1)}, bf16[272,512]{1,0:T(8,128)(2,1)S(1)}, u32[]{:S(2)}, u32[]{:S(2)}) collective-permute-start(bf16[272,512]{1,0:T(8,128)(2,1)S(1)} %collective-permute-done.2.refs_1_), channel_id=1, source_target_pairs={{0,1},{1,0},{2,3},{3,2},{4,5},{5,4},{6,7},{7,6},{8,9},{9,8},{10,11... | collective-permute-start | bytes 835592 | tf_op jit(solution)/shard_map/ppermute | solution.py:41
  28.2 4.3 %shard_map.85 = (f32[272,256]{1,0:T(8,128)S(1)}, f32[256,256]{1,0:T(8,128)S(1)}, f32[256,256]{1,0:T(8,128)S(1)}, bf16[4,512,256]{2,1,0:T(8,128)(2,1)S(1)}, bf16[...) custom-call(s32[32]{0:T(128)S(1)} %dynamic-slice_bitcast_fusion.info.refs_0_, ...), custom_call_target="tpu_custom_call" | custom-call | flops 855638016 | bytes 6291456 | tf_op jit(solution)/shard_map/pallas_call | solution.py:105
  33.1 3.5 %collective-permute-start.8 = (bf16[272,512]{1,0:T(8,128)(2,1)S(1)}, bf16[272,512]{1,0:T(8,128)(2,1)S(1)}, u32[]{:S(2)}, u32[]{:S(2)}) collective-permute-start(bf16[272,512]{1,0:T(8,128)(2,1)S(1)} %shard_map.86.refs_3_), channel_id=1, source_target_pairs={{0,1},{1,0},{2,3},{3,2},{4,5},{5,4},{6,7},{7,6},{8,9},{9,8},{10,11... | collective-permute-start | bytes 835592 | tf_op jit(solution)/shard_map/ppermute | solution.py:41
  37.7 1.2 %shard_map.87.refs_10_.refs_4_.refs_7_._ = bf16[272,512]{1,0:T(8,128)(2,1)S(1)} custom-call(s32[32]{0:T(128)S(1)} %dynamic-slice_bitcast_fusion.info.refs_0_, bf16[272,512]{1,0:T(8,128)(2,1)S(1)} %get-tuple-element.49.refs_0_, bf16[272,512]{1,0:T(8,128)(2,1)S(1)} %collective-permute-done.2.refs_1_, bf16[272,512]{1,0:T(8,128)(2,1)S(1)} %collective-permute-done.3.refs_2_, ...), custom_call_target="tpu_custom_call" | custom-call | tf_op jit(solution)/shard_map/pallas_call | solution.py:105
  41.3 1.9 %collective-permute-start.14 = (bf16[272,512]{1,0:T(8,128)(2,1)S(1)}, bf16[272,512]{1,0:T(8,128)(2,1)S(1)}, u32[]{:S(2)}, u32[]{:S(2)}) collective-permute-start(bf16[272,512]{1,0:T(8,128)(2,1)S(1)} %shard_map.87.refs_10_.refs_4_.refs_7_._), channel_id=1, source_target_pairs={{0,224},{1,33},{2,226},{3,35},{4,228},{5,37},{6,230},{7,39},{8,232... | collective-permute-start | bytes 835592 | tf_op jit(solution)/shard_map/ppermute | solution.py:41
  44.4 5.5 %collective-permute-done.12.refs_5_ = bf16[272,512]{1,0:T(8,128)(2,1)S(1)} collective-permute-done((bf16[272,512]{1,0:T(8,128)(2,1)S(1)}, bf16[272,512]{1,0:T(8,128)(2,1)S(1)}, u32[]{:S(2)}, u32[]{:S(2)}) %collective-permute-start.12) | collective-permute-done | bytes 278560 | tf_op jit(solution)/shard_map/ppermute | solution.py:41
  49.9 2.7 %collective-permute-start.15 = (bf16[272,512]{1,0:T(8,128)(2,1)S(1)}, bf16[272,512]{1,0:T(8,128)(2,1)S(1)}, u32[]{:S(2)}, u32[]{:S(2)}) collective-permute-start(bf16[272,512]{1,0:T(8,128)(2,1)S(1)} %collective-permute-done.14.refs_6_), channel_id=1, source_target_pairs={{0,224},{1,33},{2,226},{3,35},{4,228},{5,37},{6,230},{7,39},{8,232... | collective-permute-start | bytes 835592 | tf_op jit(solution)/shard_map/ppermute | solution.py:41
  52.6 1.5 %collective-permute-start.9 = (bf16[272,256]{1,0:T(8,128)(2,1)S(1)}, bf16[272,256]{1,0:T(8,128)(2,1)S(1)}, u32[]{:S(2)}, u32[]{:S(2)}) collective-permute-start(bf16[272,256]{1,0:T(8,128)(2,1)S(1)} %shard_map.88.refs_0_.refs_1_), channel_id=1, source_target_pairs={{0,8},{1,9},{2,10},{3,11},{4,12},{5,13},{6,14},{7,15},{8,16},{9,17... | collective-permute-start | bytes 417800 | tf_op jit(solution)/shard_map/ppermute | solution.py:41
  54.0 4.2 %collective-permute-done.11.refs_3_.refs_4_ = bf16[272,256]{1,0:T(8,128)(2,1)S(1)} collective-permute-done((bf16[272,256]{1,0:T(8,128)(2,1)S(1)}, bf16[272,256]{1,0:T(8,128)(2,1)S(1)}, u32[]{:S(2)}, u32[]{:S(2)}) %collective-permute-start.11) | collective-permute-done | bytes 139296 | tf_op jit(solution)/shard_map/ppermute | solution.py:41
  59.4 4.6 %shard_map.89 = (f32[4,2,272,256]{3,2,1,0:T(8,128)S(1)}, f32[4,2,272,128]{3,2,1,0:T(8,128)S(1)}, f32[8,128]{1,0:T(8,128)S(1)}) custom-call(s32[32]{0:T(128)S(1)} %dynamic-slice_bitcast_fusion.info.refs_0_, bf16[272,256]{1,0:T(8,128)(2,1)S(1)} %shard_map.88.refs_0_.refs_1_, bf16[272,256]{1,0:T(8,128)(2,1)S(1)} %collective-permute-done.9.refs_1_.refs_2_, ...), custom_call_target="tpu_custom_call" | custom-call | flops 855638016 | bytes 4194304 | tf_op jit(solution)/shard_map/pallas_call | solution.py:105
  65.6 2.7 %collective-permute-start.17 = (bf16[272,512]{1,0:T(8,128)(2,1)S(1)}, bf16[272,512]{1,0:T(8,128)(2,1)S(1)}, u32[]{:S(2)}, u32[]{:S(2)}) collective-permute-start(bf16[272,512]{1,0:T(8,128)(2,1)S(1)} %get-tuple-element.59.refs_5_), channel_id=1, source_target_pairs={{0,224},{1,33},{2,226},{3,35},{4,228},{5,37},{6,230},{7,39},{8,232... | collective-permute-start | bytes 835592 | tf_op jit(solution)/shard_map/ppermute | solution.py:41
  69.7 2.6 %shard_map.93 = (f32[4,2,272,256]{3,2,1,0:T(8,128)S(1)}, f32[4,2,272,128]{3,2,1,0:T(8,128)S(1)}, f32[8,128]{1,0:T(8,128)S(1)}) custom-call(s32[32]{0:T(128)S(1)} %dynamic-slice_bitcast_fusion.info.refs_0_, bf16[272,256]{1,0:T(8,128)(2,1)S(1)} %shard_map.88.refs_0_.refs_1_, ...), custom_call_target="tpu_custom_call", output_to_operand_aliasing={{0}: (8, {}), {1}: (9, {})} | custom-call | flops 570425344 | bytes 4194304 | tf_op jit(solution)/shard_map/pallas_call | solution.py:105
  72.3 2.2 %collective-permute-done.16.refs_0_ = bf16[272,512]{1,0:T(8,128)(2,1)S(1)} collective-permute-done((bf16[272,512]{1,0:T(8,128)(2,1)S(1)}, bf16[272,512]{1,0:T(8,128)(2,1)S(1)}, u32[]{:S(2)}, u32[]{:S(2)}) %collective-permute-start.16) | collective-permute-done | bytes 278560 | tf_op jit(solution)/shard_map/ppermute | solution.py:41
  75.1 4.4 %collective-permute-done.21.refs_6_.refs_11_ = bf16[2,256,512]{2,1,0:T(8,128)(2,1)S(1)} collective-permute-done((bf16[2,256,512]{2,1,0:T(8,128)(2,1)S(1)}, bf16[2,256,512]{2,1,0:T(8,128)(2,1)S(1)}, u32[]{:S(2)}, u32[]{:S(2)}) %collective-permute-start.21) | collective-permute-done | bytes 524320 | tf_op jit(solution)/shard_map/ppermute | solution.py:41
  79.5 2.7 %shard_map.95 = (f32[4,2,272,256]{3,2,1,0:T(8,128)S(1)}, f32[4,2,272,128]{3,2,1,0:T(8,128)S(1)}, f32[8,128]{1,0:T(8,128)S(1)}) custom-call(s32[32]{0:T(128)S(1)} %dynamic-slice_bitcast_fusion.info.refs_0_, bf16[272,256]{1,0:T(8,128)(2,1)S(1)} %shard_map.88.refs_0_.refs_1_, ...), custom_call_target="tpu_custom_call", output_to_operand_aliasing={{0}: (8, {}), {1}: (9, {})} | custom-call | flops 570425344 | bytes 4194304 | tf_op jit(solution)/shard_map/pallas_call | solution.py:105
  82.2 6.2 %collective-permute-done.20.refs_1_ = bf16[2,256,512]{2,1,0:T(8,128)(2,1)S(1)} collective-permute-done((bf16[2,256,512]{2,1,0:T(8,128)(2,1)S(1)}, bf16[2,256,512]{2,1,0:T(8,128)(2,1)S(1)}, u32[]{:S(2)}, u32[]{:S(2)}) %collective-permute-start.20) | collective-permute-done | bytes 524320 | tf_op jit(solution)/shard_map/ppermute | solution.py:41
  88.9 1.9 %shard_map.97 = (bf16[272,256]{1,0:T(8,128)(2,1)S(1)}, bf16[272,256]{1,0:T(8,128)(2,1)S(1)}, bf16[272,256]{1,0:T(8,128)(2,1)S(1)}, bf16[272,256]{1,0:T(8,128)(2,...) custom-call(s32[32]{0:T(128)S(1)} %dynamic-slice_bitcast_fusion.info, ...), custom_call_target="tpu_custom_call", output_to_operand_aliasing={{4}: (6, {}), {5}: (7, {})} | custom-call | flops 285212672 | bytes 4194304 | tf_op jit(solution)/shard_map/pallas_call | solution.py:105
  92.4 2.4 %collective-permute-done.22.b = bf16[272,256]{1,0:T(8,128)(2,1)S(1)} collective-permute-done((bf16[272,256]{1,0:T(8,128)(2,1)S(1)}, bf16[272,256]{1,0:T(8,128)(2,1)S(1)}, u32[]{:S(2)}, u32[]{:S(2)}) %collective-permute-start.22) | collective-permute-done | bytes 139296 | tf_op jit(solution)/shard_map/ppermute | solution.py:41
  94.8 1.7 %collective-permute-done.23.c = bf16[272,256]{1,0:T(8,128)(2,1)S(1)} collective-permute-done((bf16[272,256]{1,0:T(8,128)(2,1)S(1)}, bf16[272,256]{1,0:T(8,128)(2,1)S(1)}, u32[]{:S(2)}, u32[]{:S(2)}) %collective-permute-start.23) | collective-permute-done | bytes 139296 | tf_op jit(solution)/shard_map/ppermute | solution.py:41
  96.5 1.4 %collective-permute-done.24.d = bf16[272,256]{1,0:T(8,128)(2,1)S(1)} collective-permute-done((bf16[272,256]{1,0:T(8,128)(2,1)S(1)}, bf16[272,256]{1,0:T(8,128)(2,1)S(1)}, u32[]{:S(2)}, u32[]{:S(2)}) %collective-permute-start.24) | collective-permute-done | bytes 139296 | tf_op jit(solution)/shard_map/ppermute | solution.py:41
  99.1 6.0 %collective-permute-start.26 = (bf16[272,256]{1,0:T(8,128)(2,1)S(1)}, bf16[272,256]{1,0:T(8,128)(2,1)S(1)}, u32[]{:S(2)}, u32[]{:S(2)}) collective-permute-start(bf16[272,256]{1,0:T(8,128)(2,1)S(1)} %shard_map.98.refs_0_), channel_id=1, source_target_pairs={{0,2},{1,7},{2,4},{3,1},{4,6},{5,3},{6,0},{7,5},{8,10},{9,15},{10,... | collective-permute-start | bytes 417800 | tf_op jit(solution)/shard_map/ppermute | solution.py:41
  105.1 2.0 %collective-permute-done.26.refs_1_ = bf16[272,256]{1,0:T(8,128)(2,1)S(1)} collective-permute-done((bf16[272,256]{1,0:T(8,128)(2,1)S(1)}, bf16[272,256]{1,0:T(8,128)(2,1)S(1)}, u32[]{:S(2)}, u32[]{:S(2)}) %collective-permute-start.26) | collective-permute-done | bytes 139296 | tf_op jit(solution)/shard_map/ppermute | solution.py:41
  107.1 3.1 %collective-permute-start.28 = (bf16[272,256]{1,0:T(8,128)(2,1)S(1)}, bf16[272,256]{1,0:T(8,128)(2,1)S(1)}, u32[]{:S(2)}, u32[]{:S(2)}) collective-permute-start(bf16[272,256]{1,0:T(8,128)(2,1)S(1)} %collective-permute-done.26.refs_1_), channel_id=1, source_target_pairs={{0,2},{1,7},{2,4},{3,1},{4,6},{5,3},{6,0},{7,5},{8,10},{9,15},{10,... | collective-permute-start | bytes 417800 | tf_op jit(solution)/shard_map/ppermute | solution.py:41
  112.2 4.9 %collective-permute-start.32 = (bf16[272,256]{1,0:T(8,128)(2,1)S(1)}, bf16[272,256]{1,0:T(8,128)(2,1)S(1)}, u32[]{:S(2)}, u32[]{:S(2)}) collective-permute-start(bf16[272,256]{1,0:T(8,128)(2,1)S(1)} %collective-permute-done.28.refs_3_), channel_id=1, source_target_pairs={{0,1},{1,0},{2,3},{3,2},{4,5},{5,4},{6,7},{7,6},{8,9},{9,8},{10,11... | collective-permute-start | bytes 417800 | tf_op jit(solution)/shard_map/ppermute | solution.py:41
  118.1 3.8 %shard_map.99 = bf16[2048,512]{1,0:T(8,128)(2,1)} custom-call(bf16[272,256]{1,0:T(8,128)(2,1)S(1)} %shard_map.98.refs_0_, bf16[272,256]{1,0:T(8,128)(2,1)S(1)} %collective-permute-done.26.refs_1_, bf16[272,256]{1,0:T(8,128)(2,1)S(1)} %collective-permute-done.27.refs_2_, bf16[272,256]{1,0:T(8,128)(2,1)S(1)} %collective-permute-done.28.refs_3_, ...), custom_call_target="tpu_custom_call" | custom-call | flops 2147483648 | bytes 6291456 | tf_op jit(solution)/shard_map/pallas_call | solution.py:468
  (64 shorter events, 21.0 us)
Async XLA Ops:
  3.0 8.6 %collective-permute-start = (f32[8,640]{1,0:T(8,128)S(1)}, f32[8,640]{1,0:T(8,128)S(1)}, u32[]{:S(2)}, u32[]{:S(2)}) collective-permute-start(f32[8,640]{1,0:T(8,128)S(1)} %get-tuple-element.47.head), channel_id=1, source_target_pairs={{8,0},{16,8},{24,16},{32,24},{40,32},{48,40},{56,48},{64,56},{72,6... | collective-permute-start | bytes 61448 | tf_op jit(solution)/shard_map/ppermute | solution.py:520
  8.0 6.6 %collective-permute-start.1 = (f32[8,640]{1,0:T(8,128)S(1)}, f32[8,640]{1,0:T(8,128)S(1)}, u32[]{:S(2)}, u32[]{:S(2)}) collective-permute-start(f32[8,640]{1,0:T(8,128)S(1)} %get-tuple-element.48), channel_id=1, source_target_pairs={{0,8},{8,16},{16,24},{24,32},{32,40},{40,48},{48,56},{56,64},{64,7... | collective-permute-start | bytes 61448 | tf_op jit(solution)/shard_map/ppermute | solution.py:521
  15.4 6.3 %collective-permute-start.2 = (bf16[272,512]{1,0:T(8,128)(2,1)S(1)}, bf16[272,512]{1,0:T(8,128)(2,1)S(1)}, u32[]{:S(2)}, u32[]{:S(2)}) collective-permute-start(bf16[272,512]{1,0:T(8,128)(2,1)S(1)} %get-tuple-element.49.refs_0_), channel_id=1, source_target_pairs={{0,2},{1,7},{2,4},{3,1},{4,6},{5,3},{6,0},{7,5},{8,10},{9,15},{10,... | collective-permute-start | bytes 835592 | tf_op jit(solution)/shard_map/ppermute | solution.py:41
  18.2 10.0 %collective-permute-start.3 = (bf16[272,512]{1,0:T(8,128)(2,1)S(1)}, bf16[272,512]{1,0:T(8,128)(2,1)S(1)}, u32[]{:S(2)}, u32[]{:S(2)}) collective-permute-start(bf16[272,512]{1,0:T(8,128)(2,1)S(1)} %get-tuple-element.49.refs_0_), channel_id=1, source_target_pairs={{0,6},{1,3},{2,0},{3,5},{4,2},{5,7},{6,4},{7,1},{8,14},{9,11},{10,... | collective-permute-start | bytes 835592 | tf_op jit(solution)/shard_map/ppermute | solution.py:41
  18.2 10.0 %collective-permute-start.5 = (bf16[272,512]{1,0:T(8,128)(2,1)S(1)}, bf16[272,512]{1,0:T(8,128)(2,1)S(1)}, u32[]{:S(2)}, u32[]{:S(2)}) collective-permute-start(bf16[272,512]{1,0:T(8,128)(2,1)S(1)} %get-tuple-element.49.refs_0_), channel_id=1, source_target_pairs={{0,1},{1,0},{2,3},{3,2},{4,5},{5,4},{6,7},{7,6},{8,9},{9,8},{10,11... | collective-permute-start | bytes 835592 | tf_op jit(solution)/shard_map/ppermute | solution.py:41
  21.7 10.8 %collective-permute-start.4 = (bf16[272,512]{1,0:T(8,128)(2,1)S(1)}, bf16[272,512]{1,0:T(8,128)(2,1)S(1)}, u32[]{:S(2)}, u32[]{:S(2)}) collective-permute-start(bf16[272,512]{1,0:T(8,128)(2,1)S(1)} %collective-permute-done.2.refs_1_), channel_id=1, source_target_pairs={{0,2},{1,7},{2,4},{3,1},{4,6},{5,3},{6,0},{7,5},{8,10},{9,15},{10,... | collective-permute-start | bytes 835592 | tf_op jit(solution)/shard_map/ppermute | solution.py:41
  25.2 11.3 %collective-permute-start.6 = (bf16[272,512]{1,0:T(8,128)(2,1)S(1)}, bf16[272,512]{1,0:T(8,128)(2,1)S(1)}, u32[]{:S(2)}, u32[]{:S(2)}) collective-permute-start(bf16[272,512]{1,0:T(8,128)(2,1)S(1)} %collective-permute-done.2.refs_1_), channel_id=1, source_target_pairs={{0,1},{1,0},{2,3},{3,2},{4,5},{5,4},{6,7},{7,6},{8,9},{9,8},{10,11... | collective-permute-start | bytes 835592 | tf_op jit(solution)/shard_map/ppermute | solution.py:41
  28.1 8.4 %collective-permute-start.7 = (bf16[272,512]{1,0:T(8,128)(2,1)S(1)}, bf16[272,512]{1,0:T(8,128)(2,1)S(1)}, u32[]{:S(2)}, u32[]{:S(2)}) collective-permute-start(bf16[272,512]{1,0:T(8,128)(2,1)S(1)} %collective-permute-done.3.refs_2_), channel_id=1, source_target_pairs={{0,1},{1,0},{2,3},{3,2},{4,5},{5,4},{6,7},{7,6},{8,9},{9,8},{10,11... | collective-permute-start | bytes 835592 | tf_op jit(solution)/shard_map/ppermute | solution.py:41
  33.1 4.6 %collective-permute-start.8 = (bf16[272,512]{1,0:T(8,128)(2,1)S(1)}, bf16[272,512]{1,0:T(8,128)(2,1)S(1)}, u32[]{:S(2)}, u32[]{:S(2)}) collective-permute-start(bf16[272,512]{1,0:T(8,128)(2,1)S(1)} %shard_map.86.refs_3_), channel_id=1, source_target_pairs={{0,1},{1,0},{2,3},{3,2},{4,5},{5,4},{6,7},{7,6},{8,9},{9,8},{10,11... | collective-permute-start | bytes 835592 | tf_op jit(solution)/shard_map/ppermute | solution.py:41
  40.1 23.9 %collective-permute-start.18 = (bf16[4,256,512]{2,1,0:T(8,128)(2,1)S(1)}, bf16[4,256,512]{2,1,0:T(8,128)(2,1)S(1)}, u32[]{:S(2)}, u32[]{:S(2)}) collective-permute-start(bf16[4,256,512]{2,1,0:T(8,128)(2,1)S(1)} %get-tuple-element.61), channel_id=1, source_target_pairs={{0,1},{1,0},{2,3},{3,2},{4,5},{5,4},{6,7},{7,6},{8,9},{9,8},{10,11... | collective-permute-start | bytes 3145736 | tf_op jit(solution)/shard_map/ppermute | solution.py:41
  40.6 9.3 %collective-permute-start.12 = (bf16[272,512]{1,0:T(8,128)(2,1)S(1)}, bf16[272,512]{1,0:T(8,128)(2,1)S(1)}, u32[]{:S(2)}, u32[]{:S(2)}) collective-permute-start(bf16[272,512]{1,0:T(8,128)(2,1)S(1)} %shard_map.87.refs_10_.refs_4_.refs_7_._), channel_id=1, source_target_pairs={{0,32},{1,225},{2,34},{3,227},{4,36},{5,229},{6,38},{7,231},{8,40}... | collective-permute-start | bytes 835592 | tf_op jit(solution)/shard_map/ppermute | solution.py:41
  41.3 8.6 %collective-permute-start.14 = (bf16[272,512]{1,0:T(8,128)(2,1)S(1)}, bf16[272,512]{1,0:T(8,128)(2,1)S(1)}, u32[]{:S(2)}, u32[]{:S(2)}) collective-permute-start(bf16[272,512]{1,0:T(8,128)(2,1)S(1)} %shard_map.87.refs_10_.refs_4_.refs_7_._), channel_id=1, source_target_pairs={{0,224},{1,33},{2,226},{3,35},{4,228},{5,37},{6,230},{7,39},{8,232... | collective-permute-start | bytes 835592 | tf_op jit(solution)/shard_map/ppermute | solution.py:41
  44.3 8.3 %collective-permute-start.10 = (bf16[272,256]{1,0:T(8,128)(2,1)S(1)}, bf16[272,256]{1,0:T(8,128)(2,1)S(1)}, u32[]{:S(2)}, u32[]{:S(2)}) collective-permute-start(bf16[272,256]{1,0:T(8,128)(2,1)S(1)} %shard_map.88.refs_0_.refs_1_), channel_id=1, source_target_pairs={{0,16},{1,17},{2,18},{3,19},{4,20},{5,21},{6,22},{7,23},{8,24},{9,... | collective-permute-start | bytes 417800 | tf_op jit(solution)/shard_map/ppermute | solution.py:41
  49.9 15.0 %collective-permute-start.13 = (bf16[272,512]{1,0:T(8,128)(2,1)S(1)}, bf16[272,512]{1,0:T(8,128)(2,1)S(1)}, u32[]{:S(2)}, u32[]{:S(2)}) collective-permute-start(bf16[272,512]{1,0:T(8,128)(2,1)S(1)} %collective-permute-done.12.refs_5_), channel_id=1, source_target_pairs={{0,32},{1,225},{2,34},{3,227},{4,36},{5,229},{6,38},{7,231},{8,40}... | collective-permute-start | bytes 835592 | tf_op jit(solution)/shard_map/ppermute | solution.py:41
  49.9 15.0 %collective-permute-start.15 = (bf16[272,512]{1,0:T(8,128)(2,1)S(1)}, bf16[272,512]{1,0:T(8,128)(2,1)S(1)}, u32[]{:S(2)}, u32[]{:S(2)}) collective-permute-start(bf16[272,512]{1,0:T(8,128)(2,1)S(1)} %collective-permute-done.14.refs_6_), channel_id=1, source_target_pairs={{0,224},{1,33},{2,226},{3,35},{4,228},{5,37},{6,230},{7,39},{8,232... | collective-permute-start | bytes 835592 | tf_op jit(solution)/shard_map/ppermute | solution.py:41
  52.6 5.6 %collective-permute-start.11 = (bf16[272,256]{1,0:T(8,128)(2,1)S(1)}, bf16[272,256]{1,0:T(8,128)(2,1)S(1)}, u32[]{:S(2)}, u32[]{:S(2)}) collective-permute-start(bf16[272,256]{1,0:T(8,128)(2,1)S(1)} %shard_map.88.refs_0_.refs_1_), channel_id=1, source_target_pairs={{0,24},{1,25},{2,26},{3,27},{4,28},{5,29},{6,30},{7,31},{8,0},{9,1... | collective-permute-start | bytes 417800 | tf_op jit(solution)/shard_map/ppermute | solution.py:41
  52.6 6.9 %collective-permute-start.9 = (bf16[272,256]{1,0:T(8,128)(2,1)S(1)}, bf16[272,256]{1,0:T(8,128)(2,1)S(1)}, u32[]{:S(2)}, u32[]{:S(2)}) collective-permute-start(bf16[272,256]{1,0:T(8,128)(2,1)S(1)} %shard_map.88.refs_0_.refs_1_), channel_id=1, source_target_pairs={{0,8},{1,9},{2,10},{3,11},{4,12},{5,13},{6,14},{7,15},{8,16},{9,17... | collective-permute-start | bytes 417800 | tf_op jit(solution)/shard_map/ppermute | solution.py:41
  64.8 14.7 %collective-permute-start.21 = (bf16[2,256,512]{2,1,0:T(8,128)(2,1)S(1)}, bf16[2,256,512]{2,1,0:T(8,128)(2,1)S(1)}, u32[]{:S(2)}, u32[]{:S(2)}) collective-permute-start(bf16[2,256,512]{2,1,0:T(8,128)(2,1)S(1)} %get-tuple-element.69), channel_id=1, source_target_pairs={{0,4},{1,5},{2,6},{3,7},{4,0},{5,1},{6,2},{7,3},{8,12},{9,13},{10,... | collective-permute-start | bytes 1572872 | tf_op jit(solution)/shard_map/ppermute | solution.py:41
  65.5 9.0 %collective-permute-start.16 = (bf16[272,512]{1,0:T(8,128)(2,1)S(1)}, bf16[272,512]{1,0:T(8,128)(2,1)S(1)}, u32[]{:S(2)}, u32[]{:S(2)}) collective-permute-start(bf16[272,512]{1,0:T(8,128)(2,1)S(1)} %get-tuple-element.58.refs_4_), channel_id=1, source_target_pairs={{0,32},{1,225},{2,34},{3,227},{4,36},{5,229},{6,38},{7,231},{8,40}... | collective-permute-start | bytes 835592 | tf_op jit(solution)/shard_map/ppermute | solution.py:41
  65.6 8.9 %collective-permute-start.17 = (bf16[272,512]{1,0:T(8,128)(2,1)S(1)}, bf16[272,512]{1,0:T(8,128)(2,1)S(1)}, u32[]{:S(2)}, u32[]{:S(2)}) collective-permute-start(bf16[272,512]{1,0:T(8,128)(2,1)S(1)} %get-tuple-element.59.refs_5_), channel_id=1, source_target_pairs={{0,224},{1,33},{2,226},{3,35},{4,228},{5,37},{6,230},{7,39},{8,232... | collective-permute-start | bytes 835592 | tf_op jit(solution)/shard_map/ppermute | solution.py:41
  68.2 20.1 %collective-permute-start.20 = (bf16[2,256,512]{2,1,0:T(8,128)(2,1)S(1)}, bf16[2,256,512]{2,1,0:T(8,128)(2,1)S(1)}, u32[]{:S(2)}, u32[]{:S(2)}) collective-permute-start(bf16[2,256,512]{2,1,0:T(8,128)(2,1)S(1)} %get-tuple-element.67), channel_id=1, source_target_pairs={{0,2},{1,7},{2,4},{3,1},{4,6},{5,3},{6,0},{7,5},{8,10},{9,15},{10,... | collective-permute-start | bytes 1572872 | tf_op jit(solution)/shard_map/ppermute | solution.py:41
  69.1 23.3 %collective-permute-start.25 = (bf16[2,256,512]{2,1,0:T(8,128)(2,1)S(1)}, bf16[2,256,512]{2,1,0:T(8,128)(2,1)S(1)}, u32[]{:S(2)}, u32[]{:S(2)}) collective-permute-start(bf16[2,256,512]{2,1,0:T(8,128)(2,1)S(1)} %get-tuple-element.80), channel_id=1, source_target_pairs={{0,6},{1,3},{2,0},{3,5},{4,2},{5,7},{6,4},{7,1},{8,14},{9,11},{10,... | collective-permute-start | bytes 1572872 | tf_op jit(solution)/shard_map/ppermute | solution.py:41
  75.0 7.2 %collective-permute-start.19 = (bf16[272,512]{1,0:T(8,128)(2,1)S(1)}, bf16[272,512]{1,0:T(8,128)(2,1)S(1)}, u32[]{:S(2)}, u32[]{:S(2)}) collective-permute-start(bf16[272,512]{1,0:T(8,128)(2,1)S(1)} %get-tuple-element.66.refs_4_), channel_id=1, source_target_pairs={{0,32},{1,225},{2,34},{3,227},{4,36},{5,229},{6,38},{7,231},{8,40}... | collective-permute-start | bytes 835592 | tf_op jit(solution)/shard_map/ppermute | solution.py:41
  91.0 5.6 %collective-permute-start.23 = (bf16[272,256]{1,0:T(8,128)(2,1)S(1)}, bf16[272,256]{1,0:T(8,128)(2,1)S(1)}, u32[]{:S(2)}, u32[]{:S(2)}) collective-permute-start(bf16[272,256]{1,0:T(8,128)(2,1)S(1)} %get-tuple-element.78), channel_id=1, source_target_pairs={{0,16},{1,17},{2,18},{3,19},{4,20},{5,21},{6,22},{7,23},{8,24},{9,... | collective-permute-start | bytes 417800 | tf_op jit(solution)/shard_map/ppermute | solution.py:41
  91.9 6.0 %collective-permute-start.24 = (bf16[272,256]{1,0:T(8,128)(2,1)S(1)}, bf16[272,256]{1,0:T(8,128)(2,1)S(1)}, u32[]{:S(2)}, u32[]{:S(2)}) collective-permute-start(bf16[272,256]{1,0:T(8,128)(2,1)S(1)} %get-tuple-element.79), channel_id=1, source_target_pairs={{0,8},{1,9},{2,10},{3,11},{4,12},{5,13},{6,14},{7,15},{8,16},{9,17... | collective-permute-start | bytes 417800 | tf_op jit(solution)/shard_map/ppermute | solution.py:41
  99.1 8.1 %collective-permute-start.26 = (bf16[272,256]{1,0:T(8,128)(2,1)S(1)}, bf16[272,256]{1,0:T(8,128)(2,1)S(1)}, u32[]{:S(2)}, u32[]{:S(2)}) collective-permute-start(bf16[272,256]{1,0:T(8,128)(2,1)S(1)} %shard_map.98.refs_0_), channel_id=1, source_target_pairs={{0,2},{1,7},{2,4},{3,1},{4,6},{5,3},{6,0},{7,5},{8,10},{9,15},{10,... | collective-permute-start | bytes 417800 | tf_op jit(solution)/shard_map/ppermute | solution.py:41
  105.1 6.0 %collective-permute-start.27 = (bf16[272,256]{1,0:T(8,128)(2,1)S(1)}, bf16[272,256]{1,0:T(8,128)(2,1)S(1)}, u32[]{:S(2)}, u32[]{:S(2)}) collective-permute-start(bf16[272,256]{1,0:T(8,128)(2,1)S(1)} %shard_map.98.refs_0_), channel_id=1, source_target_pairs={{0,6},{1,3},{2,0},{3,5},{4,2},{5,7},{6,4},{7,1},{8,14},{9,11},{10,... | collective-permute-start | bytes 417800 | tf_op jit(solution)/shard_map/ppermute | solution.py:41
  107.1 5.1 %collective-permute-start.28 = (bf16[272,256]{1,0:T(8,128)(2,1)S(1)}, bf16[272,256]{1,0:T(8,128)(2,1)S(1)}, u32[]{:S(2)}, u32[]{:S(2)}) collective-permute-start(bf16[272,256]{1,0:T(8,128)(2,1)S(1)} %collective-permute-done.26.refs_1_), channel_id=1, source_target_pairs={{0,2},{1,7},{2,4},{3,1},{4,6},{5,3},{6,0},{7,5},{8,10},{9,15},{10,... | collective-permute-start | bytes 417800 | tf_op jit(solution)/shard_map/ppermute | solution.py:41
  110.2 6.9 %collective-permute-start.29 = (bf16[272,256]{1,0:T(8,128)(2,1)S(1)}, bf16[272,256]{1,0:T(8,128)(2,1)S(1)}, u32[]{:S(2)}, u32[]{:S(2)}) collective-permute-start(bf16[272,256]{1,0:T(8,128)(2,1)S(1)} %shard_map.98.refs_0_), channel_id=1, source_target_pairs={{0,1},{1,0},{2,3},{3,2},{4,5},{5,4},{6,7},{7,6},{8,9},{9,8},{10,11... | collective-permute-start | bytes 417800 | tf_op jit(solution)/shard_map/ppermute | solution.py:41
  111.1 6.0 %collective-permute-start.30 = (bf16[272,256]{1,0:T(8,128)(2,1)S(1)}, bf16[272,256]{1,0:T(8,128)(2,1)S(1)}, u32[]{:S(2)}, u32[]{:S(2)}) collective-permute-start(bf16[272,256]{1,0:T(8,128)(2,1)S(1)} %collective-permute-done.26.refs_1_), channel_id=1, source_target_pairs={{0,1},{1,0},{2,3},{3,2},{4,5},{5,4},{6,7},{7,6},{8,9},{9,8},{10,11... | collective-permute-start | bytes 417800 | tf_op jit(solution)/shard_map/ppermute | solution.py:41
  111.1 6.0 %collective-permute-start.31 = (bf16[272,256]{1,0:T(8,128)(2,1)S(1)}, bf16[272,256]{1,0:T(8,128)(2,1)S(1)}, u32[]{:S(2)}, u32[]{:S(2)}) collective-permute-start(bf16[272,256]{1,0:T(8,128)(2,1)S(1)} %collective-permute-done.27.refs_2_), channel_id=1, source_target_pairs={{0,1},{1,0},{2,3},{3,2},{4,5},{5,4},{6,7},{7,6},{8,9},{9,8},{10,11... | collective-permute-start | bytes 417800 | tf_op jit(solution)/shard_map/ppermute | solution.py:41
  112.2 5.9 %collective-permute-start.32 = (bf16[272,256]{1,0:T(8,128)(2,1)S(1)}, bf16[272,256]{1,0:T(8,128)(2,1)S(1)}, u32[]{:S(2)}, u32[]{:S(2)}) collective-permute-start(bf16[272,256]{1,0:T(8,128)(2,1)S(1)} %collective-permute-done.28.refs_3_), channel_id=1, source_target_pairs={{0,1},{1,0},{2,3},{3,2},{4,5},{5,4},{6,7},{7,6},{8,9},{9,8},{10,11... | collective-permute-start | bytes 417800 | tf_op jit(solution)/shard_map/ppermute | solution.py:41
  (6 other events, 24.8 us)

commit v4 on v3

--- a/solution.py
+++ b/solution.py
@@ -309,8 +309,6 @@
     queries = [refs.pop(0) for _ in range(4)]
     own = refs.pop(0) if first else None
     others = [refs.pop(0) for _ in range(1 if final else 2)]
-    if not final:
-        refs = refs[1:]
     if not first:
         state_in = [refs.pop(0) for _ in range(2)]
     if final:
@@ -378,9 +376,9 @@
 STATE = [shape((4, 2, ROWS, 2 * HD), F32), shape((4, 2, ROWS, HD), F32), shape((8, 128), F32)]
 
 
-def attend_step(step, info, queries, own, others, state, ahead=None):
+def attend_step(step, info, queries, own, others, state):
     first, final = own is not None, len(others) == 1
-    ins = [info] + queries + ([own] if first else []) + others + ([] if final else [ahead]) + list(state or [])
+    ins = [info] + queries + ([own] if first else []) + others + list(state or [])
     flops = 4 * 1088 * SEG * (len(others) + (1 if first else 0)) * COLS
     body = functools.partial(attend_kernel, step, first, final)
     if final:
@@ -394,11 +392,10 @@
 
         return call(body, outs, ins, flops=flops, moved=4 << 20, aliases=aliases)[:4]
     aliases = {} if first else {len(ins) - 2: 0, len(ins) - 1: 1}
-    ignored = 5 + len(others) + (1 if first else 0)
-    return call(body, STATE, ins, flops=flops, moved=4 << 20, aliases=aliases, far_in=(ignored,))
-
-
-def merge_kernel(info, a, b, c, d, _, out):
+    return call(body, STATE, ins, flops=flops, moved=4 << 20, aliases=aliases)
+
+
+def merge_kernel(info, a, b, c, d, out):
     parts = (a, b, c, d)
     tails = [p[SEG:, :].astype(F32) for p in parts]
     weights, end_weights = [], []
@@ -427,76 +424,62 @@
 
 BLOCK = 512
 TALL = 384
-PAIR = (0, 1, 2, 3, 0, 2, 1, 3)
-
-
-def output_kernel(*refs):
-    attended, weights = refs[:8], refs[8:12]
-    means, ids, tokens, out, coarse = refs[12:]
-
+
+
+def mark_kernel(ids, out):
+    lane = iota((128, 128), 1)
+    for r in range(TOK // 128):
+        row = ids[r : r + 1, :].astype(F32)
+        column = jnp.transpose(jnp.broadcast_to(row, (128, 128))).astype(jnp.int32)
+        rows = slice(r * 128, (r + 1) * 128)
+        out[rows, :128] = ones_where(column == lane)
+        out[rows, 128:256] = ones_where(column == lane + 128)
+        out[rows, 256:] = ones_where((column == -1) & (lane == 0))
+
+
+def output_kernel(own, first, second, third, hot, tokens, out, coarse):
     @pl.when(pl.program_id(0) == 0)
     def _():
-        acc = means[...]
-        for i, a in enumerate(attended):
-            acc = acc + dot(a[...], weights[PAIR[i]][i // 4])
-        coarse[:ROWS, :] = acc.astype(BF16)
+        total = own[...] + first[...].astype(F32) + second[...].astype(F32) + third[...].astype(F32)
+        coarse[:ROWS, :] = total.astype(BF16)
         coarse[ROWS:, :] = jnp.zeros((TALL - ROWS, FEAT), BF16)
 
-    base = pl.multiple_of(pl.program_id(0) * (BLOCK // 128), BLOCK // 128)
-    lane = iota((128, 128), 1)
-    chunks = []
-    for r in range(BLOCK // 128):
-        row = ids[pl.ds(base + r, 1), :].astype(F32)
-        column = jnp.transpose(jnp.broadcast_to(row, (128, 128))).astype(jnp.int32)
-        chunks.append(
-            jnp.concatenate(
-                [
-                    ones_where(column == lane),
-                    ones_where(column == lane + 128),
-                    ones_where((column == -1) & (lane == 0)),
-                ],
-                axis=1,
-            )
-        )
-    hot = jnp.concatenate(chunks, axis=0)
-    picked = dot(hot, coarse[...])
+    picked = dot(hot[...], coarse[...])
     out[...] = (tokens[...].astype(F32) + picked).astype(BF16)
 
 
-def output(attended, weights, means, ids, tokens):
-    whole = [WHOLE] * 14
+def output(products, hot, tokens):
     return pl.pallas_call(
         output_kernel,
         grid=(TOK // BLOCK,),
         out_shape=shape((TOK, FEAT), BF16),
-        in_specs=whole + [pl.BlockSpec((BLOCK, FEAT), lambda i: (i, 0))],
+        in_specs=[WHOLE] * 4
+        + [pl.BlockSpec((BLOCK, TALL), lambda i: (i, 0)), pl.BlockSpec((BLOCK, FEAT), lambda i: (i, 0))],
         out_specs=pl.BlockSpec((BLOCK, FEAT), lambda i: (i, 0)),
         scratch_shapes=[pltpu.VMEM((TALL, FEAT), BF16)],
         compiler_params=pltpu.CompilerParams(vmem_limit_bytes=VMEM_LIMIT),
         cost_estimate=pl.CostEstimate(flops=2 << 30, bytes_accessed=6 << 20, transcendentals=0),
-    )(*attended, *weights, means, ids, tokens)
-
-
-def cut_kernel(info, w_out, _, mine, sibling, sems):
+    )(*products, hot, tokens)
+
+
+def cut_kernel(info, w_out, sibling, sems):
     copies = []
     for i in range(4):
-        for side, out in enumerate((mine, sibling)):
-            start = pl.multiple_of(info[I_CUT + 4 * side + i] * FEAT, FEAT)
-            copies.append(pltpu.make_async_copy(w_out.at[:, pl.ds(start, FEAT)], out.at[i], sems.at[side, i]))
-            copies[-1].start()
+        start = pl.multiple_of(info[I_CUT + 4 + i] * FEAT, FEAT)
+        copies.append(pltpu.make_async_copy(w_out.at[:, pl.ds(start, FEAT)], sibling.at[i], sems.at[i]))
+        copies[-1].start()
     for copy in copies:
         copy.wait()
 
 
-def pair_kernel(info, *refs):
-    sources, outs, sems = refs[:2], refs[3:7], refs[7]
-    copies = []
-    for i, out in enumerate(outs):
-        for side, source in enumerate(sources):
-            copies.append(pltpu.make_async_copy(source.at[i], out.at[side], sems.at[side, i]))
-            copies[-1].start()
-    for copy in copies:
-        copy.wait()
+def product_kernel(info, attended, other, w_out, theirs, means, own_out, *outs):
+    for i in range(4):
+        start = pl.multiple_of(info[I_CUT + i] * FEAT, FEAT)
+        part = dot(attended[...], w_out[:, pl.ds(start, FEAT)]) + dot(other[...], theirs[i])
+        if i == 0:
+            own_out[...] = part + means[...]
+        else:
+            outs[i - 1][...] = part.astype(BF16)
 
 
 def y_far(value):
@@ -562,40 +545,35 @@
     )
     queries = [query] + [x_by(query, k) for k in (1, 2, 3)]
     one, other = z_one(kv), z_other(kv)
-    cut = shape((4, SEG, FEAT), BF16)
-    sems = [pltpu.SemaphoreType.DMA((2, 4))]
-    mine, theirs = call(
-        cut_kernel, [cut, cut], [info, w_out, kv], scratch=sems, far_in=(1, 2), far_out=(0, 1)
+    (theirs,) = call(
+        cut_kernel,
+        [shape((4, SEG, FEAT), BF16)],
+        [info, w_out],
+        scratch=[pltpu.SemaphoreType.DMA((4,))],
+        far_in=(1,),
+        far_out=(0,),
     )
     theirs = swap(theirs)
     one2, other2 = z_one(one), z_other(other)
-    *state, done = attend_step(1, info, queries, kv, [one, other], None, kv)
-    pair = shape((2, SEG, FEAT), BF16)
-    pairs = call(
-        pair_kernel,
-        [pair] * 4,
-        [info, mine, theirs, done],
-        scratch=sems,
-        far_in=range(1, 4),
-        far_out=range(4),
-    )
-    far_weights = y_far(pairs[3])
-    one2, other2 = gate(info, [one2, other2], done)
+    *state, done = attend_step(1, info, queries, kv, [one, other], None)
     one3, other3 = z_one(one2), z_other(other2)
-    one_weights = y_one(pairs[1])
-    *state, done = attend_step(2, info, queries, None, [one2, other2], state, pairs[0])
+    *state, done = attend_step(2, info, queries, None, [one2, other2], state)
     one3, other3 = gate(info, [one3, other3], done)
     one4 = z_one(one3)
-    other_weights = y_other(pairs[2])
-    *state, done = attend_step(3, info, queries, None, [one3, other3], state, far_weights)
-    one4, one_weights = gate(info, [one4, one_weights], done)
+    *state, done = attend_step(3, info, queries, None, [one3, other3], state)
     partial = attend_step(4, info, queries, None, [one4], state)
-    weights = [pairs[0], one_weights, other_weights, far_weights]
     partial = [partial[0]] + [x_by(partial[k], -k) for k in (1, 2, 3)]
-    (attended,) = call(
-        merge_kernel, [shape((ROWS, COLS), BF16)], [info] + partial + [other_weights], moved=1 << 20, far_in=(5,)
-    )
-    return output(mp_exchange(attended), weights, means, ids, tokens)
+    (attended,) = call(merge_kernel, [shape((ROWS, COLS), BF16)], [info] + partial, moved=1 << 20)
+    block = shape((ROWS, FEAT), BF16)
+    own, first, second, third = call(
+        product_kernel,
+        [shape((ROWS, FEAT), F32)] + [block] * 3,
+        [info, attended, swap(attended), w_out, theirs, means],
+        flops=2 * ROWS * 2 * COLS * 4 * FEAT,
+        moved=4 << 20,
+    )
+    (hot,) = call(mark_kernel, [shape((TOK, TALL), BF16)], [ids], flops=1 << 29, moved=3 << 20, scalars=None)
+    return output([own, y_one(first), y_other(second), y_far(third)], hot, tokens)
 
 
 def solution(mesh):

time: 122 us -> 118 us (0.967)
  the two profiles are of different devices: /device:TPU:225 before, /device:TPU:2 now
where the time goes in v4:
time: 118 us; the launch traced here: 116 us
  waiting for transfers between devices  52.6 us (45%)
  starting transfers between devices  38.3 us (32%)
  Pallas kernels  22 us (19%)
  local copies, waits for them, and re-layouts  3 us (3%)
    ppermute x25, waiting for transfers between devices, move(): return lax.ppermute(value, ('seq', 'mp'), pairs)  50.6 us
    ppermute x25, starting transfers between devices, move(): return lax.ppermute(value, ('seq', 'mp'), pairs)  32.1 us
    pallas_call x16, Pallas kernels, call(): pl.pallas_call(body, out_shape=outs, in_specs=[SMEM if i == scalars else...  18.9 us
    ppermute x1, starting transfers between devices, shards(): above = lax.ppermute(head, 'seq', [(i, i - 1) for i in range(1, count)])  4.31 us
    pallas_call x1, Pallas kernels, output(): pl.pallas_call(output_kernel, grid=(TOK // BLOCK,), out_shape=shape((TOK,...  3.06 us
  transfers between devices with their start and end apart: 27, of which 14 were waited for; matrix products, arithmetic and copies ran while one was open for 1% of the time, Pallas kernels for 13%

profile of v4, /device:TPU:2, one launch (start us, length us, event | category | flops | bytes accessed | tf_op | source)
XLA Modules:
  0.0 116.2 jit_solution(8394254753053699118)
XLA Ops:
  0.0 1.6 %copy-done.1 = bf16[2048,512]{1,0:T(8,128)(2,1)S(1)} copy-done((bf16[2048,512]{1,0:T(8,128)(2,1)S(1)}, bf16[2048,512]{1,0:T(8,128)(2,1)}, u32[]{:S(2)}) %copy-start.1) | copy-done | bytes 2097176
  3.0 4.3 %collective-permute-start = (f32[8,640]{1,0:T(8,128)S(1)}, f32[8,640]{1,0:T(8,128)S(1)}, u32[]{:S(2)}, u32[]{:S(2)}) collective-permute-start(f32[8,640]{1,0:T(8,128)S(1)} %get-tuple-element.39.head), channel_id=1, source_target_pairs={{8,0},{16,8},{24,16},{32,24},{40,32},{48,40},{56,48},{64,56},{72,6... | collective-permute-start | bytes 61448 | tf_op jit(solution)/shard_map/ppermute | solution.py:503
  7.3 1.9 %collective-permute-start.1 = (f32[8,640]{1,0:T(8,128)S(1)}, f32[8,640]{1,0:T(8,128)S(1)}, u32[]{:S(2)}, u32[]{:S(2)}) collective-permute-start(f32[8,640]{1,0:T(8,128)S(1)} %get-tuple-element.40), channel_id=1, source_target_pairs={{0,8},{8,16},{16,24},{24,32},{32,40},{40,48},{48,56},{56,64},{64,7... | collective-permute-start | bytes 61448 | tf_op jit(solution)/shard_map/ppermute | solution.py:504
  11.0 2.0 %collective-permute-done.1.below = f32[8,640]{1,0:T(8,128)S(1)} collective-permute-done((f32[8,640]{1,0:T(8,128)S(1)}, f32[8,640]{1,0:T(8,128)S(1)}, u32[]{:S(2)}, u32[]{:S(2)}) %collective-permute-start.1) | collective-permute-done | bytes 20512 | tf_op jit(solution)/shard_map/ppermute | solution.py:504
  13.9 3.2 %collective-permute-start.3 = (bf16[272,512]{1,0:T(8,128)(2,1)S(1)}, bf16[272,512]{1,0:T(8,128)(2,1)S(1)}, u32[]{:S(2)}, u32[]{:S(2)}) collective-permute-start(bf16[272,512]{1,0:T(8,128)(2,1)S(1)} %get-tuple-element.41.refs_0_), channel_id=1, source_target_pairs={{0,6},{1,3},{2,0},{3,5},{4,2},{5,7},{6,4},{7,1},{8,14},{9,11},{10,... | collective-permute-start | bytes 835592 | tf_op jit(solution)/shard_map/ppermute | solution.py:41
  17.1 6.3 %collective-permute-done.2.refs_1_ = bf16[272,512]{1,0:T(8,128)(2,1)S(1)} collective-permute-done((bf16[272,512]{1,0:T(8,128)(2,1)S(1)}, bf16[272,512]{1,0:T(8,128)(2,1)S(1)}, u32[]{:S(2)}, u32[]{:S(2)}) %collective-permute-start.2) | collective-permute-done | bytes 278560 | tf_op jit(solution)/shard_map/ppermute | solution.py:41
  23.9 4.3 %shard_map.85 = (f32[272,256]{1,0:T(8,128)S(1)}, f32[256,256]{1,0:T(8,128)S(1)}, f32[256,256]{1,0:T(8,128)S(1)}, bf16[4,512,256]{2,1,0:T(8,128)(2,1)S(1)}, bf16[...) custom-call(s32[32]{0:T(128)S(1)} %dynamic-slice_bitcast_fusion.info.refs_0_, ...), custom_call_target="tpu_custom_call" | custom-call | flops 855638016 | bytes 6291456 | tf_op jit(solution)/shard_map/pallas_call | solution.py:105
  28.2 3.0 %collective-permute-done.4.refs_0_ = bf16[272,512]{1,0:T(8,128)(2,1)S(1)} collective-permute-done((bf16[272,512]{1,0:T(8,128)(2,1)S(1)}, bf16[272,512]{1,0:T(8,128)(2,1)S(1)}, u32[]{:S(2)}, u32[]{:S(2)}) %collective-permute-start.4) | collective-permute-done | bytes 278560 | tf_op jit(solution)/shard_map/ppermute | solution.py:41
  31.8 1.5 %collective-permute-done.8.refs_7_ = bf16[272,512]{1,0:T(8,128)(2,1)S(1)} collective-permute-done((bf16[272,512]{1,0:T(8,128)(2,1)S(1)}, bf16[272,512]{1,0:T(8,128)(2,1)S(1)}, u32[]{:S(2)}, u32[]{:S(2)}) %collective-permute-start.8) | collective-permute-done | bytes 278560 | tf_op jit(solution)/shard_map/ppermute | solution.py:41
  33.3 1.2 %shard_map.87.refs_10_.refs_4_ = bf16[272,512]{1,0:T(8,128)(2,1)S(1)} custom-call(s32[32]{0:T(128)S(1)} %dynamic-slice_bitcast_fusion.info.refs_0_, bf16[272,512]{1,0:T(8,128)(2,1)S(1)} %get-tuple-element.41.refs_0_, bf16[272,512]{1,0:T(8,128)(2,1)S(1)} %collective-permute-done.2.refs_1_, bf16[272,512]{1,0:T(8,128)(2,1)S(1)} %collective-permute-done.3.refs_2_, ...), custom_call_target="tpu_custom_call" | custom-call | tf_op jit(solution)/shard_map/pallas_call | solution.py:105
  34.6 1.4 %collective-permute-start.12 = (bf16[272,512]{1,0:T(8,128)(2,1)S(1)}, bf16[272,512]{1,0:T(8,128)(2,1)S(1)}, u32[]{:S(2)}, u32[]{:S(2)}) collective-permute-start(bf16[272,512]{1,0:T(8,128)(2,1)S(1)} %shard_map.87.refs_10_.refs_4_), channel_id=1, source_target_pairs={{0,32},{1,225},{2,34},{3,227},{4,36},{5,229},{6,38},{7,231},{8,40}... | collective-permute-start | bytes 835592 | tf_op jit(solution)/shard_map/ppermute | solution.py:41
  36.0 4.9 %collective-permute-start.15 = (bf16[272,512]{1,0:T(8,128)(2,1)S(1)}, bf16[272,512]{1,0:T(8,128)(2,1)S(1)}, u32[]{:S(2)}, u32[]{:S(2)}) collective-permute-start(bf16[272,512]{1,0:T(8,128)(2,1)S(1)} %shard_map.87.refs_10_.refs_4_), channel_id=1, source_target_pairs={{0,224},{1,33},{2,226},{3,35},{4,228},{5,37},{6,230},{7,39},{8,232... | collective-permute-start | bytes 835592 | tf_op jit(solution)/shard_map/ppermute | solution.py:41
  40.9 5.2 %collective-permute-done.12.refs_5_ = bf16[272,512]{1,0:T(8,128)(2,1)S(1)} collective-permute-done((bf16[272,512]{1,0:T(8,128)(2,1)S(1)}, bf16[272,512]{1,0:T(8,128)(2,1)S(1)}, u32[]{:S(2)}, u32[]{:S(2)}) %collective-permute-start.12) | collective-permute-done | bytes 278560 | tf_op jit(solution)/shard_map/ppermute | solution.py:41
  47.0 3.7 %collective-permute-start.16 = (bf16[272,512]{1,0:T(8,128)(2,1)S(1)}, bf16[272,512]{1,0:T(8,128)(2,1)S(1)}, u32[]{:S(2)}, u32[]{:S(2)}) collective-permute-start(bf16[272,512]{1,0:T(8,128)(2,1)S(1)} %collective-permute-done.15.refs_6_), channel_id=1, source_target_pairs={{0,224},{1,33},{2,226},{3,35},{4,228},{5,37},{6,230},{7,39},{8,232... | collective-permute-start | bytes 835592 | tf_op jit(solution)/shard_map/ppermute | solution.py:41
  52.5 1.7 %collective-permute-start.10 = (bf16[272,256]{1,0:T(8,128)(2,1)S(1)}, bf16[272,256]{1,0:T(8,128)(2,1)S(1)}, u32[]{:S(2)}, u32[]{:S(2)}) collective-permute-start(bf16[272,256]{1,0:T(8,128)(2,1)S(1)} %shard_map.88.refs_0_.refs_1_), channel_id=1, source_target_pairs={{0,16},{1,17},{2,18},{3,19},{4,20},{5,21},{6,22},{7,23},{8,24},{9,... | collective-permute-start | bytes 417800 | tf_op jit(solution)/shard_map/ppermute | solution.py:41
  54.2 1.8 %collective-permute-done.13.refs_4_ = bf16[272,512]{1,0:T(8,128)(2,1)S(1)} collective-permute-done((bf16[272,512]{1,0:T(8,128)(2,1)S(1)}, bf16[272,512]{1,0:T(8,128)(2,1)S(1)}, u32[]{:S(2)}, u32[]{:S(2)}) %collective-permute-start.13) | collective-permute-done | bytes 278560 | tf_op jit(solution)/shard_map/ppermute | solution.py:41
  56.0 3.7 %collective-permute-start.17 = (bf16[272,512]{1,0:T(8,128)(2,1)S(1)}, bf16[272,512]{1,0:T(8,128)(2,1)S(1)}, u32[]{:S(2)}, u32[]{:S(2)}) collective-permute-start(bf16[272,512]{1,0:T(8,128)(2,1)S(1)} %collective-permute-done.16.refs_5_), channel_id=1, source_target_pairs={{0,224},{1,33},{2,226},{3,35},{4,228},{5,37},{6,230},{7,39},{8,232... | collective-permute-start | bytes 835592 | tf_op jit(solution)/shard_map/ppermute | solution.py:41
  59.7 4.3 %collective-permute-start.11 = (bf16[272,256]{1,0:T(8,128)(2,1)S(1)}, bf16[272,256]{1,0:T(8,128)(2,1)S(1)}, u32[]{:S(2)}, u32[]{:S(2)}) collective-permute-start(bf16[272,256]{1,0:T(8,128)(2,1)S(1)} %shard_map.88.refs_0_.refs_1_), channel_id=1, source_target_pairs={{0,24},{1,25},{2,26},{3,27},{4,28},{5,29},{6,30},{7,31},{8,0},{9,1... | collective-permute-start | bytes 417800 | tf_op jit(solution)/shard_map/ppermute | solution.py:41
  64.0 2.6 %collective-permute-done.11.refs_3_.refs_4_ = bf16[272,256]{1,0:T(8,128)(2,1)S(1)} collective-permute-done((bf16[272,256]{1,0:T(8,128)(2,1)S(1)}, bf16[272,256]{1,0:T(8,128)(2,1)S(1)}, u32[]{:S(2)}, u32[]{:S(2)}) %collective-permute-start.11) | collective-permute-done | bytes 139296 | tf_op jit(solution)/shard_map/ppermute | solution.py:41
  66.6 2.5 %collective-permute-done.9.refs_1_.refs_2_ = bf16[272,256]{1,0:T(8,128)(2,1)S(1)} collective-permute-done((bf16[272,256]{1,0:T(8,128)(2,1)S(1)}, bf16[272,256]{1,0:T(8,128)(2,1)S(1)}, u32[]{:S(2)}, u32[]{:S(2)}) %collective-permute-start.9) | collective-permute-done | bytes 139296 | tf_op jit(solution)/shard_map/ppermute | solution.py:41
  69.1 2.7 %shard_map.89 = (f32[4,2,272,256]{3,2,1,0:T(8,128)S(1)}, f32[4,2,272,128]{3,2,1,0:T(8,128)S(1)}, f32[8,128]{1,0:T(8,128)}) custom-call(s32[32]{0:T(128)S(1)} %dynamic-slice_bitcast_fusion.info.refs_0_, bf16[272,256]{1,0:T(8,128)(2,1)S(1)} %shard_map.88.refs_0_.refs_1_, bf16[272,256]{1,0:T(8,128)(2,1)S(1)} %collective-permute-done.9.refs_1_.refs_2_, ...), custom_call_target="tpu_custom_call" | custom-call | flops 855638016 | bytes 4194304 | tf_op jit(solution)/shard_map/pallas_call | solution.py:105
  73.3 1.1 shard_map.92
  74.5 8.2 %collective-permute-done.18.refs_5_ = bf16[272,512]{1,0:T(8,128)(2,1)S(1)} collective-permute-done((bf16[272,512]{1,0:T(8,128)(2,1)S(1)}, bf16[272,512]{1,0:T(8,128)(2,1)S(1)}, u32[]{:S(2)}, u32[]{:S(2)}) %collective-permute-start.18) | collective-permute-done | bytes 278560 | tf_op jit(solution)/shard_map/ppermute | solution.py:41
  83.6 3.0 %collective-permute-start.19 = (bf16[272,256]{1,0:T(8,128)(2,1)S(1)}, bf16[272,256]{1,0:T(8,128)(2,1)S(1)}, u32[]{:S(2)}, u32[]{:S(2)}) collective-permute-start(bf16[272,256]{1,0:T(8,128)(2,1)S(1)} %get-tuple-element.59), channel_id=1, source_target_pairs={{0,24},{1,25},{2,26},{3,27},{4,28},{5,29},{6,30},{7,31},{8,0},{9,1... | collective-permute-start | bytes 417800 | tf_op jit(solution)/shard_map/ppermute | solution.py:41
  86.7 1.6 %collective-permute-start.21 = (bf16[272,256]{1,0:T(8,128)(2,1)S(1)}, bf16[272,256]{1,0:T(8,128)(2,1)S(1)}, u32[]{:S(2)}, u32[]{:S(2)}) collective-permute-start(bf16[272,256]{1,0:T(8,128)(2,1)S(1)} %get-tuple-element.61), channel_id=1, source_target_pairs={{0,8},{1,9},{2,10},{3,11},{4,12},{5,13},{6,14},{7,15},{8,16},{9,17... | collective-permute-start | bytes 417800 | tf_op jit(solution)/shard_map/ppermute | solution.py:41
  88.2 2.3 %collective-permute-done.19.b = bf16[272,256]{1,0:T(8,128)(2,1)S(1)} collective-permute-done((bf16[272,256]{1,0:T(8,128)(2,1)S(1)}, bf16[272,256]{1,0:T(8,128)(2,1)S(1)}, u32[]{:S(2)}, u32[]{:S(2)}) %collective-permute-start.19) | collective-permute-done | bytes 139296 | tf_op jit(solution)/shard_map/ppermute | solution.py:41
  90.5 2.7 %collective-permute-done.20.c = bf16[272,256]{1,0:T(8,128)(2,1)S(1)} collective-permute-done((bf16[272,256]{1,0:T(8,128)(2,1)S(1)}, bf16[272,256]{1,0:T(8,128)(2,1)S(1)}, u32[]{:S(2)}, u32[]{:S(2)}) %collective-permute-start.20) | collective-permute-done | bytes 139296 | tf_op jit(solution)/shard_map/ppermute | solution.py:41
  94.4 1.3 %collective-permute-done.22.other = bf16[272,256]{1,0:T(8,128)(2,1)S(1)} collective-permute-done((bf16[272,256]{1,0:T(8,128)(2,1)S(1)}, bf16[272,256]{1,0:T(8,128)(2,1)S(1)}, u32[]{:S(2)}, u32[]{:S(2)}) %collective-permute-start.22) | collective-permute-done | bytes 139296 | tf_op jit(solution)/shard_map/ppermute | solution.py:41
  95.8 1.3 %shard_map.96 = (f32[272,512]{1,0:T(8,128)S(1)}, bf16[272,512]{1,0:T(8,128)(2,1)S(1)}, bf16[272,512]{1,0:T(8,128)(2,1)S(1)}, bf16[272,512]{1,0:T(8,128)(2,1)S(1)}) custom-call(s32[32]{0:T(128)S(1)} %dynamic-slice_bitcast_fusion.info.refs_0_, bf16[272,256]{1,0:T(8,128)(2,1)S(1)} %shard_map.94.attended, bf16[272,256]{1,0:T(8,128)(2,1)S(1)} %collective-permute-done.22.other, ...), custom_call_target="tpu_custom_call" | custom-call | flops 570425344 | bytes 4194304 | tf_op jit(solution)/shard_map/pallas_call | solution.py:105
  97.2 3.2 %collective-permute-start.25 = (bf16[272,512]{1,0:T(8,128)(2,1)S(1)}, bf16[272,512]{1,0:T(8,128)(2,1)S(1)}, u32[]{:S(2)}, u32[]{:S(2)}) collective-permute-start(bf16[272,512]{1,0:T(8,128)(2,1)S(1)} %get-tuple-element.65), channel_id=1, source_target_pairs={{0,6},{1,3},{2,0},{3,5},{4,2},{5,7},{6,4},{7,1},{8,14},{9,11},{10,... | collective-permute-start | bytes 835592 | tf_op jit(solution)/shard_map/ppermute | solution.py:41
  100.8 12.3 %collective-permute-done.24.first = bf16[272,512]{1,0:T(8,128)(2,1)S(1)} collective-permute-done((bf16[272,512]{1,0:T(8,128)(2,1)S(1)}, bf16[272,512]{1,0:T(8,128)(2,1)S(1)}, u32[]{:S(2)}, u32[]{:S(2)}) %collective-permute-start.24) | collective-permute-done | bytes 278560 | tf_op jit(solution)/shard_map/ppermute | solution.py:41
  113.1 3.1 %shard_map.98 = bf16[2048,512]{1,0:T(8,128)(2,1)} custom-call(f32[272,512]{1,0:T(8,128)S(1)} %get-tuple-element.63.own, bf16[272,512]{1,0:T(8,128)(2,1)S(1)} %collective-permute-done.24.first, bf16[272,512]{1,0:T(8,128)(2,1)S(1)} %collective-permute-done.25.second, bf16[272,512]{1,0:T(8,128)(2,1)S(1)} %collective-permute-done.26.third, ...), custom_call_target="tpu_custom_call" | custom-call | flops 2147483648 | bytes 6291456 | tf_op jit(solution)/shard_map/pallas_call | solution.py:452
  (51 shorter events, 12.0 us)
Async XLA Ops:
  0.0 1.6 %copy-start.1 = (bf16[2048,512]{1,0:T(8,128)(2,1)S(1)}, bf16[2048,512]{1,0:T(8,128)(2,1)}, u32[]{:S(2)}) copy-start(bf16[2048,512]{1,0:T(8,128)(2,1)} %tokens.5) | copy-start | bytes 6291460
  1.6 0.7 copy-start.3
  2.3 7.7 %copy-start.2 = (bf16[2048,512]{1,0:T(8,128)(2,1)S(1)}, bf16[2048,512]{1,0:T(8,128)(2,1)}, u32[]{:S(2)}) copy-start(bf16[2048,512]{1,0:T(8,128)(2,1)} %tokens.5) | copy-start | bytes 6291460
  3.0 8.0 %copy-start.4 = (f32[4096]{0:T(1024)S(1)}, f32[4096]{0:T(1024)}, u32[]{:S(2)}) copy-start(f32[4096]{0:T(1024)} %param.10) | copy-start | bytes 49156
  3.0 8.0 %collective-permute-start = (f32[8,640]{1,0:T(8,128)S(1)}, f32[8,640]{1,0:T(8,128)S(1)}, u32[]{:S(2)}, u32[]{:S(2)}) collective-permute-start(f32[8,640]{1,0:T(8,128)S(1)} %get-tuple-element.39.head), channel_id=1, source_target_pairs={{8,0},{16,8},{24,16},{32,24},{40,32},{48,40},{56,48},{64,56},{72,6... | collective-permute-start | bytes 61448 | tf_op jit(solution)/shard_map/ppermute | solution.py:503
  7.3 5.7 %collective-permute-start.1 = (f32[8,640]{1,0:T(8,128)S(1)}, f32[8,640]{1,0:T(8,128)S(1)}, u32[]{:S(2)}, u32[]{:S(2)}) collective-permute-start(f32[8,640]{1,0:T(8,128)S(1)} %get-tuple-element.40), channel_id=1, source_target_pairs={{0,8},{8,16},{16,24},{24,32},{32,40},{40,48},{48,56},{56,64},{64,7... | collective-permute-start | bytes 61448 | tf_op jit(solution)/shard_map/ppermute | solution.py:504
  13.8 9.6 %collective-permute-start.2 = (bf16[272,512]{1,0:T(8,128)(2,1)S(1)}, bf16[272,512]{1,0:T(8,128)(2,1)S(1)}, u32[]{:S(2)}, u32[]{:S(2)}) collective-permute-start(bf16[272,512]{1,0:T(8,128)(2,1)S(1)} %get-tuple-element.41.refs_0_), channel_id=1, source_target_pairs={{0,2},{1,7},{2,4},{3,1},{4,6},{5,3},{6,0},{7,5},{8,10},{9,15},{10,... | collective-permute-start | bytes 835592 | tf_op jit(solution)/shard_map/ppermute | solution.py:41
  13.9 9.5 %collective-permute-start.3 = (bf16[272,512]{1,0:T(8,128)(2,1)S(1)}, bf16[272,512]{1,0:T(8,128)(2,1)S(1)}, u32[]{:S(2)}, u32[]{:S(2)}) collective-permute-start(bf16[272,512]{1,0:T(8,128)(2,1)S(1)} %get-tuple-element.41.refs_0_), channel_id=1, source_target_pairs={{0,6},{1,3},{2,0},{3,5},{4,2},{5,7},{6,4},{7,1},{8,14},{9,11},{10,... | collective-permute-start | bytes 835592 | tf_op jit(solution)/shard_map/ppermute | solution.py:41
  17.1 6.8 %collective-permute-start.5 = (bf16[272,512]{1,0:T(8,128)(2,1)S(1)}, bf16[272,512]{1,0:T(8,128)(2,1)S(1)}, u32[]{:S(2)}, u32[]{:S(2)}) collective-permute-start(bf16[272,512]{1,0:T(8,128)(2,1)S(1)} %get-tuple-element.41.refs_0_), channel_id=1, source_target_pairs={{0,1},{1,0},{2,3},{3,2},{4,5},{5,4},{6,7},{7,6},{8,9},{9,8},{10,11... | collective-permute-start | bytes 835592 | tf_op jit(solution)/shard_map/ppermute | solution.py:41
  23.4 7.8 %collective-permute-start.4 = (bf16[272,512]{1,0:T(8,128)(2,1)S(1)}, bf16[272,512]{1,0:T(8,128)(2,1)S(1)}, u32[]{:S(2)}, u32[]{:S(2)}) collective-permute-start(bf16[272,512]{1,0:T(8,128)(2,1)S(1)} %collective-permute-done.2.refs_1_), channel_id=1, source_target_pairs={{0,2},{1,7},{2,4},{3,1},{4,6},{5,3},{6,0},{7,5},{8,10},{9,15},{10,... | collective-permute-start | bytes 835592 | tf_op jit(solution)/shard_map/ppermute | solution.py:41
  23.4 8.4 %collective-permute-start.6 = (bf16[272,512]{1,0:T(8,128)(2,1)S(1)}, bf16[272,512]{1,0:T(8,128)(2,1)S(1)}, u32[]{:S(2)}, u32[]{:S(2)}) collective-permute-start(bf16[272,512]{1,0:T(8,128)(2,1)S(1)} %collective-permute-done.2.refs_1_), channel_id=1, source_target_pairs={{0,1},{1,0},{2,3},{3,2},{4,5},{5,4},{6,7},{7,6},{8,9},{9,8},{10,11... | collective-permute-start | bytes 835592 | tf_op jit(solution)/shard_map/ppermute | solution.py:41
  23.4 8.4 %collective-permute-start.7 = (bf16[272,512]{1,0:T(8,128)(2,1)S(1)}, bf16[272,512]{1,0:T(8,128)(2,1)S(1)}, u32[]{:S(2)}, u32[]{:S(2)}) collective-permute-start(bf16[272,512]{1,0:T(8,128)(2,1)S(1)} %collective-permute-done.3.refs_2_), channel_id=1, source_target_pairs={{0,1},{1,0},{2,3},{3,2},{4,5},{5,4},{6,7},{7,6},{8,9},{9,8},{10,11... | collective-permute-start | bytes 835592 | tf_op jit(solution)/shard_map/ppermute | solution.py:41
  31.7 1.6 %collective-permute-start.8 = (bf16[272,512]{1,0:T(8,128)(2,1)S(1)}, bf16[272,512]{1,0:T(8,128)(2,1)S(1)}, u32[]{:S(2)}, u32[]{:S(2)}) collective-permute-start(bf16[272,512]{1,0:T(8,128)(2,1)S(1)} %shard_map.86.refs_3_), channel_id=1, source_target_pairs={{0,1},{1,0},{2,3},{3,2},{4,5},{5,4},{6,7},{7,6},{8,9},{9,8},{10,11... | collective-permute-start | bytes 835592 | tf_op jit(solution)/shard_map/ppermute | solution.py:41
  33.3 17.4 %copy-start = (bf16[256,4096]{1,0:T(8,128)(2,1)S(1)}, bf16[256,4096]{1,0:T(8,128)(2,1)}, u32[]{:S(2)}) copy-start(bf16[256,4096]{1,0:T(8,128)(2,1)} %w_out.3) | copy-start | bytes 6291460
  34.6 11.5 %collective-permute-start.12 = (bf16[272,512]{1,0:T(8,128)(2,1)S(1)}, bf16[272,512]{1,0:T(8,128)(2,1)S(1)}, u32[]{:S(2)}, u32[]{:S(2)}) collective-permute-start(bf16[272,512]{1,0:T(8,128)(2,1)S(1)} %shard_map.87.refs_10_.refs_4_), channel_id=1, source_target_pairs={{0,32},{1,225},{2,34},{3,227},{4,36},{5,229},{6,38},{7,231},{8,40}... | collective-permute-start | bytes 835592 | tf_op jit(solution)/shard_map/ppermute | solution.py:41
  36.0 11.1 %collective-permute-start.15 = (bf16[272,512]{1,0:T(8,128)(2,1)S(1)}, bf16[272,512]{1,0:T(8,128)(2,1)S(1)}, u32[]{:S(2)}, u32[]{:S(2)}) collective-permute-start(bf16[272,512]{1,0:T(8,128)(2,1)S(1)} %shard_map.87.refs_10_.refs_4_), channel_id=1, source_target_pairs={{0,224},{1,33},{2,226},{3,35},{4,228},{5,37},{6,230},{7,39},{8,232... | collective-permute-start | bytes 835592 | tf_op jit(solution)/shard_map/ppermute | solution.py:41
  46.1 9.9 %collective-permute-start.13 = (bf16[272,512]{1,0:T(8,128)(2,1)S(1)}, bf16[272,512]{1,0:T(8,128)(2,1)S(1)}, u32[]{:S(2)}, u32[]{:S(2)}) collective-permute-start(bf16[272,512]{1,0:T(8,128)(2,1)S(1)} %collective-permute-done.12.refs_5_), channel_id=1, source_target_pairs={{0,32},{1,225},{2,34},{3,227},{4,36},{5,229},{6,38},{7,231},{8,40}... | collective-permute-start | bytes 835592 | tf_op jit(solution)/shard_map/ppermute | solution.py:41
  47.0 9.0 %collective-permute-start.16 = (bf16[272,512]{1,0:T(8,128)(2,1)S(1)}, bf16[272,512]{1,0:T(8,128)(2,1)S(1)}, u32[]{:S(2)}, u32[]{:S(2)}) collective-permute-start(bf16[272,512]{1,0:T(8,128)(2,1)S(1)} %collective-permute-done.15.refs_6_), channel_id=1, source_target_pairs={{0,224},{1,33},{2,226},{3,35},{4,228},{5,37},{6,230},{7,39},{8,232... | collective-permute-start | bytes 835592 | tf_op jit(solution)/shard_map/ppermute | solution.py:41
  51.4 43.0 %collective-permute-start.23 = (bf16[4,256,512]{2,1,0:T(8,128)(2,1)S(1)}, bf16[4,256,512]{2,1,0:T(8,128)(2,1)S(1)}, u32[]{:S(2)}, u32[]{:S(2)}) collective-permute-start(bf16[4,256,512]{2,1,0:T(8,128)(2,1)S(1)} %shard_map.95), channel_id=1, source_target_pairs={{0,1},{1,0},{2,3},{3,2},{4,5},{5,4},{6,7},{7,6},{8,9},{9,8},{10,11... | collective-permute-start | bytes 3145736 | tf_op jit(solution)/shard_map/ppermute | solution.py:41
  52.5 11.5 %collective-permute-start.10 = (bf16[272,256]{1,0:T(8,128)(2,1)S(1)}, bf16[272,256]{1,0:T(8,128)(2,1)S(1)}, u32[]{:S(2)}, u32[]{:S(2)}) collective-permute-start(bf16[272,256]{1,0:T(8,128)(2,1)S(1)} %shard_map.88.refs_0_.refs_1_), channel_id=1, source_target_pairs={{0,16},{1,17},{2,18},{3,19},{4,20},{5,21},{6,22},{7,23},{8,24},{9,... | collective-permute-start | bytes 417800 | tf_op jit(solution)/shard_map/ppermute | solution.py:41
  56.0 16.4 %collective-permute-start.14 = (bf16[272,512]{1,0:T(8,128)(2,1)S(1)}, bf16[272,512]{1,0:T(8,128)(2,1)S(1)}, u32[]{:S(2)}, u32[]{:S(2)}) collective-permute-start(bf16[272,512]{1,0:T(8,128)(2,1)S(1)} %collective-permute-done.13.refs_4_), channel_id=1, source_target_pairs={{0,32},{1,225},{2,34},{3,227},{4,36},{5,229},{6,38},{7,231},{8,40}... | collective-permute-start | bytes 835592 | tf_op jit(solution)/shard_map/ppermute | solution.py:41
  56.0 16.4 %collective-permute-start.17 = (bf16[272,512]{1,0:T(8,128)(2,1)S(1)}, bf16[272,512]{1,0:T(8,128)(2,1)S(1)}, u32[]{:S(2)}, u32[]{:S(2)}) collective-permute-start(bf16[272,512]{1,0:T(8,128)(2,1)S(1)} %collective-permute-done.16.refs_5_), channel_id=1, source_target_pairs={{0,224},{1,33},{2,226},{3,35},{4,228},{5,37},{6,230},{7,39},{8,232... | collective-permute-start | bytes 835592 | tf_op jit(solution)/shard_map/ppermute | solution.py:41
  59.7 6.9 %collective-permute-start.11 = (bf16[272,256]{1,0:T(8,128)(2,1)S(1)}, bf16[272,256]{1,0:T(8,128)(2,1)S(1)}, u32[]{:S(2)}, u32[]{:S(2)}) collective-permute-start(bf16[272,256]{1,0:T(8,128)(2,1)S(1)} %shard_map.88.refs_0_.refs_1_), channel_id=1, source_target_pairs={{0,24},{1,25},{2,26},{3,27},{4,28},{5,29},{6,30},{7,31},{8,0},{9,1... | collective-permute-start | bytes 417800 | tf_op jit(solution)/shard_map/ppermute | solution.py:41
  64.0 5.1 %collective-permute-start.9 = (bf16[272,256]{1,0:T(8,128)(2,1)S(1)}, bf16[272,256]{1,0:T(8,128)(2,1)S(1)}, u32[]{:S(2)}, u32[]{:S(2)}) collective-permute-start(bf16[272,256]{1,0:T(8,128)(2,1)S(1)} %shard_map.88.refs_0_.refs_1_), channel_id=1, source_target_pairs={{0,8},{1,9},{2,10},{3,11},{4,12},{5,13},{6,14},{7,15},{8,16},{9,17... | collective-permute-start | bytes 417800 | tf_op jit(solution)/shard_map/ppermute | solution.py:41
  72.9 9.8 %collective-permute-start.18 = (bf16[272,512]{1,0:T(8,128)(2,1)S(1)}, bf16[272,512]{1,0:T(8,128)(2,1)S(1)}, u32[]{:S(2)}, u32[]{:S(2)}) collective-permute-start(bf16[272,512]{1,0:T(8,128)(2,1)S(1)} %get-tuple-element.52.refs_4_), channel_id=1, source_target_pairs={{0,32},{1,225},{2,34},{3,227},{4,36},{5,229},{6,38},{7,231},{8,40}... | collective-permute-start | bytes 835592 | tf_op jit(solution)/shard_map/ppermute | solution.py:41
  83.6 6.8 %collective-permute-start.19 = (bf16[272,256]{1,0:T(8,128)(2,1)S(1)}, bf16[272,256]{1,0:T(8,128)(2,1)S(1)}, u32[]{:S(2)}, u32[]{:S(2)}) collective-permute-start(bf16[272,256]{1,0:T(8,128)(2,1)S(1)} %get-tuple-element.59), channel_id=1, source_target_pairs={{0,24},{1,25},{2,26},{3,27},{4,28},{5,29},{6,30},{7,31},{8,0},{9,1... | collective-permute-start | bytes 417800 | tf_op jit(solution)/shard_map/ppermute | solution.py:41
  86.7 6.6 %collective-permute-start.20 = (bf16[272,256]{1,0:T(8,128)(2,1)S(1)}, bf16[272,256]{1,0:T(8,128)(2,1)S(1)}, u32[]{:S(2)}, u32[]{:S(2)}) collective-permute-start(bf16[272,256]{1,0:T(8,128)(2,1)S(1)} %get-tuple-element.60), channel_id=1, source_target_pairs={{0,16},{1,17},{2,18},{3,19},{4,20},{5,21},{6,22},{7,23},{8,24},{9,... | collective-permute-start | bytes 417800 | tf_op jit(solution)/shard_map/ppermute | solution.py:41
  86.7 6.6 %collective-permute-start.21 = (bf16[272,256]{1,0:T(8,128)(2,1)S(1)}, bf16[272,256]{1,0:T(8,128)(2,1)S(1)}, u32[]{:S(2)}, u32[]{:S(2)}) collective-permute-start(bf16[272,256]{1,0:T(8,128)(2,1)S(1)} %get-tuple-element.61), channel_id=1, source_target_pairs={{0,8},{1,9},{2,10},{3,11},{4,12},{5,13},{6,14},{7,15},{8,16},{9,17... | collective-permute-start | bytes 417800 | tf_op jit(solution)/shard_map/ppermute | solution.py:41
  94.3 1.4 %collective-permute-start.22 = (bf16[272,256]{1,0:T(8,128)(2,1)S(1)}, bf16[272,256]{1,0:T(8,128)(2,1)S(1)}, u32[]{:S(2)}, u32[]{:S(2)}) collective-permute-start(bf16[272,256]{1,0:T(8,128)(2,1)S(1)} %shard_map.94.attended), channel_id=1, source_target_pairs={{0,1},{1,0},{2,3},{3,2},{4,5},{5,4},{6,7},{7,6},{8,9},{9,8},{10,11... | collective-permute-start | bytes 417800 | tf_op jit(solution)/shard_map/ppermute | solution.py:41
  97.1 16.1 %collective-permute-start.24 = (bf16[272,512]{1,0:T(8,128)(2,1)S(1)}, bf16[272,512]{1,0:T(8,128)(2,1)S(1)}, u32[]{:S(2)}, u32[]{:S(2)}) collective-permute-start(bf16[272,512]{1,0:T(8,128)(2,1)S(1)} %get-tuple-element.64), channel_id=1, source_target_pairs={{0,2},{1,7},{2,4},{3,1},{4,6},{5,3},{6,0},{7,5},{8,10},{9,15},{10,... | collective-permute-start | bytes 835592 | tf_op jit(solution)/shard_map/ppermute | solution.py:41
  97.2 16.0 %collective-permute-start.25 = (bf16[272,512]{1,0:T(8,128)(2,1)S(1)}, bf16[272,512]{1,0:T(8,128)(2,1)S(1)}, u32[]{:S(2)}, u32[]{:S(2)}) collective-permute-start(bf16[272,512]{1,0:T(8,128)(2,1)S(1)} %get-tuple-element.65), channel_id=1, source_target_pairs={{0,6},{1,3},{2,0},{3,5},{4,2},{5,7},{6,4},{7,1},{8,14},{9,11},{10,... | collective-permute-start | bytes 835592 | tf_op jit(solution)/shard_map/ppermute | solution.py:41
  100.4 12.7 %collective-permute-start.26 = (bf16[272,512]{1,0:T(8,128)(2,1)S(1)}, bf16[272,512]{1,0:T(8,128)(2,1)S(1)}, u32[]{:S(2)}, u32[]{:S(2)}) collective-permute-start(bf16[272,512]{1,0:T(8,128)(2,1)S(1)} %get-tuple-element.66), channel_id=1, source_target_pairs={{0,4},{1,5},{2,6},{3,7},{4,0},{5,1},{6,2},{7,3},{8,12},{9,13},{10,... | collective-permute-start | bytes 835592 | tf_op jit(solution)/shard_map/ppermute | solution.py:41

commit v5 on v4

--- a/solution.py
+++ b/solution.py
@@ -437,10 +437,10 @@
         out[rows, 256:] = ones_where((column == -1) & (lane == 0))
 
 
-def output_kernel(own, first, second, third, hot, tokens, out, coarse):
+def output_kernel(own, first, second, hot, tokens, out, coarse):
     @pl.when(pl.program_id(0) == 0)
     def _():
-        total = own[...] + first[...].astype(F32) + second[...].astype(F32) + third[...].astype(F32)
+        total = own[...] + first[...].astype(F32) + second[...].astype(F32)
         coarse[:ROWS, :] = total.astype(BF16)
         coarse[ROWS:, :] = jnp.zeros((TALL - ROWS, FEAT), BF16)
 
@@ -453,7 +453,7 @@
         output_kernel,
         grid=(TOK // BLOCK,),
         out_shape=shape((TOK, FEAT), BF16),
-        in_specs=[WHOLE] * 4
+        in_specs=[WHOLE] * 3
         + [pl.BlockSpec((BLOCK, TALL), lambda i: (i, 0)), pl.BlockSpec((BLOCK, FEAT), lambda i: (i, 0))],
         out_specs=pl.BlockSpec((BLOCK, FEAT), lambda i: (i, 0)),
         scratch_shapes=[pltpu.VMEM((TALL, FEAT), BF16)],
@@ -462,7 +462,7 @@
     )(*products, hot, tokens)
 
 
-def cut_kernel(info, w_out, sibling, sems):
+def cut_kernel(info, w_out, _, sibling, sems):
     copies = []
     for i in range(4):
         start = pl.multiple_of(info[I_CUT + 4 + i] * FEAT, FEAT)
@@ -479,11 +479,11 @@
         if i == 0:
             own_out[...] = part + means[...]
         else:
-            outs[i - 1][...] = part.astype(BF16)
-
-
-def y_far(value):
-    return move(value, lambda z, x, y, c: (z, x, y + 2, c))
+            outs[i - 1][...] = part.astype(outs[i - 1].dtype)
+
+
+def add_kernel(a, b, out):
+    out[...] = (a[...] + b[...].astype(F32)).astype(BF16)
 
 
 def shards(tokens, flags, norm_gain, w_query, w_key, w_value, w_out):
@@ -545,20 +545,20 @@
     )
     queries = [query] + [x_by(query, k) for k in (1, 2, 3)]
     one, other = z_one(kv), z_other(kv)
+    one2, other2 = z_one(one), z_other(other)
+    *state, done = attend_step(1, info, queries, kv, [one, other], None)
     (theirs,) = call(
         cut_kernel,
         [shape((4, SEG, FEAT), BF16)],
-        [info, w_out],
+        [info, w_out, done],
         scratch=[pltpu.SemaphoreType.DMA((4,))],
-        far_in=(1,),
+        far_in=(1, 2),
         far_out=(0,),
     )
     theirs = swap(theirs)
-    one2, other2 = z_one(one), z_other(other)
-    *state, done = attend_step(1, info, queries, kv, [one, other], None)
+    one2, other2 = gate(info, [one2, other2], done)
     one3, other3 = z_one(one2), z_other(other2)
     *state, done = attend_step(2, info, queries, None, [one2, other2], state)
-    one3, other3 = gate(info, [one3, other3], done)
     one4 = z_one(one3)
     *state, done = attend_step(3, info, queries, None, [one3, other3], state)
     partial = attend_step(4, info, queries, None, [one4], state)
@@ -567,13 +567,14 @@
     block = shape((ROWS, FEAT), BF16)
     own, first, second, third = call(
         product_kernel,
-        [shape((ROWS, FEAT), F32)] + [block] * 3,
+        [shape((ROWS, FEAT), F32)] * 2 + [block] * 2,
         [info, attended, swap(attended), w_out, theirs, means],
         flops=2 * ROWS * 2 * COLS * 4 * FEAT,
         moved=4 << 20,
     )
     (hot,) = call(mark_kernel, [shape((TOK, TALL), BF16)], [ids], flops=1 << 29, moved=3 << 20, scalars=None)
-    return output([own, y_one(first), y_other(second), y_far(third)], hot, tokens)
+    (first,) = call(add_kernel, [block], [first, y_one(third)], scalars=None)
+    return output([own, y_one(first), y_other(second)], hot, tokens)
 
 
 def solution(mesh):

time: 118 us -> 113 us (0.958)
  waiting for transfers between devices: 52.6 us -> 48.3 us
    ppermute x25, waiting for transfers between devices: 50.6 us -> 46.3 us  [move(): return lax.ppermute(value, ('seq', 'mp'), pairs)]
    pallas_call x16 -> x17, Pallas kernels: 18.9 us -> 19 us  [call(): pl.pallas_call(body, out_shape=outs, in_specs=[SMEM if i == scalars else...]
where the time goes in v5:
time: 113 us; the launch traced here: 112 us
  waiting for transfers between devices  48.3 us (43%)
  starting transfers between devices  38.3 us (34%)
  Pallas kernels  22 us (19%)
  local copies, waits for them, and re-layouts  3 us (3%)
    ppermute x25, waiting for transfers between devices, move(): return lax.ppermute(value, ('seq', 'mp'), pairs)  46.3 us
    ppermute x25, starting transfers between devices, move(): return lax.ppermute(value, ('seq', 'mp'), pairs)  32 us
    pallas_call x17, Pallas kernels, call(): pl.pallas_call(body, out_shape=outs, in_specs=[SMEM if i == scalars else...  19 us
    ppermute x1, starting transfers between devices, shards(): above = lax.ppermute(head, 'seq', [(i, i - 1) for i in range(1, count)])  4.31 us
    pallas_call x1, Pallas kernels, output(): pl.pallas_call(output_kernel, grid=(TOK // BLOCK,), out_shape=shape((TOK,...  3.01 us
    unnamed x10, local copies, waits for them, and re-layouts  2.3 us
  transfers between devices with their start and end apart: 27, of which 14 were waited for; matrix products, arithmetic and copies ran while one was open for 1% of the time, Pallas kernels for 13%

profile of v5, /device:TPU:2, one launch (start us, length us, event | category | flops | bytes accessed | tf_op | source)
XLA Modules:
  0.0 111.8 jit_solution(14824289960132796395)
XLA Ops:
  0.0 1.6 %copy-done.1 = bf16[2048,512]{1,0:T(8,128)(2,1)S(1)} copy-done((bf16[2048,512]{1,0:T(8,128)(2,1)S(1)}, bf16[2048,512]{1,0:T(8,128)(2,1)}, u32[]{:S(2)}) %copy-start.1) | copy-done | bytes 2097176
  3.0 4.3 %collective-permute-start = (f32[8,640]{1,0:T(8,128)S(1)}, f32[8,640]{1,0:T(8,128)S(1)}, u32[]{:S(2)}, u32[]{:S(2)}) collective-permute-start(f32[8,640]{1,0:T(8,128)S(1)} %get-tuple-element.39.head), channel_id=1, source_target_pairs={{8,0},{16,8},{24,16},{32,24},{40,32},{48,40},{56,48},{64,56},{72,6... | collective-permute-start | bytes 61448 | tf_op jit(solution)/shard_map/ppermute | solution.py:503
  7.3 1.9 %collective-permute-start.1 = (f32[8,640]{1,0:T(8,128)S(1)}, f32[8,640]{1,0:T(8,128)S(1)}, u32[]{:S(2)}, u32[]{:S(2)}) collective-permute-start(f32[8,640]{1,0:T(8,128)S(1)} %get-tuple-element.40), channel_id=1, source_target_pairs={{0,8},{8,16},{16,24},{24,32},{32,40},{40,48},{48,56},{56,64},{64,7... | collective-permute-start | bytes 61448 | tf_op jit(solution)/shard_map/ppermute | solution.py:504
  11.0 2.0 %collective-permute-done.1.below = f32[8,640]{1,0:T(8,128)S(1)} collective-permute-done((f32[8,640]{1,0:T(8,128)S(1)}, f32[8,640]{1,0:T(8,128)S(1)}, u32[]{:S(2)}, u32[]{:S(2)}) %collective-permute-start.1) | collective-permute-done | bytes 20512 | tf_op jit(solution)/shard_map/ppermute | solution.py:504
  13.9 3.2 %collective-permute-start.3 = (bf16[272,512]{1,0:T(8,128)(2,1)S(1)}, bf16[272,512]{1,0:T(8,128)(2,1)S(1)}, u32[]{:S(2)}, u32[]{:S(2)}) collective-permute-start(bf16[272,512]{1,0:T(8,128)(2,1)S(1)} %get-tuple-element.41.refs_0_), channel_id=1, source_target_pairs={{0,6},{1,3},{2,0},{3,5},{4,2},{5,7},{6,4},{7,1},{8,14},{9,11},{10,... | collective-permute-start | bytes 835592 | tf_op jit(solution)/shard_map/ppermute | solution.py:41
  17.1 6.3 %collective-permute-done.2.refs_1_ = bf16[272,512]{1,0:T(8,128)(2,1)S(1)} collective-permute-done((bf16[272,512]{1,0:T(8,128)(2,1)S(1)}, bf16[272,512]{1,0:T(8,128)(2,1)S(1)}, u32[]{:S(2)}, u32[]{:S(2)}) %collective-permute-start.2) | collective-permute-done | bytes 278560 | tf_op jit(solution)/shard_map/ppermute | solution.py:41
  23.9 4.3 %shard_map.85 = (f32[272,256]{1,0:T(8,128)S(1)}, f32[256,256]{1,0:T(8,128)S(1)}, f32[256,256]{1,0:T(8,128)S(1)}, bf16[4,512,256]{2,1,0:T(8,128)(2,1)S(1)}, bf16[...) custom-call(s32[32]{0:T(128)S(1)} %dynamic-slice_bitcast_fusion.info.refs_0_, ...), custom_call_target="tpu_custom_call" | custom-call | flops 855638016 | bytes 6291456 | tf_op jit(solution)/shard_map/pallas_call | solution.py:105
  28.2 3.0 %collective-permute-done.4.refs_0_ = bf16[272,512]{1,0:T(8,128)(2,1)S(1)} collective-permute-done((bf16[272,512]{1,0:T(8,128)(2,1)S(1)}, bf16[272,512]{1,0:T(8,128)(2,1)S(1)}, u32[]{:S(2)}, u32[]{:S(2)}) %collective-permute-start.4) | collective-permute-done | bytes 278560 | tf_op jit(solution)/shard_map/ppermute | solution.py:41
  31.8 1.5 %collective-permute-done.8.refs_7_ = bf16[272,512]{1,0:T(8,128)(2,1)S(1)} collective-permute-done((bf16[272,512]{1,0:T(8,128)(2,1)S(1)}, bf16[272,512]{1,0:T(8,128)(2,1)S(1)}, u32[]{:S(2)}, u32[]{:S(2)}) %collective-permute-start.8) | collective-permute-done | bytes 278560 | tf_op jit(solution)/shard_map/ppermute | solution.py:41
  33.3 1.2 %shard_map.87.refs_10_.refs_4_ = bf16[272,512]{1,0:T(8,128)(2,1)S(1)} custom-call(s32[32]{0:T(128)S(1)} %dynamic-slice_bitcast_fusion.info.refs_0_, bf16[272,512]{1,0:T(8,128)(2,1)S(1)} %get-tuple-element.41.refs_0_, bf16[272,512]{1,0:T(8,128)(2,1)S(1)} %collective-permute-done.2.refs_1_, bf16[272,512]{1,0:T(8,128)(2,1)S(1)} %collective-permute-done.3.refs_2_, ...), custom_call_target="tpu_custom_call" | custom-call | tf_op jit(solution)/shard_map/pallas_call | solution.py:105
  34.6 1.4 %collective-permute-start.12 = (bf16[272,512]{1,0:T(8,128)(2,1)S(1)}, bf16[272,512]{1,0:T(8,128)(2,1)S(1)}, u32[]{:S(2)}, u32[]{:S(2)}) collective-permute-start(bf16[272,512]{1,0:T(8,128)(2,1)S(1)} %shard_map.87.refs_10_.refs_4_), channel_id=1, source_target_pairs={{0,32},{1,225},{2,34},{3,227},{4,36},{5,229},{6,38},{7,231},{8,40}... | collective-permute-start | bytes 835592 | tf_op jit(solution)/shard_map/ppermute | solution.py:41
  36.0 4.9 %collective-permute-start.14 = (bf16[272,512]{1,0:T(8,128)(2,1)S(1)}, bf16[272,512]{1,0:T(8,128)(2,1)S(1)}, u32[]{:S(2)}, u32[]{:S(2)}) collective-permute-start(bf16[272,512]{1,0:T(8,128)(2,1)S(1)} %shard_map.87.refs_10_.refs_4_), channel_id=1, source_target_pairs={{0,224},{1,33},{2,226},{3,35},{4,228},{5,37},{6,230},{7,39},{8,232... | collective-permute-start | bytes 835592 | tf_op jit(solution)/shard_map/ppermute | solution.py:41
  41.9 1.5 %collective-permute-start.10 = (bf16[272,256]{1,0:T(8,128)(2,1)S(1)}, bf16[272,256]{1,0:T(8,128)(2,1)S(1)}, u32[]{:S(2)}, u32[]{:S(2)}) collective-permute-start(bf16[272,256]{1,0:T(8,128)(2,1)S(1)} %shard_map.88.refs_0_.refs_1_), channel_id=1, source_target_pairs={{0,16},{1,17},{2,18},{3,19},{4,20},{5,21},{6,22},{7,23},{8,24},{9,... | collective-permute-start | bytes 417800 | tf_op jit(solution)/shard_map/ppermute | solution.py:41
  43.4 3.0 %collective-permute-start.11 = (bf16[272,256]{1,0:T(8,128)(2,1)S(1)}, bf16[272,256]{1,0:T(8,128)(2,1)S(1)}, u32[]{:S(2)}, u32[]{:S(2)}) collective-permute-start(bf16[272,256]{1,0:T(8,128)(2,1)S(1)} %shard_map.88.refs_0_.refs_1_), channel_id=1, source_target_pairs={{0,24},{1,25},{2,26},{3,27},{4,28},{5,29},{6,30},{7,31},{8,0},{9,1... | collective-permute-start | bytes 417800 | tf_op jit(solution)/shard_map/ppermute | solution.py:41
  46.4 1.4 %collective-permute-start.9 = (bf16[272,256]{1,0:T(8,128)(2,1)S(1)}, bf16[272,256]{1,0:T(8,128)(2,1)S(1)}, u32[]{:S(2)}, u32[]{:S(2)}) collective-permute-start(bf16[272,256]{1,0:T(8,128)(2,1)S(1)} %shard_map.88.refs_0_.refs_1_), channel_id=1, source_target_pairs={{0,8},{1,9},{2,10},{3,11},{4,12},{5,13},{6,14},{7,15},{8,16},{9,17... | collective-permute-start | bytes 417800 | tf_op jit(solution)/shard_map/ppermute | solution.py:41
  47.8 3.2 %collective-permute-start.15 = (bf16[272,512]{1,0:T(8,128)(2,1)S(1)}, bf16[272,512]{1,0:T(8,128)(2,1)S(1)}, u32[]{:S(2)}, u32[]{:S(2)}) collective-permute-start(bf16[272,512]{1,0:T(8,128)(2,1)S(1)} %collective-permute-done.14.refs_6_), channel_id=1, source_target_pairs={{0,224},{1,33},{2,226},{3,35},{4,228},{5,37},{6,230},{7,39},{8,232... | collective-permute-start | bytes 835592 | tf_op jit(solution)/shard_map/ppermute | solution.py:41
  52.9 2.1 %shard_map.89 = (f32[4,2,272,256]{3,2,1,0:T(8,128)S(1)}, f32[4,2,272,128]{3,2,1,0:T(8,128)S(1)}, f32[8,128]{1,0:T(8,128)S(1)}) custom-call(s32[32]{0:T(128)S(1)} %dynamic-slice_bitcast_fusion.info.refs_0_, bf16[272,256]{1,0:T(8,128)(2,1)S(1)} %shard_map.88.refs_0_.refs_1_, bf16[272,256]{1,0:T(8,128)(2,1)S(1)} %collective-permute-done.9.refs_1_.refs_2_, ...), custom_call_target="tpu_custom_call" | custom-call | flops 855638016 | bytes 4194304 | tf_op jit(solution)/shard_map/pallas_call | solution.py:105
  55.9 1.8 %collective-permute-done.13.refs_0_ = bf16[272,512]{1,0:T(8,128)(2,1)S(1)} collective-permute-done((bf16[272,512]{1,0:T(8,128)(2,1)S(1)}, bf16[272,512]{1,0:T(8,128)(2,1)S(1)}, u32[]{:S(2)}, u32[]{:S(2)}) %collective-permute-start.13) | collective-permute-done | bytes 278560 | tf_op jit(solution)/shard_map/ppermute | solution.py:41
  58.3 3.2 %collective-permute-start.18 = (bf16[272,512]{1,0:T(8,128)(2,1)S(1)}, bf16[272,512]{1,0:T(8,128)(2,1)S(1)}, u32[]{:S(2)}, u32[]{:S(2)}) collective-permute-start(bf16[272,512]{1,0:T(8,128)(2,1)S(1)} %get-tuple-element.51.refs_5_), channel_id=1, source_target_pairs={{0,224},{1,33},{2,226},{3,35},{4,228},{5,37},{6,230},{7,39},{8,232... | collective-permute-start | bytes 835592 | tf_op jit(solution)/shard_map/ppermute | solution.py:41
  61.5 5.3 %collective-permute-done.16.refs_4_ = bf16[272,512]{1,0:T(8,128)(2,1)S(1)} collective-permute-done((bf16[272,512]{1,0:T(8,128)(2,1)S(1)}, bf16[272,512]{1,0:T(8,128)(2,1)S(1)}, u32[]{:S(2)}, u32[]{:S(2)}) %collective-permute-start.16) | collective-permute-done | bytes 278560 | tf_op jit(solution)/shard_map/ppermute | solution.py:41
  66.8 1.1 %shard_map.91 = (f32[4,2,272,256]{3,2,1,0:T(8,128)S(1)}, f32[4,2,272,128]{3,2,1,0:T(8,128)S(1)}, f32[8,128]{1,0:T(8,128)}) custom-call(s32[32]{0:T(128)S(1)} %dynamic-slice_bitcast_fusion.info.refs_0_, bf16[272,256]{1,0:T(8,128)(2,1)S(1)} %shard_map.88.refs_0_.refs_1_, ...), custom_call_target="tpu_custom_call", output_to_operand_aliasing={{0}: (7, {}), {1}: (8, {})} | custom-call | flops 570425344 | bytes 4194304 | tf_op jit(solution)/shard_map/pallas_call | solution.py:105
  67.9 1.1 %shard_map.92 = (f32[4,2,272,256]{3,2,1,0:T(8,128)S(1)}, f32[4,2,272,128]{3,2,1,0:T(8,128)S(1)}, f32[8,128]{1,0:T(8,128)}) custom-call(s32[32]{0:T(128)S(1)} %dynamic-slice_bitcast_fusion.info.refs_0_, bf16[272,256]{1,0:T(8,128)(2,1)S(1)} %shard_map.88.refs_0_.refs_1_, ...), custom_call_target="tpu_custom_call", output_to_operand_aliasing={{0}: (7, {}), {1}: (8, {})} | custom-call | flops 570425344 | bytes 4194304 | tf_op jit(solution)/shard_map/pallas_call | solution.py:105
  69.1 5.8 %collective-permute-done.17.refs_5_ = bf16[272,512]{1,0:T(8,128)(2,1)S(1)} collective-permute-done((bf16[272,512]{1,0:T(8,128)(2,1)S(1)}, bf16[272,512]{1,0:T(8,128)(2,1)S(1)}, u32[]{:S(2)}, u32[]{:S(2)}) %collective-permute-start.17) | collective-permute-done | bytes 278560 | tf_op jit(solution)/shard_map/ppermute | solution.py:41
  75.8 4.2 %collective-permute-start.19 = (bf16[272,256]{1,0:T(8,128)(2,1)S(1)}, bf16[272,256]{1,0:T(8,128)(2,1)S(1)}, u32[]{:S(2)}, u32[]{:S(2)}) collective-permute-start(bf16[272,256]{1,0:T(8,128)(2,1)S(1)} %get-tuple-element.59), channel_id=1, source_target_pairs={{0,24},{1,25},{2,26},{3,27},{4,28},{5,29},{6,30},{7,31},{8,0},{9,1... | collective-permute-start | bytes 417800 | tf_op jit(solution)/shard_map/ppermute | solution.py:41
  81.6 2.4 %collective-permute-done.19.b = bf16[272,256]{1,0:T(8,128)(2,1)S(1)} collective-permute-done((bf16[272,256]{1,0:T(8,128)(2,1)S(1)}, bf16[272,256]{1,0:T(8,128)(2,1)S(1)}, u32[]{:S(2)}, u32[]{:S(2)}) %collective-permute-start.19) | collective-permute-done | bytes 139296 | tf_op jit(solution)/shard_map/ppermute | solution.py:41
  83.9 3.0 %collective-permute-done.20.c = bf16[272,256]{1,0:T(8,128)(2,1)S(1)} collective-permute-done((bf16[272,256]{1,0:T(8,128)(2,1)S(1)}, bf16[272,256]{1,0:T(8,128)(2,1)S(1)}, u32[]{:S(2)}, u32[]{:S(2)}) %collective-permute-start.20) | collective-permute-done | bytes 139296 | tf_op jit(solution)/shard_map/ppermute | solution.py:41
  88.1 1.3 %collective-permute-done.22.other = bf16[272,256]{1,0:T(8,128)(2,1)S(1)} collective-permute-done((bf16[272,256]{1,0:T(8,128)(2,1)S(1)}, bf16[272,256]{1,0:T(8,128)(2,1)S(1)}, u32[]{:S(2)}, u32[]{:S(2)}) %collective-permute-start.22) | collective-permute-done | bytes 139296 | tf_op jit(solution)/shard_map/ppermute | solution.py:41
  89.5 1.3 %shard_map.96 = (f32[272,512]{1,0:T(8,128)S(1)}, f32[272,512]{1,0:T(8,128)S(1)}, bf16[272,512]{1,0:T(8,128)(2,1)S(1)}, bf16[272,512]{1,0:T(8,128)(2,1)S(1)}) custom-call(s32[32]{0:T(128)S(1)} %dynamic-slice_bitcast_fusion.info.refs_0_, bf16[272,256]{1,0:T(8,128)(2,1)S(1)} %shard_map.94.attended, bf16[272,256]{1,0:T(8,128)(2,1)S(1)} %collective-permute-done.22.other, ...), custom_call_target="tpu_custom_call" | custom-call | flops 570425344 | bytes 4194304 | tf_op jit(solution)/shard_map/pallas_call | solution.py:105
  90.9 3.2 %collective-permute-start.26 = (bf16[272,512]{1,0:T(8,128)(2,1)S(1)}, bf16[272,512]{1,0:T(8,128)(2,1)S(1)}, u32[]{:S(2)}, u32[]{:S(2)}) collective-permute-start(bf16[272,512]{1,0:T(8,128)(2,1)S(1)} %get-tuple-element.66), channel_id=1, source_target_pairs={{0,6},{1,3},{2,0},{3,5},{4,2},{5,7},{6,4},{7,1},{8,14},{9,11},{10,... | collective-permute-start | bytes 835592 | tf_op jit(solution)/shard_map/ppermute | solution.py:41
  94.1 6.8 %collective-permute-done.24.b = bf16[272,512]{1,0:T(8,128)(2,1)S(1)} collective-permute-done((bf16[272,512]{1,0:T(8,128)(2,1)S(1)}, bf16[272,512]{1,0:T(8,128)(2,1)S(1)}, u32[]{:S(2)}, u32[]{:S(2)}) %collective-permute-start.24) | collective-permute-done | bytes 278560 | tf_op jit(solution)/shard_map/ppermute | solution.py:41
  101.5 7.3 %collective-permute-done.25.first = bf16[272,512]{1,0:T(8,128)(2,1)S(1)} collective-permute-done((bf16[272,512]{1,0:T(8,128)(2,1)S(1)}, bf16[272,512]{1,0:T(8,128)(2,1)S(1)}, u32[]{:S(2)}, u32[]{:S(2)}) %collective-permute-start.25) | collective-permute-done | bytes 278560 | tf_op jit(solution)/shard_map/ppermute | solution.py:41
  108.8 3.0 %shard_map.99 = bf16[2048,512]{1,0:T(8,128)(2,1)} custom-call(f32[272,512]{1,0:T(8,128)S(1)} %get-tuple-element.63.own, bf16[272,512]{1,0:T(8,128)(2,1)S(1)} %collective-permute-done.25.first, bf16[272,512]{1,0:T(8,128)(2,1)S(1)} %collective-permute-done.26.second, bf16[2048,384]{1,0:T(8,128)(2,1)S(1)} %shard_map.98.hot, bf16[2048,512]{1,0:T(8,128)(2,1)S(1)} %copy-done.2), custom_call_target="tpu_custom_call" | custom-call | flops 2147483648 | bytes 6291456 | tf_op jit(solution)/shard_map/pallas_call | solution.py:452
  (52 shorter events, 13.7 us)
Async XLA Ops:
  0.0 1.6 %copy-start.1 = (bf16[2048,512]{1,0:T(8,128)(2,1)S(1)}, bf16[2048,512]{1,0:T(8,128)(2,1)}, u32[]{:S(2)}) copy-start(bf16[2048,512]{1,0:T(8,128)(2,1)} %tokens.5) | copy-start | bytes 6291460
  1.6 0.7 copy-start.3
  2.3 7.7 %copy-start.2 = (bf16[2048,512]{1,0:T(8,128)(2,1)S(1)}, bf16[2048,512]{1,0:T(8,128)(2,1)}, u32[]{:S(2)}) copy-start(bf16[2048,512]{1,0:T(8,128)(2,1)} %tokens.5) | copy-start | bytes 6291460
  3.0 8.0 %copy-start.4 = (f32[4096]{0:T(1024)S(1)}, f32[4096]{0:T(1024)}, u32[]{:S(2)}) copy-start(f32[4096]{0:T(1024)} %param.10) | copy-start | bytes 49156
  3.0 8.0 %collective-permute-start = (f32[8,640]{1,0:T(8,128)S(1)}, f32[8,640]{1,0:T(8,128)S(1)}, u32[]{:S(2)}, u32[]{:S(2)}) collective-permute-start(f32[8,640]{1,0:T(8,128)S(1)} %get-tuple-element.39.head), channel_id=1, source_target_pairs={{8,0},{16,8},{24,16},{32,24},{40,32},{48,40},{56,48},{64,56},{72,6... | collective-permute-start | bytes 61448 | tf_op jit(solution)/shard_map/ppermute | solution.py:503
  7.3 5.7 %collective-permute-start.1 = (f32[8,640]{1,0:T(8,128)S(1)}, f32[8,640]{1,0:T(8,128)S(1)}, u32[]{:S(2)}, u32[]{:S(2)}) collective-permute-start(f32[8,640]{1,0:T(8,128)S(1)} %get-tuple-element.40), channel_id=1, source_target_pairs={{0,8},{8,16},{16,24},{24,32},{32,40},{40,48},{48,56},{56,64},{64,7... | collective-permute-start | bytes 61448 | tf_op jit(solution)/shard_map/ppermute | solution.py:504
  13.8 9.6 %collective-permute-start.2 = (bf16[272,512]{1,0:T(8,128)(2,1)S(1)}, bf16[272,512]{1,0:T(8,128)(2,1)S(1)}, u32[]{:S(2)}, u32[]{:S(2)}) collective-permute-start(bf16[272,512]{1,0:T(8,128)(2,1)S(1)} %get-tuple-element.41.refs_0_), channel_id=1, source_target_pairs={{0,2},{1,7},{2,4},{3,1},{4,6},{5,3},{6,0},{7,5},{8,10},{9,15},{10,... | collective-permute-start | bytes 835592 | tf_op jit(solution)/shard_map/ppermute | solution.py:41
  13.9 9.5 %collective-permute-start.3 = (bf16[272,512]{1,0:T(8,128)(2,1)S(1)}, bf16[272,512]{1,0:T(8,128)(2,1)S(1)}, u32[]{:S(2)}, u32[]{:S(2)}) collective-permute-start(bf16[272,512]{1,0:T(8,128)(2,1)S(1)} %get-tuple-element.41.refs_0_), channel_id=1, source_target_pairs={{0,6},{1,3},{2,0},{3,5},{4,2},{5,7},{6,4},{7,1},{8,14},{9,11},{10,... | collective-permute-start | bytes 835592 | tf_op jit(solution)/shard_map/ppermute | solution.py:41
  17.1 6.8 %collective-permute-start.5 = (bf16[272,512]{1,0:T(8,128)(2,1)S(1)}, bf16[272,512]{1,0:T(8,128)(2,1)S(1)}, u32[]{:S(2)}, u32[]{:S(2)}) collective-permute-start(bf16[272,512]{1,0:T(8,128)(2,1)S(1)} %get-tuple-element.41.refs_0_), channel_id=1, source_target_pairs={{0,1},{1,0},{2,3},{3,2},{4,5},{5,4},{6,7},{7,6},{8,9},{9,8},{10,11... | collective-permute-start | bytes 835592 | tf_op jit(solution)/shard_map/ppermute | solution.py:41
  23.4 7.8 %collective-permute-start.4 = (bf16[272,512]{1,0:T(8,128)(2,1)S(1)}, bf16[272,512]{1,0:T(8,128)(2,1)S(1)}, u32[]{:S(2)}, u32[]{:S(2)}) collective-permute-start(bf16[272,512]{1,0:T(8,128)(2,1)S(1)} %collective-permute-done.2.refs_1_), channel_id=1, source_target_pairs={{0,2},{1,7},{2,4},{3,1},{4,6},{5,3},{6,0},{7,5},{8,10},{9,15},{10,... | collective-permute-start | bytes 835592 | tf_op jit(solution)/shard_map/ppermute | solution.py:41
  23.4 8.4 %collective-permute-start.6 = (bf16[272,512]{1,0:T(8,128)(2,1)S(1)}, bf16[272,512]{1,0:T(8,128)(2,1)S(1)}, u32[]{:S(2)}, u32[]{:S(2)}) collective-permute-start(bf16[272,512]{1,0:T(8,128)(2,1)S(1)} %collective-permute-done.2.refs_1_), channel_id=1, source_target_pairs={{0,1},{1,0},{2,3},{3,2},{4,5},{5,4},{6,7},{7,6},{8,9},{9,8},{10,11... | collective-permute-start | bytes 835592 | tf_op jit(solution)/shard_map/ppermute | solution.py:41
  23.4 8.4 %collective-permute-start.7 = (bf16[272,512]{1,0:T(8,128)(2,1)S(1)}, bf16[272,512]{1,0:T(8,128)(2,1)S(1)}, u32[]{:S(2)}, u32[]{:S(2)}) collective-permute-start(bf16[272,512]{1,0:T(8,128)(2,1)S(1)} %collective-permute-done.3.refs_2_), channel_id=1, source_target_pairs={{0,1},{1,0},{2,3},{3,2},{4,5},{5,4},{6,7},{7,6},{8,9},{9,8},{10,11... | collective-permute-start | bytes 835592 | tf_op jit(solution)/shard_map/ppermute | solution.py:41
  31.7 1.6 %collective-permute-start.8 = (bf16[272,512]{1,0:T(8,128)(2,1)S(1)}, bf16[272,512]{1,0:T(8,128)(2,1)S(1)}, u32[]{:S(2)}, u32[]{:S(2)}) collective-permute-start(bf16[272,512]{1,0:T(8,128)(2,1)S(1)} %shard_map.86.refs_3_), channel_id=1, source_target_pairs={{0,1},{1,0},{2,3},{3,2},{4,5},{5,4},{6,7},{7,6},{8,9},{9,8},{10,11... | collective-permute-start | bytes 835592 | tf_op jit(solution)/shard_map/ppermute | solution.py:41
  34.6 13.2 %collective-permute-start.12 = (bf16[272,512]{1,0:T(8,128)(2,1)S(1)}, bf16[272,512]{1,0:T(8,128)(2,1)S(1)}, u32[]{:S(2)}, u32[]{:S(2)}) collective-permute-start(bf16[272,512]{1,0:T(8,128)(2,1)S(1)} %shard_map.87.refs_10_.refs_4_), channel_id=1, source_target_pairs={{0,32},{1,225},{2,34},{3,227},{4,36},{5,229},{6,38},{7,231},{8,40}... | collective-permute-start | bytes 835592 | tf_op jit(solution)/shard_map/ppermute | solution.py:41
  36.0 11.8 %collective-permute-start.14 = (bf16[272,512]{1,0:T(8,128)(2,1)S(1)}, bf16[272,512]{1,0:T(8,128)(2,1)S(1)}, u32[]{:S(2)}, u32[]{:S(2)}) collective-permute-start(bf16[272,512]{1,0:T(8,128)(2,1)S(1)} %shard_map.87.refs_10_.refs_4_), channel_id=1, source_target_pairs={{0,224},{1,33},{2,226},{3,35},{4,228},{5,37},{6,230},{7,39},{8,232... | collective-permute-start | bytes 835592 | tf_op jit(solution)/shard_map/ppermute | solution.py:41
  41.9 13.2 %copy-start = (bf16[256,4096]{1,0:T(8,128)(2,1)S(1)}, bf16[256,4096]{1,0:T(8,128)(2,1)}, u32[]{:S(2)}) copy-start(bf16[256,4096]{1,0:T(8,128)(2,1)} %w_out.3) | copy-start | bytes 6291460
  41.9 9.1 %collective-permute-start.10 = (bf16[272,256]{1,0:T(8,128)(2,1)S(1)}, bf16[272,256]{1,0:T(8,128)(2,1)S(1)}, u32[]{:S(2)}, u32[]{:S(2)}) collective-permute-start(bf16[272,256]{1,0:T(8,128)(2,1)S(1)} %shard_map.88.refs_0_.refs_1_), channel_id=1, source_target_pairs={{0,16},{1,17},{2,18},{3,19},{4,20},{5,21},{6,22},{7,23},{8,24},{9,... | collective-permute-start | bytes 417800 | tf_op jit(solution)/shard_map/ppermute | solution.py:41
  43.4 8.4 %collective-permute-start.11 = (bf16[272,256]{1,0:T(8,128)(2,1)S(1)}, bf16[272,256]{1,0:T(8,128)(2,1)S(1)}, u32[]{:S(2)}, u32[]{:S(2)}) collective-permute-start(bf16[272,256]{1,0:T(8,128)(2,1)S(1)} %shard_map.88.refs_0_.refs_1_), channel_id=1, source_target_pairs={{0,24},{1,25},{2,26},{3,27},{4,28},{5,29},{6,30},{7,31},{8,0},{9,1... | collective-permute-start | bytes 417800 | tf_op jit(solution)/shard_map/ppermute | solution.py:41
  46.4 6.5 %collective-permute-start.9 = (bf16[272,256]{1,0:T(8,128)(2,1)S(1)}, bf16[272,256]{1,0:T(8,128)(2,1)S(1)}, u32[]{:S(2)}, u32[]{:S(2)}) collective-permute-start(bf16[272,256]{1,0:T(8,128)(2,1)S(1)} %shard_map.88.refs_0_.refs_1_), channel_id=1, source_target_pairs={{0,8},{1,9},{2,10},{3,11},{4,12},{5,13},{6,14},{7,15},{8,16},{9,17... | collective-permute-start | bytes 417800 | tf_op jit(solution)/shard_map/ppermute | solution.py:41
  47.8 9.8 %collective-permute-start.13 = (bf16[272,512]{1,0:T(8,128)(2,1)S(1)}, bf16[272,512]{1,0:T(8,128)(2,1)S(1)}, u32[]{:S(2)}, u32[]{:S(2)}) collective-permute-start(bf16[272,512]{1,0:T(8,128)(2,1)S(1)} %collective-permute-done.12.refs_5_), channel_id=1, source_target_pairs={{0,32},{1,225},{2,34},{3,227},{4,36},{5,229},{6,38},{7,231},{8,40}... | collective-permute-start | bytes 835592 | tf_op jit(solution)/shard_map/ppermute | solution.py:41
  47.8 9.8 %collective-permute-start.15 = (bf16[272,512]{1,0:T(8,128)(2,1)S(1)}, bf16[272,512]{1,0:T(8,128)(2,1)S(1)}, u32[]{:S(2)}, u32[]{:S(2)}) collective-permute-start(bf16[272,512]{1,0:T(8,128)(2,1)S(1)} %collective-permute-done.14.refs_6_), channel_id=1, source_target_pairs={{0,224},{1,33},{2,226},{3,35},{4,228},{5,37},{6,230},{7,39},{8,232... | collective-permute-start | bytes 835592 | tf_op jit(solution)/shard_map/ppermute | solution.py:41
  55.8 32.4 %collective-permute-start.23 = (bf16[4,256,512]{2,1,0:T(8,128)(2,1)S(1)}, bf16[4,256,512]{2,1,0:T(8,128)(2,1)S(1)}, u32[]{:S(2)}, u32[]{:S(2)}) collective-permute-start(bf16[4,256,512]{2,1,0:T(8,128)(2,1)S(1)} %shard_map.95), channel_id=1, source_target_pairs={{0,1},{1,0},{2,3},{3,2},{4,5},{5,4},{6,7},{7,6},{8,9},{9,8},{10,11... | collective-permute-start | bytes 3145736 | tf_op jit(solution)/shard_map/ppermute | solution.py:41
  58.2 8.6 %collective-permute-start.16 = (bf16[272,512]{1,0:T(8,128)(2,1)S(1)}, bf16[272,512]{1,0:T(8,128)(2,1)S(1)}, u32[]{:S(2)}, u32[]{:S(2)}) collective-permute-start(bf16[272,512]{1,0:T(8,128)(2,1)S(1)} %get-tuple-element.50.refs_4_), channel_id=1, source_target_pairs={{0,32},{1,225},{2,34},{3,227},{4,36},{5,229},{6,38},{7,231},{8,40}... | collective-permute-start | bytes 835592 | tf_op jit(solution)/shard_map/ppermute | solution.py:41
  58.3 9.6 %collective-permute-start.18 = (bf16[272,512]{1,0:T(8,128)(2,1)S(1)}, bf16[272,512]{1,0:T(8,128)(2,1)S(1)}, u32[]{:S(2)}, u32[]{:S(2)}) collective-permute-start(bf16[272,512]{1,0:T(8,128)(2,1)S(1)} %get-tuple-element.51.refs_5_), channel_id=1, source_target_pairs={{0,224},{1,33},{2,226},{3,35},{4,228},{5,37},{6,230},{7,39},{8,232... | collective-permute-start | bytes 835592 | tf_op jit(solution)/shard_map/ppermute | solution.py:41
  66.8 8.1 %collective-permute-start.17 = (bf16[272,512]{1,0:T(8,128)(2,1)S(1)}, bf16[272,512]{1,0:T(8,128)(2,1)S(1)}, u32[]{:S(2)}, u32[]{:S(2)}) collective-permute-start(bf16[272,512]{1,0:T(8,128)(2,1)S(1)} %collective-permute-done.16.refs_4_), channel_id=1, source_target_pairs={{0,32},{1,225},{2,34},{3,227},{4,36},{5,229},{6,38},{7,231},{8,40}... | collective-permute-start | bytes 835592 | tf_op jit(solution)/shard_map/ppermute | solution.py:41
  75.8 8.2 %collective-permute-start.19 = (bf16[272,256]{1,0:T(8,128)(2,1)S(1)}, bf16[272,256]{1,0:T(8,128)(2,1)S(1)}, u32[]{:S(2)}, u32[]{:S(2)}) collective-permute-start(bf16[272,256]{1,0:T(8,128)(2,1)S(1)} %get-tuple-element.59), channel_id=1, source_target_pairs={{0,24},{1,25},{2,26},{3,27},{4,28},{5,29},{6,30},{7,31},{8,0},{9,1... | collective-permute-start | bytes 417800 | tf_op jit(solution)/shard_map/ppermute | solution.py:41
  80.0 6.9 %collective-permute-start.20 = (bf16[272,256]{1,0:T(8,128)(2,1)S(1)}, bf16[272,256]{1,0:T(8,128)(2,1)S(1)}, u32[]{:S(2)}, u32[]{:S(2)}) collective-permute-start(bf16[272,256]{1,0:T(8,128)(2,1)S(1)} %get-tuple-element.60), channel_id=1, source_target_pairs={{0,16},{1,17},{2,18},{3,19},{4,20},{5,21},{6,22},{7,23},{8,24},{9,... | collective-permute-start | bytes 417800 | tf_op jit(solution)/shard_map/ppermute | solution.py:41
  80.9 6.0 %collective-permute-start.21 = (bf16[272,256]{1,0:T(8,128)(2,1)S(1)}, bf16[272,256]{1,0:T(8,128)(2,1)S(1)}, u32[]{:S(2)}, u32[]{:S(2)}) collective-permute-start(bf16[272,256]{1,0:T(8,128)(2,1)S(1)} %get-tuple-element.61), channel_id=1, source_target_pairs={{0,8},{1,9},{2,10},{3,11},{4,12},{5,13},{6,14},{7,15},{8,16},{9,17... | collective-permute-start | bytes 417800 | tf_op jit(solution)/shard_map/ppermute | solution.py:41
  88.0 1.4 %collective-permute-start.22 = (bf16[272,256]{1,0:T(8,128)(2,1)S(1)}, bf16[272,256]{1,0:T(8,128)(2,1)S(1)}, u32[]{:S(2)}, u32[]{:S(2)}) collective-permute-start(bf16[272,256]{1,0:T(8,128)(2,1)S(1)} %shard_map.94.attended), channel_id=1, source_target_pairs={{0,1},{1,0},{2,3},{3,2},{4,5},{5,4},{6,7},{7,6},{8,9},{9,8},{10,11... | collective-permute-start | bytes 417800 | tf_op jit(solution)/shard_map/ppermute | solution.py:41
  90.8 10.1 %collective-permute-start.24 = (bf16[272,512]{1,0:T(8,128)(2,1)S(1)}, bf16[272,512]{1,0:T(8,128)(2,1)S(1)}, u32[]{:S(2)}, u32[]{:S(2)}) collective-permute-start(bf16[272,512]{1,0:T(8,128)(2,1)S(1)} %get-tuple-element.65), channel_id=1, source_target_pairs={{0,2},{1,7},{2,4},{3,1},{4,6},{5,3},{6,0},{7,5},{8,10},{9,15},{10,... | collective-permute-start | bytes 835592 | tf_op jit(solution)/shard_map/ppermute | solution.py:41
  90.9 10.6 %collective-permute-start.26 = (bf16[272,512]{1,0:T(8,128)(2,1)S(1)}, bf16[272,512]{1,0:T(8,128)(2,1)S(1)}, u32[]{:S(2)}, u32[]{:S(2)}) collective-permute-start(bf16[272,512]{1,0:T(8,128)(2,1)S(1)} %get-tuple-element.66), channel_id=1, source_target_pairs={{0,6},{1,3},{2,0},{3,5},{4,2},{5,7},{6,4},{7,1},{8,14},{9,11},{10,... | collective-permute-start | bytes 835592 | tf_op jit(solution)/shard_map/ppermute | solution.py:41
  100.9 7.8 %collective-permute-start.25 = (bf16[272,512]{1,0:T(8,128)(2,1)S(1)}, bf16[272,512]{1,0:T(8,128)(2,1)S(1)}, u32[]{:S(2)}, u32[]{:S(2)}) collective-permute-start(bf16[272,512]{1,0:T(8,128)(2,1)S(1)} %shard_map.97), channel_id=1, source_target_pairs={{0,2},{1,7},{2,4},{3,1},{4,6},{5,3},{6,0},{7,5},{8,10},{9,15},{10,... | collective-permute-start | bytes 835592 | tf_op jit(solution)/shard_map/ppermute | solution.py:41

commit v6 on v5

--- a/solution.py
+++ b/solution.py
@@ -20,7 +20,7 @@
 LOG2E = 1.4426950408889634
 LOW = -1e30
 VMEM_LIMIT = 20 * 1024 * 1024
-ROOM = 48 * 1024 * 1024
+ROOM = 47 * 1024 * 1024
 F32, BF16 = jnp.float32, jnp.bfloat16
 
 
@@ -186,7 +186,7 @@
     return out
 
 
-def norm_kernel(info, sums, counts, head, above, below, gain, means_out, u_out, bias_out):
+def norm_kernel(info, sums, counts, head, above, below, gain, _, means_out, u_out, bias_out):
     g = gain[pl.ds(info[I_MP], 1), :]
     last = iota((SEG, 128), 0) == SEG - 1
     size = counts[...] + jnp.where(last, above[0:1, FEAT:], 0.0)
@@ -223,32 +223,31 @@
     return scale, wide(column, 2)
 
 
-def product(acc, blocks, weight, rows):
-    for i, u in enumerate(blocks):
-        acc = acc + dot(u[:rows, :], weight[i])
+def load_kernel(_, *refs):
+    sources, outs, done, sems = refs[:3], refs[3:6], refs[6], refs[7]
+    copies = []
+    for n in range(3):
+        for i in range(4):
+            rows = pl.ds(i * (WIDTH // 4), WIDTH // 4)
+            copies.append(pltpu.make_async_copy(sources[n].at[rows, :], outs[n].at[rows, :], sems.at[n, i]))
+            copies[-1].start()
+    done[...] = jnp.zeros_like(done)
+    for copy in copies:
+        copy.wait()
+
+
+def product(info, acc, blocks, which, weight, rows):
+    for i, u in zip(which, blocks):
+        start = pl.multiple_of(info[I_SRC + i] * FEAT, FEAT)
+        part = dot(u[:rows, :], weight[pl.ds(start, FEAT), :])
+        acc = part if acc is None else acc + part
     return acc
 
 
 def early_kernel(info, *refs):
-    blocks, weights = refs[:4], refs[4:7]
-    sums, kept, early, sems = refs[7:10], refs[10:13], refs[13:16], refs[16]
-    copies = {}
-    for side, (which, target) in enumerate(((EARLY, early), (LATE, kept))):
-        for i in range(4):
-            start = pl.multiple_of(info[I_SRC + which[i]] * FEAT, FEAT)
-            for n in range(3):
-                copies[side, i, n] = pltpu.make_async_copy(
-                    weights[n].at[pl.ds(start, FEAT), :], target[n].at[i], sems.at[side, i, n]
-                )
-                copies[side, i, n].start()
-    for i, u in enumerate(blocks):
-        for n, rows in enumerate((ROWS, SEG, SEG)):
-            copies[0, i, n].wait()
-            part = dot(u[:rows, :], early[n][i])
-            sums[n][...] = part if i == 0 else sums[n][...] + part
-    for i in range(4):
-        for n in range(3):
-            copies[1, i, n].wait()
+    blocks, weights, sums = refs[:4], refs[4:7], refs[7:]
+    for n, rows in enumerate((ROWS, SEG, SEG)):
+        sums[n][...] = product(info, None, blocks, EARLY, weights[n], rows)
 
 
 def square_rows(blocks):
@@ -262,8 +261,8 @@
     blocks, late = refs[:8], [refs[i] for i in LATE]
     w_key, w_value, keys, values, bias, kv_out = refs[8:]
     _, column = row_scale(square_rows(blocks))
-    kv_out[:SEG, :COLS] = (product(keys[...], late, w_key, SEG) * column).astype(BF16)
-    kv_out[:SEG, COLS:] = (product(values[...], late, w_value, SEG) * column).astype(BF16)
+    kv_out[:SEG, :COLS] = (product(info, keys[...], late, LATE, w_key, SEG) * column).astype(BF16)
+    kv_out[:SEG, COLS:] = (product(info, values[...], late, LATE, w_value, SEG) * column).astype(BF16)
     kv_out[SEG:, :] = bias[...]
 
 
@@ -271,7 +270,7 @@
     blocks, late = refs[:8], [refs[i] for i in LATE]
     w_query, partial, _, q_out = refs[8:]
     scale, column = row_scale(square_rows(blocks))
-    query = product(partial[...], late, w_query, ROWS)
+    query = product(info, partial[...], late, LATE, w_query, ROWS)
     q_out[:SEG, :] = (query[:SEG] * column * SCORE).astype(BF16)
     extra = query[SEG:] * scale[2:3, :] * SCORE
     q_out[SEG:, :] = jnp.where(iota((16, COLS), 0) == 0, extra, 0.0).astype(BF16)
@@ -422,7 +421,7 @@
     out[SEG:, :] = jnp.where(iota((16, COLS), 0) == 0, end, 0.0).astype(BF16)
 
 
-BLOCK = 512
+BLOCK = 256
 TALL = 384
 
 
@@ -502,6 +501,16 @@
     count = NZ * NX
     above = lax.ppermute(head, "seq", [(i, i - 1) for i in range(1, count)])
     below = lax.ppermute(tail, "seq", [(i, i + 1) for i in range(count - 1)])
+    *weights, loaded = call(
+        load_kernel,
+        [shape((WIDTH, COLS), BF16)] * 3 + [shape((8, 128), F32)],
+        [tail, w_query, w_key, w_value],
+        scalars=None,
+        moved=12 << 20,
+        scratch=[pltpu.SemaphoreType.DMA((3, 4))],
+        far_in=range(4),
+        room=ROOM,
+    )
     sums, sizes = call(
         pool_kernel,
         [shape((SEG, FEAT), F32), shape((SEG, 128), F32)],
@@ -514,33 +523,29 @@
     means, u, bias = call(
         norm_kernel,
         [shape((ROWS, FEAT), F32), shape((ROWS, FEAT), BF16), shape((16, FEAT), BF16)],
-        [info, sums, sizes, head, above, below, norm_gain.reshape(8, FEAT)],
+        [info, sums, sizes, head, above, below, norm_gain.reshape(8, FEAT), loaded],
     )
     first, sibling, second = y_one(u), swap(u), y_other(u)
     across = swap(first)
     part, part_query = shape((SEG, COLS), F32), shape((ROWS, COLS), F32)
-    kept = shape((4, FEAT, COLS), BF16)
-    queried, keyed, valued, *late = call(
+    queried, keyed, valued = call(
         early_kernel,
-        [part_query, part, part] + [kept] * 3,
-        [info, u, first, second, sibling, w_query, w_key, w_value],
-        scratch=[pltpu.VMEM((4, FEAT, COLS), BF16)] * 3 + [pltpu.SemaphoreType.DMA((2, 4, 3))],
+        [part_query, part, part],
+        [info, u, first, second, sibling, *weights],
         flops=ROWS * WIDTH * 3 * COLS,
-        moved=6 << 20,
-        far_in=(5, 6, 7),
-        room=ROOM,
-    )
-    (far,) = gate(info, [y_one(first)], queried)
+        moved=3 << 20,
+    )
+    far = y_one(first)
     blocks = [u, first, second, far, sibling, across, swap(second), swap(far)]
     (kv,) = call(
         key_value_kernel,
         [shape((ROWS, 2 * COLS), BF16)],
-        [info] + blocks + [late[1], late[2], keyed, valued, bias],
+        [info] + blocks + [weights[1], weights[2], keyed, valued, bias],
     )
     (query,) = call(
         query_kernel,
         [shape((ROWS, COLS), BF16)],
-        [info] + blocks + [late[0], queried, kv],
+        [info] + blocks + [weights[0], queried, kv],
         far_in=(11,),
     )
     queries = [query] + [x_by(query, k) for k in (1, 2, 3)]

time: 113 us -> 115 us (1.018)
    ppermute x25, waiting for transfers between devices: 46.3 us -> 48.4 us  [move(): return lax.ppermute(value, ('seq', 'mp'), pairs)]
    ppermute x1, waiting for transfers between devices: 2 us -> 0.01 us  [shards(): below = lax.ppermute(tail, 'seq', [(i, i + 1) for i in range(count - 1)])]
    pallas_call x1, Pallas kernels: 3.01 us -> 4.43 us  [output(): pl.pallas_call(output_kernel, grid=(TOK // BLOCK,), out_shape=shape((TOK,...]
  transfers between devices with their start and end apart: 27 -> 27, of which waited for: 14 -> 13; matrix products, arithmetic and copies ran while one was open for 1% -> 1% of each run, Pallas kernels for 13% -> 13%
where the time goes in v6:
time: 115 us; the launch traced here: 113 us
  waiting for transfers between devices  48.4 us (42%)
  starting transfers between devices  38.7 us (34%)
  Pallas kernels  23 us (20%)
  local copies, waits for them, and re-layouts  3 us (3%)
    ppermute x25, waiting for transfers between devices, move(): return lax.ppermute(value, ('seq', 'mp'), pairs)  48.4 us
    ppermute x25, starting transfers between devices, move(): return lax.ppermute(value, ('seq', 'mp'), pairs)  32.5 us
    pallas_call x17, Pallas kernels, call(): pl.pallas_call(body, out_shape=outs, in_specs=[SMEM if i == scalars else...  18.6 us
    pallas_call x1, Pallas kernels, output(): pl.pallas_call(output_kernel, grid=(TOK // BLOCK,), out_shape=shape((TOK,...  4.43 us
    ppermute x1, starting transfers between devices, shards(): above = lax.ppermute(head, 'seq', [(i, i - 1) for i in range(1, count)])  4.31 us
    unnamed x10, local copies, waits for them, and re-layouts  2.3 us
  transfers between devices with their start and end apart: 27, of which 13 were waited for; matrix products, arithmetic and copies ran while one was open for 1% of the time, Pallas kernels for 13%

profile of v6, /device:TPU:2, one launch (start us, length us, event | category | flops | bytes accessed | tf_op | source)
XLA Modules:
  0.0 113.4 jit_solution(17159956857390722324)
XLA Ops:
  0.0 1.6 %copy-done.1 = bf16[2048,512]{1,0:T(8,128)(2,1)S(1)} copy-done((bf16[2048,512]{1,0:T(8,128)(2,1)S(1)}, bf16[2048,512]{1,0:T(8,128)(2,1)}, u32[]{:S(2)}) %copy-start.1) | copy-done | bytes 2097176
  3.0 4.3 %collective-permute-start = (f32[8,640]{1,0:T(8,128)S(1)}, f32[8,640]{1,0:T(8,128)S(1)}, u32[]{:S(2)}, u32[]{:S(2)}) collective-permute-start(f32[8,640]{1,0:T(8,128)S(1)} %get-tuple-element.40.head), channel_id=1, source_target_pairs={{8,0},{16,8},{24,16},{32,24},{40,32},{48,40},{56,48},{64,56},{72,6... | collective-permute-start | bytes 61448 | tf_op jit(solution)/shard_map/ppermute | solution.py:502
  7.3 1.9 %collective-permute-start.1 = (f32[8,640]{1,0:T(8,128)S(1)}, f32[8,640]{1,0:T(8,128)S(1)}, u32[]{:S(2)}, u32[]{:S(2)}) collective-permute-start(f32[8,640]{1,0:T(8,128)S(1)} %get-tuple-element.41._), channel_id=1, source_target_pairs={{0,8},{8,16},{16,24},{24,32},{32,40},{40,48},{48,56},{56,64},{64,7... | collective-permute-start | bytes 61448 | tf_op jit(solution)/shard_map/ppermute | solution.py:503
  11.0 2.9 %shard_map.84 = (bf16[4096,256]{1,0:T(8,128)(2,1)S(1)}, bf16[4096,256]{1,0:T(8,128)(2,1)S(1)}, bf16[4096,256]{1,0:T(8,128)(2,1)S(1)}, f32[8,128]{1,0:T(8,128)S(1)}) custom-call(f32[8,640]{1,0:T(8,128)S(1)} %get-tuple-element.41._, bf16[4096,256]{1,0:T(8,128)(2,1)} %refs_0_.1, bf16[4096,256]{1,0:T(8,128)(2,1)} %refs_1_.1, bf16[4096,256]{1,0:T(8,128)(2,1)} %refs_2_.1), custom_call_target="tpu_custom_call" | custom-call | bytes 12582912 | tf_op jit(solution)/shard_map/pallas_call | solution.py:105
  14.7 1.4 %collective-permute-start.2 = (bf16[272,512]{1,0:T(8,128)(2,1)S(1)}, bf16[272,512]{1,0:T(8,128)(2,1)S(1)}, u32[]{:S(2)}, u32[]{:S(2)}) collective-permute-start(bf16[272,512]{1,0:T(8,128)(2,1)S(1)} %get-tuple-element.43.refs_0_), channel_id=1, source_target_pairs={{0,2},{1,7},{2,4},{3,1},{4,6},{5,3},{6,0},{7,5},{8,10},{9,15},{10,... | collective-permute-start | bytes 835592 | tf_op jit(solution)/shard_map/ppermute | solution.py:41
  16.1 1.9 %collective-permute-start.3 = (bf16[272,512]{1,0:T(8,128)(2,1)S(1)}, bf16[272,512]{1,0:T(8,128)(2,1)S(1)}, u32[]{:S(2)}, u32[]{:S(2)}) collective-permute-start(bf16[272,512]{1,0:T(8,128)(2,1)S(1)} %get-tuple-element.43.refs_0_), channel_id=1, source_target_pairs={{0,6},{1,3},{2,0},{3,5},{4,2},{5,7},{6,4},{7,1},{8,14},{9,11},{10,... | collective-permute-start | bytes 835592 | tf_op jit(solution)/shard_map/ppermute | solution.py:41
  18.0 6.8 %collective-permute-done.2.refs_1_ = bf16[272,512]{1,0:T(8,128)(2,1)S(1)} collective-permute-done((bf16[272,512]{1,0:T(8,128)(2,1)S(1)}, bf16[272,512]{1,0:T(8,128)(2,1)S(1)}, u32[]{:S(2)}, u32[]{:S(2)}) %collective-permute-start.2) | collective-permute-done | bytes 278560 | tf_op jit(solution)/shard_map/ppermute | solution.py:41
  25.9 6.6 %collective-permute-done.4.refs_3_ = bf16[272,512]{1,0:T(8,128)(2,1)S(1)} collective-permute-done((bf16[272,512]{1,0:T(8,128)(2,1)S(1)}, bf16[272,512]{1,0:T(8,128)(2,1)S(1)}, u32[]{:S(2)}, u32[]{:S(2)}) %collective-permute-start.4) | collective-permute-done | bytes 278560 | tf_op jit(solution)/shard_map/ppermute | solution.py:41
  32.5 1.5 %shard_map.86 = (f32[272,256]{1,0:T(8,128)S(1)}, f32[256,256]{1,0:T(8,128)S(1)}, f32[256,256]{1,0:T(8,128)S(1)}) custom-call(s32[32]{0:T(128)S(1)} %dynamic-slice_bitcast_fusion.info.refs_0_, bf16[272,512]{1,0:T(8,128)(2,1)S(1)} %get-tuple-element.43.refs_0_, bf16[272,512]{1,0:T(8,128)(2,1)S(1)} %collective-permute-done.2.refs_1_, ...), custom_call_target="tpu_custom_call" | custom-call | flops 855638016 | bytes 3145728 | tf_op jit(solution)/shard_map/pallas_call | solution.py:105
  34.1 1.3 %shard_map.87.refs_10_.refs_4_ = bf16[272,512]{1,0:T(8,128)(2,1)S(1)} custom-call(s32[32]{0:T(128)S(1)} %dynamic-slice_bitcast_fusion.info.refs_0_, bf16[272,512]{1,0:T(8,128)(2,1)S(1)} %get-tuple-element.43.refs_0_, bf16[272,512]{1,0:T(8,128)(2,1)S(1)} %collective-permute-done.2.refs_1_, bf16[272,512]{1,0:T(8,128)(2,1)S(1)} %collective-permute-done.3.refs_2_, ...), custom_call_target="tpu_custom_call" | custom-call | tf_op jit(solution)/shard_map/pallas_call | solution.py:105
  35.4 1.4 %collective-permute-start.12 = (bf16[272,512]{1,0:T(8,128)(2,1)S(1)}, bf16[272,512]{1,0:T(8,128)(2,1)S(1)}, u32[]{:S(2)}, u32[]{:S(2)}) collective-permute-start(bf16[272,512]{1,0:T(8,128)(2,1)S(1)} %shard_map.87.refs_10_.refs_4_), channel_id=1, source_target_pairs={{0,32},{1,225},{2,34},{3,227},{4,36},{5,229},{6,38},{7,231},{8,40}... | collective-permute-start | bytes 835592 | tf_op jit(solution)/shard_map/ppermute | solution.py:41
  36.8 4.0 %collective-permute-start.14 = (bf16[272,512]{1,0:T(8,128)(2,1)S(1)}, bf16[272,512]{1,0:T(8,128)(2,1)S(1)}, u32[]{:S(2)}, u32[]{:S(2)}) collective-permute-start(bf16[272,512]{1,0:T(8,128)(2,1)S(1)} %shard_map.87.refs_10_.refs_4_), channel_id=1, source_target_pairs={{0,224},{1,33},{2,226},{3,35},{4,228},{5,37},{6,230},{7,39},{8,232... | collective-permute-start | bytes 835592 | tf_op jit(solution)/shard_map/ppermute | solution.py:41
  41.9 1.5 %collective-permute-start.9 = (bf16[272,256]{1,0:T(8,128)(2,1)S(1)}, bf16[272,256]{1,0:T(8,128)(2,1)S(1)}, u32[]{:S(2)}, u32[]{:S(2)}) collective-permute-start(bf16[272,256]{1,0:T(8,128)(2,1)S(1)} %shard_map.88.refs_0_.refs_1_), channel_id=1, source_target_pairs={{0,8},{1,9},{2,10},{3,11},{4,12},{5,13},{6,14},{7,15},{8,16},{9,17... | collective-permute-start | bytes 417800 | tf_op jit(solution)/shard_map/ppermute | solution.py:41
  43.4 4.4 %collective-permute-start.10 = (bf16[272,256]{1,0:T(8,128)(2,1)S(1)}, bf16[272,256]{1,0:T(8,128)(2,1)S(1)}, u32[]{:S(2)}, u32[]{:S(2)}) collective-permute-start(bf16[272,256]{1,0:T(8,128)(2,1)S(1)} %shard_map.88.refs_0_.refs_1_), channel_id=1, source_target_pairs={{0,16},{1,17},{2,18},{3,19},{4,20},{5,21},{6,22},{7,23},{8,24},{9,... | collective-permute-start | bytes 417800 | tf_op jit(solution)/shard_map/ppermute | solution.py:41
  47.8 3.2 %collective-permute-start.15 = (bf16[272,512]{1,0:T(8,128)(2,1)S(1)}, bf16[272,512]{1,0:T(8,128)(2,1)S(1)}, u32[]{:S(2)}, u32[]{:S(2)}) collective-permute-start(bf16[272,512]{1,0:T(8,128)(2,1)S(1)} %collective-permute-done.14.refs_6_), channel_id=1, source_target_pairs={{0,224},{1,33},{2,226},{3,35},{4,228},{5,37},{6,230},{7,39},{8,232... | collective-permute-start | bytes 835592 | tf_op jit(solution)/shard_map/ppermute | solution.py:41
  51.0 1.2 %collective-permute-done.10.refs_2_.refs_3_ = bf16[272,256]{1,0:T(8,128)(2,1)S(1)} collective-permute-done((bf16[272,256]{1,0:T(8,128)(2,1)S(1)}, bf16[272,256]{1,0:T(8,128)(2,1)S(1)}, u32[]{:S(2)}, u32[]{:S(2)}) %collective-permute-start.10) | collective-permute-done | bytes 139296 | tf_op jit(solution)/shard_map/ppermute | solution.py:41
  52.3 2.2 %collective-permute-done.11.refs_3_.refs_4_ = bf16[272,256]{1,0:T(8,128)(2,1)S(1)} collective-permute-done((bf16[272,256]{1,0:T(8,128)(2,1)S(1)}, bf16[272,256]{1,0:T(8,128)(2,1)S(1)}, u32[]{:S(2)}, u32[]{:S(2)}) %collective-permute-start.11) | collective-permute-done | bytes 139296 | tf_op jit(solution)/shard_map/ppermute | solution.py:41
  54.5 2.1 %shard_map.89 = (f32[4,2,272,256]{3,2,1,0:T(8,128)S(1)}, f32[4,2,272,128]{3,2,1,0:T(8,128)S(1)}, f32[8,128]{1,0:T(8,128)S(1)}) custom-call(s32[32]{0:T(128)S(1)} %dynamic-slice_bitcast_fusion.info.refs_0_, bf16[272,256]{1,0:T(8,128)(2,1)S(1)} %shard_map.88.refs_0_.refs_1_, bf16[272,256]{1,0:T(8,128)(2,1)S(1)} %collective-permute-done.9.refs_1_.refs_2_, ...), custom_call_target="tpu_custom_call" | custom-call | flops 855638016 | bytes 4194304 | tf_op jit(solution)/shard_map/pallas_call | solution.py:105
  58.1 4.9 %collective-permute-start.18 = (bf16[272,512]{1,0:T(8,128)(2,1)S(1)}, bf16[272,512]{1,0:T(8,128)(2,1)S(1)}, u32[]{:S(2)}, u32[]{:S(2)}) collective-permute-start(bf16[272,512]{1,0:T(8,128)(2,1)S(1)} %get-tuple-element.53.refs_5_), channel_id=1, source_target_pairs={{0,224},{1,33},{2,226},{3,35},{4,228},{5,37},{6,230},{7,39},{8,232... | collective-permute-start | bytes 835592 | tf_op jit(solution)/shard_map/ppermute | solution.py:41
  63.0 4.9 %collective-permute-done.16.refs_4_ = bf16[272,512]{1,0:T(8,128)(2,1)S(1)} collective-permute-done((bf16[272,512]{1,0:T(8,128)(2,1)S(1)}, bf16[272,512]{1,0:T(8,128)(2,1)S(1)}, u32[]{:S(2)}, u32[]{:S(2)}) %collective-permute-start.16) | collective-permute-done | bytes 278560 | tf_op jit(solution)/shard_map/ppermute | solution.py:41
  67.9 1.1 %shard_map.91 = (f32[4,2,272,256]{3,2,1,0:T(8,128)S(1)}, f32[4,2,272,128]{3,2,1,0:T(8,128)S(1)}, f32[8,128]{1,0:T(8,128)}) custom-call(s32[32]{0:T(128)S(1)} %dynamic-slice_bitcast_fusion.info.refs_0_, bf16[272,256]{1,0:T(8,128)(2,1)S(1)} %shard_map.88.refs_0_.refs_1_, ...), custom_call_target="tpu_custom_call", output_to_operand_aliasing={{0}: (7, {}), {1}: (8, {})} | custom-call | flops 570425344 | bytes 4194304 | tf_op jit(solution)/shard_map/pallas_call | solution.py:105
  70.5 6.0 %collective-permute-done.17.refs_5_ = bf16[272,512]{1,0:T(8,128)(2,1)S(1)} collective-permute-done((bf16[272,512]{1,0:T(8,128)(2,1)S(1)}, bf16[272,512]{1,0:T(8,128)(2,1)S(1)}, u32[]{:S(2)}, u32[]{:S(2)}) %collective-permute-start.17) | collective-permute-done | bytes 278560 | tf_op jit(solution)/shard_map/ppermute | solution.py:41
  77.4 2.6 %collective-permute-start.19 = (bf16[272,256]{1,0:T(8,128)(2,1)S(1)}, bf16[272,256]{1,0:T(8,128)(2,1)S(1)}, u32[]{:S(2)}, u32[]{:S(2)}) collective-permute-start(bf16[272,256]{1,0:T(8,128)(2,1)S(1)} %get-tuple-element.61), channel_id=1, source_target_pairs={{0,24},{1,25},{2,26},{3,27},{4,28},{5,29},{6,30},{7,31},{8,0},{9,1... | collective-permute-start | bytes 417800 | tf_op jit(solution)/shard_map/ppermute | solution.py:41
  80.0 2.3 %collective-permute-start.21 = (bf16[272,256]{1,0:T(8,128)(2,1)S(1)}, bf16[272,256]{1,0:T(8,128)(2,1)S(1)}, u32[]{:S(2)}, u32[]{:S(2)}) collective-permute-start(bf16[272,256]{1,0:T(8,128)(2,1)S(1)} %get-tuple-element.63), channel_id=1, source_target_pairs={{0,8},{1,9},{2,10},{3,11},{4,12},{5,13},{6,14},{7,15},{8,16},{9,17... | collective-permute-start | bytes 417800 | tf_op jit(solution)/shard_map/ppermute | solution.py:41
  82.3 1.7 %collective-permute-done.19.b = bf16[272,256]{1,0:T(8,128)(2,1)S(1)} collective-permute-done((bf16[272,256]{1,0:T(8,128)(2,1)S(1)}, bf16[272,256]{1,0:T(8,128)(2,1)S(1)}, u32[]{:S(2)}, u32[]{:S(2)}) %collective-permute-start.19) | collective-permute-done | bytes 139296 | tf_op jit(solution)/shard_map/ppermute | solution.py:41
  83.9 2.6 %collective-permute-done.20.c = bf16[272,256]{1,0:T(8,128)(2,1)S(1)} collective-permute-done((bf16[272,256]{1,0:T(8,128)(2,1)S(1)}, bf16[272,256]{1,0:T(8,128)(2,1)S(1)}, u32[]{:S(2)}, u32[]{:S(2)}) %collective-permute-start.20) | collective-permute-done | bytes 139296 | tf_op jit(solution)/shard_map/ppermute | solution.py:41
  88.4 1.3 %collective-permute-done.22.other = bf16[272,256]{1,0:T(8,128)(2,1)S(1)} collective-permute-done((bf16[272,256]{1,0:T(8,128)(2,1)S(1)}, bf16[272,256]{1,0:T(8,128)(2,1)S(1)}, u32[]{:S(2)}, u32[]{:S(2)}) %collective-permute-start.22) | collective-permute-done | bytes 139296 | tf_op jit(solution)/shard_map/ppermute | solution.py:41
  89.7 1.3 %shard_map.96 = (f32[272,512]{1,0:T(8,128)S(1)}, f32[272,512]{1,0:T(8,128)S(1)}, bf16[272,512]{1,0:T(8,128)(2,1)S(1)}, bf16[272,512]{1,0:T(8,128)(2,1)S(1)}) custom-call(s32[32]{0:T(128)S(1)} %dynamic-slice_bitcast_fusion.info.refs_0_, bf16[272,256]{1,0:T(8,128)(2,1)S(1)} %shard_map.94.attended, bf16[272,256]{1,0:T(8,128)(2,1)S(1)} %collective-permute-done.22.other, ...), custom_call_target="tpu_custom_call" | custom-call | flops 570425344 | bytes 4194304 | tf_op jit(solution)/shard_map/pallas_call | solution.py:105
  91.1 3.2 %collective-permute-start.26 = (bf16[272,512]{1,0:T(8,128)(2,1)S(1)}, bf16[272,512]{1,0:T(8,128)(2,1)S(1)}, u32[]{:S(2)}, u32[]{:S(2)}) collective-permute-start(bf16[272,512]{1,0:T(8,128)(2,1)S(1)} %get-tuple-element.68), channel_id=1, source_target_pairs={{0,6},{1,3},{2,0},{3,5},{4,2},{5,7},{6,4},{7,1},{8,14},{9,11},{10,... | collective-permute-start | bytes 835592 | tf_op jit(solution)/shard_map/ppermute | solution.py:41
  94.3 6.8 %collective-permute-done.24.b = bf16[272,512]{1,0:T(8,128)(2,1)S(1)} collective-permute-done((bf16[272,512]{1,0:T(8,128)(2,1)S(1)}, bf16[272,512]{1,0:T(8,128)(2,1)S(1)}, u32[]{:S(2)}, u32[]{:S(2)}) %collective-permute-start.24) | collective-permute-done | bytes 278560 | tf_op jit(solution)/shard_map/ppermute | solution.py:41
  101.7 7.3 %collective-permute-done.25.first = bf16[272,512]{1,0:T(8,128)(2,1)S(1)} collective-permute-done((bf16[272,512]{1,0:T(8,128)(2,1)S(1)}, bf16[272,512]{1,0:T(8,128)(2,1)S(1)}, u32[]{:S(2)}, u32[]{:S(2)}) %collective-permute-start.25) | collective-permute-done | bytes 278560 | tf_op jit(solution)/shard_map/ppermute | solution.py:41
  109.0 4.4 %shard_map.99 = bf16[2048,512]{1,0:T(8,128)(2,1)} custom-call(f32[272,512]{1,0:T(8,128)S(1)} %get-tuple-element.65.own, bf16[272,512]{1,0:T(8,128)(2,1)S(1)} %collective-permute-done.25.first, bf16[272,512]{1,0:T(8,128)(2,1)S(1)} %collective-permute-done.26.second, bf16[2048,384]{1,0:T(8,128)(2,1)S(1)} %shard_map.98.hot, bf16[2048,512]{1,0:T(8,128)(2,1)S(1)} %copy-done.2), custom_call_target="tpu_custom_call" | custom-call | flops 2147483648 | bytes 6291456 | tf_op jit(solution)/shard_map/pallas_call | solution.py:451
  (52 shorter events, 12.3 us)
Async XLA Ops:
  0.0 1.6 %copy-start.1 = (bf16[2048,512]{1,0:T(8,128)(2,1)S(1)}, bf16[2048,512]{1,0:T(8,128)(2,1)}, u32[]{:S(2)}) copy-start(bf16[2048,512]{1,0:T(8,128)(2,1)} %tokens.5) | copy-start | bytes 6291460
  1.6 0.7 copy-start.3
  2.3 7.7 %copy-start.2 = (bf16[2048,512]{1,0:T(8,128)(2,1)S(1)}, bf16[2048,512]{1,0:T(8,128)(2,1)}, u32[]{:S(2)}) copy-start(bf16[2048,512]{1,0:T(8,128)(2,1)} %tokens.5) | copy-start | bytes 6291460
  3.0 8.0 %copy-start.4 = (f32[4096]{0:T(1024)S(1)}, f32[4096]{0:T(1024)}, u32[]{:S(2)}) copy-start(f32[4096]{0:T(1024)} %param.10) | copy-start | bytes 49156
  3.0 10.9 %collective-permute-start = (f32[8,640]{1,0:T(8,128)S(1)}, f32[8,640]{1,0:T(8,128)S(1)}, u32[]{:S(2)}, u32[]{:S(2)}) collective-permute-start(f32[8,640]{1,0:T(8,128)S(1)} %get-tuple-element.40.head), channel_id=1, source_target_pairs={{8,0},{16,8},{24,16},{32,24},{40,32},{48,40},{56,48},{64,56},{72,6... | collective-permute-start | bytes 61448 | tf_op jit(solution)/shard_map/ppermute | solution.py:502
  7.3 6.6 %collective-permute-start.1 = (f32[8,640]{1,0:T(8,128)S(1)}, f32[8,640]{1,0:T(8,128)S(1)}, u32[]{:S(2)}, u32[]{:S(2)}) collective-permute-start(f32[8,640]{1,0:T(8,128)S(1)} %get-tuple-element.41._), channel_id=1, source_target_pairs={{0,8},{8,16},{16,24},{24,32},{32,40},{40,48},{48,56},{56,64},{64,7... | collective-permute-start | bytes 61448 | tf_op jit(solution)/shard_map/ppermute | solution.py:503
  14.7 10.1 %collective-permute-start.2 = (bf16[272,512]{1,0:T(8,128)(2,1)S(1)}, bf16[272,512]{1,0:T(8,128)(2,1)S(1)}, u32[]{:S(2)}, u32[]{:S(2)}) collective-permute-start(bf16[272,512]{1,0:T(8,128)(2,1)S(1)} %get-tuple-element.43.refs_0_), channel_id=1, source_target_pairs={{0,2},{1,7},{2,4},{3,1},{4,6},{5,3},{6,0},{7,5},{8,10},{9,15},{10,... | collective-permute-start | bytes 835592 | tf_op jit(solution)/shard_map/ppermute | solution.py:41
  16.1 9.8 %collective-permute-start.3 = (bf16[272,512]{1,0:T(8,128)(2,1)S(1)}, bf16[272,512]{1,0:T(8,128)(2,1)S(1)}, u32[]{:S(2)}, u32[]{:S(2)}) collective-permute-start(bf16[272,512]{1,0:T(8,128)(2,1)S(1)} %get-tuple-element.43.refs_0_), channel_id=1, source_target_pairs={{0,6},{1,3},{2,0},{3,5},{4,2},{5,7},{6,4},{7,1},{8,14},{9,11},{10,... | collective-permute-start | bytes 835592 | tf_op jit(solution)/shard_map/ppermute | solution.py:41
  24.7 7.8 %collective-permute-start.4 = (bf16[272,512]{1,0:T(8,128)(2,1)S(1)}, bf16[272,512]{1,0:T(8,128)(2,1)S(1)}, u32[]{:S(2)}, u32[]{:S(2)}) collective-permute-start(bf16[272,512]{1,0:T(8,128)(2,1)S(1)} %collective-permute-done.2.refs_1_), channel_id=1, source_target_pairs={{0,2},{1,7},{2,4},{3,1},{4,6},{5,3},{6,0},{7,5},{8,10},{9,15},{10,... | collective-permute-start | bytes 835592 | tf_op jit(solution)/shard_map/ppermute | solution.py:41
  25.4 7.2 %collective-permute-start.5 = (bf16[272,512]{1,0:T(8,128)(2,1)S(1)}, bf16[272,512]{1,0:T(8,128)(2,1)S(1)}, u32[]{:S(2)}, u32[]{:S(2)}) collective-permute-start(bf16[272,512]{1,0:T(8,128)(2,1)S(1)} %get-tuple-element.43.refs_0_), channel_id=1, source_target_pairs={{0,1},{1,0},{2,3},{3,2},{4,5},{5,4},{6,7},{7,6},{8,9},{9,8},{10,11... | collective-permute-start | bytes 835592 | tf_op jit(solution)/shard_map/ppermute | solution.py:41
  25.4 8.7 %collective-permute-start.6 = (bf16[272,512]{1,0:T(8,128)(2,1)S(1)}, bf16[272,512]{1,0:T(8,128)(2,1)S(1)}, u32[]{:S(2)}, u32[]{:S(2)}) collective-permute-start(bf16[272,512]{1,0:T(8,128)(2,1)S(1)} %collective-permute-done.2.refs_1_), channel_id=1, source_target_pairs={{0,1},{1,0},{2,3},{3,2},{4,5},{5,4},{6,7},{7,6},{8,9},{9,8},{10,11... | collective-permute-start | bytes 835592 | tf_op jit(solution)/shard_map/ppermute | solution.py:41
  25.9 8.2 %collective-permute-start.7 = (bf16[272,512]{1,0:T(8,128)(2,1)S(1)}, bf16[272,512]{1,0:T(8,128)(2,1)S(1)}, u32[]{:S(2)}, u32[]{:S(2)}) collective-permute-start(bf16[272,512]{1,0:T(8,128)(2,1)S(1)} %collective-permute-done.3.refs_2_), channel_id=1, source_target_pairs={{0,1},{1,0},{2,3},{3,2},{4,5},{5,4},{6,7},{7,6},{8,9},{9,8},{10,11... | collective-permute-start | bytes 835592 | tf_op jit(solution)/shard_map/ppermute | solution.py:41
  32.5 1.6 %collective-permute-start.8 = (bf16[272,512]{1,0:T(8,128)(2,1)S(1)}, bf16[272,512]{1,0:T(8,128)(2,1)S(1)}, u32[]{:S(2)}, u32[]{:S(2)}) collective-permute-start(bf16[272,512]{1,0:T(8,128)(2,1)S(1)} %collective-permute-done.4.refs_3_), channel_id=1, source_target_pairs={{0,1},{1,0},{2,3},{3,2},{4,5},{5,4},{6,7},{7,6},{8,9},{9,8},{10,11... | collective-permute-start | bytes 835592 | tf_op jit(solution)/shard_map/ppermute | solution.py:41
  35.4 12.4 %collective-permute-start.12 = (bf16[272,512]{1,0:T(8,128)(2,1)S(1)}, bf16[272,512]{1,0:T(8,128)(2,1)S(1)}, u32[]{:S(2)}, u32[]{:S(2)}) collective-permute-start(bf16[272,512]{1,0:T(8,128)(2,1)S(1)} %shard_map.87.refs_10_.refs_4_), channel_id=1, source_target_pairs={{0,32},{1,225},{2,34},{3,227},{4,36},{5,229},{6,38},{7,231},{8,40}... | collective-permute-start | bytes 835592 | tf_op jit(solution)/shard_map/ppermute | solution.py:41
  36.8 11.0 %collective-permute-start.14 = (bf16[272,512]{1,0:T(8,128)(2,1)S(1)}, bf16[272,512]{1,0:T(8,128)(2,1)S(1)}, u32[]{:S(2)}, u32[]{:S(2)}) collective-permute-start(bf16[272,512]{1,0:T(8,128)(2,1)S(1)} %shard_map.87.refs_10_.refs_4_), channel_id=1, source_target_pairs={{0,224},{1,33},{2,226},{3,35},{4,228},{5,37},{6,230},{7,39},{8,232... | collective-permute-start | bytes 835592 | tf_op jit(solution)/shard_map/ppermute | solution.py:41
  41.8 14.8 %copy-start = (bf16[256,4096]{1,0:T(8,128)(2,1)S(1)}, bf16[256,4096]{1,0:T(8,128)(2,1)}, u32[]{:S(2)}) copy-start(bf16[256,4096]{1,0:T(8,128)(2,1)} %w_out.3) | copy-start | bytes 6291460
  41.9 9.2 %collective-permute-start.9 = (bf16[272,256]{1,0:T(8,128)(2,1)S(1)}, bf16[272,256]{1,0:T(8,128)(2,1)S(1)}, u32[]{:S(2)}, u32[]{:S(2)}) collective-permute-start(bf16[272,256]{1,0:T(8,128)(2,1)S(1)} %shard_map.88.refs_0_.refs_1_), channel_id=1, source_target_pairs={{0,8},{1,9},{2,10},{3,11},{4,12},{5,13},{6,14},{7,15},{8,16},{9,17... | collective-permute-start | bytes 417800 | tf_op jit(solution)/shard_map/ppermute | solution.py:41
  43.4 8.9 %collective-permute-start.10 = (bf16[272,256]{1,0:T(8,128)(2,1)S(1)}, bf16[272,256]{1,0:T(8,128)(2,1)S(1)}, u32[]{:S(2)}, u32[]{:S(2)}) collective-permute-start(bf16[272,256]{1,0:T(8,128)(2,1)S(1)} %shard_map.88.refs_0_.refs_1_), channel_id=1, source_target_pairs={{0,16},{1,17},{2,18},{3,19},{4,20},{5,21},{6,22},{7,23},{8,24},{9,... | collective-permute-start | bytes 417800 | tf_op jit(solution)/shard_map/ppermute | solution.py:41
  47.8 6.7 %collective-permute-start.11 = (bf16[272,256]{1,0:T(8,128)(2,1)S(1)}, bf16[272,256]{1,0:T(8,128)(2,1)S(1)}, u32[]{:S(2)}, u32[]{:S(2)}) collective-permute-start(bf16[272,256]{1,0:T(8,128)(2,1)S(1)} %shard_map.88.refs_0_.refs_1_), channel_id=1, source_target_pairs={{0,24},{1,25},{2,26},{3,27},{4,28},{5,29},{6,30},{7,31},{8,0},{9,1... | collective-permute-start | bytes 417800 | tf_op jit(solution)/shard_map/ppermute | solution.py:41
  47.8 9.6 %collective-permute-start.13 = (bf16[272,512]{1,0:T(8,128)(2,1)S(1)}, bf16[272,512]{1,0:T(8,128)(2,1)S(1)}, u32[]{:S(2)}, u32[]{:S(2)}) collective-permute-start(bf16[272,512]{1,0:T(8,128)(2,1)S(1)} %collective-permute-done.12.refs_5_), channel_id=1, source_target_pairs={{0,32},{1,225},{2,34},{3,227},{4,36},{5,229},{6,38},{7,231},{8,40}... | collective-permute-start | bytes 835592 | tf_op jit(solution)/shard_map/ppermute | solution.py:41
  47.8 9.6 %collective-permute-start.15 = (bf16[272,512]{1,0:T(8,128)(2,1)S(1)}, bf16[272,512]{1,0:T(8,128)(2,1)S(1)}, u32[]{:S(2)}, u32[]{:S(2)}) collective-permute-start(bf16[272,512]{1,0:T(8,128)(2,1)S(1)} %collective-permute-done.14.refs_6_), channel_id=1, source_target_pairs={{0,224},{1,33},{2,226},{3,35},{4,228},{5,37},{6,230},{7,39},{8,232... | collective-permute-start | bytes 835592 | tf_op jit(solution)/shard_map/ppermute | solution.py:41
  57.3 31.0 %collective-permute-start.23 = (bf16[4,256,512]{2,1,0:T(8,128)(2,1)S(1)}, bf16[4,256,512]{2,1,0:T(8,128)(2,1)S(1)}, u32[]{:S(2)}, u32[]{:S(2)}) collective-permute-start(bf16[4,256,512]{2,1,0:T(8,128)(2,1)S(1)} %shard_map.95), channel_id=1, source_target_pairs={{0,1},{1,0},{2,3},{3,2},{4,5},{5,4},{6,7},{7,6},{8,9},{9,8},{10,11... | collective-permute-start | bytes 3145736 | tf_op jit(solution)/shard_map/ppermute | solution.py:41
  58.0 9.9 %collective-permute-start.16 = (bf16[272,512]{1,0:T(8,128)(2,1)S(1)}, bf16[272,512]{1,0:T(8,128)(2,1)S(1)}, u32[]{:S(2)}, u32[]{:S(2)}) collective-permute-start(bf16[272,512]{1,0:T(8,128)(2,1)S(1)} %get-tuple-element.52.refs_4_), channel_id=1, source_target_pairs={{0,32},{1,225},{2,34},{3,227},{4,36},{5,229},{6,38},{7,231},{8,40}... | collective-permute-start | bytes 835592 | tf_op jit(solution)/shard_map/ppermute | solution.py:41
  58.1 11.3 %collective-permute-start.18 = (bf16[272,512]{1,0:T(8,128)(2,1)S(1)}, bf16[272,512]{1,0:T(8,128)(2,1)S(1)}, u32[]{:S(2)}, u32[]{:S(2)}) collective-permute-start(bf16[272,512]{1,0:T(8,128)(2,1)S(1)} %get-tuple-element.53.refs_5_), channel_id=1, source_target_pairs={{0,224},{1,33},{2,226},{3,35},{4,228},{5,37},{6,230},{7,39},{8,232... | collective-permute-start | bytes 835592 | tf_op jit(solution)/shard_map/ppermute | solution.py:41
  67.9 8.6 %collective-permute-start.17 = (bf16[272,512]{1,0:T(8,128)(2,1)S(1)}, bf16[272,512]{1,0:T(8,128)(2,1)S(1)}, u32[]{:S(2)}, u32[]{:S(2)}) collective-permute-start(bf16[272,512]{1,0:T(8,128)(2,1)S(1)} %collective-permute-done.16.refs_4_), channel_id=1, source_target_pairs={{0,32},{1,225},{2,34},{3,227},{4,36},{5,229},{6,38},{7,231},{8,40}... | collective-permute-start | bytes 835592 | tf_op jit(solution)/shard_map/ppermute | solution.py:41
  77.4 6.5 %collective-permute-start.19 = (bf16[272,256]{1,0:T(8,128)(2,1)S(1)}, bf16[272,256]{1,0:T(8,128)(2,1)S(1)}, u32[]{:S(2)}, u32[]{:S(2)}) collective-permute-start(bf16[272,256]{1,0:T(8,128)(2,1)S(1)} %get-tuple-element.61), channel_id=1, source_target_pairs={{0,24},{1,25},{2,26},{3,27},{4,28},{5,29},{6,30},{7,31},{8,0},{9,1... | collective-permute-start | bytes 417800 | tf_op jit(solution)/shard_map/ppermute | solution.py:41
  80.0 6.6 %collective-permute-start.20 = (bf16[272,256]{1,0:T(8,128)(2,1)S(1)}, bf16[272,256]{1,0:T(8,128)(2,1)S(1)}, u32[]{:S(2)}, u32[]{:S(2)}) collective-permute-start(bf16[272,256]{1,0:T(8,128)(2,1)S(1)} %get-tuple-element.62), channel_id=1, source_target_pairs={{0,16},{1,17},{2,18},{3,19},{4,20},{5,21},{6,22},{7,23},{8,24},{9,... | collective-permute-start | bytes 417800 | tf_op jit(solution)/shard_map/ppermute | solution.py:41
  80.0 7.2 %collective-permute-start.21 = (bf16[272,256]{1,0:T(8,128)(2,1)S(1)}, bf16[272,256]{1,0:T(8,128)(2,1)S(1)}, u32[]{:S(2)}, u32[]{:S(2)}) collective-permute-start(bf16[272,256]{1,0:T(8,128)(2,1)S(1)} %get-tuple-element.63), channel_id=1, source_target_pairs={{0,8},{1,9},{2,10},{3,11},{4,12},{5,13},{6,14},{7,15},{8,16},{9,17... | collective-permute-start | bytes 417800 | tf_op jit(solution)/shard_map/ppermute | solution.py:41
  88.3 1.4 %collective-permute-start.22 = (bf16[272,256]{1,0:T(8,128)(2,1)S(1)}, bf16[272,256]{1,0:T(8,128)(2,1)S(1)}, u32[]{:S(2)}, u32[]{:S(2)}) collective-permute-start(bf16[272,256]{1,0:T(8,128)(2,1)S(1)} %shard_map.94.attended), channel_id=1, source_target_pairs={{0,1},{1,0},{2,3},{3,2},{4,5},{5,4},{6,7},{7,6},{8,9},{9,8},{10,11... | collective-permute-start | bytes 417800 | tf_op jit(solution)/shard_map/ppermute | solution.py:41
  91.0 10.1 %collective-permute-start.24 = (bf16[272,512]{1,0:T(8,128)(2,1)S(1)}, bf16[272,512]{1,0:T(8,128)(2,1)S(1)}, u32[]{:S(2)}, u32[]{:S(2)}) collective-permute-start(bf16[272,512]{1,0:T(8,128)(2,1)S(1)} %get-tuple-element.67), channel_id=1, source_target_pairs={{0,2},{1,7},{2,4},{3,1},{4,6},{5,3},{6,0},{7,5},{8,10},{9,15},{10,... | collective-permute-start | bytes 835592 | tf_op jit(solution)/shard_map/ppermute | solution.py:41
  91.1 10.6 %collective-permute-start.26 = (bf16[272,512]{1,0:T(8,128)(2,1)S(1)}, bf16[272,512]{1,0:T(8,128)(2,1)S(1)}, u32[]{:S(2)}, u32[]{:S(2)}) collective-permute-start(bf16[272,512]{1,0:T(8,128)(2,1)S(1)} %get-tuple-element.68), channel_id=1, source_target_pairs={{0,6},{1,3},{2,0},{3,5},{4,2},{5,7},{6,4},{7,1},{8,14},{9,11},{10,... | collective-permute-start | bytes 835592 | tf_op jit(solution)/shard_map/ppermute | solution.py:41
  101.2 7.8 %collective-permute-start.25 = (bf16[272,512]{1,0:T(8,128)(2,1)S(1)}, bf16[272,512]{1,0:T(8,128)(2,1)S(1)}, u32[]{:S(2)}, u32[]{:S(2)}) collective-permute-start(bf16[272,512]{1,0:T(8,128)(2,1)S(1)} %shard_map.97), channel_id=1, source_target_pairs={{0,2},{1,7},{2,4},{3,1},{4,6},{5,3},{6,0},{7,5},{8,10},{9,15},{10,... | collective-permute-start | bytes 835592 | tf_op jit(solution)/shard_map/ppermute | solution.py:41

commit v7 on v6

--- a/solution.py
+++ b/solution.py
@@ -303,10 +303,11 @@
     return jnp.concatenate([values, jnp.ones(values.shape, BF16)], axis=1)
 
 
-def attend_kernel(step, first, final, info, *refs):
+def attend_kernel(step, has_own, info, *refs):
+    first, final = step == 1, step == 4
     refs = list(refs)
     queries = [refs.pop(0) for _ in range(4)]
-    own = refs.pop(0) if first else None
+    own = refs.pop(0) if has_own else None
     others = [refs.pop(0) for _ in range(1 if final else 2)]
     if not first:
         state_in = [refs.pop(0) for _ in range(2)]
@@ -319,6 +320,7 @@
     if first:
         acc[...] = jnp.zeros_like(acc)
         m[...] = jnp.full(m.shape, LOW, F32)
+    if has_own:
         bias = own[SEG : SEG + 1, :SEG].astype(F32) * LOG2E
         for j in range(4):
 
@@ -376,10 +378,10 @@
 
 
 def attend_step(step, info, queries, own, others, state):
-    first, final = own is not None, len(others) == 1
-    ins = [info] + queries + ([own] if first else []) + others + list(state or [])
-    flops = 4 * 1088 * SEG * (len(others) + (1 if first else 0)) * COLS
-    body = functools.partial(attend_kernel, step, first, final)
+    first, final, has_own = step == 1, step == 4, own is not None
+    ins = [info] + queries + ([own] if has_own else []) + others + list(state or [])
+    flops = 4 * 1088 * SEG * (len(others) + 1) * COLS
+    body = functools.partial(attend_kernel, step, has_own)
     if final:
         outs = [shape((ROWS, COLS), BF16)] * 4 + STATE[:2]
         aliases = {len(ins) - 2: 4, len(ins) - 1: 5}
@@ -387,7 +389,7 @@
         def body(*refs):
             refs = list(refs)
             payloads, state = refs[-6:-2], refs[-2:]
-            attend_kernel(step, first, final, *refs[:-8], *state, *payloads)
+            attend_kernel(step, has_own, *refs[:-8], *state, *payloads)
 
         return call(body, outs, ins, flops=flops, moved=4 << 20, aliases=aliases)[:4]
     aliases = {} if first else {len(ins) - 2: 0, len(ins) - 1: 1}
@@ -421,7 +423,7 @@
     out[SEG:, :] = jnp.where(iota((16, COLS), 0) == 0, end, 0.0).astype(BF16)
 
 
-BLOCK = 256
+BLOCK = 512
 TALL = 384
 
 
@@ -551,7 +553,7 @@
     queries = [query] + [x_by(query, k) for k in (1, 2, 3)]
     one, other = z_one(kv), z_other(kv)
     one2, other2 = z_one(one), z_other(other)
-    *state, done = attend_step(1, info, queries, kv, [one, other], None)
+    *state, done = attend_step(1, info, queries, None, [one, other], None)
     (theirs,) = call(
         cut_kernel,
         [shape((4, SEG, FEAT), BF16)],
@@ -563,9 +565,10 @@
     theirs = swap(theirs)
     one2, other2 = gate(info, [one2, other2], done)
     one3, other3 = z_one(one2), z_other(other2)
-    *state, done = attend_step(2, info, queries, None, [one2, other2], state)
-    one4 = z_one(one3)
-    *state, done = attend_step(3, info, queries, None, [one3, other3], state)
+    *state, done = attend_step(2, info, queries, kv, [one2, other2], state)
+    (one3_sent,) = gate(info, [one3], done)
+    one4 = z_one(one3_sent)
+    *state, done = attend_step(3, info, queries, None, [one3_sent, other3], state)
     partial = attend_step(4, info, queries, None, [one4], state)
     partial = [partial[0]] + [x_by(partial[k], -k) for k in (1, 2, 3)]
     (attended,) = call(merge_kernel, [shape((ROWS, COLS), BF16)], [info] + partial, moved=1 << 20)

time: 115 us -> 114 us (level)
  Pallas kernels: 23 us -> 21.7 us
    pallas_call x1, Pallas kernels: 4.43 us -> 3.01 us  [output(): pl.pallas_call(output_kernel, grid=(TOK // BLOCK,), out_shape=shape((TOK,...]
    pallas_call x17 -> x18, Pallas kernels: 18.6 us -> 18.7 us  [call(): pl.pallas_call(body, out_shape=outs, in_specs=[SMEM if i == scalars else...]
where the time goes in v7:
time: 114 us; the launch traced here: 112 us
  waiting for transfers between devices  47.5 us (42%)
  starting transfers between devices  39.8 us (35%)
  Pallas kernels  21.7 us (19%)
  local copies, waits for them, and re-layouts  3 us (3%)
    ppermute x25, waiting for transfers between devices, move(): return lax.ppermute(value, ('seq', 'mp'), pairs)  47.5 us
    ppermute x25, starting transfers between devices, move(): return lax.ppermute(value, ('seq', 'mp'), pairs)  33.6 us
    pallas_call x18, Pallas kernels, call(): pl.pallas_call(body, out_shape=outs, in_specs=[SMEM if i == scalars else...  18.7 us
    ppermute x1, starting transfers between devices, shards(): above = lax.ppermute(head, 'seq', [(i, i - 1) for i in range(1, count)])  4.31 us
    pallas_call x1, Pallas kernels, output(): pl.pallas_call(output_kernel, grid=(TOK // BLOCK,), out_shape=shape((TOK,...  3.01 us
    unnamed x10, local copies, waits for them, and re-layouts  2.3 us
  transfers between devices with their start and end apart: 27, of which 13 were waited for; matrix products, arithmetic and copies ran while one was open for 1% of the time, Pallas kernels for 13%

profile of v7, /device:TPU:2, one launch (start us, length us, event | category | flops | bytes accessed | tf_op | source)
XLA Modules:
  0.0 112.3 jit_solution(13217933773386542645)
XLA Ops:
  0.0 1.6 %copy-done.1 = bf16[2048,512]{1,0:T(8,128)(2,1)S(1)} copy-done((bf16[2048,512]{1,0:T(8,128)(2,1)S(1)}, bf16[2048,512]{1,0:T(8,128)(2,1)}, u32[]{:S(2)}) %copy-start.1) | copy-done | bytes 2097176
  3.0 4.3 %collective-permute-start = (f32[8,640]{1,0:T(8,128)S(1)}, f32[8,640]{1,0:T(8,128)S(1)}, u32[]{:S(2)}, u32[]{:S(2)}) collective-permute-start(f32[8,640]{1,0:T(8,128)S(1)} %get-tuple-element.41.head), channel_id=1, source_target_pairs={{8,0},{16,8},{24,16},{32,24},{40,32},{48,40},{56,48},{64,56},{72,6... | collective-permute-start | bytes 61448 | tf_op jit(solution)/shard_map/ppermute | solution.py:504
  7.3 1.9 %collective-permute-start.1 = (f32[8,640]{1,0:T(8,128)S(1)}, f32[8,640]{1,0:T(8,128)S(1)}, u32[]{:S(2)}, u32[]{:S(2)}) collective-permute-start(f32[8,640]{1,0:T(8,128)S(1)} %get-tuple-element.42._), channel_id=1, source_target_pairs={{0,8},{8,16},{16,24},{24,32},{32,40},{40,48},{48,56},{56,64},{64,7... | collective-permute-start | bytes 61448 | tf_op jit(solution)/shard_map/ppermute | solution.py:505
  11.0 2.9 %shard_map.84 = (bf16[4096,256]{1,0:T(8,128)(2,1)S(1)}, bf16[4096,256]{1,0:T(8,128)(2,1)S(1)}, bf16[4096,256]{1,0:T(8,128)(2,1)S(1)}, f32[8,128]{1,0:T(8,128)S(1)}) custom-call(f32[8,640]{1,0:T(8,128)S(1)} %get-tuple-element.42._, bf16[4096,256]{1,0:T(8,128)(2,1)} %refs_0_.1, bf16[4096,256]{1,0:T(8,128)(2,1)} %refs_1_.1, bf16[4096,256]{1,0:T(8,128)(2,1)} %refs_2_.1), custom_call_target="tpu_custom_call" | custom-call | bytes 12582912 | tf_op jit(solution)/shard_map/pallas_call | solution.py:105
  14.7 1.4 %collective-permute-start.2 = (bf16[272,512]{1,0:T(8,128)(2,1)S(1)}, bf16[272,512]{1,0:T(8,128)(2,1)S(1)}, u32[]{:S(2)}, u32[]{:S(2)}) collective-permute-start(bf16[272,512]{1,0:T(8,128)(2,1)S(1)} %get-tuple-element.44.refs_0_), channel_id=1, source_target_pairs={{0,2},{1,7},{2,4},{3,1},{4,6},{5,3},{6,0},{7,5},{8,10},{9,15},{10,... | collective-permute-start | bytes 835592 | tf_op jit(solution)/shard_map/ppermute | solution.py:41
  16.1 1.9 %collective-permute-start.3 = (bf16[272,512]{1,0:T(8,128)(2,1)S(1)}, bf16[272,512]{1,0:T(8,128)(2,1)S(1)}, u32[]{:S(2)}, u32[]{:S(2)}) collective-permute-start(bf16[272,512]{1,0:T(8,128)(2,1)S(1)} %get-tuple-element.44.refs_0_), channel_id=1, source_target_pairs={{0,6},{1,3},{2,0},{3,5},{4,2},{5,7},{6,4},{7,1},{8,14},{9,11},{10,... | collective-permute-start | bytes 835592 | tf_op jit(solution)/shard_map/ppermute | solution.py:41
  18.0 6.8 %collective-permute-done.2.refs_1_ = bf16[272,512]{1,0:T(8,128)(2,1)S(1)} collective-permute-done((bf16[272,512]{1,0:T(8,128)(2,1)S(1)}, bf16[272,512]{1,0:T(8,128)(2,1)S(1)}, u32[]{:S(2)}, u32[]{:S(2)}) %collective-permute-start.2) | collective-permute-done | bytes 278560 | tf_op jit(solution)/shard_map/ppermute | solution.py:41
  25.9 6.6 %collective-permute-done.4.refs_3_ = bf16[272,512]{1,0:T(8,128)(2,1)S(1)} collective-permute-done((bf16[272,512]{1,0:T(8,128)(2,1)S(1)}, bf16[272,512]{1,0:T(8,128)(2,1)S(1)}, u32[]{:S(2)}, u32[]{:S(2)}) %collective-permute-start.4) | collective-permute-done | bytes 278560 | tf_op jit(solution)/shard_map/ppermute | solution.py:41
  32.5 1.5 %shard_map.86 = (f32[272,256]{1,0:T(8,128)S(1)}, f32[256,256]{1,0:T(8,128)S(1)}, f32[256,256]{1,0:T(8,128)S(1)}) custom-call(s32[32]{0:T(128)S(1)} %dynamic-slice_bitcast_fusion.info.refs_0_, bf16[272,512]{1,0:T(8,128)(2,1)S(1)} %get-tuple-element.44.refs_0_, bf16[272,512]{1,0:T(8,128)(2,1)S(1)} %collective-permute-done.2.refs_1_, ...), custom_call_target="tpu_custom_call" | custom-call | flops 855638016 | bytes 3145728 | tf_op jit(solution)/shard_map/pallas_call | solution.py:105
  34.1 1.3 %shard_map.87.refs_10_.refs_4_ = bf16[272,512]{1,0:T(8,128)(2,1)S(1)} custom-call(s32[32]{0:T(128)S(1)} %dynamic-slice_bitcast_fusion.info.refs_0_, bf16[272,512]{1,0:T(8,128)(2,1)S(1)} %get-tuple-element.44.refs_0_, bf16[272,512]{1,0:T(8,128)(2,1)S(1)} %collective-permute-done.2.refs_1_, bf16[272,512]{1,0:T(8,128)(2,1)S(1)} %collective-permute-done.3.refs_2_, ...), custom_call_target="tpu_custom_call" | custom-call | tf_op jit(solution)/shard_map/pallas_call | solution.py:105
  35.4 1.4 %collective-permute-start.12 = (bf16[272,512]{1,0:T(8,128)(2,1)S(1)}, bf16[272,512]{1,0:T(8,128)(2,1)S(1)}, u32[]{:S(2)}, u32[]{:S(2)}) collective-permute-start(bf16[272,512]{1,0:T(8,128)(2,1)S(1)} %shard_map.87.refs_10_.refs_4_), channel_id=1, source_target_pairs={{0,32},{1,225},{2,34},{3,227},{4,36},{5,229},{6,38},{7,231},{8,40}... | collective-permute-start | bytes 835592 | tf_op jit(solution)/shard_map/ppermute | solution.py:41
  36.8 4.0 %collective-permute-start.14 = (bf16[272,512]{1,0:T(8,128)(2,1)S(1)}, bf16[272,512]{1,0:T(8,128)(2,1)S(1)}, u32[]{:S(2)}, u32[]{:S(2)}) collective-permute-start(bf16[272,512]{1,0:T(8,128)(2,1)S(1)} %shard_map.87.refs_10_.refs_4_), channel_id=1, source_target_pairs={{0,224},{1,33},{2,226},{3,35},{4,228},{5,37},{6,230},{7,39},{8,232... | collective-permute-start | bytes 835592 | tf_op jit(solution)/shard_map/ppermute | solution.py:41
  41.9 1.5 %collective-permute-start.9 = (bf16[272,256]{1,0:T(8,128)(2,1)S(1)}, bf16[272,256]{1,0:T(8,128)(2,1)S(1)}, u32[]{:S(2)}, u32[]{:S(2)}) collective-permute-start(bf16[272,256]{1,0:T(8,128)(2,1)S(1)} %shard_map.88.refs_0_.refs_1_), channel_id=1, source_target_pairs={{0,8},{1,9},{2,10},{3,11},{4,12},{5,13},{6,14},{7,15},{8,16},{9,17... | collective-permute-start | bytes 417800 | tf_op jit(solution)/shard_map/ppermute | solution.py:41
  43.4 4.4 %collective-permute-start.10 = (bf16[272,256]{1,0:T(8,128)(2,1)S(1)}, bf16[272,256]{1,0:T(8,128)(2,1)S(1)}, u32[]{:S(2)}, u32[]{:S(2)}) collective-permute-start(bf16[272,256]{1,0:T(8,128)(2,1)S(1)} %shard_map.88.refs_0_.refs_1_), channel_id=1, source_target_pairs={{0,16},{1,17},{2,18},{3,19},{4,20},{5,21},{6,22},{7,23},{8,24},{9,... | collective-permute-start | bytes 417800 | tf_op jit(solution)/shard_map/ppermute | solution.py:41
  47.8 3.2 %collective-permute-start.15 = (bf16[272,512]{1,0:T(8,128)(2,1)S(1)}, bf16[272,512]{1,0:T(8,128)(2,1)S(1)}, u32[]{:S(2)}, u32[]{:S(2)}) collective-permute-start(bf16[272,512]{1,0:T(8,128)(2,1)S(1)} %collective-permute-done.14.refs_5_), channel_id=1, source_target_pairs={{0,224},{1,33},{2,226},{3,35},{4,228},{5,37},{6,230},{7,39},{8,232... | collective-permute-start | bytes 835592 | tf_op jit(solution)/shard_map/ppermute | solution.py:41
  51.0 1.2 %collective-permute-done.10.refs_2_.refs_3_ = bf16[272,256]{1,0:T(8,128)(2,1)S(1)} collective-permute-done((bf16[272,256]{1,0:T(8,128)(2,1)S(1)}, bf16[272,256]{1,0:T(8,128)(2,1)S(1)}, u32[]{:S(2)}, u32[]{:S(2)}) %collective-permute-start.10) | collective-permute-done | bytes 139296 | tf_op jit(solution)/shard_map/ppermute | solution.py:41
  52.3 2.2 %collective-permute-done.11.refs_3_.refs_4_ = bf16[272,256]{1,0:T(8,128)(2,1)S(1)} collective-permute-done((bf16[272,256]{1,0:T(8,128)(2,1)S(1)}, bf16[272,256]{1,0:T(8,128)(2,1)S(1)}, u32[]{:S(2)}, u32[]{:S(2)}) %collective-permute-start.11) | collective-permute-done | bytes 139296 | tf_op jit(solution)/shard_map/ppermute | solution.py:41
  57.5 4.1 %collective-permute-start.18 = (bf16[272,512]{1,0:T(8,128)(2,1)S(1)}, bf16[272,512]{1,0:T(8,128)(2,1)S(1)}, u32[]{:S(2)}, u32[]{:S(2)}) collective-permute-start(bf16[272,512]{1,0:T(8,128)(2,1)S(1)} %get-tuple-element.54.refs_6_), channel_id=1, source_target_pairs={{0,224},{1,33},{2,226},{3,35},{4,228},{5,37},{6,230},{7,39},{8,232... | collective-permute-start | bytes 835592 | tf_op jit(solution)/shard_map/ppermute | solution.py:41
  61.6 2.1 %shard_map.91 = (f32[4,2,272,256]{3,2,1,0:T(8,128)S(1)}, f32[4,2,272,128]{3,2,1,0:T(8,128)S(1)}, f32[8,128]{1,0:T(8,128)S(1)}) custom-call(s32[32]{0:T(128)S(1)} %dynamic-slice_bitcast_fusion.info.refs_0_, bf16[272,256]{1,0:T(8,128)(2,1)S(1)} %shard_map.88.refs_0_.refs_1_, ...), custom_call_target="tpu_custom_call", output_to_operand_aliasing={{0}: (8, {}), {1}: (9, {})} | custom-call | flops 855638016 | bytes 4194304 | tf_op jit(solution)/shard_map/pallas_call | solution.py:105
  63.7 2.9 %collective-permute-done.16.refs_0_ = bf16[272,512]{1,0:T(8,128)(2,1)S(1)} collective-permute-done((bf16[272,512]{1,0:T(8,128)(2,1)S(1)}, bf16[272,512]{1,0:T(8,128)(2,1)S(1)}, u32[]{:S(2)}, u32[]{:S(2)}) %collective-permute-start.16) | collective-permute-done | bytes 278560 | tf_op jit(solution)/shard_map/ppermute | solution.py:41
  68.0 1.1 %shard_map.93 = (f32[4,2,272,256]{3,2,1,0:T(8,128)S(1)}, f32[4,2,272,128]{3,2,1,0:T(8,128)S(1)}, f32[8,128]{1,0:T(8,128)}) custom-call(s32[32]{0:T(128)S(1)} %dynamic-slice_bitcast_fusion.info.refs_0_, bf16[272,256]{1,0:T(8,128)(2,1)S(1)} %shard_map.88.refs_0_.refs_1_, ...), custom_call_target="tpu_custom_call", output_to_operand_aliasing={{0}: (7, {}), {1}: (8, {})} | custom-call | flops 855638016 | bytes 4194304 | tf_op jit(solution)/shard_map/pallas_call | solution.py:105
  69.2 6.6 %collective-permute-done.17.refs_5_ = bf16[272,512]{1,0:T(8,128)(2,1)S(1)} collective-permute-done((bf16[272,512]{1,0:T(8,128)(2,1)S(1)}, bf16[272,512]{1,0:T(8,128)(2,1)S(1)}, u32[]{:S(2)}, u32[]{:S(2)}) %collective-permute-start.17) | collective-permute-done | bytes 278560 | tf_op jit(solution)/shard_map/ppermute | solution.py:41
  76.6 4.3 %collective-permute-start.19 = (bf16[272,256]{1,0:T(8,128)(2,1)S(1)}, bf16[272,256]{1,0:T(8,128)(2,1)S(1)}, u32[]{:S(2)}, u32[]{:S(2)}) collective-permute-start(bf16[272,256]{1,0:T(8,128)(2,1)S(1)} %get-tuple-element.63), channel_id=1, source_target_pairs={{0,24},{1,25},{2,26},{3,27},{4,28},{5,29},{6,30},{7,31},{8,0},{9,1... | collective-permute-start | bytes 417800 | tf_op jit(solution)/shard_map/ppermute | solution.py:41
  80.9 1.8 %collective-permute-start.21 = (bf16[272,256]{1,0:T(8,128)(2,1)S(1)}, bf16[272,256]{1,0:T(8,128)(2,1)S(1)}, u32[]{:S(2)}, u32[]{:S(2)}) collective-permute-start(bf16[272,256]{1,0:T(8,128)(2,1)S(1)} %get-tuple-element.65), channel_id=1, source_target_pairs={{0,8},{1,9},{2,10},{3,11},{4,12},{5,13},{6,14},{7,15},{8,16},{9,17... | collective-permute-start | bytes 417800 | tf_op jit(solution)/shard_map/ppermute | solution.py:41
  82.7 1.2 %collective-permute-done.19.b = bf16[272,256]{1,0:T(8,128)(2,1)S(1)} collective-permute-done((bf16[272,256]{1,0:T(8,128)(2,1)S(1)}, bf16[272,256]{1,0:T(8,128)(2,1)S(1)}, u32[]{:S(2)}, u32[]{:S(2)}) %collective-permute-start.19) | collective-permute-done | bytes 139296 | tf_op jit(solution)/shard_map/ppermute | solution.py:41
  84.0 3.5 %collective-permute-done.20.c = bf16[272,256]{1,0:T(8,128)(2,1)S(1)} collective-permute-done((bf16[272,256]{1,0:T(8,128)(2,1)S(1)}, bf16[272,256]{1,0:T(8,128)(2,1)S(1)}, u32[]{:S(2)}, u32[]{:S(2)}) %collective-permute-start.20) | collective-permute-done | bytes 139296 | tf_op jit(solution)/shard_map/ppermute | solution.py:41
  88.7 1.3 %collective-permute-done.22.other = bf16[272,256]{1,0:T(8,128)(2,1)S(1)} collective-permute-done((bf16[272,256]{1,0:T(8,128)(2,1)S(1)}, bf16[272,256]{1,0:T(8,128)(2,1)S(1)}, u32[]{:S(2)}, u32[]{:S(2)}) %collective-permute-start.22) | collective-permute-done | bytes 139296 | tf_op jit(solution)/shard_map/ppermute | solution.py:41
  90.0 1.3 %shard_map.97 = (f32[272,512]{1,0:T(8,128)S(1)}, f32[272,512]{1,0:T(8,128)S(1)}, bf16[272,512]{1,0:T(8,128)(2,1)S(1)}, bf16[272,512]{1,0:T(8,128)(2,1)S(1)}) custom-call(s32[32]{0:T(128)S(1)} %dynamic-slice_bitcast_fusion.info.refs_0_, bf16[272,256]{1,0:T(8,128)(2,1)S(1)} %shard_map.95.attended, bf16[272,256]{1,0:T(8,128)(2,1)S(1)} %collective-permute-done.22.other, ...), custom_call_target="tpu_custom_call" | custom-call | flops 570425344 | bytes 4194304 | tf_op jit(solution)/shard_map/pallas_call | solution.py:105
  91.4 3.2 %collective-permute-start.26 = (bf16[272,512]{1,0:T(8,128)(2,1)S(1)}, bf16[272,512]{1,0:T(8,128)(2,1)S(1)}, u32[]{:S(2)}, u32[]{:S(2)}) collective-permute-start(bf16[272,512]{1,0:T(8,128)(2,1)S(1)} %get-tuple-element.70), channel_id=1, source_target_pairs={{0,6},{1,3},{2,0},{3,5},{4,2},{5,7},{6,4},{7,1},{8,14},{9,11},{10,... | collective-permute-start | bytes 835592 | tf_op jit(solution)/shard_map/ppermute | solution.py:41
  94.6 6.8 %collective-permute-done.24.b = bf16[272,512]{1,0:T(8,128)(2,1)S(1)} collective-permute-done((bf16[272,512]{1,0:T(8,128)(2,1)S(1)}, bf16[272,512]{1,0:T(8,128)(2,1)S(1)}, u32[]{:S(2)}, u32[]{:S(2)}) %collective-permute-start.24) | collective-permute-done | bytes 278560 | tf_op jit(solution)/shard_map/ppermute | solution.py:41
  102.0 7.3 %collective-permute-done.25.first = bf16[272,512]{1,0:T(8,128)(2,1)S(1)} collective-permute-done((bf16[272,512]{1,0:T(8,128)(2,1)S(1)}, bf16[272,512]{1,0:T(8,128)(2,1)S(1)}, u32[]{:S(2)}, u32[]{:S(2)}) %collective-permute-start.25) | collective-permute-done | bytes 278560 | tf_op jit(solution)/shard_map/ppermute | solution.py:41
  109.3 3.0 %shard_map.100 = bf16[2048,512]{1,0:T(8,128)(2,1)} custom-call(f32[272,512]{1,0:T(8,128)S(1)} %get-tuple-element.67.own, bf16[272,512]{1,0:T(8,128)(2,1)S(1)} %collective-permute-done.25.first, bf16[272,512]{1,0:T(8,128)(2,1)S(1)} %collective-permute-done.26.second, bf16[2048,384]{1,0:T(8,128)(2,1)S(1)} %shard_map.99.hot, bf16[2048,512]{1,0:T(8,128)(2,1)S(1)} %copy-done.2), custom_call_target="tpu_custom_call" | custom-call | flops 2147483648 | bytes 6291456 | tf_op jit(solution)/shard_map/pallas_call | solution.py:453
  (53 shorter events, 13.2 us)
Async XLA Ops:
  0.0 1.6 %copy-start.1 = (bf16[2048,512]{1,0:T(8,128)(2,1)S(1)}, bf16[2048,512]{1,0:T(8,128)(2,1)}, u32[]{:S(2)}) copy-start(bf16[2048,512]{1,0:T(8,128)(2,1)} %tokens.5) | copy-start | bytes 6291460
  1.6 0.7 copy-start.3
  2.3 7.7 %copy-start.2 = (bf16[2048,512]{1,0:T(8,128)(2,1)S(1)}, bf16[2048,512]{1,0:T(8,128)(2,1)}, u32[]{:S(2)}) copy-start(bf16[2048,512]{1,0:T(8,128)(2,1)} %tokens.5) | copy-start | bytes 6291460
  3.0 8.0 %copy-start.4 = (f32[4096]{0:T(1024)S(1)}, f32[4096]{0:T(1024)}, u32[]{:S(2)}) copy-start(f32[4096]{0:T(1024)} %param.10) | copy-start | bytes 49156
  3.0 10.9 %collective-permute-start = (f32[8,640]{1,0:T(8,128)S(1)}, f32[8,640]{1,0:T(8,128)S(1)}, u32[]{:S(2)}, u32[]{:S(2)}) collective-permute-start(f32[8,640]{1,0:T(8,128)S(1)} %get-tuple-element.41.head), channel_id=1, source_target_pairs={{8,0},{16,8},{24,16},{32,24},{40,32},{48,40},{56,48},{64,56},{72,6... | collective-permute-start | bytes 61448 | tf_op jit(solution)/shard_map/ppermute | solution.py:504
  7.3 6.6 %collective-permute-start.1 = (f32[8,640]{1,0:T(8,128)S(1)}, f32[8,640]{1,0:T(8,128)S(1)}, u32[]{:S(2)}, u32[]{:S(2)}) collective-permute-start(f32[8,640]{1,0:T(8,128)S(1)} %get-tuple-element.42._), channel_id=1, source_target_pairs={{0,8},{8,16},{16,24},{24,32},{32,40},{40,48},{48,56},{56,64},{64,7... | collective-permute-start | bytes 61448 | tf_op jit(solution)/shard_map/ppermute | solution.py:505
  14.7 10.1 %collective-permute-start.2 = (bf16[272,512]{1,0:T(8,128)(2,1)S(1)}, bf16[272,512]{1,0:T(8,128)(2,1)S(1)}, u32[]{:S(2)}, u32[]{:S(2)}) collective-permute-start(bf16[272,512]{1,0:T(8,128)(2,1)S(1)} %get-tuple-element.44.refs_0_), channel_id=1, source_target_pairs={{0,2},{1,7},{2,4},{3,1},{4,6},{5,3},{6,0},{7,5},{8,10},{9,15},{10,... | collective-permute-start | bytes 835592 | tf_op jit(solution)/shard_map/ppermute | solution.py:41
  16.1 9.8 %collective-permute-start.3 = (bf16[272,512]{1,0:T(8,128)(2,1)S(1)}, bf16[272,512]{1,0:T(8,128)(2,1)S(1)}, u32[]{:S(2)}, u32[]{:S(2)}) collective-permute-start(bf16[272,512]{1,0:T(8,128)(2,1)S(1)} %get-tuple-element.44.refs_0_), channel_id=1, source_target_pairs={{0,6},{1,3},{2,0},{3,5},{4,2},{5,7},{6,4},{7,1},{8,14},{9,11},{10,... | collective-permute-start | bytes 835592 | tf_op jit(solution)/shard_map/ppermute | solution.py:41
  24.7 7.8 %collective-permute-start.4 = (bf16[272,512]{1,0:T(8,128)(2,1)S(1)}, bf16[272,512]{1,0:T(8,128)(2,1)S(1)}, u32[]{:S(2)}, u32[]{:S(2)}) collective-permute-start(bf16[272,512]{1,0:T(8,128)(2,1)S(1)} %collective-permute-done.2.refs_1_), channel_id=1, source_target_pairs={{0,2},{1,7},{2,4},{3,1},{4,6},{5,3},{6,0},{7,5},{8,10},{9,15},{10,... | collective-permute-start | bytes 835592 | tf_op jit(solution)/shard_map/ppermute | solution.py:41
  25.4 7.2 %collective-permute-start.5 = (bf16[272,512]{1,0:T(8,128)(2,1)S(1)}, bf16[272,512]{1,0:T(8,128)(2,1)S(1)}, u32[]{:S(2)}, u32[]{:S(2)}) collective-permute-start(bf16[272,512]{1,0:T(8,128)(2,1)S(1)} %get-tuple-element.44.refs_0_), channel_id=1, source_target_pairs={{0,1},{1,0},{2,3},{3,2},{4,5},{5,4},{6,7},{7,6},{8,9},{9,8},{10,11... | collective-permute-start | bytes 835592 | tf_op jit(solution)/shard_map/ppermute | solution.py:41
  25.4 8.7 %collective-permute-start.6 = (bf16[272,512]{1,0:T(8,128)(2,1)S(1)}, bf16[272,512]{1,0:T(8,128)(2,1)S(1)}, u32[]{:S(2)}, u32[]{:S(2)}) collective-permute-start(bf16[272,512]{1,0:T(8,128)(2,1)S(1)} %collective-permute-done.2.refs_1_), channel_id=1, source_target_pairs={{0,1},{1,0},{2,3},{3,2},{4,5},{5,4},{6,7},{7,6},{8,9},{9,8},{10,11... | collective-permute-start | bytes 835592 | tf_op jit(solution)/shard_map/ppermute | solution.py:41
  25.9 8.2 %collective-permute-start.7 = (bf16[272,512]{1,0:T(8,128)(2,1)S(1)}, bf16[272,512]{1,0:T(8,128)(2,1)S(1)}, u32[]{:S(2)}, u32[]{:S(2)}) collective-permute-start(bf16[272,512]{1,0:T(8,128)(2,1)S(1)} %collective-permute-done.3.refs_2_), channel_id=1, source_target_pairs={{0,1},{1,0},{2,3},{3,2},{4,5},{5,4},{6,7},{7,6},{8,9},{9,8},{10,11... | collective-permute-start | bytes 835592 | tf_op jit(solution)/shard_map/ppermute | solution.py:41
  32.5 1.6 %collective-permute-start.8 = (bf16[272,512]{1,0:T(8,128)(2,1)S(1)}, bf16[272,512]{1,0:T(8,128)(2,1)S(1)}, u32[]{:S(2)}, u32[]{:S(2)}) collective-permute-start(bf16[272,512]{1,0:T(8,128)(2,1)S(1)} %collective-permute-done.4.refs_3_), channel_id=1, source_target_pairs={{0,1},{1,0},{2,3},{3,2},{4,5},{5,4},{6,7},{7,6},{8,9},{9,8},{10,11... | collective-permute-start | bytes 835592 | tf_op jit(solution)/shard_map/ppermute | solution.py:41
  35.4 12.4 %collective-permute-start.12 = (bf16[272,512]{1,0:T(8,128)(2,1)S(1)}, bf16[272,512]{1,0:T(8,128)(2,1)S(1)}, u32[]{:S(2)}, u32[]{:S(2)}) collective-permute-start(bf16[272,512]{1,0:T(8,128)(2,1)S(1)} %shard_map.87.refs_10_.refs_4_), channel_id=1, source_target_pairs={{0,32},{1,225},{2,34},{3,227},{4,36},{5,229},{6,38},{7,231},{8,40}... | collective-permute-start | bytes 835592 | tf_op jit(solution)/shard_map/ppermute | solution.py:41
  36.8 11.0 %collective-permute-start.14 = (bf16[272,512]{1,0:T(8,128)(2,1)S(1)}, bf16[272,512]{1,0:T(8,128)(2,1)S(1)}, u32[]{:S(2)}, u32[]{:S(2)}) collective-permute-start(bf16[272,512]{1,0:T(8,128)(2,1)S(1)} %shard_map.87.refs_10_.refs_4_), channel_id=1, source_target_pairs={{0,224},{1,33},{2,226},{3,35},{4,228},{5,37},{6,230},{7,39},{8,232... | collective-permute-start | bytes 835592 | tf_op jit(solution)/shard_map/ppermute | solution.py:41
  41.8 13.4 %copy-start = (bf16[256,4096]{1,0:T(8,128)(2,1)S(1)}, bf16[256,4096]{1,0:T(8,128)(2,1)}, u32[]{:S(2)}) copy-start(bf16[256,4096]{1,0:T(8,128)(2,1)} %w_out.3) | copy-start | bytes 6291460
  41.9 9.2 %collective-permute-start.9 = (bf16[272,256]{1,0:T(8,128)(2,1)S(1)}, bf16[272,256]{1,0:T(8,128)(2,1)S(1)}, u32[]{:S(2)}, u32[]{:S(2)}) collective-permute-start(bf16[272,256]{1,0:T(8,128)(2,1)S(1)} %shard_map.88.refs_0_.refs_1_), channel_id=1, source_target_pairs={{0,8},{1,9},{2,10},{3,11},{4,12},{5,13},{6,14},{7,15},{8,16},{9,17... | collective-permute-start | bytes 417800 | tf_op jit(solution)/shard_map/ppermute | solution.py:41
  43.4 8.9 %collective-permute-start.10 = (bf16[272,256]{1,0:T(8,128)(2,1)S(1)}, bf16[272,256]{1,0:T(8,128)(2,1)S(1)}, u32[]{:S(2)}, u32[]{:S(2)}) collective-permute-start(bf16[272,256]{1,0:T(8,128)(2,1)S(1)} %shard_map.88.refs_0_.refs_1_), channel_id=1, source_target_pairs={{0,16},{1,17},{2,18},{3,19},{4,20},{5,21},{6,22},{7,23},{8,24},{9,... | collective-permute-start | bytes 417800 | tf_op jit(solution)/shard_map/ppermute | solution.py:41
  47.8 6.7 %collective-permute-start.11 = (bf16[272,256]{1,0:T(8,128)(2,1)S(1)}, bf16[272,256]{1,0:T(8,128)(2,1)S(1)}, u32[]{:S(2)}, u32[]{:S(2)}) collective-permute-start(bf16[272,256]{1,0:T(8,128)(2,1)S(1)} %shard_map.88.refs_0_.refs_1_), channel_id=1, source_target_pairs={{0,24},{1,25},{2,26},{3,27},{4,28},{5,29},{6,30},{7,31},{8,0},{9,1... | collective-permute-start | bytes 417800 | tf_op jit(solution)/shard_map/ppermute | solution.py:41
  47.8 9.0 %collective-permute-start.13 = (bf16[272,512]{1,0:T(8,128)(2,1)S(1)}, bf16[272,512]{1,0:T(8,128)(2,1)S(1)}, u32[]{:S(2)}, u32[]{:S(2)}) collective-permute-start(bf16[272,512]{1,0:T(8,128)(2,1)S(1)} %collective-permute-done.12.refs_4_), channel_id=1, source_target_pairs={{0,32},{1,225},{2,34},{3,227},{4,36},{5,229},{6,38},{7,231},{8,40}... | collective-permute-start | bytes 835592 | tf_op jit(solution)/shard_map/ppermute | solution.py:41
  47.8 9.0 %collective-permute-start.15 = (bf16[272,512]{1,0:T(8,128)(2,1)S(1)}, bf16[272,512]{1,0:T(8,128)(2,1)S(1)}, u32[]{:S(2)}, u32[]{:S(2)}) collective-permute-start(bf16[272,512]{1,0:T(8,128)(2,1)S(1)} %collective-permute-done.14.refs_5_), channel_id=1, source_target_pairs={{0,224},{1,33},{2,226},{3,35},{4,228},{5,37},{6,230},{7,39},{8,232... | collective-permute-start | bytes 835592 | tf_op jit(solution)/shard_map/ppermute | solution.py:41
  55.9 32.7 %collective-permute-start.23 = (bf16[4,256,512]{2,1,0:T(8,128)(2,1)S(1)}, bf16[4,256,512]{2,1,0:T(8,128)(2,1)S(1)}, u32[]{:S(2)}, u32[]{:S(2)}) collective-permute-start(bf16[4,256,512]{2,1,0:T(8,128)(2,1)S(1)} %shard_map.96), channel_id=1, source_target_pairs={{0,1},{1,0},{2,3},{3,2},{4,5},{5,4},{6,7},{7,6},{8,9},{9,8},{10,11... | collective-permute-start | bytes 3145736 | tf_op jit(solution)/shard_map/ppermute | solution.py:41
  57.4 9.1 %collective-permute-start.16 = (bf16[272,512]{1,0:T(8,128)(2,1)S(1)}, bf16[272,512]{1,0:T(8,128)(2,1)S(1)}, u32[]{:S(2)}, u32[]{:S(2)}) collective-permute-start(bf16[272,512]{1,0:T(8,128)(2,1)S(1)} %get-tuple-element.53.refs_5_), channel_id=1, source_target_pairs={{0,32},{1,225},{2,34},{3,227},{4,36},{5,229},{6,38},{7,231},{8,40}... | collective-permute-start | bytes 835592 | tf_op jit(solution)/shard_map/ppermute | solution.py:41
  57.5 10.5 %collective-permute-start.18 = (bf16[272,512]{1,0:T(8,128)(2,1)S(1)}, bf16[272,512]{1,0:T(8,128)(2,1)S(1)}, u32[]{:S(2)}, u32[]{:S(2)}) collective-permute-start(bf16[272,512]{1,0:T(8,128)(2,1)S(1)} %get-tuple-element.54.refs_6_), channel_id=1, source_target_pairs={{0,224},{1,33},{2,226},{3,35},{4,228},{5,37},{6,230},{7,39},{8,232... | collective-permute-start | bytes 835592 | tf_op jit(solution)/shard_map/ppermute | solution.py:41
  67.1 8.7 %collective-permute-start.17 = (bf16[272,512]{1,0:T(8,128)(2,1)S(1)}, bf16[272,512]{1,0:T(8,128)(2,1)S(1)}, u32[]{:S(2)}, u32[]{:S(2)}) collective-permute-start(bf16[272,512]{1,0:T(8,128)(2,1)S(1)} %shard_map.92.refs_4_), channel_id=1, source_target_pairs={{0,32},{1,225},{2,34},{3,227},{4,36},{5,229},{6,38},{7,231},{8,40}... | collective-permute-start | bytes 835592 | tf_op jit(solution)/shard_map/ppermute | solution.py:41
  76.6 7.3 %collective-permute-start.19 = (bf16[272,256]{1,0:T(8,128)(2,1)S(1)}, bf16[272,256]{1,0:T(8,128)(2,1)S(1)}, u32[]{:S(2)}, u32[]{:S(2)}) collective-permute-start(bf16[272,256]{1,0:T(8,128)(2,1)S(1)} %get-tuple-element.63), channel_id=1, source_target_pairs={{0,24},{1,25},{2,26},{3,27},{4,28},{5,29},{6,30},{7,31},{8,0},{9,1... | collective-permute-start | bytes 417800 | tf_op jit(solution)/shard_map/ppermute | solution.py:41
  80.9 6.6 %collective-permute-start.20 = (bf16[272,256]{1,0:T(8,128)(2,1)S(1)}, bf16[272,256]{1,0:T(8,128)(2,1)S(1)}, u32[]{:S(2)}, u32[]{:S(2)}) collective-permute-start(bf16[272,256]{1,0:T(8,128)(2,1)S(1)} %get-tuple-element.64), channel_id=1, source_target_pairs={{0,16},{1,17},{2,18},{3,19},{4,20},{5,21},{6,22},{7,23},{8,24},{9,... | collective-permute-start | bytes 417800 | tf_op jit(solution)/shard_map/ppermute | solution.py:41
  80.9 6.5 %collective-permute-start.21 = (bf16[272,256]{1,0:T(8,128)(2,1)S(1)}, bf16[272,256]{1,0:T(8,128)(2,1)S(1)}, u32[]{:S(2)}, u32[]{:S(2)}) collective-permute-start(bf16[272,256]{1,0:T(8,128)(2,1)S(1)} %get-tuple-element.65), channel_id=1, source_target_pairs={{0,8},{1,9},{2,10},{3,11},{4,12},{5,13},{6,14},{7,15},{8,16},{9,17... | collective-permute-start | bytes 417800 | tf_op jit(solution)/shard_map/ppermute | solution.py:41
  88.6 1.4 %collective-permute-start.22 = (bf16[272,256]{1,0:T(8,128)(2,1)S(1)}, bf16[272,256]{1,0:T(8,128)(2,1)S(1)}, u32[]{:S(2)}, u32[]{:S(2)}) collective-permute-start(bf16[272,256]{1,0:T(8,128)(2,1)S(1)} %shard_map.95.attended), channel_id=1, source_target_pairs={{0,1},{1,0},{2,3},{3,2},{4,5},{5,4},{6,7},{7,6},{8,9},{9,8},{10,11... | collective-permute-start | bytes 417800 | tf_op jit(solution)/shard_map/ppermute | solution.py:41
  91.3 10.1 %collective-permute-start.24 = (bf16[272,512]{1,0:T(8,128)(2,1)S(1)}, bf16[272,512]{1,0:T(8,128)(2,1)S(1)}, u32[]{:S(2)}, u32[]{:S(2)}) collective-permute-start(bf16[272,512]{1,0:T(8,128)(2,1)S(1)} %get-tuple-element.69), channel_id=1, source_target_pairs={{0,2},{1,7},{2,4},{3,1},{4,6},{5,3},{6,0},{7,5},{8,10},{9,15},{10,... | collective-permute-start | bytes 835592 | tf_op jit(solution)/shard_map/ppermute | solution.py:41
  91.4 10.6 %collective-permute-start.26 = (bf16[272,512]{1,0:T(8,128)(2,1)S(1)}, bf16[272,512]{1,0:T(8,128)(2,1)S(1)}, u32[]{:S(2)}, u32[]{:S(2)}) collective-permute-start(bf16[272,512]{1,0:T(8,128)(2,1)S(1)} %get-tuple-element.70), channel_id=1, source_target_pairs={{0,6},{1,3},{2,0},{3,5},{4,2},{5,7},{6,4},{7,1},{8,14},{9,11},{10,... | collective-permute-start | bytes 835592 | tf_op jit(solution)/shard_map/ppermute | solution.py:41
  101.5 7.8 %collective-permute-start.25 = (bf16[272,512]{1,0:T(8,128)(2,1)S(1)}, bf16[272,512]{1,0:T(8,128)(2,1)S(1)}, u32[]{:S(2)}, u32[]{:S(2)}) collective-permute-start(bf16[272,512]{1,0:T(8,128)(2,1)S(1)} %shard_map.98), channel_id=1, source_target_pairs={{0,2},{1,7},{2,4},{3,1},{4,6},{5,3},{6,0},{7,5},{8,10},{9,15},{10,... | collective-permute-start | bytes 835592 | tf_op jit(solution)/shard_map/ppermute | solution.py:41

commit v8 on v7

--- a/solution.py
+++ b/solution.py
@@ -21,6 +21,8 @@
 LOW = -1e30
 VMEM_LIMIT = 20 * 1024 * 1024
 ROOM = 47 * 1024 * 1024
+EDGE_ROOM = 51 * 1024 * 1024
+PIECES = 8
 F32, BF16 = jnp.float32, jnp.bfloat16
 
 
@@ -147,7 +149,14 @@
     return jnp.where(condition, 1.0, 0.0).astype(BF16)
 
 
-def edge_kernel(flags, tokens, ids_out, head_out, tail_out, marks):
+def edge_kernel(flags_in, tokens_in, tokens, ids_out, head_out, tail_out, marks, flags, sems):
+    copies = [pltpu.make_async_copy(flags_in, flags, sems.at[PIECES])]
+    for i in range(PIECES):
+        rows = pl.ds(i * (TOK // PIECES), TOK // PIECES)
+        copies.append(pltpu.make_async_copy(tokens_in.at[rows, :], tokens.at[rows, :], sems.at[i]))
+    for copy in copies:
+        copy.start()
+    copies[0].wait()
     f = flags[...].astype(F32).astype(BF16)
     upto = ones_where(iota((128, 128), 0) <= iota((128, 128), 1))
     inside = dot(f, upto)
@@ -157,6 +166,8 @@
     wanted = jnp.where(iota((16, 128), 0) < 8, -1, SEG - 1)
     for r in range(16):
         marks[:, r * 128 : (r + 1) * 128] = ones_where(ids_out[r : r + 1, :] == wanted)
+    for copy in copies[1:]:
+        copy.wait()
     sums = dot(marks[...], tokens[...])
     counts = dot(marks[...], jnp.ones((TOK, 128), BF16))
     head_out[:, :FEAT] = sums[:8]
@@ -491,14 +502,20 @@
     seq, mp = lax.axis_index("seq"), lax.axis_index("mp")
     info = jnp.asarray(device_table())[seq * (NY * NC) + mp]
     edge = shape((8, FEAT + 128), F32)
-    ids, head, tail = call(
+    tokens, ids, head, tail = call(
         edge_kernel,
-        [shape((16, 128), jnp.int32), edge, edge],
+        [shape((TOK, FEAT), BF16), shape((16, 128), jnp.int32), edge, edge],
         [flags.reshape(16, 128), tokens],
         scalars=None,
         flops=1 << 28,
         moved=2 << 20,
-        scratch=[pltpu.VMEM((16, TOK), BF16)],
+        scratch=[
+            pltpu.VMEM((16, TOK), BF16),
+            pltpu.VMEM((16, 128), jnp.int32),
+            pltpu.SemaphoreType.DMA((PIECES + 1,)),
+        ],
+        far_in=(0, 1),
+        room=EDGE_ROOM,
     )
     count = NZ * NX
     above = lax.ppermute(head, "seq", [(i, i - 1) for i in range(1, count)])

time: 114 us -> 114 us (level)
  local copies, waits for them, and re-layouts: 3 us -> 1.41 us
  Pallas kernels: 21.7 us -> 23 us
    unnamed x10 -> x6, local copies, waits for them, and re-layouts: 2.3 us -> 0.71 us
    pallas_call x18, Pallas kernels: 18.7 us -> 20 us  [call(): pl.pallas_call(body, out_shape=outs, in_specs=[SMEM if i == scalars else...]
where the time goes in v8:
time: 114 us; the launch traced here: 112 us
  waiting for transfers between devices  47.6 us (42%)
  starting transfers between devices  39.6 us (35%)
  Pallas kernels  23 us (20%)
  local copies, waits for them, and re-layouts  1.41 us (1%)
    ppermute x25, waiting for transfers between devices, move(): return lax.ppermute(value, ('seq', 'mp'), pairs)  47.6 us
    ppermute x25, starting transfers between devices, move(): return lax.ppermute(value, ('seq', 'mp'), pairs)  33.5 us
    pallas_call x18, Pallas kernels, call(): pl.pallas_call(body, out_shape=outs, in_specs=[SMEM if i == scalars else...  20 us
    ppermute x1, starting transfers between devices, shards(): above = lax.ppermute(head, 'seq', [(i, i - 1) for i in range(1, count)])  4.18 us
    pallas_call x1, Pallas kernels, output(): pl.pallas_call(output_kernel, grid=(TOK // BLOCK,), out_shape=shape((TOK,...  3.03 us
  transfers between devices with their start and end apart: 27, of which 13 were waited for; matrix products, arithmetic and copies ran while one was open for 1% of the time, Pallas kernels for 13%

profile of v8, /device:TPU:2, one launch (start us, length us, event | category | flops | bytes accessed | tf_op | source)
XLA Modules:
  0.0 112.0 jit_solution(3930269479214275532)
XLA Ops:
  0.7 2.0 %shard_map.82 = (bf16[2048,512]{1,0:T(8,128)(2,1)S(1)}, s32[16,128]{1,0:T(8,128)S(1)}, f32[8,640]{1,0:T(8,128)S(1)}, f32[8,640]{1,0:T(8,128)S(1)}) custom-call(s32[16,128]{1,0:T(8,128)S(1)} %bitcast.3, bf16[2048,512]{1,0:T(8,128)(2,1)} %tokens_in.1), custom_call_target="tpu_custom_call" | custom-call | flops 268435456 | bytes 2097152 | tf_op jit(solution)/shard_map/pallas_call | solution.py:107
  2.8 4.2 %collective-permute-start = (f32[8,640]{1,0:T(8,128)S(1)}, f32[8,640]{1,0:T(8,128)S(1)}, u32[]{:S(2)}, u32[]{:S(2)}) collective-permute-start(f32[8,640]{1,0:T(8,128)S(1)} %get-tuple-element.43.head), channel_id=1, source_target_pairs={{8,0},{16,8},{24,16},{32,24},{40,32},{48,40},{56,48},{64,56},{72,6... | collective-permute-start | bytes 61448 | tf_op jit(solution)/shard_map/ppermute | solution.py:521
  6.9 1.9 %collective-permute-start.1 = (f32[8,640]{1,0:T(8,128)S(1)}, f32[8,640]{1,0:T(8,128)S(1)}, u32[]{:S(2)}, u32[]{:S(2)}) collective-permute-start(f32[8,640]{1,0:T(8,128)S(1)} %get-tuple-element.44._), channel_id=1, source_target_pairs={{0,8},{8,16},{16,24},{24,32},{32,40},{40,48},{48,56},{56,64},{64,7... | collective-permute-start | bytes 61448 | tf_op jit(solution)/shard_map/ppermute | solution.py:522
  10.6 2.9 %shard_map.84 = (bf16[4096,256]{1,0:T(8,128)(2,1)S(1)}, bf16[4096,256]{1,0:T(8,128)(2,1)S(1)}, bf16[4096,256]{1,0:T(8,128)(2,1)S(1)}, f32[8,128]{1,0:T(8,128)S(1)}) custom-call(f32[8,640]{1,0:T(8,128)S(1)} %get-tuple-element.44._, bf16[4096,256]{1,0:T(8,128)(2,1)} %refs_0_.1, bf16[4096,256]{1,0:T(8,128)(2,1)} %refs_1_.1, bf16[4096,256]{1,0:T(8,128)(2,1)} %refs_2_.1), custom_call_target="tpu_custom_call" | custom-call | bytes 12582912 | tf_op jit(solution)/shard_map/pallas_call | solution.py:107
  14.3 1.4 %collective-permute-start.2 = (bf16[272,512]{1,0:T(8,128)(2,1)S(1)}, bf16[272,512]{1,0:T(8,128)(2,1)S(1)}, u32[]{:S(2)}, u32[]{:S(2)}) collective-permute-start(bf16[272,512]{1,0:T(8,128)(2,1)S(1)} %get-tuple-element.46.refs_0_), channel_id=1, source_target_pairs={{0,2},{1,7},{2,4},{3,1},{4,6},{5,3},{6,0},{7,5},{8,10},{9,15},{10,... | collective-permute-start | bytes 835592 | tf_op jit(solution)/shard_map/ppermute | solution.py:43
  15.7 1.9 %collective-permute-start.3 = (bf16[272,512]{1,0:T(8,128)(2,1)S(1)}, bf16[272,512]{1,0:T(8,128)(2,1)S(1)}, u32[]{:S(2)}, u32[]{:S(2)}) collective-permute-start(bf16[272,512]{1,0:T(8,128)(2,1)S(1)} %get-tuple-element.46.refs_0_), channel_id=1, source_target_pairs={{0,6},{1,3},{2,0},{3,5},{4,2},{5,7},{6,4},{7,1},{8,14},{9,11},{10,... | collective-permute-start | bytes 835592 | tf_op jit(solution)/shard_map/ppermute | solution.py:43
  17.6 6.8 %collective-permute-done.2.refs_1_ = bf16[272,512]{1,0:T(8,128)(2,1)S(1)} collective-permute-done((bf16[272,512]{1,0:T(8,128)(2,1)S(1)}, bf16[272,512]{1,0:T(8,128)(2,1)S(1)}, u32[]{:S(2)}, u32[]{:S(2)}) %collective-permute-start.2) | collective-permute-done | bytes 278560 | tf_op jit(solution)/shard_map/ppermute | solution.py:43
  25.5 6.6 %collective-permute-done.4.refs_3_ = bf16[272,512]{1,0:T(8,128)(2,1)S(1)} collective-permute-done((bf16[272,512]{1,0:T(8,128)(2,1)S(1)}, bf16[272,512]{1,0:T(8,128)(2,1)S(1)}, u32[]{:S(2)}, u32[]{:S(2)}) %collective-permute-start.4) | collective-permute-done | bytes 278560 | tf_op jit(solution)/shard_map/ppermute | solution.py:43
  32.2 1.5 %shard_map.86 = (f32[272,256]{1,0:T(8,128)S(1)}, f32[256,256]{1,0:T(8,128)S(1)}, f32[256,256]{1,0:T(8,128)S(1)}) custom-call(s32[32]{0:T(128)S(1)} %dynamic-slice_bitcast_fusion.info.refs_0_, bf16[272,512]{1,0:T(8,128)(2,1)S(1)} %get-tuple-element.46.refs_0_, bf16[272,512]{1,0:T(8,128)(2,1)S(1)} %collective-permute-done.2.refs_1_, ...), custom_call_target="tpu_custom_call" | custom-call | flops 855638016 | bytes 3145728 | tf_op jit(solution)/shard_map/pallas_call | solution.py:107
  33.7 1.3 %shard_map.87.refs_10_.refs_4_ = bf16[272,512]{1,0:T(8,128)(2,1)S(1)} custom-call(s32[32]{0:T(128)S(1)} %dynamic-slice_bitcast_fusion.info.refs_0_, bf16[272,512]{1,0:T(8,128)(2,1)S(1)} %get-tuple-element.46.refs_0_, bf16[272,512]{1,0:T(8,128)(2,1)S(1)} %collective-permute-done.2.refs_1_, bf16[272,512]{1,0:T(8,128)(2,1)S(1)} %collective-permute-done.3.refs_2_, ...), custom_call_target="tpu_custom_call" | custom-call | tf_op jit(solution)/shard_map/pallas_call | solution.py:107
  35.0 1.4 %collective-permute-start.12 = (bf16[272,512]{1,0:T(8,128)(2,1)S(1)}, bf16[272,512]{1,0:T(8,128)(2,1)S(1)}, u32[]{:S(2)}, u32[]{:S(2)}) collective-permute-start(bf16[272,512]{1,0:T(8,128)(2,1)S(1)} %shard_map.87.refs_10_.refs_4_), channel_id=1, source_target_pairs={{0,32},{1,225},{2,34},{3,227},{4,36},{5,229},{6,38},{7,231},{8,40}... | collective-permute-start | bytes 835592 | tf_op jit(solution)/shard_map/ppermute | solution.py:43
  36.4 4.0 %collective-permute-start.14 = (bf16[272,512]{1,0:T(8,128)(2,1)S(1)}, bf16[272,512]{1,0:T(8,128)(2,1)S(1)}, u32[]{:S(2)}, u32[]{:S(2)}) collective-permute-start(bf16[272,512]{1,0:T(8,128)(2,1)S(1)} %shard_map.87.refs_10_.refs_4_), channel_id=1, source_target_pairs={{0,224},{1,33},{2,226},{3,35},{4,228},{5,37},{6,230},{7,39},{8,232... | collective-permute-start | bytes 835592 | tf_op jit(solution)/shard_map/ppermute | solution.py:43
  41.5 1.6 %collective-permute-start.9 = (bf16[272,256]{1,0:T(8,128)(2,1)S(1)}, bf16[272,256]{1,0:T(8,128)(2,1)S(1)}, u32[]{:S(2)}, u32[]{:S(2)}) collective-permute-start(bf16[272,256]{1,0:T(8,128)(2,1)S(1)} %shard_map.88.refs_0_.refs_1_), channel_id=1, source_target_pairs={{0,8},{1,9},{2,10},{3,11},{4,12},{5,13},{6,14},{7,15},{8,16},{9,17... | collective-permute-start | bytes 417800 | tf_op jit(solution)/shard_map/ppermute | solution.py:43
  43.0 4.4 %collective-permute-start.10 = (bf16[272,256]{1,0:T(8,128)(2,1)S(1)}, bf16[272,256]{1,0:T(8,128)(2,1)S(1)}, u32[]{:S(2)}, u32[]{:S(2)}) collective-permute-start(bf16[272,256]{1,0:T(8,128)(2,1)S(1)} %shard_map.88.refs_0_.refs_1_), channel_id=1, source_target_pairs={{0,16},{1,17},{2,18},{3,19},{4,20},{5,21},{6,22},{7,23},{8,24},{9,... | collective-permute-start | bytes 417800 | tf_op jit(solution)/shard_map/ppermute | solution.py:43
  47.5 3.2 %collective-permute-start.15 = (bf16[272,512]{1,0:T(8,128)(2,1)S(1)}, bf16[272,512]{1,0:T(8,128)(2,1)S(1)}, u32[]{:S(2)}, u32[]{:S(2)}) collective-permute-start(bf16[272,512]{1,0:T(8,128)(2,1)S(1)} %collective-permute-done.14.refs_5_), channel_id=1, source_target_pairs={{0,224},{1,33},{2,226},{3,35},{4,228},{5,37},{6,230},{7,39},{8,232... | collective-permute-start | bytes 835592 | tf_op jit(solution)/shard_map/ppermute | solution.py:43
  50.7 1.2 %collective-permute-done.10.refs_2_.refs_3_ = bf16[272,256]{1,0:T(8,128)(2,1)S(1)} collective-permute-done((bf16[272,256]{1,0:T(8,128)(2,1)S(1)}, bf16[272,256]{1,0:T(8,128)(2,1)S(1)}, u32[]{:S(2)}, u32[]{:S(2)}) %collective-permute-start.10) | collective-permute-done | bytes 139296 | tf_op jit(solution)/shard_map/ppermute | solution.py:43
  51.9 2.2 %collective-permute-done.11.refs_3_.refs_4_ = bf16[272,256]{1,0:T(8,128)(2,1)S(1)} collective-permute-done((bf16[272,256]{1,0:T(8,128)(2,1)S(1)}, bf16[272,256]{1,0:T(8,128)(2,1)S(1)}, u32[]{:S(2)}, u32[]{:S(2)}) %collective-permute-start.11) | collective-permute-done | bytes 139296 | tf_op jit(solution)/shard_map/ppermute | solution.py:43
  57.1 4.1 %collective-permute-start.18 = (bf16[272,512]{1,0:T(8,128)(2,1)S(1)}, bf16[272,512]{1,0:T(8,128)(2,1)S(1)}, u32[]{:S(2)}, u32[]{:S(2)}) collective-permute-start(bf16[272,512]{1,0:T(8,128)(2,1)S(1)} %get-tuple-element.56.refs_6_), channel_id=1, source_target_pairs={{0,224},{1,33},{2,226},{3,35},{4,228},{5,37},{6,230},{7,39},{8,232... | collective-permute-start | bytes 835592 | tf_op jit(solution)/shard_map/ppermute | solution.py:43
  61.2 2.1 %shard_map.91 = (f32[4,2,272,256]{3,2,1,0:T(8,128)S(1)}, f32[4,2,272,128]{3,2,1,0:T(8,128)S(1)}, f32[8,128]{1,0:T(8,128)S(1)}) custom-call(s32[32]{0:T(128)S(1)} %dynamic-slice_bitcast_fusion.info.refs_0_, bf16[272,256]{1,0:T(8,128)(2,1)S(1)} %shard_map.88.refs_0_.refs_1_, ...), custom_call_target="tpu_custom_call", output_to_operand_aliasing={{0}: (8, {}), {1}: (9, {})} | custom-call | flops 855638016 | bytes 4194304 | tf_op jit(solution)/shard_map/pallas_call | solution.py:107
  63.3 2.9 %collective-permute-done.16.refs_0_ = bf16[272,512]{1,0:T(8,128)(2,1)S(1)} collective-permute-done((bf16[272,512]{1,0:T(8,128)(2,1)S(1)}, bf16[272,512]{1,0:T(8,128)(2,1)S(1)}, u32[]{:S(2)}, u32[]{:S(2)}) %collective-permute-start.16) | collective-permute-done | bytes 278560 | tf_op jit(solution)/shard_map/ppermute | solution.py:43
  67.6 1.1 %shard_map.93 = (f32[4,2,272,256]{3,2,1,0:T(8,128)S(1)}, f32[4,2,272,128]{3,2,1,0:T(8,128)S(1)}, f32[8,128]{1,0:T(8,128)}) custom-call(s32[32]{0:T(128)S(1)} %dynamic-slice_bitcast_fusion.info.refs_0_, bf16[272,256]{1,0:T(8,128)(2,1)S(1)} %shard_map.88.refs_0_.refs_1_, ...), custom_call_target="tpu_custom_call", output_to_operand_aliasing={{0}: (7, {}), {1}: (8, {})} | custom-call | flops 855638016 | bytes 4194304 | tf_op jit(solution)/shard_map/pallas_call | solution.py:107
  68.8 6.6 %collective-permute-done.17.refs_5_ = bf16[272,512]{1,0:T(8,128)(2,1)S(1)} collective-permute-done((bf16[272,512]{1,0:T(8,128)(2,1)S(1)}, bf16[272,512]{1,0:T(8,128)(2,1)S(1)}, u32[]{:S(2)}, u32[]{:S(2)}) %collective-permute-start.17) | collective-permute-done | bytes 278560 | tf_op jit(solution)/shard_map/ppermute | solution.py:43
  76.3 4.3 %collective-permute-start.19 = (bf16[272,256]{1,0:T(8,128)(2,1)S(1)}, bf16[272,256]{1,0:T(8,128)(2,1)S(1)}, u32[]{:S(2)}, u32[]{:S(2)}) collective-permute-start(bf16[272,256]{1,0:T(8,128)(2,1)S(1)} %get-tuple-element.65), channel_id=1, source_target_pairs={{0,24},{1,25},{2,26},{3,27},{4,28},{5,29},{6,30},{7,31},{8,0},{9,1... | collective-permute-start | bytes 417800 | tf_op jit(solution)/shard_map/ppermute | solution.py:43
  80.6 1.8 %collective-permute-start.21 = (bf16[272,256]{1,0:T(8,128)(2,1)S(1)}, bf16[272,256]{1,0:T(8,128)(2,1)S(1)}, u32[]{:S(2)}, u32[]{:S(2)}) collective-permute-start(bf16[272,256]{1,0:T(8,128)(2,1)S(1)} %get-tuple-element.67), channel_id=1, source_target_pairs={{0,8},{1,9},{2,10},{3,11},{4,12},{5,13},{6,14},{7,15},{8,16},{9,17... | collective-permute-start | bytes 417800 | tf_op jit(solution)/shard_map/ppermute | solution.py:43
  82.3 1.2 %collective-permute-done.19.b = bf16[272,256]{1,0:T(8,128)(2,1)S(1)} collective-permute-done((bf16[272,256]{1,0:T(8,128)(2,1)S(1)}, bf16[272,256]{1,0:T(8,128)(2,1)S(1)}, u32[]{:S(2)}, u32[]{:S(2)}) %collective-permute-start.19) | collective-permute-done | bytes 139296 | tf_op jit(solution)/shard_map/ppermute | solution.py:43
  83.6 3.5 %collective-permute-done.20.c = bf16[272,256]{1,0:T(8,128)(2,1)S(1)} collective-permute-done((bf16[272,256]{1,0:T(8,128)(2,1)S(1)}, bf16[272,256]{1,0:T(8,128)(2,1)S(1)}, u32[]{:S(2)}, u32[]{:S(2)}) %collective-permute-start.20) | collective-permute-done | bytes 139296 | tf_op jit(solution)/shard_map/ppermute | solution.py:43
  88.3 1.3 %collective-permute-done.22.other = bf16[272,256]{1,0:T(8,128)(2,1)S(1)} collective-permute-done((bf16[272,256]{1,0:T(8,128)(2,1)S(1)}, bf16[272,256]{1,0:T(8,128)(2,1)S(1)}, u32[]{:S(2)}, u32[]{:S(2)}) %collective-permute-start.22) | collective-permute-done | bytes 139296 | tf_op jit(solution)/shard_map/ppermute | solution.py:43
  89.7 1.3 %shard_map.97 = (f32[272,512]{1,0:T(8,128)S(1)}, f32[272,512]{1,0:T(8,128)S(1)}, bf16[272,512]{1,0:T(8,128)(2,1)S(1)}, bf16[272,512]{1,0:T(8,128)(2,1)S(1)}) custom-call(s32[32]{0:T(128)S(1)} %dynamic-slice_bitcast_fusion.info.refs_0_, bf16[272,256]{1,0:T(8,128)(2,1)S(1)} %shard_map.95.attended, bf16[272,256]{1,0:T(8,128)(2,1)S(1)} %collective-permute-done.22.other, ...), custom_call_target="tpu_custom_call" | custom-call | flops 570425344 | bytes 4194304 | tf_op jit(solution)/shard_map/pallas_call | solution.py:107
  91.1 3.2 %collective-permute-start.26 = (bf16[272,512]{1,0:T(8,128)(2,1)S(1)}, bf16[272,512]{1,0:T(8,128)(2,1)S(1)}, u32[]{:S(2)}, u32[]{:S(2)}) collective-permute-start(bf16[272,512]{1,0:T(8,128)(2,1)S(1)} %get-tuple-element.72), channel_id=1, source_target_pairs={{0,6},{1,3},{2,0},{3,5},{4,2},{5,7},{6,4},{7,1},{8,14},{9,11},{10,... | collective-permute-start | bytes 835592 | tf_op jit(solution)/shard_map/ppermute | solution.py:43
  94.3 6.8 %collective-permute-done.24.b = bf16[272,512]{1,0:T(8,128)(2,1)S(1)} collective-permute-done((bf16[272,512]{1,0:T(8,128)(2,1)S(1)}, bf16[272,512]{1,0:T(8,128)(2,1)S(1)}, u32[]{:S(2)}, u32[]{:S(2)}) %collective-permute-start.24) | collective-permute-done | bytes 278560 | tf_op jit(solution)/shard_map/ppermute | solution.py:43
  101.7 7.3 %collective-permute-done.25.first = bf16[272,512]{1,0:T(8,128)(2,1)S(1)} collective-permute-done((bf16[272,512]{1,0:T(8,128)(2,1)S(1)}, bf16[272,512]{1,0:T(8,128)(2,1)S(1)}, u32[]{:S(2)}, u32[]{:S(2)}) %collective-permute-start.25) | collective-permute-done | bytes 278560 | tf_op jit(solution)/shard_map/ppermute | solution.py:43
  108.9 3.0 %shard_map.100 = bf16[2048,512]{1,0:T(8,128)(2,1)} custom-call(f32[272,512]{1,0:T(8,128)S(1)} %get-tuple-element.69.own, bf16[272,512]{1,0:T(8,128)(2,1)S(1)} %collective-permute-done.25.first, bf16[272,512]{1,0:T(8,128)(2,1)S(1)} %collective-permute-done.26.second, bf16[2048,384]{1,0:T(8,128)(2,1)S(1)} %shard_map.99.hot, ...), custom_call_target="tpu_custom_call" | custom-call | flops 2147483648 | bytes 6291456 | tf_op jit(solution)/shard_map/pallas_call | solution.py:464
  (49 shorter events, 12.5 us)
Async XLA Ops:
  0.0 0.7 copy-start.1
  2.7 7.9 %copy-start.2 = (f32[4096]{0:T(1024)S(1)}, f32[4096]{0:T(1024)}, u32[]{:S(2)}) copy-start(f32[4096]{0:T(1024)} %param.10) | copy-start | bytes 49156
  2.8 10.8 %collective-permute-start = (f32[8,640]{1,0:T(8,128)S(1)}, f32[8,640]{1,0:T(8,128)S(1)}, u32[]{:S(2)}, u32[]{:S(2)}) collective-permute-start(f32[8,640]{1,0:T(8,128)S(1)} %get-tuple-element.43.head), channel_id=1, source_target_pairs={{8,0},{16,8},{24,16},{32,24},{40,32},{48,40},{56,48},{64,56},{72,6... | collective-permute-start | bytes 61448 | tf_op jit(solution)/shard_map/ppermute | solution.py:521
  6.9 6.6 %collective-permute-start.1 = (f32[8,640]{1,0:T(8,128)S(1)}, f32[8,640]{1,0:T(8,128)S(1)}, u32[]{:S(2)}, u32[]{:S(2)}) collective-permute-start(f32[8,640]{1,0:T(8,128)S(1)} %get-tuple-element.44._), channel_id=1, source_target_pairs={{0,8},{8,16},{16,24},{24,32},{32,40},{40,48},{48,56},{56,64},{64,7... | collective-permute-start | bytes 61448 | tf_op jit(solution)/shard_map/ppermute | solution.py:522
  14.3 10.1 %collective-permute-start.2 = (bf16[272,512]{1,0:T(8,128)(2,1)S(1)}, bf16[272,512]{1,0:T(8,128)(2,1)S(1)}, u32[]{:S(2)}, u32[]{:S(2)}) collective-permute-start(bf16[272,512]{1,0:T(8,128)(2,1)S(1)} %get-tuple-element.46.refs_0_), channel_id=1, source_target_pairs={{0,2},{1,7},{2,4},{3,1},{4,6},{5,3},{6,0},{7,5},{8,10},{9,15},{10,... | collective-permute-start | bytes 835592 | tf_op jit(solution)/shard_map/ppermute | solution.py:43
  15.7 9.8 %collective-permute-start.3 = (bf16[272,512]{1,0:T(8,128)(2,1)S(1)}, bf16[272,512]{1,0:T(8,128)(2,1)S(1)}, u32[]{:S(2)}, u32[]{:S(2)}) collective-permute-start(bf16[272,512]{1,0:T(8,128)(2,1)S(1)} %get-tuple-element.46.refs_0_), channel_id=1, source_target_pairs={{0,6},{1,3},{2,0},{3,5},{4,2},{5,7},{6,4},{7,1},{8,14},{9,11},{10,... | collective-permute-start | bytes 835592 | tf_op jit(solution)/shard_map/ppermute | solution.py:43
  24.4 7.8 %collective-permute-start.4 = (bf16[272,512]{1,0:T(8,128)(2,1)S(1)}, bf16[272,512]{1,0:T(8,128)(2,1)S(1)}, u32[]{:S(2)}, u32[]{:S(2)}) collective-permute-start(bf16[272,512]{1,0:T(8,128)(2,1)S(1)} %collective-permute-done.2.refs_1_), channel_id=1, source_target_pairs={{0,2},{1,7},{2,4},{3,1},{4,6},{5,3},{6,0},{7,5},{8,10},{9,15},{10,... | collective-permute-start | bytes 835592 | tf_op jit(solution)/shard_map/ppermute | solution.py:43
  25.0 7.2 %collective-permute-start.5 = (bf16[272,512]{1,0:T(8,128)(2,1)S(1)}, bf16[272,512]{1,0:T(8,128)(2,1)S(1)}, u32[]{:S(2)}, u32[]{:S(2)}) collective-permute-start(bf16[272,512]{1,0:T(8,128)(2,1)S(1)} %get-tuple-element.46.refs_0_), channel_id=1, source_target_pairs={{0,1},{1,0},{2,3},{3,2},{4,5},{5,4},{6,7},{7,6},{8,9},{9,8},{10,11... | collective-permute-start | bytes 835592 | tf_op jit(solution)/shard_map/ppermute | solution.py:43
  25.0 8.7 %collective-permute-start.6 = (bf16[272,512]{1,0:T(8,128)(2,1)S(1)}, bf16[272,512]{1,0:T(8,128)(2,1)S(1)}, u32[]{:S(2)}, u32[]{:S(2)}) collective-permute-start(bf16[272,512]{1,0:T(8,128)(2,1)S(1)} %collective-permute-done.2.refs_1_), channel_id=1, source_target_pairs={{0,1},{1,0},{2,3},{3,2},{4,5},{5,4},{6,7},{7,6},{8,9},{9,8},{10,11... | collective-permute-start | bytes 835592 | tf_op jit(solution)/shard_map/ppermute | solution.py:43
  25.5 8.2 %collective-permute-start.7 = (bf16[272,512]{1,0:T(8,128)(2,1)S(1)}, bf16[272,512]{1,0:T(8,128)(2,1)S(1)}, u32[]{:S(2)}, u32[]{:S(2)}) collective-permute-start(bf16[272,512]{1,0:T(8,128)(2,1)S(1)} %collective-permute-done.3.refs_2_), channel_id=1, source_target_pairs={{0,1},{1,0},{2,3},{3,2},{4,5},{5,4},{6,7},{7,6},{8,9},{9,8},{10,11... | collective-permute-start | bytes 835592 | tf_op jit(solution)/shard_map/ppermute | solution.py:43
  32.2 1.6 %collective-permute-start.8 = (bf16[272,512]{1,0:T(8,128)(2,1)S(1)}, bf16[272,512]{1,0:T(8,128)(2,1)S(1)}, u32[]{:S(2)}, u32[]{:S(2)}) collective-permute-start(bf16[272,512]{1,0:T(8,128)(2,1)S(1)} %collective-permute-done.4.refs_3_), channel_id=1, source_target_pairs={{0,1},{1,0},{2,3},{3,2},{4,5},{5,4},{6,7},{7,6},{8,9},{9,8},{10,11... | collective-permute-start | bytes 835592 | tf_op jit(solution)/shard_map/ppermute | solution.py:43
  35.0 12.4 %collective-permute-start.12 = (bf16[272,512]{1,0:T(8,128)(2,1)S(1)}, bf16[272,512]{1,0:T(8,128)(2,1)S(1)}, u32[]{:S(2)}, u32[]{:S(2)}) collective-permute-start(bf16[272,512]{1,0:T(8,128)(2,1)S(1)} %shard_map.87.refs_10_.refs_4_), channel_id=1, source_target_pairs={{0,32},{1,225},{2,34},{3,227},{4,36},{5,229},{6,38},{7,231},{8,40}... | collective-permute-start | bytes 835592 | tf_op jit(solution)/shard_map/ppermute | solution.py:43
  36.4 11.0 %collective-permute-start.14 = (bf16[272,512]{1,0:T(8,128)(2,1)S(1)}, bf16[272,512]{1,0:T(8,128)(2,1)S(1)}, u32[]{:S(2)}, u32[]{:S(2)}) collective-permute-start(bf16[272,512]{1,0:T(8,128)(2,1)S(1)} %shard_map.87.refs_10_.refs_4_), channel_id=1, source_target_pairs={{0,224},{1,33},{2,226},{3,35},{4,228},{5,37},{6,230},{7,39},{8,232... | collective-permute-start | bytes 835592 | tf_op jit(solution)/shard_map/ppermute | solution.py:43
  41.5 13.4 %copy-start = (bf16[256,4096]{1,0:T(8,128)(2,1)S(1)}, bf16[256,4096]{1,0:T(8,128)(2,1)}, u32[]{:S(2)}) copy-start(bf16[256,4096]{1,0:T(8,128)(2,1)} %w_out.3) | copy-start | bytes 6291460
  41.5 9.2 %collective-permute-start.9 = (bf16[272,256]{1,0:T(8,128)(2,1)S(1)}, bf16[272,256]{1,0:T(8,128)(2,1)S(1)}, u32[]{:S(2)}, u32[]{:S(2)}) collective-permute-start(bf16[272,256]{1,0:T(8,128)(2,1)S(1)} %shard_map.88.refs_0_.refs_1_), channel_id=1, source_target_pairs={{0,8},{1,9},{2,10},{3,11},{4,12},{5,13},{6,14},{7,15},{8,16},{9,17... | collective-permute-start | bytes 417800 | tf_op jit(solution)/shard_map/ppermute | solution.py:43
  43.0 8.9 %collective-permute-start.10 = (bf16[272,256]{1,0:T(8,128)(2,1)S(1)}, bf16[272,256]{1,0:T(8,128)(2,1)S(1)}, u32[]{:S(2)}, u32[]{:S(2)}) collective-permute-start(bf16[272,256]{1,0:T(8,128)(2,1)S(1)} %shard_map.88.refs_0_.refs_1_), channel_id=1, source_target_pairs={{0,16},{1,17},{2,18},{3,19},{4,20},{5,21},{6,22},{7,23},{8,24},{9,... | collective-permute-start | bytes 417800 | tf_op jit(solution)/shard_map/ppermute | solution.py:43
  47.4 6.7 %collective-permute-start.11 = (bf16[272,256]{1,0:T(8,128)(2,1)S(1)}, bf16[272,256]{1,0:T(8,128)(2,1)S(1)}, u32[]{:S(2)}, u32[]{:S(2)}) collective-permute-start(bf16[272,256]{1,0:T(8,128)(2,1)S(1)} %shard_map.88.refs_0_.refs_1_), channel_id=1, source_target_pairs={{0,24},{1,25},{2,26},{3,27},{4,28},{5,29},{6,30},{7,31},{8,0},{9,1... | collective-permute-start | bytes 417800 | tf_op jit(solution)/shard_map/ppermute | solution.py:43
  47.4 9.1 %collective-permute-start.13 = (bf16[272,512]{1,0:T(8,128)(2,1)S(1)}, bf16[272,512]{1,0:T(8,128)(2,1)S(1)}, u32[]{:S(2)}, u32[]{:S(2)}) collective-permute-start(bf16[272,512]{1,0:T(8,128)(2,1)S(1)} %collective-permute-done.12.refs_4_), channel_id=1, source_target_pairs={{0,32},{1,225},{2,34},{3,227},{4,36},{5,229},{6,38},{7,231},{8,40}... | collective-permute-start | bytes 835592 | tf_op jit(solution)/shard_map/ppermute | solution.py:43
  47.5 9.0 %collective-permute-start.15 = (bf16[272,512]{1,0:T(8,128)(2,1)S(1)}, bf16[272,512]{1,0:T(8,128)(2,1)S(1)}, u32[]{:S(2)}, u32[]{:S(2)}) collective-permute-start(bf16[272,512]{1,0:T(8,128)(2,1)S(1)} %collective-permute-done.14.refs_5_), channel_id=1, source_target_pairs={{0,224},{1,33},{2,226},{3,35},{4,228},{5,37},{6,230},{7,39},{8,232... | collective-permute-start | bytes 835592 | tf_op jit(solution)/shard_map/ppermute | solution.py:43
  55.6 32.7 %collective-permute-start.23 = (bf16[4,256,512]{2,1,0:T(8,128)(2,1)S(1)}, bf16[4,256,512]{2,1,0:T(8,128)(2,1)S(1)}, u32[]{:S(2)}, u32[]{:S(2)}) collective-permute-start(bf16[4,256,512]{2,1,0:T(8,128)(2,1)S(1)} %shard_map.96), channel_id=1, source_target_pairs={{0,1},{1,0},{2,3},{3,2},{4,5},{5,4},{6,7},{7,6},{8,9},{9,8},{10,11... | collective-permute-start | bytes 3145736 | tf_op jit(solution)/shard_map/ppermute | solution.py:43
  57.0 9.1 %collective-permute-start.16 = (bf16[272,512]{1,0:T(8,128)(2,1)S(1)}, bf16[272,512]{1,0:T(8,128)(2,1)S(1)}, u32[]{:S(2)}, u32[]{:S(2)}) collective-permute-start(bf16[272,512]{1,0:T(8,128)(2,1)S(1)} %get-tuple-element.55.refs_5_), channel_id=1, source_target_pairs={{0,32},{1,225},{2,34},{3,227},{4,36},{5,229},{6,38},{7,231},{8,40}... | collective-permute-start | bytes 835592 | tf_op jit(solution)/shard_map/ppermute | solution.py:43
  57.1 10.5 %collective-permute-start.18 = (bf16[272,512]{1,0:T(8,128)(2,1)S(1)}, bf16[272,512]{1,0:T(8,128)(2,1)S(1)}, u32[]{:S(2)}, u32[]{:S(2)}) collective-permute-start(bf16[272,512]{1,0:T(8,128)(2,1)S(1)} %get-tuple-element.56.refs_6_), channel_id=1, source_target_pairs={{0,224},{1,33},{2,226},{3,35},{4,228},{5,37},{6,230},{7,39},{8,232... | collective-permute-start | bytes 835592 | tf_op jit(solution)/shard_map/ppermute | solution.py:43
  66.7 8.6 %collective-permute-start.17 = (bf16[272,512]{1,0:T(8,128)(2,1)S(1)}, bf16[272,512]{1,0:T(8,128)(2,1)S(1)}, u32[]{:S(2)}, u32[]{:S(2)}) collective-permute-start(bf16[272,512]{1,0:T(8,128)(2,1)S(1)} %shard_map.92.refs_4_), channel_id=1, source_target_pairs={{0,32},{1,225},{2,34},{3,227},{4,36},{5,229},{6,38},{7,231},{8,40}... | collective-permute-start | bytes 835592 | tf_op jit(solution)/shard_map/ppermute | solution.py:43
  76.3 7.3 %collective-permute-start.19 = (bf16[272,256]{1,0:T(8,128)(2,1)S(1)}, bf16[272,256]{1,0:T(8,128)(2,1)S(1)}, u32[]{:S(2)}, u32[]{:S(2)}) collective-permute-start(bf16[272,256]{1,0:T(8,128)(2,1)S(1)} %get-tuple-element.65), channel_id=1, source_target_pairs={{0,24},{1,25},{2,26},{3,27},{4,28},{5,29},{6,30},{7,31},{8,0},{9,1... | collective-permute-start | bytes 417800 | tf_op jit(solution)/shard_map/ppermute | solution.py:43
  80.5 6.6 %collective-permute-start.20 = (bf16[272,256]{1,0:T(8,128)(2,1)S(1)}, bf16[272,256]{1,0:T(8,128)(2,1)S(1)}, u32[]{:S(2)}, u32[]{:S(2)}) collective-permute-start(bf16[272,256]{1,0:T(8,128)(2,1)S(1)} %get-tuple-element.66), channel_id=1, source_target_pairs={{0,16},{1,17},{2,18},{3,19},{4,20},{5,21},{6,22},{7,23},{8,24},{9,... | collective-permute-start | bytes 417800 | tf_op jit(solution)/shard_map/ppermute | solution.py:43
  80.6 6.5 %collective-permute-start.21 = (bf16[272,256]{1,0:T(8,128)(2,1)S(1)}, bf16[272,256]{1,0:T(8,128)(2,1)S(1)}, u32[]{:S(2)}, u32[]{:S(2)}) collective-permute-start(bf16[272,256]{1,0:T(8,128)(2,1)S(1)} %get-tuple-element.67), channel_id=1, source_target_pairs={{0,8},{1,9},{2,10},{3,11},{4,12},{5,13},{6,14},{7,15},{8,16},{9,17... | collective-permute-start | bytes 417800 | tf_op jit(solution)/shard_map/ppermute | solution.py:43
  88.2 1.4 %collective-permute-start.22 = (bf16[272,256]{1,0:T(8,128)(2,1)S(1)}, bf16[272,256]{1,0:T(8,128)(2,1)S(1)}, u32[]{:S(2)}, u32[]{:S(2)}) collective-permute-start(bf16[272,256]{1,0:T(8,128)(2,1)S(1)} %shard_map.95.attended), channel_id=1, source_target_pairs={{0,1},{1,0},{2,3},{3,2},{4,5},{5,4},{6,7},{7,6},{8,9},{9,8},{10,11... | collective-permute-start | bytes 417800 | tf_op jit(solution)/shard_map/ppermute | solution.py:43
  91.0 10.1 %collective-permute-start.24 = (bf16[272,512]{1,0:T(8,128)(2,1)S(1)}, bf16[272,512]{1,0:T(8,128)(2,1)S(1)}, u32[]{:S(2)}, u32[]{:S(2)}) collective-permute-start(bf16[272,512]{1,0:T(8,128)(2,1)S(1)} %get-tuple-element.71), channel_id=1, source_target_pairs={{0,2},{1,7},{2,4},{3,1},{4,6},{5,3},{6,0},{7,5},{8,10},{9,15},{10,... | collective-permute-start | bytes 835592 | tf_op jit(solution)/shard_map/ppermute | solution.py:43
  91.1 10.6 %collective-permute-start.26 = (bf16[272,512]{1,0:T(8,128)(2,1)S(1)}, bf16[272,512]{1,0:T(8,128)(2,1)S(1)}, u32[]{:S(2)}, u32[]{:S(2)}) collective-permute-start(bf16[272,512]{1,0:T(8,128)(2,1)S(1)} %get-tuple-element.72), channel_id=1, source_target_pairs={{0,6},{1,3},{2,0},{3,5},{4,2},{5,7},{6,4},{7,1},{8,14},{9,11},{10,... | collective-permute-start | bytes 835592 | tf_op jit(solution)/shard_map/ppermute | solution.py:43
  101.1 7.8 %collective-permute-start.25 = (bf16[272,512]{1,0:T(8,128)(2,1)S(1)}, bf16[272,512]{1,0:T(8,128)(2,1)S(1)}, u32[]{:S(2)}, u32[]{:S(2)}) collective-permute-start(bf16[272,512]{1,0:T(8,128)(2,1)S(1)} %shard_map.98), channel_id=1, source_target_pairs={{0,2},{1,7},{2,4},{3,1},{4,6},{5,3},{6,0},{7,5},{8,10},{9,15},{10,... | collective-permute-start | bytes 835592 | tf_op jit(solution)/shard_map/ppermute | solution.py:43

commit v9 on v8

--- a/solution.py
+++ b/solution.py
@@ -197,7 +197,7 @@
     return out
 
 
-def norm_kernel(info, sums, counts, head, above, below, gain, _, means_out, u_out, bias_out):
+def norm_kernel(info, sums, counts, head, above, below, gain, means_out, u_out, bias_out):
     g = gain[pl.ds(info[I_MP], 1), :]
     last = iota((SEG, 128), 0) == SEG - 1
     size = counts[...] + jnp.where(last, above[0:1, FEAT:], 0.0)
@@ -234,15 +234,14 @@
     return scale, wide(column, 2)
 
 
-def load_kernel(_, *refs):
-    sources, outs, done, sems = refs[:3], refs[3:6], refs[6], refs[7]
+def load_kernel(*refs):
+    sources, outs, sems = refs[:3], refs[4:7], refs[8]
     copies = []
     for n in range(3):
         for i in range(4):
             rows = pl.ds(i * (WIDTH // 4), WIDTH // 4)
             copies.append(pltpu.make_async_copy(sources[n].at[rows, :], outs[n].at[rows, :], sems.at[n, i]))
             copies[-1].start()
-    done[...] = jnp.zeros_like(done)
     for copy in copies:
         copy.wait()
 
@@ -520,16 +519,6 @@
     count = NZ * NX
     above = lax.ppermute(head, "seq", [(i, i - 1) for i in range(1, count)])
     below = lax.ppermute(tail, "seq", [(i, i + 1) for i in range(count - 1)])
-    *weights, loaded = call(
-        load_kernel,
-        [shape((WIDTH, COLS), BF16)] * 3 + [shape((8, 128), F32)],
-        [tail, w_query, w_key, w_value],
-        scalars=None,
-        moved=12 << 20,
-        scratch=[pltpu.SemaphoreType.DMA((3, 4))],
-        far_in=range(4),
-        room=ROOM,
-    )
     sums, sizes = call(
         pool_kernel,
         [shape((SEG, FEAT), F32), shape((SEG, 128), F32)],
@@ -542,9 +531,21 @@
     means, u, bias = call(
         norm_kernel,
         [shape((ROWS, FEAT), F32), shape((ROWS, FEAT), BF16), shape((16, FEAT), BF16)],
-        [info, sums, sizes, head, above, below, norm_gain.reshape(8, FEAT), loaded],
-    )
-    first, sibling, second = y_one(u), swap(u), y_other(u)
+        [info, sums, sizes, head, above, below, norm_gain.reshape(8, FEAT)],
+    )
+    *weights, handed = call(
+        load_kernel,
+        [shape((WIDTH, COLS), BF16)] * 3 + [shape(u.shape, BF16)],
+        [w_query, w_key, w_value, u],
+        scalars=None,
+        moved=12 << 20,
+        scratch=[pltpu.SemaphoreType.DMA((3, 4))],
+        aliases={3: 3},
+        far_in=range(4),
+        far_out=(3,),
+        room=ROOM,
+    )
+    first, sibling, second = y_one(u), swap(handed), y_other(u)
     across = swap(first)
     part, part_query = shape((SEG, COLS), F32), shape((ROWS, COLS), F32)
     queried, keyed, valued = call(

time: 114 us -> 113 us (level)
    ppermute x1, waiting for transfers between devices: 0.01 us -> 2 us  [shards(): below = lax.ppermute(tail, 'seq', [(i, i + 1) for i in range(count - 1)])]
    ppermute x25, waiting for transfers between devices: 47.6 us -> 45.6 us  [move(): return lax.ppermute(value, ('seq', 'mp'), pairs)]
  transfers between devices with their start and end apart: 27 -> 27, of which waited for: 13 -> 14; matrix products, arithmetic and copies ran while one was open for 1% -> 1% of each run, Pallas kernels for 13% -> 13%
where the time goes in v9:
time: 113 us; the launch traced here: 112 us
  waiting for transfers between devices  47.6 us (42%)
  starting transfers between devices  39.6 us (35%)
  Pallas kernels  23 us (20%)
  local copies, waits for them, and re-layouts  1.43 us (1%)
    ppermute x25, waiting for transfers between devices, move(): return lax.ppermute(value, ('seq', 'mp'), pairs)  45.6 us
    ppermute x25, starting transfers between devices, move(): return lax.ppermute(value, ('seq', 'mp'), pairs)  33.5 us
    pallas_call x18, Pallas kernels, call(): pl.pallas_call(body, out_shape=outs, in_specs=[SMEM if i == scalars else...  20 us
    ppermute x1, starting transfers between devices, shards(): above = lax.ppermute(head, 'seq', [(i, i - 1) for i in range(1, count)])  4.18 us
    pallas_call x1, Pallas kernels, output(): pl.pallas_call(output_kernel, grid=(TOK // BLOCK,), out_shape=shape((TOK,...  3.03 us
  transfers between devices with their start and end apart: 27, of which 14 were waited for; matrix products, arithmetic and copies ran while one was open for 1% of the time, Pallas kernels for 13%

profile of v9, /device:TPU:2, one launch (start us, length us, event | category | flops | bytes accessed | tf_op | source)
XLA Modules:
  0.0 112.1 jit_solution(3189118006606790420)
XLA Ops:
  0.7 2.0 %shard_map.82 = (bf16[2048,512]{1,0:T(8,128)(2,1)S(1)}, s32[16,128]{1,0:T(8,128)S(1)}, f32[8,640]{1,0:T(8,128)S(1)}, f32[8,640]{1,0:T(8,128)S(1)}) custom-call(s32[16,128]{1,0:T(8,128)S(1)} %bitcast.3, bf16[2048,512]{1,0:T(8,128)(2,1)} %tokens_in.1), custom_call_target="tpu_custom_call" | custom-call | flops 268435456 | bytes 2097152 | tf_op jit(solution)/shard_map/pallas_call | solution.py:107
  2.8 4.2 %collective-permute-start = (f32[8,640]{1,0:T(8,128)S(1)}, f32[8,640]{1,0:T(8,128)S(1)}, u32[]{:S(2)}, u32[]{:S(2)}) collective-permute-start(f32[8,640]{1,0:T(8,128)S(1)} %get-tuple-element.43.head), channel_id=1, source_target_pairs={{8,0},{16,8},{24,16},{32,24},{40,32},{48,40},{56,48},{64,56},{72,6... | collective-permute-start | bytes 61448 | tf_op jit(solution)/shard_map/ppermute | solution.py:520
  6.9 1.9 %collective-permute-start.1 = (f32[8,640]{1,0:T(8,128)S(1)}, f32[8,640]{1,0:T(8,128)S(1)}, u32[]{:S(2)}, u32[]{:S(2)}) collective-permute-start(f32[8,640]{1,0:T(8,128)S(1)} %get-tuple-element.44), channel_id=1, source_target_pairs={{0,8},{8,16},{16,24},{24,32},{32,40},{40,48},{48,56},{56,64},{64,7... | collective-permute-start | bytes 61448 | tf_op jit(solution)/shard_map/ppermute | solution.py:521
  10.6 2.0 %collective-permute-done.1.below = f32[8,640]{1,0:T(8,128)S(1)} collective-permute-done((f32[8,640]{1,0:T(8,128)S(1)}, f32[8,640]{1,0:T(8,128)S(1)}, u32[]{:S(2)}, u32[]{:S(2)}) %collective-permute-start.1) | collective-permute-done | bytes 20512 | tf_op jit(solution)/shard_map/ppermute | solution.py:521
  13.5 3.2 %collective-permute-start.3 = (bf16[272,512]{1,0:T(8,128)(2,1)S(1)}, bf16[272,512]{1,0:T(8,128)(2,1)S(1)}, u32[]{:S(2)}, u32[]{:S(2)}) collective-permute-start(bf16[272,512]{1,0:T(8,128)(2,1)S(1)} %get-tuple-element.45.refs_0_), channel_id=1, source_target_pairs={{0,6},{1,3},{2,0},{3,5},{4,2},{5,7},{6,4},{7,1},{8,14},{9,11},{10,... | collective-permute-start | bytes 835592 | tf_op jit(solution)/shard_map/ppermute | solution.py:43
  16.7 6.3 %collective-permute-done.2.refs_1_ = bf16[272,512]{1,0:T(8,128)(2,1)S(1)} collective-permute-done((bf16[272,512]{1,0:T(8,128)(2,1)S(1)}, bf16[272,512]{1,0:T(8,128)(2,1)S(1)}, u32[]{:S(2)}, u32[]{:S(2)}) %collective-permute-start.2) | collective-permute-done | bytes 278560 | tf_op jit(solution)/shard_map/ppermute | solution.py:43
  23.0 2.9 %shard_map.85 = (bf16[4096,256]{1,0:T(8,128)(2,1)S(1)}, bf16[4096,256]{1,0:T(8,128)(2,1)S(1)}, bf16[4096,256]{1,0:T(8,128)(2,1)S(1)}, bf16[272,512]{1,0:T(8,128)(2,1)S(1)}) custom-call(bf16[4096,256]{1,0:T(8,128)(2,1)} %refs_0_.1, bf16[4096,256]{1,0:T(8,128)(2,1)} %refs_1_.1, bf16[4096,256]{1,0:T(8,128)(2,1)} %refs_2_.1, ...), custom_call_target="tpu_custom_call", output_to_operand_aliasing={{3}: (3, {})} | custom-call | bytes 12582912 | tf_op jit(solution)/shard_map/pallas_call | solution.py:107
  26.6 4.1 %collective-permute-done.4.refs_3_ = bf16[272,512]{1,0:T(8,128)(2,1)S(1)} collective-permute-done((bf16[272,512]{1,0:T(8,128)(2,1)S(1)}, bf16[272,512]{1,0:T(8,128)(2,1)S(1)}, u32[]{:S(2)}, u32[]{:S(2)}) %collective-permute-start.4) | collective-permute-done | bytes 278560 | tf_op jit(solution)/shard_map/ppermute | solution.py:43
  30.8 1.6 %shard_map.86 = (f32[272,256]{1,0:T(8,128)S(1)}, f32[256,256]{1,0:T(8,128)S(1)}, f32[256,256]{1,0:T(8,128)S(1)}) custom-call(s32[32]{0:T(128)S(1)} %dynamic-slice_bitcast_fusion.info.refs_0_, bf16[272,512]{1,0:T(8,128)(2,1)S(1)} %get-tuple-element.45.refs_0_, bf16[272,512]{1,0:T(8,128)(2,1)S(1)} %collective-permute-done.2.refs_1_, ...), custom_call_target="tpu_custom_call" | custom-call | flops 855638016 | bytes 3145728 | tf_op jit(solution)/shard_map/pallas_call | solution.py:107
  32.4 1.3 %shard_map.87.refs_10_.refs_4_ = bf16[272,512]{1,0:T(8,128)(2,1)S(1)} custom-call(s32[32]{0:T(128)S(1)} %dynamic-slice_bitcast_fusion.info.refs_0_, bf16[272,512]{1,0:T(8,128)(2,1)S(1)} %get-tuple-element.45.refs_0_, bf16[272,512]{1,0:T(8,128)(2,1)S(1)} %collective-permute-done.2.refs_1_, bf16[272,512]{1,0:T(8,128)(2,1)S(1)} %collective-permute-done.3.refs_2_, ...), custom_call_target="tpu_custom_call" | custom-call | tf_op jit(solution)/shard_map/pallas_call | solution.py:107
  33.6 1.4 %collective-permute-start.12 = (bf16[272,512]{1,0:T(8,128)(2,1)S(1)}, bf16[272,512]{1,0:T(8,128)(2,1)S(1)}, u32[]{:S(2)}, u32[]{:S(2)}) collective-permute-start(bf16[272,512]{1,0:T(8,128)(2,1)S(1)} %shard_map.87.refs_10_.refs_4_), channel_id=1, source_target_pairs={{0,32},{1,225},{2,34},{3,227},{4,36},{5,229},{6,38},{7,231},{8,40}... | collective-permute-start | bytes 835592 | tf_op jit(solution)/shard_map/ppermute | solution.py:43
  35.0 4.9 %collective-permute-start.14 = (bf16[272,512]{1,0:T(8,128)(2,1)S(1)}, bf16[272,512]{1,0:T(8,128)(2,1)S(1)}, u32[]{:S(2)}, u32[]{:S(2)}) collective-permute-start(bf16[272,512]{1,0:T(8,128)(2,1)S(1)} %shard_map.87.refs_10_.refs_4_), channel_id=1, source_target_pairs={{0,224},{1,33},{2,226},{3,35},{4,228},{5,37},{6,230},{7,39},{8,232... | collective-permute-start | bytes 835592 | tf_op jit(solution)/shard_map/ppermute | solution.py:43
  41.2 6.2 %collective-permute-start.10 = (bf16[272,256]{1,0:T(8,128)(2,1)S(1)}, bf16[272,256]{1,0:T(8,128)(2,1)S(1)}, u32[]{:S(2)}, u32[]{:S(2)}) collective-permute-start(bf16[272,256]{1,0:T(8,128)(2,1)S(1)} %shard_map.88.refs_0_.refs_1_), channel_id=1, source_target_pairs={{0,16},{1,17},{2,18},{3,19},{4,20},{5,21},{6,22},{7,23},{8,24},{9,... | collective-permute-start | bytes 417800 | tf_op jit(solution)/shard_map/ppermute | solution.py:43
  47.5 3.2 %collective-permute-start.15 = (bf16[272,512]{1,0:T(8,128)(2,1)S(1)}, bf16[272,512]{1,0:T(8,128)(2,1)S(1)}, u32[]{:S(2)}, u32[]{:S(2)}) collective-permute-start(bf16[272,512]{1,0:T(8,128)(2,1)S(1)} %collective-permute-done.14.refs_5_), channel_id=1, source_target_pairs={{0,224},{1,33},{2,226},{3,35},{4,228},{5,37},{6,230},{7,39},{8,232... | collective-permute-start | bytes 835592 | tf_op jit(solution)/shard_map/ppermute | solution.py:43
  50.7 1.2 %collective-permute-done.10.refs_2_.refs_3_ = bf16[272,256]{1,0:T(8,128)(2,1)S(1)} collective-permute-done((bf16[272,256]{1,0:T(8,128)(2,1)S(1)}, bf16[272,256]{1,0:T(8,128)(2,1)S(1)}, u32[]{:S(2)}, u32[]{:S(2)}) %collective-permute-start.10) | collective-permute-done | bytes 139296 | tf_op jit(solution)/shard_map/ppermute | solution.py:43
  51.9 2.2 %collective-permute-done.11.refs_3_.refs_4_ = bf16[272,256]{1,0:T(8,128)(2,1)S(1)} collective-permute-done((bf16[272,256]{1,0:T(8,128)(2,1)S(1)}, bf16[272,256]{1,0:T(8,128)(2,1)S(1)}, u32[]{:S(2)}, u32[]{:S(2)}) %collective-permute-start.11) | collective-permute-done | bytes 139296 | tf_op jit(solution)/shard_map/ppermute | solution.py:43
  55.7 1.2 %collective-permute-done.13.refs_0_ = bf16[272,512]{1,0:T(8,128)(2,1)S(1)} collective-permute-done((bf16[272,512]{1,0:T(8,128)(2,1)S(1)}, bf16[272,512]{1,0:T(8,128)(2,1)S(1)}, u32[]{:S(2)}, u32[]{:S(2)}) %collective-permute-start.13) | collective-permute-done | bytes 278560 | tf_op jit(solution)/shard_map/ppermute | solution.py:43
  57.5 3.7 %collective-permute-start.18 = (bf16[272,512]{1,0:T(8,128)(2,1)S(1)}, bf16[272,512]{1,0:T(8,128)(2,1)S(1)}, u32[]{:S(2)}, u32[]{:S(2)}) collective-permute-start(bf16[272,512]{1,0:T(8,128)(2,1)S(1)} %get-tuple-element.56.refs_6_), channel_id=1, source_target_pairs={{0,224},{1,33},{2,226},{3,35},{4,228},{5,37},{6,230},{7,39},{8,232... | collective-permute-start | bytes 835592 | tf_op jit(solution)/shard_map/ppermute | solution.py:43
  61.2 2.1 %shard_map.91 = (f32[4,2,272,256]{3,2,1,0:T(8,128)S(1)}, f32[4,2,272,128]{3,2,1,0:T(8,128)S(1)}, f32[8,128]{1,0:T(8,128)S(1)}) custom-call(s32[32]{0:T(128)S(1)} %dynamic-slice_bitcast_fusion.info.refs_0_, bf16[272,256]{1,0:T(8,128)(2,1)S(1)} %shard_map.88.refs_0_.refs_1_, ...), custom_call_target="tpu_custom_call", output_to_operand_aliasing={{0}: (8, {}), {1}: (9, {})} | custom-call | flops 855638016 | bytes 4194304 | tf_op jit(solution)/shard_map/pallas_call | solution.py:107
  63.2 2.9 %collective-permute-done.16.refs_0_ = bf16[272,512]{1,0:T(8,128)(2,1)S(1)} collective-permute-done((bf16[272,512]{1,0:T(8,128)(2,1)S(1)}, bf16[272,512]{1,0:T(8,128)(2,1)S(1)}, u32[]{:S(2)}, u32[]{:S(2)}) %collective-permute-start.16) | collective-permute-done | bytes 278560 | tf_op jit(solution)/shard_map/ppermute | solution.py:43
  67.6 1.1 %shard_map.93 = (f32[4,2,272,256]{3,2,1,0:T(8,128)S(1)}, f32[4,2,272,128]{3,2,1,0:T(8,128)S(1)}, f32[8,128]{1,0:T(8,128)}) custom-call(s32[32]{0:T(128)S(1)} %dynamic-slice_bitcast_fusion.info.refs_0_, bf16[272,256]{1,0:T(8,128)(2,1)S(1)} %shard_map.88.refs_0_.refs_1_, ...), custom_call_target="tpu_custom_call", output_to_operand_aliasing={{0}: (7, {}), {1}: (8, {})} | custom-call | flops 855638016 | bytes 4194304 | tf_op jit(solution)/shard_map/pallas_call | solution.py:107
  68.7 6.6 %collective-permute-done.17.refs_5_ = bf16[272,512]{1,0:T(8,128)(2,1)S(1)} collective-permute-done((bf16[272,512]{1,0:T(8,128)(2,1)S(1)}, bf16[272,512]{1,0:T(8,128)(2,1)S(1)}, u32[]{:S(2)}, u32[]{:S(2)}) %collective-permute-start.17) | collective-permute-done | bytes 278560 | tf_op jit(solution)/shard_map/ppermute | solution.py:43
  76.2 4.4 %collective-permute-start.19 = (bf16[272,256]{1,0:T(8,128)(2,1)S(1)}, bf16[272,256]{1,0:T(8,128)(2,1)S(1)}, u32[]{:S(2)}, u32[]{:S(2)}) collective-permute-start(bf16[272,256]{1,0:T(8,128)(2,1)S(1)} %get-tuple-element.65), channel_id=1, source_target_pairs={{0,24},{1,25},{2,26},{3,27},{4,28},{5,29},{6,30},{7,31},{8,0},{9,1... | collective-permute-start | bytes 417800 | tf_op jit(solution)/shard_map/ppermute | solution.py:43
  80.8 1.5 %collective-permute-start.21 = (bf16[272,256]{1,0:T(8,128)(2,1)S(1)}, bf16[272,256]{1,0:T(8,128)(2,1)S(1)}, u32[]{:S(2)}, u32[]{:S(2)}) collective-permute-start(bf16[272,256]{1,0:T(8,128)(2,1)S(1)} %get-tuple-element.67), channel_id=1, source_target_pairs={{0,8},{1,9},{2,10},{3,11},{4,12},{5,13},{6,14},{7,15},{8,16},{9,17... | collective-permute-start | bytes 417800 | tf_op jit(solution)/shard_map/ppermute | solution.py:43
  82.3 1.6 %collective-permute-done.19.b = bf16[272,256]{1,0:T(8,128)(2,1)S(1)} collective-permute-done((bf16[272,256]{1,0:T(8,128)(2,1)S(1)}, bf16[272,256]{1,0:T(8,128)(2,1)S(1)}, u32[]{:S(2)}, u32[]{:S(2)}) %collective-permute-start.19) | collective-permute-done | bytes 139296 | tf_op jit(solution)/shard_map/ppermute | solution.py:43
  83.9 3.3 %collective-permute-done.20.c = bf16[272,256]{1,0:T(8,128)(2,1)S(1)} collective-permute-done((bf16[272,256]{1,0:T(8,128)(2,1)S(1)}, bf16[272,256]{1,0:T(8,128)(2,1)S(1)}, u32[]{:S(2)}, u32[]{:S(2)}) %collective-permute-start.20) | collective-permute-done | bytes 139296 | tf_op jit(solution)/shard_map/ppermute | solution.py:43
  88.4 1.3 %collective-permute-done.22.other = bf16[272,256]{1,0:T(8,128)(2,1)S(1)} collective-permute-done((bf16[272,256]{1,0:T(8,128)(2,1)S(1)}, bf16[272,256]{1,0:T(8,128)(2,1)S(1)}, u32[]{:S(2)}, u32[]{:S(2)}) %collective-permute-start.22) | collective-permute-done | bytes 139296 | tf_op jit(solution)/shard_map/ppermute | solution.py:43
  89.7 1.3 %shard_map.97 = (f32[272,512]{1,0:T(8,128)S(1)}, f32[272,512]{1,0:T(8,128)S(1)}, bf16[272,512]{1,0:T(8,128)(2,1)S(1)}, bf16[272,512]{1,0:T(8,128)(2,1)S(1)}) custom-call(s32[32]{0:T(128)S(1)} %dynamic-slice_bitcast_fusion.info.refs_0_, bf16[272,256]{1,0:T(8,128)(2,1)S(1)} %shard_map.95.attended, bf16[272,256]{1,0:T(8,128)(2,1)S(1)} %collective-permute-done.22.other, ...), custom_call_target="tpu_custom_call" | custom-call | flops 570425344 | bytes 4194304 | tf_op jit(solution)/shard_map/pallas_call | solution.py:107
  91.1 3.2 %collective-permute-start.26 = (bf16[272,512]{1,0:T(8,128)(2,1)S(1)}, bf16[272,512]{1,0:T(8,128)(2,1)S(1)}, u32[]{:S(2)}, u32[]{:S(2)}) collective-permute-start(bf16[272,512]{1,0:T(8,128)(2,1)S(1)} %get-tuple-element.72), channel_id=1, source_target_pairs={{0,6},{1,3},{2,0},{3,5},{4,2},{5,7},{6,4},{7,1},{8,14},{9,11},{10,... | collective-permute-start | bytes 835592 | tf_op jit(solution)/shard_map/ppermute | solution.py:43
  94.4 6.8 %collective-permute-done.24.b = bf16[272,512]{1,0:T(8,128)(2,1)S(1)} collective-permute-done((bf16[272,512]{1,0:T(8,128)(2,1)S(1)}, bf16[272,512]{1,0:T(8,128)(2,1)S(1)}, u32[]{:S(2)}, u32[]{:S(2)}) %collective-permute-start.24) | collective-permute-done | bytes 278560 | tf_op jit(solution)/shard_map/ppermute | solution.py:43
  101.7 7.3 %collective-permute-done.25.first = bf16[272,512]{1,0:T(8,128)(2,1)S(1)} collective-permute-done((bf16[272,512]{1,0:T(8,128)(2,1)S(1)}, bf16[272,512]{1,0:T(8,128)(2,1)S(1)}, u32[]{:S(2)}, u32[]{:S(2)}) %collective-permute-start.25) | collective-permute-done | bytes 278560 | tf_op jit(solution)/shard_map/ppermute | solution.py:43
  109.0 3.0 %shard_map.100 = bf16[2048,512]{1,0:T(8,128)(2,1)} custom-call(f32[272,512]{1,0:T(8,128)S(1)} %get-tuple-element.69.own, bf16[272,512]{1,0:T(8,128)(2,1)S(1)} %collective-permute-done.25.first, bf16[272,512]{1,0:T(8,128)(2,1)S(1)} %collective-permute-done.26.second, bf16[2048,384]{1,0:T(8,128)(2,1)S(1)} %shard_map.99.hot, ...), custom_call_target="tpu_custom_call" | custom-call | flops 2147483648 | bytes 6291456 | tf_op jit(solution)/shard_map/pallas_call | solution.py:463
  (50 shorter events, 11.9 us)
Async XLA Ops:
  0.0 0.7 copy-start.1
  2.7 7.8 %copy-start.2 = (f32[4096]{0:T(1024)S(1)}, f32[4096]{0:T(1024)}, u32[]{:S(2)}) copy-start(f32[4096]{0:T(1024)} %param.10) | copy-start | bytes 49156
  2.8 7.9 %collective-permute-start = (f32[8,640]{1,0:T(8,128)S(1)}, f32[8,640]{1,0:T(8,128)S(1)}, u32[]{:S(2)}, u32[]{:S(2)}) collective-permute-start(f32[8,640]{1,0:T(8,128)S(1)} %get-tuple-element.43.head), channel_id=1, source_target_pairs={{8,0},{16,8},{24,16},{32,24},{40,32},{48,40},{56,48},{64,56},{72,6... | collective-permute-start | bytes 61448 | tf_op jit(solution)/shard_map/ppermute | solution.py:520
  6.9 5.7 %collective-permute-start.1 = (f32[8,640]{1,0:T(8,128)S(1)}, f32[8,640]{1,0:T(8,128)S(1)}, u32[]{:S(2)}, u32[]{:S(2)}) collective-permute-start(f32[8,640]{1,0:T(8,128)S(1)} %get-tuple-element.44), channel_id=1, source_target_pairs={{0,8},{8,16},{16,24},{24,32},{32,40},{40,48},{48,56},{56,64},{64,7... | collective-permute-start | bytes 61448 | tf_op jit(solution)/shard_map/ppermute | solution.py:521
  13.4 9.6 %collective-permute-start.2 = (bf16[272,512]{1,0:T(8,128)(2,1)S(1)}, bf16[272,512]{1,0:T(8,128)(2,1)S(1)}, u32[]{:S(2)}, u32[]{:S(2)}) collective-permute-start(bf16[272,512]{1,0:T(8,128)(2,1)S(1)} %get-tuple-element.45.refs_0_), channel_id=1, source_target_pairs={{0,2},{1,7},{2,4},{3,1},{4,6},{5,3},{6,0},{7,5},{8,10},{9,15},{10,... | collective-permute-start | bytes 835592 | tf_op jit(solution)/shard_map/ppermute | solution.py:43
  13.5 13.0 %collective-permute-start.3 = (bf16[272,512]{1,0:T(8,128)(2,1)S(1)}, bf16[272,512]{1,0:T(8,128)(2,1)S(1)}, u32[]{:S(2)}, u32[]{:S(2)}) collective-permute-start(bf16[272,512]{1,0:T(8,128)(2,1)S(1)} %get-tuple-element.45.refs_0_), channel_id=1, source_target_pairs={{0,6},{1,3},{2,0},{3,5},{4,2},{5,7},{6,4},{7,1},{8,14},{9,11},{10,... | collective-permute-start | bytes 835592 | tf_op jit(solution)/shard_map/ppermute | solution.py:43
  23.0 7.8 %collective-permute-start.4 = (bf16[272,512]{1,0:T(8,128)(2,1)S(1)}, bf16[272,512]{1,0:T(8,128)(2,1)S(1)}, u32[]{:S(2)}, u32[]{:S(2)}) collective-permute-start(bf16[272,512]{1,0:T(8,128)(2,1)S(1)} %collective-permute-done.2.refs_1_), channel_id=1, source_target_pairs={{0,2},{1,7},{2,4},{3,1},{4,6},{5,3},{6,0},{7,5},{8,10},{9,15},{10,... | collective-permute-start | bytes 835592 | tf_op jit(solution)/shard_map/ppermute | solution.py:43
  25.9 4.8 %collective-permute-start.5 = (bf16[272,512]{1,0:T(8,128)(2,1)S(1)}, bf16[272,512]{1,0:T(8,128)(2,1)S(1)}, u32[]{:S(2)}, u32[]{:S(2)}) collective-permute-start(bf16[272,512]{1,0:T(8,128)(2,1)S(1)} %get-tuple-element.46), channel_id=1, source_target_pairs={{0,1},{1,0},{2,3},{3,2},{4,5},{5,4},{6,7},{7,6},{8,9},{9,8},{10,11... | collective-permute-start | bytes 835592 | tf_op jit(solution)/shard_map/ppermute | solution.py:43
  26.0 6.3 %collective-permute-start.6 = (bf16[272,512]{1,0:T(8,128)(2,1)S(1)}, bf16[272,512]{1,0:T(8,128)(2,1)S(1)}, u32[]{:S(2)}, u32[]{:S(2)}) collective-permute-start(bf16[272,512]{1,0:T(8,128)(2,1)S(1)} %collective-permute-done.2.refs_1_), channel_id=1, source_target_pairs={{0,1},{1,0},{2,3},{3,2},{4,5},{5,4},{6,7},{7,6},{8,9},{9,8},{10,11... | collective-permute-start | bytes 835592 | tf_op jit(solution)/shard_map/ppermute | solution.py:43
  26.5 5.8 %collective-permute-start.7 = (bf16[272,512]{1,0:T(8,128)(2,1)S(1)}, bf16[272,512]{1,0:T(8,128)(2,1)S(1)}, u32[]{:S(2)}, u32[]{:S(2)}) collective-permute-start(bf16[272,512]{1,0:T(8,128)(2,1)S(1)} %collective-permute-done.3.refs_2_), channel_id=1, source_target_pairs={{0,1},{1,0},{2,3},{3,2},{4,5},{5,4},{6,7},{7,6},{8,9},{9,8},{10,11... | collective-permute-start | bytes 835592 | tf_op jit(solution)/shard_map/ppermute | solution.py:43
  30.8 1.6 %collective-permute-start.8 = (bf16[272,512]{1,0:T(8,128)(2,1)S(1)}, bf16[272,512]{1,0:T(8,128)(2,1)S(1)}, u32[]{:S(2)}, u32[]{:S(2)}) collective-permute-start(bf16[272,512]{1,0:T(8,128)(2,1)S(1)} %collective-permute-done.4.refs_3_), channel_id=1, source_target_pairs={{0,1},{1,0},{2,3},{3,2},{4,5},{5,4},{6,7},{7,6},{8,9},{9,8},{10,11... | collective-permute-start | bytes 835592 | tf_op jit(solution)/shard_map/ppermute | solution.py:43
  33.6 13.8 %collective-permute-start.12 = (bf16[272,512]{1,0:T(8,128)(2,1)S(1)}, bf16[272,512]{1,0:T(8,128)(2,1)S(1)}, u32[]{:S(2)}, u32[]{:S(2)}) collective-permute-start(bf16[272,512]{1,0:T(8,128)(2,1)S(1)} %shard_map.87.refs_10_.refs_4_), channel_id=1, source_target_pairs={{0,32},{1,225},{2,34},{3,227},{4,36},{5,229},{6,38},{7,231},{8,40}... | collective-permute-start | bytes 835592 | tf_op jit(solution)/shard_map/ppermute | solution.py:43
  35.0 12.4 %collective-permute-start.14 = (bf16[272,512]{1,0:T(8,128)(2,1)S(1)}, bf16[272,512]{1,0:T(8,128)(2,1)S(1)}, u32[]{:S(2)}, u32[]{:S(2)}) collective-permute-start(bf16[272,512]{1,0:T(8,128)(2,1)S(1)} %shard_map.87.refs_10_.refs_4_), channel_id=1, source_target_pairs={{0,224},{1,33},{2,226},{3,35},{4,228},{5,37},{6,230},{7,39},{8,232... | collective-permute-start | bytes 835592 | tf_op jit(solution)/shard_map/ppermute | solution.py:43
  40.9 13.9 %copy-start = (bf16[256,4096]{1,0:T(8,128)(2,1)S(1)}, bf16[256,4096]{1,0:T(8,128)(2,1)}, u32[]{:S(2)}) copy-start(bf16[256,4096]{1,0:T(8,128)(2,1)} %w_out.3) | copy-start | bytes 6291460
  41.0 9.7 %collective-permute-start.9 = (bf16[272,256]{1,0:T(8,128)(2,1)S(1)}, bf16[272,256]{1,0:T(8,128)(2,1)S(1)}, u32[]{:S(2)}, u32[]{:S(2)}) collective-permute-start(bf16[272,256]{1,0:T(8,128)(2,1)S(1)} %shard_map.88.refs_0_.refs_1_), channel_id=1, source_target_pairs={{0,8},{1,9},{2,10},{3,11},{4,12},{5,13},{6,14},{7,15},{8,16},{9,17... | collective-permute-start | bytes 417800 | tf_op jit(solution)/shard_map/ppermute | solution.py:43
  41.2 10.7 %collective-permute-start.10 = (bf16[272,256]{1,0:T(8,128)(2,1)S(1)}, bf16[272,256]{1,0:T(8,128)(2,1)S(1)}, u32[]{:S(2)}, u32[]{:S(2)}) collective-permute-start(bf16[272,256]{1,0:T(8,128)(2,1)S(1)} %shard_map.88.refs_0_.refs_1_), channel_id=1, source_target_pairs={{0,16},{1,17},{2,18},{3,19},{4,20},{5,21},{6,22},{7,23},{8,24},{9,... | collective-permute-start | bytes 417800 | tf_op jit(solution)/shard_map/ppermute | solution.py:43
  47.4 6.7 %collective-permute-start.11 = (bf16[272,256]{1,0:T(8,128)(2,1)S(1)}, bf16[272,256]{1,0:T(8,128)(2,1)S(1)}, u32[]{:S(2)}, u32[]{:S(2)}) collective-permute-start(bf16[272,256]{1,0:T(8,128)(2,1)S(1)} %shard_map.88.refs_0_.refs_1_), channel_id=1, source_target_pairs={{0,24},{1,25},{2,26},{3,27},{4,28},{5,29},{6,30},{7,31},{8,0},{9,1... | collective-permute-start | bytes 417800 | tf_op jit(solution)/shard_map/ppermute | solution.py:43
  47.4 9.4 %collective-permute-start.13 = (bf16[272,512]{1,0:T(8,128)(2,1)S(1)}, bf16[272,512]{1,0:T(8,128)(2,1)S(1)}, u32[]{:S(2)}, u32[]{:S(2)}) collective-permute-start(bf16[272,512]{1,0:T(8,128)(2,1)S(1)} %collective-permute-done.12.refs_4_), channel_id=1, source_target_pairs={{0,32},{1,225},{2,34},{3,227},{4,36},{5,229},{6,38},{7,231},{8,40}... | collective-permute-start | bytes 835592 | tf_op jit(solution)/shard_map/ppermute | solution.py:43
  47.5 9.4 %collective-permute-start.15 = (bf16[272,512]{1,0:T(8,128)(2,1)S(1)}, bf16[272,512]{1,0:T(8,128)(2,1)S(1)}, u32[]{:S(2)}, u32[]{:S(2)}) collective-permute-start(bf16[272,512]{1,0:T(8,128)(2,1)S(1)} %collective-permute-done.14.refs_5_), channel_id=1, source_target_pairs={{0,224},{1,33},{2,226},{3,35},{4,228},{5,37},{6,230},{7,39},{8,232... | collective-permute-start | bytes 835592 | tf_op jit(solution)/shard_map/ppermute | solution.py:43
  55.6 32.8 %collective-permute-start.23 = (bf16[4,256,512]{2,1,0:T(8,128)(2,1)S(1)}, bf16[4,256,512]{2,1,0:T(8,128)(2,1)S(1)}, u32[]{:S(2)}, u32[]{:S(2)}) collective-permute-start(bf16[4,256,512]{2,1,0:T(8,128)(2,1)S(1)} %shard_map.96), channel_id=1, source_target_pairs={{0,1},{1,0},{2,3},{3,2},{4,5},{5,4},{6,7},{7,6},{8,9},{9,8},{10,11... | collective-permute-start | bytes 3145736 | tf_op jit(solution)/shard_map/ppermute | solution.py:43
  57.4 8.7 %collective-permute-start.16 = (bf16[272,512]{1,0:T(8,128)(2,1)S(1)}, bf16[272,512]{1,0:T(8,128)(2,1)S(1)}, u32[]{:S(2)}, u32[]{:S(2)}) collective-permute-start(bf16[272,512]{1,0:T(8,128)(2,1)S(1)} %get-tuple-element.55.refs_5_), channel_id=1, source_target_pairs={{0,32},{1,225},{2,34},{3,227},{4,36},{5,229},{6,38},{7,231},{8,40}... | collective-permute-start | bytes 835592 | tf_op jit(solution)/shard_map/ppermute | solution.py:43
  57.5 10.1 %collective-permute-start.18 = (bf16[272,512]{1,0:T(8,128)(2,1)S(1)}, bf16[272,512]{1,0:T(8,128)(2,1)S(1)}, u32[]{:S(2)}, u32[]{:S(2)}) collective-permute-start(bf16[272,512]{1,0:T(8,128)(2,1)S(1)} %get-tuple-element.56.refs_6_), channel_id=1, source_target_pairs={{0,224},{1,33},{2,226},{3,35},{4,228},{5,37},{6,230},{7,39},{8,232... | collective-permute-start | bytes 835592 | tf_op jit(solution)/shard_map/ppermute | solution.py:43
  66.7 8.6 %collective-permute-start.17 = (bf16[272,512]{1,0:T(8,128)(2,1)S(1)}, bf16[272,512]{1,0:T(8,128)(2,1)S(1)}, u32[]{:S(2)}, u32[]{:S(2)}) collective-permute-start(bf16[272,512]{1,0:T(8,128)(2,1)S(1)} %shard_map.92.refs_4_), channel_id=1, source_target_pairs={{0,32},{1,225},{2,34},{3,227},{4,36},{5,229},{6,38},{7,231},{8,40}... | collective-permute-start | bytes 835592 | tf_op jit(solution)/shard_map/ppermute | solution.py:43
  76.2 7.7 %collective-permute-start.19 = (bf16[272,256]{1,0:T(8,128)(2,1)S(1)}, bf16[272,256]{1,0:T(8,128)(2,1)S(1)}, u32[]{:S(2)}, u32[]{:S(2)}) collective-permute-start(bf16[272,256]{1,0:T(8,128)(2,1)S(1)} %get-tuple-element.65), channel_id=1, source_target_pairs={{0,24},{1,25},{2,26},{3,27},{4,28},{5,29},{6,30},{7,31},{8,0},{9,1... | collective-permute-start | bytes 417800 | tf_op jit(solution)/shard_map/ppermute | solution.py:43
  80.6 6.6 %collective-permute-start.20 = (bf16[272,256]{1,0:T(8,128)(2,1)S(1)}, bf16[272,256]{1,0:T(8,128)(2,1)S(1)}, u32[]{:S(2)}, u32[]{:S(2)}) collective-permute-start(bf16[272,256]{1,0:T(8,128)(2,1)S(1)} %get-tuple-element.66), channel_id=1, source_target_pairs={{0,16},{1,17},{2,18},{3,19},{4,20},{5,21},{6,22},{7,23},{8,24},{9,... | collective-permute-start | bytes 417800 | tf_op jit(solution)/shard_map/ppermute | solution.py:43
  80.8 6.4 %collective-permute-start.21 = (bf16[272,256]{1,0:T(8,128)(2,1)S(1)}, bf16[272,256]{1,0:T(8,128)(2,1)S(1)}, u32[]{:S(2)}, u32[]{:S(2)}) collective-permute-start(bf16[272,256]{1,0:T(8,128)(2,1)S(1)} %get-tuple-element.67), channel_id=1, source_target_pairs={{0,8},{1,9},{2,10},{3,11},{4,12},{5,13},{6,14},{7,15},{8,16},{9,17... | collective-permute-start | bytes 417800 | tf_op jit(solution)/shard_map/ppermute | solution.py:43
  88.3 1.4 %collective-permute-start.22 = (bf16[272,256]{1,0:T(8,128)(2,1)S(1)}, bf16[272,256]{1,0:T(8,128)(2,1)S(1)}, u32[]{:S(2)}, u32[]{:S(2)}) collective-permute-start(bf16[272,256]{1,0:T(8,128)(2,1)S(1)} %shard_map.95.attended), channel_id=1, source_target_pairs={{0,1},{1,0},{2,3},{3,2},{4,5},{5,4},{6,7},{7,6},{8,9},{9,8},{10,11... | collective-permute-start | bytes 417800 | tf_op jit(solution)/shard_map/ppermute | solution.py:43
  91.0 10.1 %collective-permute-start.24 = (bf16[272,512]{1,0:T(8,128)(2,1)S(1)}, bf16[272,512]{1,0:T(8,128)(2,1)S(1)}, u32[]{:S(2)}, u32[]{:S(2)}) collective-permute-start(bf16[272,512]{1,0:T(8,128)(2,1)S(1)} %get-tuple-element.71), channel_id=1, source_target_pairs={{0,2},{1,7},{2,4},{3,1},{4,6},{5,3},{6,0},{7,5},{8,10},{9,15},{10,... | collective-permute-start | bytes 835592 | tf_op jit(solution)/shard_map/ppermute | solution.py:43
  91.1 10.6 %collective-permute-start.26 = (bf16[272,512]{1,0:T(8,128)(2,1)S(1)}, bf16[272,512]{1,0:T(8,128)(2,1)S(1)}, u32[]{:S(2)}, u32[]{:S(2)}) collective-permute-start(bf16[272,512]{1,0:T(8,128)(2,1)S(1)} %get-tuple-element.72), channel_id=1, source_target_pairs={{0,6},{1,3},{2,0},{3,5},{4,2},{5,7},{6,4},{7,1},{8,14},{9,11},{10,... | collective-permute-start | bytes 835592 | tf_op jit(solution)/shard_map/ppermute | solution.py:43
  101.2 7.8 %collective-permute-start.25 = (bf16[272,512]{1,0:T(8,128)(2,1)S(1)}, bf16[272,512]{1,0:T(8,128)(2,1)S(1)}, u32[]{:S(2)}, u32[]{:S(2)}) collective-permute-start(bf16[272,512]{1,0:T(8,128)(2,1)S(1)} %shard_map.98), channel_id=1, source_target_pairs={{0,2},{1,7},{2,4},{3,1},{4,6},{5,3},{6,0},{7,5},{8,10},{9,15},{10,... | collective-permute-start | bytes 835592 | tf_op jit(solution)/shard_map/ppermute | solution.py:43

commit v10 on v9

--- a/solution.py
+++ b/solution.py
@@ -473,12 +473,14 @@
     )(*products, hot, tokens)
 
 
-def cut_kernel(info, w_out, _, sibling, sems):
+def first_step_kernel(*refs):
+    info, w_out, sibling, sems = refs[0], refs[7], refs[11], refs[12]
     copies = []
     for i in range(4):
         start = pl.multiple_of(info[I_CUT + 4 + i] * FEAT, FEAT)
         copies.append(pltpu.make_async_copy(w_out.at[:, pl.ds(start, FEAT)], sibling.at[i], sems.at[i]))
         copies[-1].start()
+    attend_kernel(1, False, *refs[:7], *refs[8:11])
     for copy in copies:
         copy.wait()
 
@@ -571,14 +573,15 @@
     queries = [query] + [x_by(query, k) for k in (1, 2, 3)]
     one, other = z_one(kv), z_other(kv)
     one2, other2 = z_one(one), z_other(other)
-    *state, done = attend_step(1, info, queries, None, [one, other], None)
-    (theirs,) = call(
-        cut_kernel,
-        [shape((4, SEG, FEAT), BF16)],
-        [info, w_out, done],
+    *state, done, theirs = call(
+        first_step_kernel,
+        STATE + [shape((4, SEG, FEAT), BF16)],
+        [info] + queries + [one, other, w_out],
+        flops=4 * 1088 * SEG * 3 * COLS,
+        moved=4 << 20,
         scratch=[pltpu.SemaphoreType.DMA((4,))],
-        far_in=(1, 2),
-        far_out=(0,),
+        far_in=(7,),
+        far_out=(3,),
     )
     theirs = swap(theirs)
     one2, other2 = gate(info, [one2, other2], done)

time: 113 us -> 113 us (level)
    pallas_call x18 -> x17, Pallas kernels: 20 us -> 19.5 us  [call(): pl.pallas_call(body, out_shape=outs, in_specs=[SMEM if i == scalars else...]
where the time goes in v10:
time: 113 us; the launch traced here: 112 us
  waiting for transfers between devices  48.3 us (43%)
  starting transfers between devices  39.8 us (35%)
  Pallas kernels  22.5 us (20%)
  local copies, waits for them, and re-layouts  1.43 us (1%)
    ppermute x25, waiting for transfers between devices, move(): return lax.ppermute(value, ('seq', 'mp'), pairs)  46.3 us
    ppermute x25, starting transfers between devices, move(): return lax.ppermute(value, ('seq', 'mp'), pairs)  33.7 us
    pallas_call x17, Pallas kernels, call(): pl.pallas_call(body, out_shape=outs, in_specs=[SMEM if i == scalars else...  19.5 us
    ppermute x1, starting transfers between devices, shards(): above = lax.ppermute(head, 'seq', [(i, i - 1) for i in range(1, count)])  4.18 us
    pallas_call x1, Pallas kernels, output(): pl.pallas_call(output_kernel, grid=(TOK // BLOCK,), out_shape=shape((TOK,...  3.03 us
  transfers between devices with their start and end apart: 27, of which 14 were waited for; matrix products, arithmetic and copies ran while one was open for 1% of the time, Pallas kernels for 13%

profile of v10, /device:TPU:2, one launch (start us, length us, event | category | flops | bytes accessed | tf_op | source)
XLA Modules:
  0.0 112.3 jit_solution(2254959551760805532)
XLA Ops:
  0.7 2.0 %shard_map.82 = (bf16[2048,512]{1,0:T(8,128)(2,1)S(1)}, s32[16,128]{1,0:T(8,128)S(1)}, f32[8,640]{1,0:T(8,128)S(1)}, f32[8,640]{1,0:T(8,128)S(1)}) custom-call(s32[16,128]{1,0:T(8,128)S(1)} %bitcast.3, bf16[2048,512]{1,0:T(8,128)(2,1)} %tokens_in.1), custom_call_target="tpu_custom_call" | custom-call | flops 268435456 | bytes 2097152 | tf_op jit(solution)/shard_map/pallas_call | solution.py:107
  2.8 4.2 %collective-permute-start = (f32[8,640]{1,0:T(8,128)S(1)}, f32[8,640]{1,0:T(8,128)S(1)}, u32[]{:S(2)}, u32[]{:S(2)}) collective-permute-start(f32[8,640]{1,0:T(8,128)S(1)} %get-tuple-element.44.head), channel_id=1, source_target_pairs={{8,0},{16,8},{24,16},{32,24},{40,32},{48,40},{56,48},{64,56},{72,6... | collective-permute-start | bytes 61448 | tf_op jit(solution)/shard_map/ppermute | solution.py:522
  6.9 1.9 %collective-permute-start.1 = (f32[8,640]{1,0:T(8,128)S(1)}, f32[8,640]{1,0:T(8,128)S(1)}, u32[]{:S(2)}, u32[]{:S(2)}) collective-permute-start(f32[8,640]{1,0:T(8,128)S(1)} %get-tuple-element.45), channel_id=1, source_target_pairs={{0,8},{8,16},{16,24},{24,32},{32,40},{40,48},{48,56},{56,64},{64,7... | collective-permute-start | bytes 61448 | tf_op jit(solution)/shard_map/ppermute | solution.py:523
  10.6 2.0 %collective-permute-done.1.below = f32[8,640]{1,0:T(8,128)S(1)} collective-permute-done((f32[8,640]{1,0:T(8,128)S(1)}, f32[8,640]{1,0:T(8,128)S(1)}, u32[]{:S(2)}, u32[]{:S(2)}) %collective-permute-start.1) | collective-permute-done | bytes 20512 | tf_op jit(solution)/shard_map/ppermute | solution.py:523
  13.5 3.2 %collective-permute-start.3 = (bf16[272,512]{1,0:T(8,128)(2,1)S(1)}, bf16[272,512]{1,0:T(8,128)(2,1)S(1)}, u32[]{:S(2)}, u32[]{:S(2)}) collective-permute-start(bf16[272,512]{1,0:T(8,128)(2,1)S(1)} %get-tuple-element.46.refs_0_), channel_id=1, source_target_pairs={{0,6},{1,3},{2,0},{3,5},{4,2},{5,7},{6,4},{7,1},{8,14},{9,11},{10,... | collective-permute-start | bytes 835592 | tf_op jit(solution)/shard_map/ppermute | solution.py:43
  16.7 6.3 %collective-permute-done.2.refs_1_ = bf16[272,512]{1,0:T(8,128)(2,1)S(1)} collective-permute-done((bf16[272,512]{1,0:T(8,128)(2,1)S(1)}, bf16[272,512]{1,0:T(8,128)(2,1)S(1)}, u32[]{:S(2)}, u32[]{:S(2)}) %collective-permute-start.2) | collective-permute-done | bytes 278560 | tf_op jit(solution)/shard_map/ppermute | solution.py:43
  23.0 2.9 %shard_map.85 = (bf16[4096,256]{1,0:T(8,128)(2,1)S(1)}, bf16[4096,256]{1,0:T(8,128)(2,1)S(1)}, bf16[4096,256]{1,0:T(8,128)(2,1)S(1)}, bf16[272,512]{1,0:T(8,128)(2,1)S(1)}) custom-call(bf16[4096,256]{1,0:T(8,128)(2,1)} %refs_0_.1, bf16[4096,256]{1,0:T(8,128)(2,1)} %refs_1_.1, bf16[4096,256]{1,0:T(8,128)(2,1)} %refs_2_.1, ...), custom_call_target="tpu_custom_call", output_to_operand_aliasing={{3}: (3, {})} | custom-call | bytes 12582912 | tf_op jit(solution)/shard_map/pallas_call | solution.py:107
  26.6 4.1 %collective-permute-done.4.refs_3_ = bf16[272,512]{1,0:T(8,128)(2,1)S(1)} collective-permute-done((bf16[272,512]{1,0:T(8,128)(2,1)S(1)}, bf16[272,512]{1,0:T(8,128)(2,1)S(1)}, u32[]{:S(2)}, u32[]{:S(2)}) %collective-permute-start.4) | collective-permute-done | bytes 278560 | tf_op jit(solution)/shard_map/ppermute | solution.py:43
  30.8 1.6 %shard_map.86 = (f32[272,256]{1,0:T(8,128)S(1)}, f32[256,256]{1,0:T(8,128)S(1)}, f32[256,256]{1,0:T(8,128)S(1)}) custom-call(s32[32]{0:T(128)S(1)} %dynamic-slice_bitcast_fusion.info.refs_0_, bf16[272,512]{1,0:T(8,128)(2,1)S(1)} %get-tuple-element.46.refs_0_, bf16[272,512]{1,0:T(8,128)(2,1)S(1)} %collective-permute-done.2.refs_1_, ...), custom_call_target="tpu_custom_call" | custom-call | flops 855638016 | bytes 3145728 | tf_op jit(solution)/shard_map/pallas_call | solution.py:107
  32.4 1.3 %shard_map.87.refs_10_.refs_4_ = bf16[272,512]{1,0:T(8,128)(2,1)S(1)} custom-call(s32[32]{0:T(128)S(1)} %dynamic-slice_bitcast_fusion.info.refs_0_, bf16[272,512]{1,0:T(8,128)(2,1)S(1)} %get-tuple-element.46.refs_0_, bf16[272,512]{1,0:T(8,128)(2,1)S(1)} %collective-permute-done.2.refs_1_, bf16[272,512]{1,0:T(8,128)(2,1)S(1)} %collective-permute-done.3.refs_2_, ...), custom_call_target="tpu_custom_call" | custom-call | tf_op jit(solution)/shard_map/pallas_call | solution.py:107
  33.6 1.4 %collective-permute-start.12 = (bf16[272,512]{1,0:T(8,128)(2,1)S(1)}, bf16[272,512]{1,0:T(8,128)(2,1)S(1)}, u32[]{:S(2)}, u32[]{:S(2)}) collective-permute-start(bf16[272,512]{1,0:T(8,128)(2,1)S(1)} %shard_map.87.refs_10_.refs_4_), channel_id=1, source_target_pairs={{0,32},{1,225},{2,34},{3,227},{4,36},{5,229},{6,38},{7,231},{8,40}... | collective-permute-start | bytes 835592 | tf_op jit(solution)/shard_map/ppermute | solution.py:43
  35.0 4.9 %collective-permute-start.14 = (bf16[272,512]{1,0:T(8,128)(2,1)S(1)}, bf16[272,512]{1,0:T(8,128)(2,1)S(1)}, u32[]{:S(2)}, u32[]{:S(2)}) collective-permute-start(bf16[272,512]{1,0:T(8,128)(2,1)S(1)} %shard_map.87.refs_10_.refs_4_), channel_id=1, source_target_pairs={{0,224},{1,33},{2,226},{3,35},{4,228},{5,37},{6,230},{7,39},{8,232... | collective-permute-start | bytes 835592 | tf_op jit(solution)/shard_map/ppermute | solution.py:43
  41.2 6.2 %collective-permute-start.10 = (bf16[272,256]{1,0:T(8,128)(2,1)S(1)}, bf16[272,256]{1,0:T(8,128)(2,1)S(1)}, u32[]{:S(2)}, u32[]{:S(2)}) collective-permute-start(bf16[272,256]{1,0:T(8,128)(2,1)S(1)} %shard_map.88.refs_1_.refs_0_), channel_id=1, source_target_pairs={{0,16},{1,17},{2,18},{3,19},{4,20},{5,21},{6,22},{7,23},{8,24},{9,... | collective-permute-start | bytes 417800 | tf_op jit(solution)/shard_map/ppermute | solution.py:43
  47.4 3.2 %collective-permute-start.15 = (bf16[272,512]{1,0:T(8,128)(2,1)S(1)}, bf16[272,512]{1,0:T(8,128)(2,1)S(1)}, u32[]{:S(2)}, u32[]{:S(2)}) collective-permute-start(bf16[272,512]{1,0:T(8,128)(2,1)S(1)} %collective-permute-done.14.refs_6_), channel_id=1, source_target_pairs={{0,224},{1,33},{2,226},{3,35},{4,228},{5,37},{6,230},{7,39},{8,232... | collective-permute-start | bytes 835592 | tf_op jit(solution)/shard_map/ppermute | solution.py:43
  50.7 1.2 %collective-permute-done.10.refs_3_.refs_2_ = bf16[272,256]{1,0:T(8,128)(2,1)S(1)} collective-permute-done((bf16[272,256]{1,0:T(8,128)(2,1)S(1)}, bf16[272,256]{1,0:T(8,128)(2,1)S(1)}, u32[]{:S(2)}, u32[]{:S(2)}) %collective-permute-start.10) | collective-permute-done | bytes 139296 | tf_op jit(solution)/shard_map/ppermute | solution.py:43
  51.9 2.2 %collective-permute-done.11.refs_4_.refs_3_ = bf16[272,256]{1,0:T(8,128)(2,1)S(1)} collective-permute-done((bf16[272,256]{1,0:T(8,128)(2,1)S(1)}, bf16[272,256]{1,0:T(8,128)(2,1)S(1)}, u32[]{:S(2)}, u32[]{:S(2)}) %collective-permute-start.11) | collective-permute-done | bytes 139296 | tf_op jit(solution)/shard_map/ppermute | solution.py:43
  55.1 1.7 %collective-permute-done.13.refs_0_ = bf16[272,512]{1,0:T(8,128)(2,1)S(1)} collective-permute-done((bf16[272,512]{1,0:T(8,128)(2,1)S(1)}, bf16[272,512]{1,0:T(8,128)(2,1)S(1)}, u32[]{:S(2)}, u32[]{:S(2)}) %collective-permute-start.13) | collective-permute-done | bytes 278560 | tf_op jit(solution)/shard_map/ppermute | solution.py:43
  57.5 3.2 %collective-permute-start.18 = (bf16[272,512]{1,0:T(8,128)(2,1)S(1)}, bf16[272,512]{1,0:T(8,128)(2,1)S(1)}, u32[]{:S(2)}, u32[]{:S(2)}) collective-permute-start(bf16[272,512]{1,0:T(8,128)(2,1)S(1)} %get-tuple-element.57.refs_6_), channel_id=1, source_target_pairs={{0,224},{1,33},{2,226},{3,35},{4,228},{5,37},{6,230},{7,39},{8,232... | collective-permute-start | bytes 835592 | tf_op jit(solution)/shard_map/ppermute | solution.py:43
  60.7 2.1 %shard_map.91 = (f32[4,2,272,256]{3,2,1,0:T(8,128)S(1)}, f32[4,2,272,128]{3,2,1,0:T(8,128)S(1)}, f32[8,128]{1,0:T(8,128)S(1)}) custom-call(s32[32]{0:T(128)S(1)} %dynamic-slice_bitcast_fusion.info.refs_0_, bf16[272,256]{1,0:T(8,128)(2,1)S(1)} %shard_map.88.refs_1_.refs_0_, ...), custom_call_target="tpu_custom_call", output_to_operand_aliasing={{0}: (8, {}), {1}: (9, {})} | custom-call | flops 855638016 | bytes 4194304 | tf_op jit(solution)/shard_map/pallas_call | solution.py:107
  62.8 3.1 %collective-permute-done.16.refs_0_ = bf16[272,512]{1,0:T(8,128)(2,1)S(1)} collective-permute-done((bf16[272,512]{1,0:T(8,128)(2,1)S(1)}, bf16[272,512]{1,0:T(8,128)(2,1)S(1)}, u32[]{:S(2)}, u32[]{:S(2)}) %collective-permute-start.16) | collective-permute-done | bytes 278560 | tf_op jit(solution)/shard_map/ppermute | solution.py:43
  67.1 1.1 %shard_map.93 = (f32[4,2,272,256]{3,2,1,0:T(8,128)S(1)}, f32[4,2,272,128]{3,2,1,0:T(8,128)S(1)}, f32[8,128]{1,0:T(8,128)}) custom-call(s32[32]{0:T(128)S(1)} %dynamic-slice_bitcast_fusion.info.refs_0_, bf16[272,256]{1,0:T(8,128)(2,1)S(1)} %shard_map.88.refs_1_.refs_0_, ...), custom_call_target="tpu_custom_call", output_to_operand_aliasing={{0}: (7, {}), {1}: (8, {})} | custom-call | flops 855638016 | bytes 4194304 | tf_op jit(solution)/shard_map/pallas_call | solution.py:107
  68.2 6.6 %collective-permute-done.17.refs_5_ = bf16[272,512]{1,0:T(8,128)(2,1)S(1)} collective-permute-done((bf16[272,512]{1,0:T(8,128)(2,1)S(1)}, bf16[272,512]{1,0:T(8,128)(2,1)S(1)}, u32[]{:S(2)}, u32[]{:S(2)}) %collective-permute-start.17) | collective-permute-done | bytes 278560 | tf_op jit(solution)/shard_map/ppermute | solution.py:43
  75.7 5.2 %collective-permute-start.19 = (bf16[272,256]{1,0:T(8,128)(2,1)S(1)}, bf16[272,256]{1,0:T(8,128)(2,1)S(1)}, u32[]{:S(2)}, u32[]{:S(2)}) collective-permute-start(bf16[272,256]{1,0:T(8,128)(2,1)S(1)} %get-tuple-element.66), channel_id=1, source_target_pairs={{0,24},{1,25},{2,26},{3,27},{4,28},{5,29},{6,30},{7,31},{8,0},{9,1... | collective-permute-start | bytes 417800 | tf_op jit(solution)/shard_map/ppermute | solution.py:43
  81.3 1.2 %collective-permute-start.21 = (bf16[272,256]{1,0:T(8,128)(2,1)S(1)}, bf16[272,256]{1,0:T(8,128)(2,1)S(1)}, u32[]{:S(2)}, u32[]{:S(2)}) collective-permute-start(bf16[272,256]{1,0:T(8,128)(2,1)S(1)} %get-tuple-element.68), channel_id=1, source_target_pairs={{0,8},{1,9},{2,10},{3,11},{4,12},{5,13},{6,14},{7,15},{8,16},{9,17... | collective-permute-start | bytes 417800 | tf_op jit(solution)/shard_map/ppermute | solution.py:43
  82.5 1.4 %collective-permute-done.19.b = bf16[272,256]{1,0:T(8,128)(2,1)S(1)} collective-permute-done((bf16[272,256]{1,0:T(8,128)(2,1)S(1)}, bf16[272,256]{1,0:T(8,128)(2,1)S(1)}, u32[]{:S(2)}, u32[]{:S(2)}) %collective-permute-start.19) | collective-permute-done | bytes 139296 | tf_op jit(solution)/shard_map/ppermute | solution.py:43
  83.9 3.6 %collective-permute-done.20.c = bf16[272,256]{1,0:T(8,128)(2,1)S(1)} collective-permute-done((bf16[272,256]{1,0:T(8,128)(2,1)S(1)}, bf16[272,256]{1,0:T(8,128)(2,1)S(1)}, u32[]{:S(2)}, u32[]{:S(2)}) %collective-permute-start.20) | collective-permute-done | bytes 139296 | tf_op jit(solution)/shard_map/ppermute | solution.py:43
  88.7 1.3 %collective-permute-done.22.other = bf16[272,256]{1,0:T(8,128)(2,1)S(1)} collective-permute-done((bf16[272,256]{1,0:T(8,128)(2,1)S(1)}, bf16[272,256]{1,0:T(8,128)(2,1)S(1)}, u32[]{:S(2)}, u32[]{:S(2)}) %collective-permute-start.22) | collective-permute-done | bytes 139296 | tf_op jit(solution)/shard_map/ppermute | solution.py:43
  90.0 1.3 %shard_map.96 = (f32[272,512]{1,0:T(8,128)S(1)}, f32[272,512]{1,0:T(8,128)S(1)}, bf16[272,512]{1,0:T(8,128)(2,1)S(1)}, bf16[272,512]{1,0:T(8,128)(2,1)S(1)}) custom-call(s32[32]{0:T(128)S(1)} %dynamic-slice_bitcast_fusion.info.refs_0_, bf16[272,256]{1,0:T(8,128)(2,1)S(1)} %shard_map.95.attended, bf16[272,256]{1,0:T(8,128)(2,1)S(1)} %collective-permute-done.22.other, ...), custom_call_target="tpu_custom_call" | custom-call | flops 570425344 | bytes 4194304 | tf_op jit(solution)/shard_map/pallas_call | solution.py:107
  91.4 3.2 %collective-permute-start.26 = (bf16[272,512]{1,0:T(8,128)(2,1)S(1)}, bf16[272,512]{1,0:T(8,128)(2,1)S(1)}, u32[]{:S(2)}, u32[]{:S(2)}) collective-permute-start(bf16[272,512]{1,0:T(8,128)(2,1)S(1)} %get-tuple-element.74), channel_id=1, source_target_pairs={{0,6},{1,3},{2,0},{3,5},{4,2},{5,7},{6,4},{7,1},{8,14},{9,11},{10,... | collective-permute-start | bytes 835592 | tf_op jit(solution)/shard_map/ppermute | solution.py:43
  94.6 6.8 %collective-permute-done.24.b = bf16[272,512]{1,0:T(8,128)(2,1)S(1)} collective-permute-done((bf16[272,512]{1,0:T(8,128)(2,1)S(1)}, bf16[272,512]{1,0:T(8,128)(2,1)S(1)}, u32[]{:S(2)}, u32[]{:S(2)}) %collective-permute-start.24) | collective-permute-done | bytes 278560 | tf_op jit(solution)/shard_map/ppermute | solution.py:43
  102.0 7.3 %collective-permute-done.25.first = bf16[272,512]{1,0:T(8,128)(2,1)S(1)} collective-permute-done((bf16[272,512]{1,0:T(8,128)(2,1)S(1)}, bf16[272,512]{1,0:T(8,128)(2,1)S(1)}, u32[]{:S(2)}, u32[]{:S(2)}) %collective-permute-start.25) | collective-permute-done | bytes 278560 | tf_op jit(solution)/shard_map/ppermute | solution.py:43
  109.3 3.0 %shard_map.99 = bf16[2048,512]{1,0:T(8,128)(2,1)} custom-call(f32[272,512]{1,0:T(8,128)S(1)} %get-tuple-element.71.own, bf16[272,512]{1,0:T(8,128)(2,1)S(1)} %collective-permute-done.25.first, bf16[272,512]{1,0:T(8,128)(2,1)S(1)} %collective-permute-done.26.second, bf16[2048,384]{1,0:T(8,128)(2,1)S(1)} %shard_map.98.hot, ...), custom_call_target="tpu_custom_call" | custom-call | flops 2147483648 | bytes 6291456 | tf_op jit(solution)/shard_map/pallas_call | solution.py:463
  (49 shorter events, 11.3 us)
Async XLA Ops:
  0.0 0.7 copy-start.1
  2.7 7.8 %copy-start.2 = (f32[4096]{0:T(1024)S(1)}, f32[4096]{0:T(1024)}, u32[]{:S(2)}) copy-start(f32[4096]{0:T(1024)} %param.10) | copy-start | bytes 49156
  2.8 7.9 %collective-permute-start = (f32[8,640]{1,0:T(8,128)S(1)}, f32[8,640]{1,0:T(8,128)S(1)}, u32[]{:S(2)}, u32[]{:S(2)}) collective-permute-start(f32[8,640]{1,0:T(8,128)S(1)} %get-tuple-element.44.head), channel_id=1, source_target_pairs={{8,0},{16,8},{24,16},{32,24},{40,32},{48,40},{56,48},{64,56},{72,6... | collective-permute-start | bytes 61448 | tf_op jit(solution)/shard_map/ppermute | solution.py:522
  6.9 5.7 %collective-permute-start.1 = (f32[8,640]{1,0:T(8,128)S(1)}, f32[8,640]{1,0:T(8,128)S(1)}, u32[]{:S(2)}, u32[]{:S(2)}) collective-permute-start(f32[8,640]{1,0:T(8,128)S(1)} %get-tuple-element.45), channel_id=1, source_target_pairs={{0,8},{8,16},{16,24},{24,32},{32,40},{40,48},{48,56},{56,64},{64,7... | collective-permute-start | bytes 61448 | tf_op jit(solution)/shard_map/ppermute | solution.py:523
  13.4 9.6 %collective-permute-start.2 = (bf16[272,512]{1,0:T(8,128)(2,1)S(1)}, bf16[272,512]{1,0:T(8,128)(2,1)S(1)}, u32[]{:S(2)}, u32[]{:S(2)}) collective-permute-start(bf16[272,512]{1,0:T(8,128)(2,1)S(1)} %get-tuple-element.46.refs_0_), channel_id=1, source_target_pairs={{0,2},{1,7},{2,4},{3,1},{4,6},{5,3},{6,0},{7,5},{8,10},{9,15},{10,... | collective-permute-start | bytes 835592 | tf_op jit(solution)/shard_map/ppermute | solution.py:43
  13.5 13.0 %collective-permute-start.3 = (bf16[272,512]{1,0:T(8,128)(2,1)S(1)}, bf16[272,512]{1,0:T(8,128)(2,1)S(1)}, u32[]{:S(2)}, u32[]{:S(2)}) collective-permute-start(bf16[272,512]{1,0:T(8,128)(2,1)S(1)} %get-tuple-element.46.refs_0_), channel_id=1, source_target_pairs={{0,6},{1,3},{2,0},{3,5},{4,2},{5,7},{6,4},{7,1},{8,14},{9,11},{10,... | collective-permute-start | bytes 835592 | tf_op jit(solution)/shard_map/ppermute | solution.py:43
  23.0 7.8 %collective-permute-start.4 = (bf16[272,512]{1,0:T(8,128)(2,1)S(1)}, bf16[272,512]{1,0:T(8,128)(2,1)S(1)}, u32[]{:S(2)}, u32[]{:S(2)}) collective-permute-start(bf16[272,512]{1,0:T(8,128)(2,1)S(1)} %collective-permute-done.2.refs_1_), channel_id=1, source_target_pairs={{0,2},{1,7},{2,4},{3,1},{4,6},{5,3},{6,0},{7,5},{8,10},{9,15},{10,... | collective-permute-start | bytes 835592 | tf_op jit(solution)/shard_map/ppermute | solution.py:43
  25.9 4.8 %collective-permute-start.5 = (bf16[272,512]{1,0:T(8,128)(2,1)S(1)}, bf16[272,512]{1,0:T(8,128)(2,1)S(1)}, u32[]{:S(2)}, u32[]{:S(2)}) collective-permute-start(bf16[272,512]{1,0:T(8,128)(2,1)S(1)} %get-tuple-element.47), channel_id=1, source_target_pairs={{0,1},{1,0},{2,3},{3,2},{4,5},{5,4},{6,7},{7,6},{8,9},{9,8},{10,11... | collective-permute-start | bytes 835592 | tf_op jit(solution)/shard_map/ppermute | solution.py:43
  26.0 6.3 %collective-permute-start.6 = (bf16[272,512]{1,0:T(8,128)(2,1)S(1)}, bf16[272,512]{1,0:T(8,128)(2,1)S(1)}, u32[]{:S(2)}, u32[]{:S(2)}) collective-permute-start(bf16[272,512]{1,0:T(8,128)(2,1)S(1)} %collective-permute-done.2.refs_1_), channel_id=1, source_target_pairs={{0,1},{1,0},{2,3},{3,2},{4,5},{5,4},{6,7},{7,6},{8,9},{9,8},{10,11... | collective-permute-start | bytes 835592 | tf_op jit(solution)/shard_map/ppermute | solution.py:43
  26.5 5.8 %collective-permute-start.7 = (bf16[272,512]{1,0:T(8,128)(2,1)S(1)}, bf16[272,512]{1,0:T(8,128)(2,1)S(1)}, u32[]{:S(2)}, u32[]{:S(2)}) collective-permute-start(bf16[272,512]{1,0:T(8,128)(2,1)S(1)} %collective-permute-done.3.refs_2_), channel_id=1, source_target_pairs={{0,1},{1,0},{2,3},{3,2},{4,5},{5,4},{6,7},{7,6},{8,9},{9,8},{10,11... | collective-permute-start | bytes 835592 | tf_op jit(solution)/shard_map/ppermute | solution.py:43
  30.8 1.6 %collective-permute-start.8 = (bf16[272,512]{1,0:T(8,128)(2,1)S(1)}, bf16[272,512]{1,0:T(8,128)(2,1)S(1)}, u32[]{:S(2)}, u32[]{:S(2)}) collective-permute-start(bf16[272,512]{1,0:T(8,128)(2,1)S(1)} %collective-permute-done.4.refs_3_), channel_id=1, source_target_pairs={{0,1},{1,0},{2,3},{3,2},{4,5},{5,4},{6,7},{7,6},{8,9},{9,8},{10,11... | collective-permute-start | bytes 835592 | tf_op jit(solution)/shard_map/ppermute | solution.py:43
  33.6 13.8 %collective-permute-start.12 = (bf16[272,512]{1,0:T(8,128)(2,1)S(1)}, bf16[272,512]{1,0:T(8,128)(2,1)S(1)}, u32[]{:S(2)}, u32[]{:S(2)}) collective-permute-start(bf16[272,512]{1,0:T(8,128)(2,1)S(1)} %shard_map.87.refs_10_.refs_4_), channel_id=1, source_target_pairs={{0,32},{1,225},{2,34},{3,227},{4,36},{5,229},{6,38},{7,231},{8,40}... | collective-permute-start | bytes 835592 | tf_op jit(solution)/shard_map/ppermute | solution.py:43
  35.0 12.4 %collective-permute-start.14 = (bf16[272,512]{1,0:T(8,128)(2,1)S(1)}, bf16[272,512]{1,0:T(8,128)(2,1)S(1)}, u32[]{:S(2)}, u32[]{:S(2)}) collective-permute-start(bf16[272,512]{1,0:T(8,128)(2,1)S(1)} %shard_map.87.refs_10_.refs_4_), channel_id=1, source_target_pairs={{0,224},{1,33},{2,226},{3,35},{4,228},{5,37},{6,230},{7,39},{8,232... | collective-permute-start | bytes 835592 | tf_op jit(solution)/shard_map/ppermute | solution.py:43
  39.9 14.2 %copy-start = (bf16[256,4096]{1,0:T(8,128)(2,1)S(1)}, bf16[256,4096]{1,0:T(8,128)(2,1)}, u32[]{:S(2)}) copy-start(bf16[256,4096]{1,0:T(8,128)(2,1)} %w_out.1) | copy-start | bytes 6291460
  41.0 9.7 %collective-permute-start.9 = (bf16[272,256]{1,0:T(8,128)(2,1)S(1)}, bf16[272,256]{1,0:T(8,128)(2,1)S(1)}, u32[]{:S(2)}, u32[]{:S(2)}) collective-permute-start(bf16[272,256]{1,0:T(8,128)(2,1)S(1)} %shard_map.88.refs_1_.refs_0_), channel_id=1, source_target_pairs={{0,8},{1,9},{2,10},{3,11},{4,12},{5,13},{6,14},{7,15},{8,16},{9,17... | collective-permute-start | bytes 417800 | tf_op jit(solution)/shard_map/ppermute | solution.py:43
  41.2 10.7 %collective-permute-start.10 = (bf16[272,256]{1,0:T(8,128)(2,1)S(1)}, bf16[272,256]{1,0:T(8,128)(2,1)S(1)}, u32[]{:S(2)}, u32[]{:S(2)}) collective-permute-start(bf16[272,256]{1,0:T(8,128)(2,1)S(1)} %shard_map.88.refs_1_.refs_0_), channel_id=1, source_target_pairs={{0,16},{1,17},{2,18},{3,19},{4,20},{5,21},{6,22},{7,23},{8,24},{9,... | collective-permute-start | bytes 417800 | tf_op jit(solution)/shard_map/ppermute | solution.py:43
  47.4 6.7 %collective-permute-start.11 = (bf16[272,256]{1,0:T(8,128)(2,1)S(1)}, bf16[272,256]{1,0:T(8,128)(2,1)S(1)}, u32[]{:S(2)}, u32[]{:S(2)}) collective-permute-start(bf16[272,256]{1,0:T(8,128)(2,1)S(1)} %shard_map.88.refs_1_.refs_0_), channel_id=1, source_target_pairs={{0,24},{1,25},{2,26},{3,27},{4,28},{5,29},{6,30},{7,31},{8,0},{9,1... | collective-permute-start | bytes 417800 | tf_op jit(solution)/shard_map/ppermute | solution.py:43
  47.4 9.4 %collective-permute-start.13 = (bf16[272,512]{1,0:T(8,128)(2,1)S(1)}, bf16[272,512]{1,0:T(8,128)(2,1)S(1)}, u32[]{:S(2)}, u32[]{:S(2)}) collective-permute-start(bf16[272,512]{1,0:T(8,128)(2,1)S(1)} %collective-permute-done.12.refs_5_), channel_id=1, source_target_pairs={{0,32},{1,225},{2,34},{3,227},{4,36},{5,229},{6,38},{7,231},{8,40}... | collective-permute-start | bytes 835592 | tf_op jit(solution)/shard_map/ppermute | solution.py:43
  47.4 9.4 %collective-permute-start.15 = (bf16[272,512]{1,0:T(8,128)(2,1)S(1)}, bf16[272,512]{1,0:T(8,128)(2,1)S(1)}, u32[]{:S(2)}, u32[]{:S(2)}) collective-permute-start(bf16[272,512]{1,0:T(8,128)(2,1)S(1)} %collective-permute-done.14.refs_6_), channel_id=1, source_target_pairs={{0,224},{1,33},{2,226},{3,35},{4,228},{5,37},{6,230},{7,39},{8,232... | collective-permute-start | bytes 835592 | tf_op jit(solution)/shard_map/ppermute | solution.py:43
  55.0 33.7 %collective-permute-start.23 = (bf16[4,256,512]{2,1,0:T(8,128)(2,1)S(1)}, bf16[4,256,512]{2,1,0:T(8,128)(2,1)S(1)}, u32[]{:S(2)}, u32[]{:S(2)}) collective-permute-start(bf16[4,256,512]{2,1,0:T(8,128)(2,1)S(1)} %get-tuple-element.69), channel_id=1, source_target_pairs={{0,1},{1,0},{2,3},{3,2},{4,5},{5,4},{6,7},{7,6},{8,9},{9,8},{10,11... | collective-permute-start | bytes 3145736 | tf_op jit(solution)/shard_map/ppermute | solution.py:43
  57.4 8.5 %collective-permute-start.16 = (bf16[272,512]{1,0:T(8,128)(2,1)S(1)}, bf16[272,512]{1,0:T(8,128)(2,1)S(1)}, u32[]{:S(2)}, u32[]{:S(2)}) collective-permute-start(bf16[272,512]{1,0:T(8,128)(2,1)S(1)} %get-tuple-element.56.refs_5_), channel_id=1, source_target_pairs={{0,32},{1,225},{2,34},{3,227},{4,36},{5,229},{6,38},{7,231},{8,40}... | collective-permute-start | bytes 835592 | tf_op jit(solution)/shard_map/ppermute | solution.py:43
  57.5 9.6 %collective-permute-start.18 = (bf16[272,512]{1,0:T(8,128)(2,1)S(1)}, bf16[272,512]{1,0:T(8,128)(2,1)S(1)}, u32[]{:S(2)}, u32[]{:S(2)}) collective-permute-start(bf16[272,512]{1,0:T(8,128)(2,1)S(1)} %get-tuple-element.57.refs_6_), channel_id=1, source_target_pairs={{0,224},{1,33},{2,226},{3,35},{4,228},{5,37},{6,230},{7,39},{8,232... | collective-permute-start | bytes 835592 | tf_op jit(solution)/shard_map/ppermute | solution.py:43
  66.4 8.4 %collective-permute-start.17 = (bf16[272,512]{1,0:T(8,128)(2,1)S(1)}, bf16[272,512]{1,0:T(8,128)(2,1)S(1)}, u32[]{:S(2)}, u32[]{:S(2)}) collective-permute-start(bf16[272,512]{1,0:T(8,128)(2,1)S(1)} %shard_map.92.refs_4_), channel_id=1, source_target_pairs={{0,32},{1,225},{2,34},{3,227},{4,36},{5,229},{6,38},{7,231},{8,40}... | collective-permute-start | bytes 835592 | tf_op jit(solution)/shard_map/ppermute | solution.py:43
  75.7 8.2 %collective-permute-start.19 = (bf16[272,256]{1,0:T(8,128)(2,1)S(1)}, bf16[272,256]{1,0:T(8,128)(2,1)S(1)}, u32[]{:S(2)}, u32[]{:S(2)}) collective-permute-start(bf16[272,256]{1,0:T(8,128)(2,1)S(1)} %get-tuple-element.66), channel_id=1, source_target_pairs={{0,24},{1,25},{2,26},{3,27},{4,28},{5,29},{6,30},{7,31},{8,0},{9,1... | collective-permute-start | bytes 417800 | tf_op jit(solution)/shard_map/ppermute | solution.py:43
  80.9 6.6 %collective-permute-start.20 = (bf16[272,256]{1,0:T(8,128)(2,1)S(1)}, bf16[272,256]{1,0:T(8,128)(2,1)S(1)}, u32[]{:S(2)}, u32[]{:S(2)}) collective-permute-start(bf16[272,256]{1,0:T(8,128)(2,1)S(1)} %get-tuple-element.67), channel_id=1, source_target_pairs={{0,16},{1,17},{2,18},{3,19},{4,20},{5,21},{6,22},{7,23},{8,24},{9,... | collective-permute-start | bytes 417800 | tf_op jit(solution)/shard_map/ppermute | solution.py:43
  81.3 6.2 %collective-permute-start.21 = (bf16[272,256]{1,0:T(8,128)(2,1)S(1)}, bf16[272,256]{1,0:T(8,128)(2,1)S(1)}, u32[]{:S(2)}, u32[]{:S(2)}) collective-permute-start(bf16[272,256]{1,0:T(8,128)(2,1)S(1)} %get-tuple-element.68), channel_id=1, source_target_pairs={{0,8},{1,9},{2,10},{3,11},{4,12},{5,13},{6,14},{7,15},{8,16},{9,17... | collective-permute-start | bytes 417800 | tf_op jit(solution)/shard_map/ppermute | solution.py:43
  88.6 1.4 %collective-permute-start.22 = (bf16[272,256]{1,0:T(8,128)(2,1)S(1)}, bf16[272,256]{1,0:T(8,128)(2,1)S(1)}, u32[]{:S(2)}, u32[]{:S(2)}) collective-permute-start(bf16[272,256]{1,0:T(8,128)(2,1)S(1)} %shard_map.95.attended), channel_id=1, source_target_pairs={{0,1},{1,0},{2,3},{3,2},{4,5},{5,4},{6,7},{7,6},{8,9},{9,8},{10,11... | collective-permute-start | bytes 417800 | tf_op jit(solution)/shard_map/ppermute | solution.py:43
  91.3 10.1 %collective-permute-start.24 = (bf16[272,512]{1,0:T(8,128)(2,1)S(1)}, bf16[272,512]{1,0:T(8,128)(2,1)S(1)}, u32[]{:S(2)}, u32[]{:S(2)}) collective-permute-start(bf16[272,512]{1,0:T(8,128)(2,1)S(1)} %get-tuple-element.73), channel_id=1, source_target_pairs={{0,2},{1,7},{2,4},{3,1},{4,6},{5,3},{6,0},{7,5},{8,10},{9,15},{10,... | collective-permute-start | bytes 835592 | tf_op jit(solution)/shard_map/ppermute | solution.py:43
  91.4 10.6 %collective-permute-start.26 = (bf16[272,512]{1,0:T(8,128)(2,1)S(1)}, bf16[272,512]{1,0:T(8,128)(2,1)S(1)}, u32[]{:S(2)}, u32[]{:S(2)}) collective-permute-start(bf16[272,512]{1,0:T(8,128)(2,1)S(1)} %get-tuple-element.74), channel_id=1, source_target_pairs={{0,6},{1,3},{2,0},{3,5},{4,2},{5,7},{6,4},{7,1},{8,14},{9,11},{10,... | collective-permute-start | bytes 835592 | tf_op jit(solution)/shard_map/ppermute | solution.py:43
  101.5 7.8 %collective-permute-start.25 = (bf16[272,512]{1,0:T(8,128)(2,1)S(1)}, bf16[272,512]{1,0:T(8,128)(2,1)S(1)}, u32[]{:S(2)}, u32[]{:S(2)}) collective-permute-start(bf16[272,512]{1,0:T(8,128)(2,1)S(1)} %shard_map.97), channel_id=1, source_target_pairs={{0,2},{1,7},{2,4},{3,1},{4,6},{5,3},{6,0},{7,5},{8,10},{9,15},{10,... | collective-permute-start | bytes 835592 | tf_op jit(solution)/shard_map/ppermute | solution.py:43

commit v11 on v10

--- a/solution.py
+++ b/solution.py
@@ -433,7 +433,7 @@
     out[SEG:, :] = jnp.where(iota((16, COLS), 0) == 0, end, 0.0).astype(BF16)
 
 
-BLOCK = 512
+BLOCK = 1024
 TALL = 384
 
 

time: 113 us -> 112 us (level)
  no operation moved by 1% of the time
where the time goes in v11:
time: 112 us
  waiting for transfers between devices  48.3 us (43%)
  starting transfers between devices  39.8 us (36%)
  Pallas kernels  22 us (20%)
  local copies, waits for them, and re-layouts  1.43 us (1%)
    ppermute x25, waiting for transfers between devices, move(): return lax.ppermute(value, ('seq', 'mp'), pairs)  46.3 us
    ppermute x25, starting transfers between devices, move(): return lax.ppermute(value, ('seq', 'mp'), pairs)  33.7 us
    pallas_call x17, Pallas kernels, call(): pl.pallas_call(body, out_shape=outs, in_specs=[SMEM if i == scalars else...  19.5 us
    ppermute x1, starting transfers between devices, shards(): above = lax.ppermute(head, 'seq', [(i, i - 1) for i in range(1, count)])  4.18 us
    pallas_call x1, Pallas kernels, output(): pl.pallas_call(output_kernel, grid=(TOK // BLOCK,), out_shape=shape((TOK,...  2.52 us
  transfers between devices with their start and end apart: 27, of which 14 were waited for; matrix products, arithmetic and copies ran while one was open for 1% of the time, Pallas kernels for 13%

profile of v11, /device:TPU:2, one launch (start us, length us, event | category | flops | bytes accessed | tf_op | source)
XLA Modules:
  0.0 111.8 jit_solution(4353050263142210569)
XLA Ops:
  0.7 2.0 %shard_map.82 = (bf16[2048,512]{1,0:T(8,128)(2,1)S(1)}, s32[16,128]{1,0:T(8,128)S(1)}, f32[8,640]{1,0:T(8,128)S(1)}, f32[8,640]{1,0:T(8,128)S(1)}) custom-call(s32[16,128]{1,0:T(8,128)S(1)} %bitcast.3, bf16[2048,512]{1,0:T(8,128)(2,1)} %tokens_in.1), custom_call_target="tpu_custom_call" | custom-call | flops 268435456 | bytes 2097152 | tf_op jit(solution)/shard_map/pallas_call | solution.py:107
  2.8 4.2 %collective-permute-start = (f32[8,640]{1,0:T(8,128)S(1)}, f32[8,640]{1,0:T(8,128)S(1)}, u32[]{:S(2)}, u32[]{:S(2)}) collective-permute-start(f32[8,640]{1,0:T(8,128)S(1)} %get-tuple-element.44.head), channel_id=1, source_target_pairs={{8,0},{16,8},{24,16},{32,24},{40,32},{48,40},{56,48},{64,56},{72,6... | collective-permute-start | bytes 61448 | tf_op jit(solution)/shard_map/ppermute | solution.py:522
  6.9 1.9 %collective-permute-start.1 = (f32[8,640]{1,0:T(8,128)S(1)}, f32[8,640]{1,0:T(8,128)S(1)}, u32[]{:S(2)}, u32[]{:S(2)}) collective-permute-start(f32[8,640]{1,0:T(8,128)S(1)} %get-tuple-element.45), channel_id=1, source_target_pairs={{0,8},{8,16},{16,24},{24,32},{32,40},{40,48},{48,56},{56,64},{64,7... | collective-permute-start | bytes 61448 | tf_op jit(solution)/shard_map/ppermute | solution.py:523
  10.6 2.0 %collective-permute-done.1.below = f32[8,640]{1,0:T(8,128)S(1)} collective-permute-done((f32[8,640]{1,0:T(8,128)S(1)}, f32[8,640]{1,0:T(8,128)S(1)}, u32[]{:S(2)}, u32[]{:S(2)}) %collective-permute-start.1) | collective-permute-done | bytes 20512 | tf_op jit(solution)/shard_map/ppermute | solution.py:523
  13.5 3.2 %collective-permute-start.3 = (bf16[272,512]{1,0:T(8,128)(2,1)S(1)}, bf16[272,512]{1,0:T(8,128)(2,1)S(1)}, u32[]{:S(2)}, u32[]{:S(2)}) collective-permute-start(bf16[272,512]{1,0:T(8,128)(2,1)S(1)} %get-tuple-element.46.refs_0_), channel_id=1, source_target_pairs={{0,6},{1,3},{2,0},{3,5},{4,2},{5,7},{6,4},{7,1},{8,14},{9,11},{10,... | collective-permute-start | bytes 835592 | tf_op jit(solution)/shard_map/ppermute | solution.py:43
  16.7 6.3 %collective-permute-done.2.refs_1_ = bf16[272,512]{1,0:T(8,128)(2,1)S(1)} collective-permute-done((bf16[272,512]{1,0:T(8,128)(2,1)S(1)}, bf16[272,512]{1,0:T(8,128)(2,1)S(1)}, u32[]{:S(2)}, u32[]{:S(2)}) %collective-permute-start.2) | collective-permute-done | bytes 278560 | tf_op jit(solution)/shard_map/ppermute | solution.py:43
  23.0 2.9 %shard_map.85 = (bf16[4096,256]{1,0:T(8,128)(2,1)S(1)}, bf16[4096,256]{1,0:T(8,128)(2,1)S(1)}, bf16[4096,256]{1,0:T(8,128)(2,1)S(1)}, bf16[272,512]{1,0:T(8,128)(2,1)S(1)}) custom-call(bf16[4096,256]{1,0:T(8,128)(2,1)} %refs_0_.1, bf16[4096,256]{1,0:T(8,128)(2,1)} %refs_1_.1, bf16[4096,256]{1,0:T(8,128)(2,1)} %refs_2_.1, ...), custom_call_target="tpu_custom_call", output_to_operand_aliasing={{3}: (3, {})} | custom-call | bytes 12582912 | tf_op jit(solution)/shard_map/pallas_call | solution.py:107
  26.6 4.1 %collective-permute-done.4.refs_3_ = bf16[272,512]{1,0:T(8,128)(2,1)S(1)} collective-permute-done((bf16[272,512]{1,0:T(8,128)(2,1)S(1)}, bf16[272,512]{1,0:T(8,128)(2,1)S(1)}, u32[]{:S(2)}, u32[]{:S(2)}) %collective-permute-start.4) | collective-permute-done | bytes 278560 | tf_op jit(solution)/shard_map/ppermute | solution.py:43
  30.8 1.6 %shard_map.86 = (f32[272,256]{1,0:T(8,128)S(1)}, f32[256,256]{1,0:T(8,128)S(1)}, f32[256,256]{1,0:T(8,128)S(1)}) custom-call(s32[32]{0:T(128)S(1)} %dynamic-slice_bitcast_fusion.info.refs_0_, bf16[272,512]{1,0:T(8,128)(2,1)S(1)} %get-tuple-element.46.refs_0_, bf16[272,512]{1,0:T(8,128)(2,1)S(1)} %collective-permute-done.2.refs_1_, ...), custom_call_target="tpu_custom_call" | custom-call | flops 855638016 | bytes 3145728 | tf_op jit(solution)/shard_map/pallas_call | solution.py:107
  32.4 1.3 %shard_map.87.refs_10_.refs_4_ = bf16[272,512]{1,0:T(8,128)(2,1)S(1)} custom-call(s32[32]{0:T(128)S(1)} %dynamic-slice_bitcast_fusion.info.refs_0_, bf16[272,512]{1,0:T(8,128)(2,1)S(1)} %get-tuple-element.46.refs_0_, bf16[272,512]{1,0:T(8,128)(2,1)S(1)} %collective-permute-done.2.refs_1_, bf16[272,512]{1,0:T(8,128)(2,1)S(1)} %collective-permute-done.3.refs_2_, ...), custom_call_target="tpu_custom_call" | custom-call | tf_op jit(solution)/shard_map/pallas_call | solution.py:107
  33.6 1.4 %collective-permute-start.12 = (bf16[272,512]{1,0:T(8,128)(2,1)S(1)}, bf16[272,512]{1,0:T(8,128)(2,1)S(1)}, u32[]{:S(2)}, u32[]{:S(2)}) collective-permute-start(bf16[272,512]{1,0:T(8,128)(2,1)S(1)} %shard_map.87.refs_10_.refs_4_), channel_id=1, source_target_pairs={{0,32},{1,225},{2,34},{3,227},{4,36},{5,229},{6,38},{7,231},{8,40}... | collective-permute-start | bytes 835592 | tf_op jit(solution)/shard_map/ppermute | solution.py:43
  35.0 4.9 %collective-permute-start.14 = (bf16[272,512]{1,0:T(8,128)(2,1)S(1)}, bf16[272,512]{1,0:T(8,128)(2,1)S(1)}, u32[]{:S(2)}, u32[]{:S(2)}) collective-permute-start(bf16[272,512]{1,0:T(8,128)(2,1)S(1)} %shard_map.87.refs_10_.refs_4_), channel_id=1, source_target_pairs={{0,224},{1,33},{2,226},{3,35},{4,228},{5,37},{6,230},{7,39},{8,232... | collective-permute-start | bytes 835592 | tf_op jit(solution)/shard_map/ppermute | solution.py:43
  41.2 6.2 %collective-permute-start.10 = (bf16[272,256]{1,0:T(8,128)(2,1)S(1)}, bf16[272,256]{1,0:T(8,128)(2,1)S(1)}, u32[]{:S(2)}, u32[]{:S(2)}) collective-permute-start(bf16[272,256]{1,0:T(8,128)(2,1)S(1)} %shard_map.88.refs_1_.refs_0_), channel_id=1, source_target_pairs={{0,16},{1,17},{2,18},{3,19},{4,20},{5,21},{6,22},{7,23},{8,24},{9,... | collective-permute-start | bytes 417800 | tf_op jit(solution)/shard_map/ppermute | solution.py:43
  47.4 3.2 %collective-permute-start.15 = (bf16[272,512]{1,0:T(8,128)(2,1)S(1)}, bf16[272,512]{1,0:T(8,128)(2,1)S(1)}, u32[]{:S(2)}, u32[]{:S(2)}) collective-permute-start(bf16[272,512]{1,0:T(8,128)(2,1)S(1)} %collective-permute-done.14.refs_6_), channel_id=1, source_target_pairs={{0,224},{1,33},{2,226},{3,35},{4,228},{5,37},{6,230},{7,39},{8,232... | collective-permute-start | bytes 835592 | tf_op jit(solution)/shard_map/ppermute | solution.py:43
  50.7 1.2 %collective-permute-done.10.refs_3_.refs_2_ = bf16[272,256]{1,0:T(8,128)(2,1)S(1)} collective-permute-done((bf16[272,256]{1,0:T(8,128)(2,1)S(1)}, bf16[272,256]{1,0:T(8,128)(2,1)S(1)}, u32[]{:S(2)}, u32[]{:S(2)}) %collective-permute-start.10) | collective-permute-done | bytes 139296 | tf_op jit(solution)/shard_map/ppermute | solution.py:43
  51.9 2.2 %collective-permute-done.11.refs_4_.refs_3_ = bf16[272,256]{1,0:T(8,128)(2,1)S(1)} collective-permute-done((bf16[272,256]{1,0:T(8,128)(2,1)S(1)}, bf16[272,256]{1,0:T(8,128)(2,1)S(1)}, u32[]{:S(2)}, u32[]{:S(2)}) %collective-permute-start.11) | collective-permute-done | bytes 139296 | tf_op jit(solution)/shard_map/ppermute | solution.py:43
  55.1 1.7 %collective-permute-done.13.refs_0_ = bf16[272,512]{1,0:T(8,128)(2,1)S(1)} collective-permute-done((bf16[272,512]{1,0:T(8,128)(2,1)S(1)}, bf16[272,512]{1,0:T(8,128)(2,1)S(1)}, u32[]{:S(2)}, u32[]{:S(2)}) %collective-permute-start.13) | collective-permute-done | bytes 278560 | tf_op jit(solution)/shard_map/ppermute | solution.py:43
  57.5 3.2 %collective-permute-start.18 = (bf16[272,512]{1,0:T(8,128)(2,1)S(1)}, bf16[272,512]{1,0:T(8,128)(2,1)S(1)}, u32[]{:S(2)}, u32[]{:S(2)}) collective-permute-start(bf16[272,512]{1,0:T(8,128)(2,1)S(1)} %get-tuple-element.57.refs_6_), channel_id=1, source_target_pairs={{0,224},{1,33},{2,226},{3,35},{4,228},{5,37},{6,230},{7,39},{8,232... | collective-permute-start | bytes 835592 | tf_op jit(solution)/shard_map/ppermute | solution.py:43
  60.7 2.1 %shard_map.91 = (f32[4,2,272,256]{3,2,1,0:T(8,128)S(1)}, f32[4,2,272,128]{3,2,1,0:T(8,128)S(1)}, f32[8,128]{1,0:T(8,128)S(1)}) custom-call(s32[32]{0:T(128)S(1)} %dynamic-slice_bitcast_fusion.info.refs_0_, bf16[272,256]{1,0:T(8,128)(2,1)S(1)} %shard_map.88.refs_1_.refs_0_, ...), custom_call_target="tpu_custom_call", output_to_operand_aliasing={{0}: (8, {}), {1}: (9, {})} | custom-call | flops 855638016 | bytes 4194304 | tf_op jit(solution)/shard_map/pallas_call | solution.py:107
  62.8 3.1 %collective-permute-done.16.refs_0_ = bf16[272,512]{1,0:T(8,128)(2,1)S(1)} collective-permute-done((bf16[272,512]{1,0:T(8,128)(2,1)S(1)}, bf16[272,512]{1,0:T(8,128)(2,1)S(1)}, u32[]{:S(2)}, u32[]{:S(2)}) %collective-permute-start.16) | collective-permute-done | bytes 278560 | tf_op jit(solution)/shard_map/ppermute | solution.py:43
  67.1 1.1 %shard_map.93 = (f32[4,2,272,256]{3,2,1,0:T(8,128)S(1)}, f32[4,2,272,128]{3,2,1,0:T(8,128)S(1)}, f32[8,128]{1,0:T(8,128)}) custom-call(s32[32]{0:T(128)S(1)} %dynamic-slice_bitcast_fusion.info.refs_0_, bf16[272,256]{1,0:T(8,128)(2,1)S(1)} %shard_map.88.refs_1_.refs_0_, ...), custom_call_target="tpu_custom_call", output_to_operand_aliasing={{0}: (7, {}), {1}: (8, {})} | custom-call | flops 855638016 | bytes 4194304 | tf_op jit(solution)/shard_map/pallas_call | solution.py:107
  68.2 6.6 %collective-permute-done.17.refs_5_ = bf16[272,512]{1,0:T(8,128)(2,1)S(1)} collective-permute-done((bf16[272,512]{1,0:T(8,128)(2,1)S(1)}, bf16[272,512]{1,0:T(8,128)(2,1)S(1)}, u32[]{:S(2)}, u32[]{:S(2)}) %collective-permute-start.17) | collective-permute-done | bytes 278560 | tf_op jit(solution)/shard_map/ppermute | solution.py:43
  75.7 5.2 %collective-permute-start.19 = (bf16[272,256]{1,0:T(8,128)(2,1)S(1)}, bf16[272,256]{1,0:T(8,128)(2,1)S(1)}, u32[]{:S(2)}, u32[]{:S(2)}) collective-permute-start(bf16[272,256]{1,0:T(8,128)(2,1)S(1)} %get-tuple-element.66), channel_id=1, source_target_pairs={{0,24},{1,25},{2,26},{3,27},{4,28},{5,29},{6,30},{7,31},{8,0},{9,1... | collective-permute-start | bytes 417800 | tf_op jit(solution)/shard_map/ppermute | solution.py:43
  81.3 1.2 %collective-permute-start.21 = (bf16[272,256]{1,0:T(8,128)(2,1)S(1)}, bf16[272,256]{1,0:T(8,128)(2,1)S(1)}, u32[]{:S(2)}, u32[]{:S(2)}) collective-permute-start(bf16[272,256]{1,0:T(8,128)(2,1)S(1)} %get-tuple-element.68), channel_id=1, source_target_pairs={{0,8},{1,9},{2,10},{3,11},{4,12},{5,13},{6,14},{7,15},{8,16},{9,17... | collective-permute-start | bytes 417800 | tf_op jit(solution)/shard_map/ppermute | solution.py:43
  82.5 1.4 %collective-permute-done.19.b = bf16[272,256]{1,0:T(8,128)(2,1)S(1)} collective-permute-done((bf16[272,256]{1,0:T(8,128)(2,1)S(1)}, bf16[272,256]{1,0:T(8,128)(2,1)S(1)}, u32[]{:S(2)}, u32[]{:S(2)}) %collective-permute-start.19) | collective-permute-done | bytes 139296 | tf_op jit(solution)/shard_map/ppermute | solution.py:43
  83.9 3.6 %collective-permute-done.20.c = bf16[272,256]{1,0:T(8,128)(2,1)S(1)} collective-permute-done((bf16[272,256]{1,0:T(8,128)(2,1)S(1)}, bf16[272,256]{1,0:T(8,128)(2,1)S(1)}, u32[]{:S(2)}, u32[]{:S(2)}) %collective-permute-start.20) | collective-permute-done | bytes 139296 | tf_op jit(solution)/shard_map/ppermute | solution.py:43
  88.7 1.3 %collective-permute-done.22.other = bf16[272,256]{1,0:T(8,128)(2,1)S(1)} collective-permute-done((bf16[272,256]{1,0:T(8,128)(2,1)S(1)}, bf16[272,256]{1,0:T(8,128)(2,1)S(1)}, u32[]{:S(2)}, u32[]{:S(2)}) %collective-permute-start.22) | collective-permute-done | bytes 139296 | tf_op jit(solution)/shard_map/ppermute | solution.py:43
  90.0 1.3 %shard_map.96 = (f32[272,512]{1,0:T(8,128)S(1)}, f32[272,512]{1,0:T(8,128)S(1)}, bf16[272,512]{1,0:T(8,128)(2,1)S(1)}, bf16[272,512]{1,0:T(8,128)(2,1)S(1)}) custom-call(s32[32]{0:T(128)S(1)} %dynamic-slice_bitcast_fusion.info.refs_0_, bf16[272,256]{1,0:T(8,128)(2,1)S(1)} %shard_map.95.attended, bf16[272,256]{1,0:T(8,128)(2,1)S(1)} %collective-permute-done.22.other, ...), custom_call_target="tpu_custom_call" | custom-call | flops 570425344 | bytes 4194304 | tf_op jit(solution)/shard_map/pallas_call | solution.py:107
  91.4 3.2 %collective-permute-start.26 = (bf16[272,512]{1,0:T(8,128)(2,1)S(1)}, bf16[272,512]{1,0:T(8,128)(2,1)S(1)}, u32[]{:S(2)}, u32[]{:S(2)}) collective-permute-start(bf16[272,512]{1,0:T(8,128)(2,1)S(1)} %get-tuple-element.74), channel_id=1, source_target_pairs={{0,6},{1,3},{2,0},{3,5},{4,2},{5,7},{6,4},{7,1},{8,14},{9,11},{10,... | collective-permute-start | bytes 835592 | tf_op jit(solution)/shard_map/ppermute | solution.py:43
  94.6 6.8 %collective-permute-done.24.b = bf16[272,512]{1,0:T(8,128)(2,1)S(1)} collective-permute-done((bf16[272,512]{1,0:T(8,128)(2,1)S(1)}, bf16[272,512]{1,0:T(8,128)(2,1)S(1)}, u32[]{:S(2)}, u32[]{:S(2)}) %collective-permute-start.24) | collective-permute-done | bytes 278560 | tf_op jit(solution)/shard_map/ppermute | solution.py:43
  102.0 7.3 %collective-permute-done.25.first = bf16[272,512]{1,0:T(8,128)(2,1)S(1)} collective-permute-done((bf16[272,512]{1,0:T(8,128)(2,1)S(1)}, bf16[272,512]{1,0:T(8,128)(2,1)S(1)}, u32[]{:S(2)}, u32[]{:S(2)}) %collective-permute-start.25) | collective-permute-done | bytes 278560 | tf_op jit(solution)/shard_map/ppermute | solution.py:43
  109.3 2.5 %shard_map.99 = bf16[2048,512]{1,0:T(8,128)(2,1)} custom-call(f32[272,512]{1,0:T(8,128)S(1)} %get-tuple-element.71.own, bf16[272,512]{1,0:T(8,128)(2,1)S(1)} %collective-permute-done.25.first, bf16[272,512]{1,0:T(8,128)(2,1)S(1)} %collective-permute-done.26.second, bf16[2048,384]{1,0:T(8,128)(2,1)S(1)} %shard_map.98.hot, ...), custom_call_target="tpu_custom_call" | custom-call | flops 2147483648 | bytes 6291456 | tf_op jit(solution)/shard_map/pallas_call | solution.py:463
  (49 shorter events, 11.3 us)
Async XLA Ops:
  0.0 0.7 copy-start.1
  2.7 7.8 %copy-start.2 = (f32[4096]{0:T(1024)S(1)}, f32[4096]{0:T(1024)}, u32[]{:S(2)}) copy-start(f32[4096]{0:T(1024)} %param.10) | copy-start | bytes 49156
  2.8 7.9 %collective-permute-start = (f32[8,640]{1,0:T(8,128)S(1)}, f32[8,640]{1,0:T(8,128)S(1)}, u32[]{:S(2)}, u32[]{:S(2)}) collective-permute-start(f32[8,640]{1,0:T(8,128)S(1)} %get-tuple-element.44.head), channel_id=1, source_target_pairs={{8,0},{16,8},{24,16},{32,24},{40,32},{48,40},{56,48},{64,56},{72,6... | collective-permute-start | bytes 61448 | tf_op jit(solution)/shard_map/ppermute | solution.py:522
  6.9 5.7 %collective-permute-start.1 = (f32[8,640]{1,0:T(8,128)S(1)}, f32[8,640]{1,0:T(8,128)S(1)}, u32[]{:S(2)}, u32[]{:S(2)}) collective-permute-start(f32[8,640]{1,0:T(8,128)S(1)} %get-tuple-element.45), channel_id=1, source_target_pairs={{0,8},{8,16},{16,24},{24,32},{32,40},{40,48},{48,56},{56,64},{64,7... | collective-permute-start | bytes 61448 | tf_op jit(solution)/shard_map/ppermute | solution.py:523
  13.4 9.6 %collective-permute-start.2 = (bf16[272,512]{1,0:T(8,128)(2,1)S(1)}, bf16[272,512]{1,0:T(8,128)(2,1)S(1)}, u32[]{:S(2)}, u32[]{:S(2)}) collective-permute-start(bf16[272,512]{1,0:T(8,128)(2,1)S(1)} %get-tuple-element.46.refs_0_), channel_id=1, source_target_pairs={{0,2},{1,7},{2,4},{3,1},{4,6},{5,3},{6,0},{7,5},{8,10},{9,15},{10,... | collective-permute-start | bytes 835592 | tf_op jit(solution)/shard_map/ppermute | solution.py:43
  13.5 13.0 %collective-permute-start.3 = (bf16[272,512]{1,0:T(8,128)(2,1)S(1)}, bf16[272,512]{1,0:T(8,128)(2,1)S(1)}, u32[]{:S(2)}, u32[]{:S(2)}) collective-permute-start(bf16[272,512]{1,0:T(8,128)(2,1)S(1)} %get-tuple-element.46.refs_0_), channel_id=1, source_target_pairs={{0,6},{1,3},{2,0},{3,5},{4,2},{5,7},{6,4},{7,1},{8,14},{9,11},{10,... | collective-permute-start | bytes 835592 | tf_op jit(solution)/shard_map/ppermute | solution.py:43
  23.0 7.8 %collective-permute-start.4 = (bf16[272,512]{1,0:T(8,128)(2,1)S(1)}, bf16[272,512]{1,0:T(8,128)(2,1)S(1)}, u32[]{:S(2)}, u32[]{:S(2)}) collective-permute-start(bf16[272,512]{1,0:T(8,128)(2,1)S(1)} %collective-permute-done.2.refs_1_), channel_id=1, source_target_pairs={{0,2},{1,7},{2,4},{3,1},{4,6},{5,3},{6,0},{7,5},{8,10},{9,15},{10,... | collective-permute-start | bytes 835592 | tf_op jit(solution)/shard_map/ppermute | solution.py:43
  25.9 4.8 %collective-permute-start.5 = (bf16[272,512]{1,0:T(8,128)(2,1)S(1)}, bf16[272,512]{1,0:T(8,128)(2,1)S(1)}, u32[]{:S(2)}, u32[]{:S(2)}) collective-permute-start(bf16[272,512]{1,0:T(8,128)(2,1)S(1)} %get-tuple-element.47), channel_id=1, source_target_pairs={{0,1},{1,0},{2,3},{3,2},{4,5},{5,4},{6,7},{7,6},{8,9},{9,8},{10,11... | collective-permute-start | bytes 835592 | tf_op jit(solution)/shard_map/ppermute | solution.py:43
  26.0 6.3 %collective-permute-start.6 = (bf16[272,512]{1,0:T(8,128)(2,1)S(1)}, bf16[272,512]{1,0:T(8,128)(2,1)S(1)}, u32[]{:S(2)}, u32[]{:S(2)}) collective-permute-start(bf16[272,512]{1,0:T(8,128)(2,1)S(1)} %collective-permute-done.2.refs_1_), channel_id=1, source_target_pairs={{0,1},{1,0},{2,3},{3,2},{4,5},{5,4},{6,7},{7,6},{8,9},{9,8},{10,11... | collective-permute-start | bytes 835592 | tf_op jit(solution)/shard_map/ppermute | solution.py:43
  26.5 5.8 %collective-permute-start.7 = (bf16[272,512]{1,0:T(8,128)(2,1)S(1)}, bf16[272,512]{1,0:T(8,128)(2,1)S(1)}, u32[]{:S(2)}, u32[]{:S(2)}) collective-permute-start(bf16[272,512]{1,0:T(8,128)(2,1)S(1)} %collective-permute-done.3.refs_2_), channel_id=1, source_target_pairs={{0,1},{1,0},{2,3},{3,2},{4,5},{5,4},{6,7},{7,6},{8,9},{9,8},{10,11... | collective-permute-start | bytes 835592 | tf_op jit(solution)/shard_map/ppermute | solution.py:43
  30.8 1.6 %collective-permute-start.8 = (bf16[272,512]{1,0:T(8,128)(2,1)S(1)}, bf16[272,512]{1,0:T(8,128)(2,1)S(1)}, u32[]{:S(2)}, u32[]{:S(2)}) collective-permute-start(bf16[272,512]{1,0:T(8,128)(2,1)S(1)} %collective-permute-done.4.refs_3_), channel_id=1, source_target_pairs={{0,1},{1,0},{2,3},{3,2},{4,5},{5,4},{6,7},{7,6},{8,9},{9,8},{10,11... | collective-permute-start | bytes 835592 | tf_op jit(solution)/shard_map/ppermute | solution.py:43
  33.6 13.8 %collective-permute-start.12 = (bf16[272,512]{1,0:T(8,128)(2,1)S(1)}, bf16[272,512]{1,0:T(8,128)(2,1)S(1)}, u32[]{:S(2)}, u32[]{:S(2)}) collective-permute-start(bf16[272,512]{1,0:T(8,128)(2,1)S(1)} %shard_map.87.refs_10_.refs_4_), channel_id=1, source_target_pairs={{0,32},{1,225},{2,34},{3,227},{4,36},{5,229},{6,38},{7,231},{8,40}... | collective-permute-start | bytes 835592 | tf_op jit(solution)/shard_map/ppermute | solution.py:43
  35.0 12.4 %collective-permute-start.14 = (bf16[272,512]{1,0:T(8,128)(2,1)S(1)}, bf16[272,512]{1,0:T(8,128)(2,1)S(1)}, u32[]{:S(2)}, u32[]{:S(2)}) collective-permute-start(bf16[272,512]{1,0:T(8,128)(2,1)S(1)} %shard_map.87.refs_10_.refs_4_), channel_id=1, source_target_pairs={{0,224},{1,33},{2,226},{3,35},{4,228},{5,37},{6,230},{7,39},{8,232... | collective-permute-start | bytes 835592 | tf_op jit(solution)/shard_map/ppermute | solution.py:43
  39.9 14.2 %copy-start = (bf16[256,4096]{1,0:T(8,128)(2,1)S(1)}, bf16[256,4096]{1,0:T(8,128)(2,1)}, u32[]{:S(2)}) copy-start(bf16[256,4096]{1,0:T(8,128)(2,1)} %w_out.1) | copy-start | bytes 6291460
  41.0 9.7 %collective-permute-start.9 = (bf16[272,256]{1,0:T(8,128)(2,1)S(1)}, bf16[272,256]{1,0:T(8,128)(2,1)S(1)}, u32[]{:S(2)}, u32[]{:S(2)}) collective-permute-start(bf16[272,256]{1,0:T(8,128)(2,1)S(1)} %shard_map.88.refs_1_.refs_0_), channel_id=1, source_target_pairs={{0,8},{1,9},{2,10},{3,11},{4,12},{5,13},{6,14},{7,15},{8,16},{9,17... | collective-permute-start | bytes 417800 | tf_op jit(solution)/shard_map/ppermute | solution.py:43
  41.2 10.7 %collective-permute-start.10 = (bf16[272,256]{1,0:T(8,128)(2,1)S(1)}, bf16[272,256]{1,0:T(8,128)(2,1)S(1)}, u32[]{:S(2)}, u32[]{:S(2)}) collective-permute-start(bf16[272,256]{1,0:T(8,128)(2,1)S(1)} %shard_map.88.refs_1_.refs_0_), channel_id=1, source_target_pairs={{0,16},{1,17},{2,18},{3,19},{4,20},{5,21},{6,22},{7,23},{8,24},{9,... | collective-permute-start | bytes 417800 | tf_op jit(solution)/shard_map/ppermute | solution.py:43
  47.4 6.7 %collective-permute-start.11 = (bf16[272,256]{1,0:T(8,128)(2,1)S(1)}, bf16[272,256]{1,0:T(8,128)(2,1)S(1)}, u32[]{:S(2)}, u32[]{:S(2)}) collective-permute-start(bf16[272,256]{1,0:T(8,128)(2,1)S(1)} %shard_map.88.refs_1_.refs_0_), channel_id=1, source_target_pairs={{0,24},{1,25},{2,26},{3,27},{4,28},{5,29},{6,30},{7,31},{8,0},{9,1... | collective-permute-start | bytes 417800 | tf_op jit(solution)/shard_map/ppermute | solution.py:43
  47.4 9.4 %collective-permute-start.13 = (bf16[272,512]{1,0:T(8,128)(2,1)S(1)}, bf16[272,512]{1,0:T(8,128)(2,1)S(1)}, u32[]{:S(2)}, u32[]{:S(2)}) collective-permute-start(bf16[272,512]{1,0:T(8,128)(2,1)S(1)} %collective-permute-done.12.refs_5_), channel_id=1, source_target_pairs={{0,32},{1,225},{2,34},{3,227},{4,36},{5,229},{6,38},{7,231},{8,40}... | collective-permute-start | bytes 835592 | tf_op jit(solution)/shard_map/ppermute | solution.py:43
  47.4 9.4 %collective-permute-start.15 = (bf16[272,512]{1,0:T(8,128)(2,1)S(1)}, bf16[272,512]{1,0:T(8,128)(2,1)S(1)}, u32[]{:S(2)}, u32[]{:S(2)}) collective-permute-start(bf16[272,512]{1,0:T(8,128)(2,1)S(1)} %collective-permute-done.14.refs_6_), channel_id=1, source_target_pairs={{0,224},{1,33},{2,226},{3,35},{4,228},{5,37},{6,230},{7,39},{8,232... | collective-permute-start | bytes 835592 | tf_op jit(solution)/shard_map/ppermute | solution.py:43
  55.0 33.7 %collective-permute-start.23 = (bf16[4,256,512]{2,1,0:T(8,128)(2,1)S(1)}, bf16[4,256,512]{2,1,0:T(8,128)(2,1)S(1)}, u32[]{:S(2)}, u32[]{:S(2)}) collective-permute-start(bf16[4,256,512]{2,1,0:T(8,128)(2,1)S(1)} %get-tuple-element.69), channel_id=1, source_target_pairs={{0,1},{1,0},{2,3},{3,2},{4,5},{5,4},{6,7},{7,6},{8,9},{9,8},{10,11... | collective-permute-start | bytes 3145736 | tf_op jit(solution)/shard_map/ppermute | solution.py:43
  57.4 8.5 %collective-permute-start.16 = (bf16[272,512]{1,0:T(8,128)(2,1)S(1)}, bf16[272,512]{1,0:T(8,128)(2,1)S(1)}, u32[]{:S(2)}, u32[]{:S(2)}) collective-permute-start(bf16[272,512]{1,0:T(8,128)(2,1)S(1)} %get-tuple-element.56.refs_5_), channel_id=1, source_target_pairs={{0,32},{1,225},{2,34},{3,227},{4,36},{5,229},{6,38},{7,231},{8,40}... | collective-permute-start | bytes 835592 | tf_op jit(solution)/shard_map/ppermute | solution.py:43
  57.5 9.6 %collective-permute-start.18 = (bf16[272,512]{1,0:T(8,128)(2,1)S(1)}, bf16[272,512]{1,0:T(8,128)(2,1)S(1)}, u32[]{:S(2)}, u32[]{:S(2)}) collective-permute-start(bf16[272,512]{1,0:T(8,128)(2,1)S(1)} %get-tuple-element.57.refs_6_), channel_id=1, source_target_pairs={{0,224},{1,33},{2,226},{3,35},{4,228},{5,37},{6,230},{7,39},{8,232... | collective-permute-start | bytes 835592 | tf_op jit(solution)/shard_map/ppermute | solution.py:43
  66.4 8.4 %collective-permute-start.17 = (bf16[272,512]{1,0:T(8,128)(2,1)S(1)}, bf16[272,512]{1,0:T(8,128)(2,1)S(1)}, u32[]{:S(2)}, u32[]{:S(2)}) collective-permute-start(bf16[272,512]{1,0:T(8,128)(2,1)S(1)} %shard_map.92.refs_4_), channel_id=1, source_target_pairs={{0,32},{1,225},{2,34},{3,227},{4,36},{5,229},{6,38},{7,231},{8,40}... | collective-permute-start | bytes 835592 | tf_op jit(solution)/shard_map/ppermute | solution.py:43
  75.7 8.2 %collective-permute-start.19 = (bf16[272,256]{1,0:T(8,128)(2,1)S(1)}, bf16[272,256]{1,0:T(8,128)(2,1)S(1)}, u32[]{:S(2)}, u32[]{:S(2)}) collective-permute-start(bf16[272,256]{1,0:T(8,128)(2,1)S(1)} %get-tuple-element.66), channel_id=1, source_target_pairs={{0,24},{1,25},{2,26},{3,27},{4,28},{5,29},{6,30},{7,31},{8,0},{9,1... | collective-permute-start | bytes 417800 | tf_op jit(solution)/shard_map/ppermute | solution.py:43
  80.9 6.6 %collective-permute-start.20 = (bf16[272,256]{1,0:T(8,128)(2,1)S(1)}, bf16[272,256]{1,0:T(8,128)(2,1)S(1)}, u32[]{:S(2)}, u32[]{:S(2)}) collective-permute-start(bf16[272,256]{1,0:T(8,128)(2,1)S(1)} %get-tuple-element.67), channel_id=1, source_target_pairs={{0,16},{1,17},{2,18},{3,19},{4,20},{5,21},{6,22},{7,23},{8,24},{9,... | collective-permute-start | bytes 417800 | tf_op jit(solution)/shard_map/ppermute | solution.py:43
  81.3 6.2 %collective-permute-start.21 = (bf16[272,256]{1,0:T(8,128)(2,1)S(1)}, bf16[272,256]{1,0:T(8,128)(2,1)S(1)}, u32[]{:S(2)}, u32[]{:S(2)}) collective-permute-start(bf16[272,256]{1,0:T(8,128)(2,1)S(1)} %get-tuple-element.68), channel_id=1, source_target_pairs={{0,8},{1,9},{2,10},{3,11},{4,12},{5,13},{6,14},{7,15},{8,16},{9,17... | collective-permute-start | bytes 417800 | tf_op jit(solution)/shard_map/ppermute | solution.py:43
  88.6 1.4 %collective-permute-start.22 = (bf16[272,256]{1,0:T(8,128)(2,1)S(1)}, bf16[272,256]{1,0:T(8,128)(2,1)S(1)}, u32[]{:S(2)}, u32[]{:S(2)}) collective-permute-start(bf16[272,256]{1,0:T(8,128)(2,1)S(1)} %shard_map.95.attended), channel_id=1, source_target_pairs={{0,1},{1,0},{2,3},{3,2},{4,5},{5,4},{6,7},{7,6},{8,9},{9,8},{10,11... | collective-permute-start | bytes 417800 | tf_op jit(solution)/shard_map/ppermute | solution.py:43
  91.3 10.1 %collective-permute-start.24 = (bf16[272,512]{1,0:T(8,128)(2,1)S(1)}, bf16[272,512]{1,0:T(8,128)(2,1)S(1)}, u32[]{:S(2)}, u32[]{:S(2)}) collective-permute-start(bf16[272,512]{1,0:T(8,128)(2,1)S(1)} %get-tuple-element.73), channel_id=1, source_target_pairs={{0,2},{1,7},{2,4},{3,1},{4,6},{5,3},{6,0},{7,5},{8,10},{9,15},{10,... | collective-permute-start | bytes 835592 | tf_op jit(solution)/shard_map/ppermute | solution.py:43
  91.4 10.6 %collective-permute-start.26 = (bf16[272,512]{1,0:T(8,128)(2,1)S(1)}, bf16[272,512]{1,0:T(8,128)(2,1)S(1)}, u32[]{:S(2)}, u32[]{:S(2)}) collective-permute-start(bf16[272,512]{1,0:T(8,128)(2,1)S(1)} %get-tuple-element.74), channel_id=1, source_target_pairs={{0,6},{1,3},{2,0},{3,5},{4,2},{5,7},{6,4},{7,1},{8,14},{9,11},{10,... | collective-permute-start | bytes 835592 | tf_op jit(solution)/shard_map/ppermute | solution.py:43
  101.5 7.8 %collective-permute-start.25 = (bf16[272,512]{1,0:T(8,128)(2,1)S(1)}, bf16[272,512]{1,0:T(8,128)(2,1)S(1)}, u32[]{:S(2)}, u32[]{:S(2)}) collective-permute-start(bf16[272,512]{1,0:T(8,128)(2,1)S(1)} %shard_map.97), channel_id=1, source_target_pairs={{0,2},{1,7},{2,4},{3,1},{4,6},{5,3},{6,0},{7,5},{8,10},{9,15},{10,... | collective-permute-start | bytes 835592 | tf_op jit(solution)/shard_map/ppermute | solution.py:43
